TPU v7x, 32 devices: a whole 2x2x4 slice. The times are simulated.
32 devices in a mesh: section: 2 (over x), replica: 4 (over z), shard: 4 (over y, core).
Axes of the slice: x: 2, y: 2, z: 4, core: 2. Of those that a mesh axis runs over, the one named last changes fastest.
Arguments:
- tokens_in: bfloat16 [2048, 2048], P(('replica', 'shard')), may hold values from -6 to 6
- positions: int32 [2048], P(('replica', 'shard')), may hold values from 0 to 63, as said below
- attn_gain: float32 [2, 2048], P('section'), may hold values from 0.25 to 1.75
- qkv_weight: bfloat16 [2, 2048, 3072], P('section', 'shard'), may hold values from -0.125 to 0.125
- out_weight: bfloat16 [2, 2048, 2048], P('section', 'shard'), may hold values from -0.375 to 0.375
- mlp_gain: float32 [2, 2048], P('section'), may hold values from 0.25 to 1.75
- gate_up_weight: bfloat16 [2, 2048, 16384], P('section', 'shard'), may hold values from -0.125 to 0.125
- down_weight: bfloat16 [2, 8192, 2048], P('section', 'shard'), may hold values from -0.0625 to 0.0625
- cotangent: bfloat16 [2048, 2048], P(('replica', 'shard')), may hold values from -6 to 6
Outputs:
- block_out: bfloat16 [2, 2048, 2048], P('section', ('replica', 'shard'))
- grad_in: float32 [2, 2048, 2048], P('section', ('replica', 'shard'))
- attn_gain_grad: float32 [2, 2048], P('section')
- qkv_grad: float32 [2, 2048, 3072], P('section', ('replica', 'shard'))
- out_grad: float32 [2, 2048, 2048], P('section', ('replica', 'shard'))
- mlp_gain_grad: float32 [2, 2048], P('section')
- gate_up_grad: float32 [2, 2048, 16384], P('section', ('replica', 'shard'))
- down_grad: float32 [2, 8192, 2048], P('section', ('replica', 'shard'))
Inputs may be any that keep to these rules, and one draw needn't show every extreme that they name: `positions`: within each sequence of 64 tokens the first position is 0 and every later one is the previous plus 1 or is 0; a token sees the earlier tokens back to the last position 0.
All inputs are finite; a program needn't handle non-finite values.
Results may differ from a plain program's by a relative error of at most 0.023.
Values may be sent and summed in bfloat16 or wider, within the bound.
A program may use at most 640 MiB of HBM per device.

v0:
```python
import jax
import jax.numpy as jnp
from jax import lax
from jax.sharding import PartitionSpec as P

D = 2048
HEADS = 32
KV_HEADS = 8
HEAD = 64
FF = 8192
SEQ = 64
MICRO = 2


EPSILON = 1e-05
ROPE_BASE = 500000.0
CONTRACT_LAST = (((1,), (1,)), ((), ()))


def shifted(value, axis, steps):
    count = lax.axis_size(axis)
    initial, last = (max(0, -steps), min(count, count - steps))
    return lax.ppermute(value, axis, [(source, source + steps) for source in range(initial, last)])


def rope_tables(seq_pos):
    half_index = jnp.arange(HEAD // 2, dtype=jnp.float32)
    frequency = jnp.power(ROPE_BASE, -2.0 * half_index / HEAD)
    angles = seq_pos.astype(jnp.float32)[:, None] * frequency[None, :]
    return (jnp.cos(angles)[:, None, :], jnp.sin(angles)[:, None, :])


def rotate(vectors, cosine, sine):
    first_half = vectors[..., : HEAD // 2]
    second_half = vectors[..., HEAD // 2 :]
    return jnp.concatenate(
        [first_half * cosine - second_half * sine, second_half * cosine + first_half * sine], -1
    )


def unrotate(grads_rot, cosine, sine):
    first_half = grads_rot[..., : HEAD // 2]
    second_half = grads_rot[..., HEAD // 2 :]
    return jnp.concatenate(
        [first_half * cosine + second_half * sine, second_half * cosine - first_half * sine], -1
    )


def visible(seq_pos):
    row_index = jnp.arange(SEQ)[:, None]
    col_index = jnp.arange(SEQ)[None, :]
    return (col_index <= row_index) & (row_index - col_index <= seq_pos[:, None])


def rms_parts(values):
    inverse = lax.rsqrt(jnp.mean(values * values, -1, keepdims=True) + EPSILON)
    return (values * inverse, inverse)


def norm_back(grad_normed, normal_rows, inverse, gain_row):
    scaled = grad_normed * gain_row
    gain_term = jnp.sum(grad_normed * normal_rows, 0)
    grad_rows = inverse * (scaled - normal_rows * jnp.mean(scaled * normal_rows, -1, keepdims=True))
    return (grad_rows, gain_term)


def layer_forward(layer_in, seq_pos, gain_pair, matrices):
    qkv_full, out_full, gate_up_full, down_full = matrices
    state = layer_in.astype(jnp.float32)
    normal_one, scale_one = rms_parts(state)
    normed = (normal_one * gain_pair[0]).astype(jnp.bfloat16)
    projected = jnp.dot(normed, qkv_full, preferred_element_type=jnp.float32)
    cosine, sine = rope_tables(seq_pos)
    kv_cols = KV_HEADS * HEAD
    queries = rotate(projected[:, :D].reshape(SEQ, HEADS, HEAD), cosine, sine).astype(jnp.bfloat16)
    keys_in = rotate(
        projected[:, D : D + kv_cols].reshape(SEQ, KV_HEADS, HEAD), cosine, sine
    ).astype(jnp.bfloat16)
    values_in = projected[:, D + kv_cols :].reshape(SEQ, KV_HEADS, HEAD).astype(jnp.bfloat16)
    grouped = queries.reshape(SEQ, KV_HEADS, HEADS // KV_HEADS, HEAD)
    scores = jnp.einsum(
        "qgrd,kgd->grqk", grouped, keys_in, preferred_element_type=jnp.float32
    ) * HEAD ** (-0.5)
    masked = jnp.where(visible(seq_pos), scores, -1e30)
    top_score = jnp.max(masked, -1, keepdims=True)
    expon = jnp.exp(masked - top_score)
    total = jnp.sum(expon, -1, keepdims=True)
    log_total = top_score + jnp.log(total)
    probs = (expon / total).astype(jnp.bfloat16)
    attended = (
        jnp.einsum("grqk,kgd->qgrd", probs, values_in, preferred_element_type=jnp.float32)
        .reshape(SEQ, D)
        .astype(jnp.bfloat16)
    )
    middle = state + jnp.dot(attended, out_full, preferred_element_type=jnp.float32)
    normal_two, scale_two = rms_parts(middle)
    normed_two = (normal_two * gain_pair[1]).astype(jnp.bfloat16)
    gate_up = jnp.dot(normed_two, gate_up_full, preferred_element_type=jnp.float32)
    hidden_act = (jax.nn.silu(gate_up[:, :FF]) * gate_up[:, FF:]).astype(jnp.bfloat16)
    result = middle + jnp.dot(hidden_act, down_full, preferred_element_type=jnp.float32)
    kept_vals = (
        normal_one,
        scale_one,
        normed,
        queries,
        keys_in,
        values_in,
        log_total,
        attended,
        normal_two,
        scale_two,
        normed_two,
        gate_up,
        hidden_act,
    )
    return (result, kept_vals)


def attention_back(grad_out, queries, keys_in, values_in, log_total, allowed):
    grouped = queries.reshape(SEQ, KV_HEADS, HEADS // KV_HEADS, HEAD)
    grad_grouped = grad_out.reshape(SEQ, KV_HEADS, HEADS // KV_HEADS, HEAD)
    scale_factor = HEAD ** (-0.5)
    scores = (
        jnp.einsum("qgrd,kgd->grqk", grouped, keys_in, preferred_element_type=jnp.float32)
        * scale_factor
    )
    probs = jnp.exp(jnp.where(allowed, scores, -1e30) - log_total)
    grad_probs = jnp.einsum(
        "qgrd,kgd->grqk", grad_grouped, values_in, preferred_element_type=jnp.float32
    )
    grad_values = jnp.einsum(
        "grqk,qgrd->kgd",
        probs.astype(jnp.bfloat16),
        grad_grouped,
        preferred_element_type=jnp.float32,
    )
    row_dot = jnp.sum(probs * grad_probs, -1, keepdims=True)
    grad_scores = (probs * (grad_probs - row_dot)).astype(jnp.bfloat16)
    grad_queries = (
        jnp.einsum(
            "grqk,kgd->qgrd", grad_scores, keys_in, preferred_element_type=jnp.float32
        ).reshape(SEQ, HEADS, HEAD)
        * scale_factor
    )
    grad_keys = (
        jnp.einsum("grqk,qgrd->kgd", grad_scores, grouped, preferred_element_type=jnp.float32)
        * scale_factor
    )
    return (grad_queries, grad_keys, grad_values)


def layer_backward(upstream, seq_pos, kept_vals, gain_pair, matrices):
    (
        normal_one,
        scale_one,
        normed,
        queries,
        keys_in,
        values_in,
        log_total,
        attended,
        normal_two,
        scale_two,
        normed_two,
        gate_up,
        hidden_act,
    ) = kept_vals
    qkv_full, out_full, gate_up_full, down_full = matrices
    grad_hidden = lax.dot_general(
        upstream, down_full, CONTRACT_LAST, preferred_element_type=jnp.float32
    )
    gate_part = gate_up[:, :FF]
    up_part = gate_up[:, FF:]
    sigmoid_gate = jax.nn.sigmoid(gate_part)
    grad_gate = grad_hidden * up_part * sigmoid_gate * (1.0 + gate_part * (1.0 - sigmoid_gate))
    grad_up = grad_hidden * gate_part * sigmoid_gate
    grad_gate_up = jnp.concatenate([grad_gate, grad_up], 1).astype(jnp.bfloat16)
    grad_normed_two = lax.dot_general(
        grad_gate_up, gate_up_full, CONTRACT_LAST, preferred_element_type=jnp.float32
    )
    grad_middle_norm, gain_two = norm_back(grad_normed_two, normal_two, scale_two, gain_pair[1])
    grad_middle = upstream.astype(jnp.float32) + grad_middle_norm
    grad_branch = grad_middle.astype(jnp.bfloat16)
    grad_attended = lax.dot_general(
        grad_branch, out_full, CONTRACT_LAST, preferred_element_type=jnp.float32
    ).astype(jnp.bfloat16)
    grad_queries, grad_keys, grad_values = attention_back(
        grad_attended, queries, keys_in, values_in, log_total, visible(seq_pos)
    )
    cosine, sine = rope_tables(seq_pos)
    kv_cols = KV_HEADS * HEAD
    grad_projected = jnp.concatenate(
        [
            unrotate(grad_queries, cosine, sine).reshape(SEQ, D),
            unrotate(grad_keys, cosine, sine).reshape(SEQ, kv_cols),
            grad_values.reshape(SEQ, kv_cols),
        ],
        1,
    ).astype(jnp.bfloat16)
    grad_normed = lax.dot_general(
        grad_projected, qkv_full, CONTRACT_LAST, preferred_element_type=jnp.float32
    )
    grad_state_norm, gain_one = norm_back(grad_normed, normal_one, scale_one, gain_pair[0])
    return (
        grad_middle + grad_state_norm,
        (grad_projected, grad_branch, grad_gate_up, upstream),
        (gain_one, gain_two),
    )


def row_terms(left_op, right_op):
    return lax.dot_general(
        left_op, right_op, (((0,), (0,)), ((), ())), preferred_element_type=jnp.float32
    )


def store_at(buffers, values_now, slot_at, is_valid):
    return jax.tree.map(
        lambda buffer, member: jnp.where(
            is_valid, lax.dynamic_update_index_in_dim(buffer, member, slot_at, 0), buffer
        ),
        buffers,
        values_now,
    )


def empty_like_stack(values_now):
    return jax.tree.map(lambda member: jnp.zeros((MICRO,) + member.shape, member.dtype), values_now)


def on_device(
    tokens_in,
    positions,
    attn_gain,
    qkv_weight,
    out_weight,
    mlp_gain,
    gate_up_weight,
    down_weight,
    cotangent,
):
    sections = lax.axis_size("section")
    section_at = lax.axis_index("section")
    is_first = section_at == 0
    is_last = section_at == sections - 1
    tick_count = MICRO + sections - 1
    gain_pair = (attn_gain[0], mlp_gain[0])
    gathered = (
        lax.all_gather(qkv_weight, "shard", axis=1, tiled=True),
        lax.all_gather(out_weight, "shard", axis=1, tiled=True),
        lax.all_gather(gate_up_weight, "shard", axis=1, tiled=True),
        lax.all_gather(down_weight, "shard", axis=1, tiled=True),
    )
    matrices = tuple((stacked[0] for stack_index, stacked in enumerate(gathered)))
    kept_all = None
    received = jnp.zeros((SEQ, D), jnp.bfloat16)
    block_out = jnp.zeros(tokens_in.shape, jnp.bfloat16)
    for tick_at in range(tick_count):
        micro_at = tick_at - section_at
        is_valid = (micro_at >= 0) & (micro_at < MICRO)
        clipped = jnp.clip(micro_at, 0, MICRO - 1)
        start_row = clipped * SEQ
        fresh_rows = lax.dynamic_slice_in_dim(tokens_in, start_row, SEQ, 0)
        layer_in = jnp.where(is_first, fresh_rows, received)
        seq_pos = lax.dynamic_slice_in_dim(positions, start_row, SEQ, 0)
        result, kept_vals = layer_forward(layer_in, seq_pos, gain_pair, matrices)
        result_low = result.astype(jnp.bfloat16)
        block_out = jnp.where(
            is_valid,
            lax.dynamic_update_slice_in_dim(block_out, result_low, start_row, 0),
            block_out,
        )
        if kept_all is None:
            kept_all = empty_like_stack(kept_vals)
        kept_all = store_at(kept_all, kept_vals, clipped, is_valid)
        if tick_at + 1 < tick_count:
            received = shifted(result_low, "section", 1)
    received_grad = jnp.zeros((SEQ, D), jnp.bfloat16)
    grad_in = jnp.zeros(tokens_in.shape, jnp.float32)
    grads_kept = None
    gain_sums = (jnp.zeros((D,), jnp.float32), jnp.zeros((D,), jnp.float32))
    for tick_at in range(tick_count):
        micro_at = tick_at - (sections - 1 - section_at)
        is_valid = (micro_at >= 0) & (micro_at < MICRO)
        clipped = jnp.clip(micro_at, 0, MICRO - 1)
        start_row = clipped * SEQ
        given_rows = lax.dynamic_slice_in_dim(cotangent, start_row, SEQ, 0)
        upstream = jnp.where(is_last, given_rows, received_grad)
        seq_pos = lax.dynamic_slice_in_dim(positions, start_row, SEQ, 0)
        kept_now = jax.tree.map(
            lambda buffer: lax.dynamic_index_in_dim(buffer, clipped, 0, keepdims=False), kept_all
        )
        grad_state, grad_parts, gain_terms = layer_backward(
            upstream, seq_pos, kept_now, gain_pair, matrices
        )
        grad_low = grad_state.astype(jnp.bfloat16)
        grad_value = jnp.where(
            is_first, grad_state, lax.optimization_barrier(grad_low).astype(jnp.float32)
        )
        grad_in = jnp.where(
            is_valid, lax.dynamic_update_slice_in_dim(grad_in, grad_value, start_row, 0), grad_in
        )
        if grads_kept is None:
            grads_kept = empty_like_stack(grad_parts)
        grads_kept = store_at(grads_kept, grad_parts, clipped, is_valid)
        gain_sums = (
            gain_sums[0] + jnp.where(is_valid, gain_terms[0], 0.0),
            gain_sums[1] + jnp.where(is_valid, gain_terms[1], 0.0),
        )
        if tick_at + 1 < tick_count:
            received_grad = shifted(grad_low, "section", -1)

    def flatten(stacked):
        return stacked.reshape((MICRO * SEQ,) + stacked.shape[2:])

    pairs = (
        (flatten(kept_all[2]), flatten(grads_kept[0])),
        (flatten(kept_all[7]), flatten(grads_kept[1])),
        (flatten(kept_all[10]), flatten(grads_kept[2])),
        (flatten(kept_all[12]), flatten(grads_kept[3])),
    )
    weight_grads = [
        lax.psum_scatter(
            row_terms(left_op, right_op), ("replica", "shard"), scatter_dimension=0, tiled=True
        )
        for left_op, right_op in pairs
    ]
    total_gains = lax.psum((gain_sums[0], gain_sums[1]), ("replica", "shard"))
    return (
        block_out[None],
        grad_in[None],
        total_gains[0][None],
        weight_grads[0][None],
        weight_grads[1][None],
        total_gains[1][None],
        weight_grads[2][None],
        weight_grads[3][None],
    )


def solution(mesh):
    placed = (
        P(("replica", "shard"), None),
        P(("replica", "shard")),
        P("section", None),
        P("section", "shard", None),
        P("section", "shard", None),
        P("section", None),
        P("section", "shard", None),
        P("section", "shard", None),
        P(("replica", "shard"), None),
    )
    return jax.shard_map(
        on_device,
        mesh=mesh,
        in_specs=placed,
        out_specs=(
            P("section", ("replica", "shard"), None),
            P("section", ("replica", "shard"), None),
            P("section", None),
            P("section", ("replica", "shard"), None),
            P("section", ("replica", "shard"), None),
            P("section", None),
            P("section", ("replica", "shard"), None),
            P("section", ("replica", "shard"), None),
        ),
        check_vma=False,
    )
```

profile of v0, /device:TPU:11, one launch (start us, length us, event | category | flops | bytes accessed | tf_op | source)
XLA Modules:
  0.0 3487.2 jit_solution(10220671255095278189)
XLA Ops:
  18.6 74.7 %all-gather.5.cloned.1.call-done = bf16[1,2048,3072]{2,1,0:T(8,128)(2,1)} async-done(((bf16[1,512,3072]{2,1,0:T(8,128)(2,1)}), bf16[1,2048,3072]{2,1,0:T(8,128)(2,1)}) %all-gather.5.cloned.1.call-update) | async-done | bytes 12582928 | tf_op jit(solution)/shard_map/all_gather | solution.py:249
  93.3 6.9 fusion.34
  107.5 2.2 fusion.193
  113.6 39.6 %all-gather.7.cloned.1.call-done = bf16[1,2048,2048]{2,1,0:T(8,128)(2,1)} async-done(((bf16[1,512,2048]{2,1,0:T(8,128)(2,1)}), bf16[1,2048,2048]{2,1,0:T(8,128)(2,1)}) %all-gather.7.cloned.1.call-update) | async-done | bytes 8388624 | tf_op jit(solution)/shard_map/all_gather | solution.py:250
  153.2 5.1 multiply_reduce_fusion.5
  160.9 386.5 %all-gather.9.cloned.1.call-done = bf16[1,2048,16384]{2,1,0:T(8,128)(2,1)} async-done(((bf16[1,512,16384]{2,1,0:T(8,128)(2,1)}), bf16[1,2048,16384]{2,1,0:T(8,128)(2,1)}) %all-gather.9.cloned.1.call-update) | async-done | bytes 67108880 | tf_op jit(solution)/shard_map/all_gather | solution.py:251
  547.5 4.3 broadcast_in_dim.259
  551.8 38.6 %bitcast_dynamic-update-slice_fusion = (f32[2,64,16384]{2,1,0:T(8,128)}, f32[64,16384]{1,0:T(8,128)}) fusion(f32[2,64,16384]{2,1,0:T(8,128)} %broadcast_in_dim.259, s32[]{:T(128)S(6)} %min.19, pred[]{:T(512)S(6)} %and.37, bf16[1,2048,16384]{2,1,0:T(8,128)(2,1)} %all-gather.9.cloned.1.call-done, f32[64,2048]{1,0:T(8,128)S(1)} %get-tuple-element.150, ...), kind=kOutput, calls=%fused_computation.56 | convolution fusion | flops 4296409088 | bytes 76030472 | tf_op jit(solution)/shard_map/dot_general | solution.py:98
  591.9 4.2 bitcast_dynamic-update-slice_fusion.1
  596.2 154.3 %all-gather.11.cloned.1.call-done = bf16[1,8192,2048]{2,1,0:T(8,128)(2,1)} async-done(((bf16[1,2048,2048]{2,1,0:T(8,128)(2,1)}), bf16[1,8192,2048]{2,1,0:T(8,128)(2,1)}) %all-gather.11.cloned.1.call-update) | async-done | bytes 33554448 | tf_op jit(solution)/shard_map/all_gather | solution.py:252
  751.3 17.6 select_dynamic-update-slice_fusion.5
  768.9 1.8 collective-permute-start
  775.1 3.6 collective-permute-done
  779.5 6.9 fusion.32
  795.0 2.0 fusion.346
  798.5 5.3 multiply_reduce_fusion.4
  803.8 28.7 fusion.49
  832.6 4.2 fusion.147
  836.9 14.6 select_dynamic-update-slice_fusion.4
  854.9 2.2 fusion.194
  859.8 1.9 copy.275
  864.5 7.0 fusion.30
  877.1 2.1 subtract_convert_fusion
  884.9 2.0 fusion.347
  887.7 5.3 multiply_reduce_fusion.3
  894.1 28.8 fusion.48
  922.9 9.5 dynamic-slice_bitcast_fusion
  932.6 18.7 fusion.103
  951.4 29.4 fusion.225
  982.3 2.0 bitcast_dynamic-update-slice_fusion.6
  985.1 6.8 fusion.77
  991.9 2.0 copy.283
  996.7 2.5 fusion.195
  999.3 2.5 constant_dynamic-slice_fusion.1
  1008.2 9.4 fusion.220
  1018.6 4.5 collective-permute-start.2
  1025.9 1.9 copy.276
  1027.8 1.8 fusion.235
  1029.6 18.5 fusion.100
  1048.1 29.1 fusion.215
  1077.9 2.4 fusion.239
  1081.0 6.7 fusion.80
  1089.3 1.7 multiply_reduce_fusion.1
  1093.7 9.4 fusion.210
  1104.2 3.6 collective-permute-start.3
  1111.7 18.1 fusion.97
  1129.8 29.1 fusion.205
  1159.6 2.0 fusion.238
  1161.7 9.8 convolution_bitcast_fusion.3
  1179.5 6.8 fusion.83
  1187.4 2.5 multiply_reduce_fusion
  1199.2 10.4 convolution_bitcast_fusion.2
  1209.7 4.3 fusion.146
  1214.0 25.2 convolution_bitcast_fusion.1
  1239.4 2.6 broadcast_in_dim.288
  1243.7 3.5 fusion.117
  1247.2 3.5 fusion.118
  1250.7 47.0 %convolution_bitcast_fusion = f32[2048,16384]{1,0:T(8,128)} fusion(bf16[2,64,2048]{2,1,0:T(8,128)(2,1)S(1)} %copy-done.25, bf16[2,64,16384]{2,1,0:T(8,128)(2,1)} %fusion.118), kind=kOutput, calls=%fused_computation | convolution fusion | flops 8589934592 | bytes 138936320 | tf_op jit(solution)/shard_map/dot_general | solution.py:212
  1300.1 14.0 fusion.92
  1315.7 9.3 fusion.200
  1325.3 50.8 %all-reduce = (f32[1,2048]{1,0:T(1,128)}, f32[1,2048]{1,0:T(1,128)}) all-reduce(f32[1,2048]{1,0:T(1,128)S(1)} %bitcast.756, f32[1,2048]{1,0:T(1,128)S(1)} %bitcast.757), channel_id=1, replica_groups=mesh['section'=2,'replica'=4,'shard'=4] {'replica','shard'}, use_global_device_ids=true, to_apply=%region_24.25 | all-reduce | flops 4096 | bytes 32768 | tf_op jit(solution)/shard_map/psum | solution.py:328
  1376.2 223.5 %reduce-scatter.5.cloned.1.call-done = f32[128,3072]{1,0:T(8,128)} async-done(((f32[2048,3072]{1,0:T(8,128)}), f32[128,3072]{1,0:T(8,128)}) %reduce-scatter.5.cloned.1.call-update) | async-done | bytes 1572880 | tf_op jit(solution)/shard_map/reduce_scatter | solution.py:323
  1599.6 640.2 %reduce-scatter.11.cloned.1.call-done = f32[512,2048]{1,0:T(8,128)} async-done(((f32[8192,2048]{1,0:T(8,128)}), f32[512,2048]{1,0:T(8,128)}) %reduce-scatter.11.cloned.1.call-update) | async-done | bytes 4194320 | tf_op jit(solution)/shard_map/reduce_scatter | solution.py:323
  2239.8 1240.4 %reduce-scatter.9.cloned.1.call-done = f32[128,16384]{1,0:T(8,128)} async-done(((f32[2048,16384]{1,0:T(8,128)}), f32[128,16384]{1,0:T(8,128)}) %reduce-scatter.9.cloned.1.call-update) | async-done | bytes 8388624 | tf_op jit(solution)/shard_map/reduce_scatter | solution.py:323
  (487 shorter events, 114.9 us)
Async XLA Ops:
  7.2 86.1 %all-gather.5.cloned.1.call-start = ((), (), s32[]{:S(2)}) async-start(), calls=%async_computation.4 | async-start | bytes 15728640 | tf_op jit(solution)/shard_map/all_gather | solution.py:249
  7.9 145.3 %all-gather.7.cloned.1.call-start = ((), (), s32[]{:S(2)}) async-start(), calls=%async_computation.5 | async-start | bytes 10485760 | tf_op jit(solution)/shard_map/all_gather | solution.py:250
  8.7 538.8 %all-gather.9.cloned.1.call-start = ((), (), s32[]{:S(2)}) async-start(), calls=%async_computation.6 | async-start | bytes 83886080 | tf_op jit(solution)/shard_map/all_gather | solution.py:251
  9.4 83.9 %copy-start.61 = (f32[1,2048]{1,0:T(1,128)S(1)}, f32[1,2048]{1,0:T(1,128)}, u32[]{:S(2)}) copy-start(f32[1,2048]{1,0:T(1,128)} %param.11) | copy-start | bytes 24580
  9.4 741.0 %all-gather.11.cloned.1.call-start = ((), (), s32[]{:S(2)}) async-start(), calls=%async_computation.7 | async-start | bytes 41943040 | tf_op jit(solution)/shard_map/all_gather | solution.py:252
  10.0 1366.2 %reduce-scatter.7.cloned.1.call-start = ((), (), s32[]{:S(2)}) async-start(), calls=%async_computation.9 | async-start | bytes 17825792 | tf_op jit(solution)/shard_map/reduce_scatter | solution.py:323
  11.3 91.6 %copy-start.89 = (f32[64,32]{1,0:T(8,128)}, f32[64,32]{1,0:T(8,128)S(1)}, u32[]{:S(2)}) copy-start(f32[64,32]{1,0:T(8,128)S(1)} %copy.155) | copy-start | bytes 24580
  11.4 91.5 %copy-start.90 = (f32[64,32]{1,0:T(8,128)}, f32[64,32]{1,0:T(8,128)S(1)}, u32[]{:S(2)}) copy-start(f32[64,32]{1,0:T(8,128)S(1)} %copy.153) | copy-start | bytes 24580
  14.3 85.9 %copy-start.118 = (f32[64]{0:T(128)}, f32[64]{0:T(128)S(1)}, u32[]{:S(2)}) copy-start(f32[64]{0:T(128)S(1)} %add_rsqrt_fusion.5) | copy-start | bytes 772
  14.4 85.8 %copy-start.125 = (f32[2,64,1]{1,2,0:T(1,128)}, f32[2,64,1]{1,2,0:T(1,128)S(1)}, u32[]{:S(2)}) copy-start(f32[2,64,1]{1,2,0:T(1,128)S(1)} %constant_dynamic-update-slice_fusion.6) | copy-start | bytes 1540
  110.7 47.6 %copy-start.74 = (bf16[64,8,32]{2,0,1:T(8,128)(2,1)}, bf16[64,8,32]{2,0,1:T(8,128)(2,1)S(1)}, u32[]{:S(2)}) copy-start(bf16[64,8,32]{2,0,1:T(8,128)(2,1)S(1)} %get-tuple-element.91) | copy-start | bytes 98308
  159.7 392.1 %copy-start.54 = (bf16[2,64,8,64]{3,1,2,0:T(8,128)(2,1)}, bf16[2,64,8,64]{3,1,2,0:T(8,128)(2,1)S(1)}, u32[]{:S(2)}) copy-start(bf16[2,64,8,64]{3,1,2,0:T(8,128)(2,1)S(1)} %copy_dynamic-update-slice_fusion) | copy-start | bytes 393220
  751.3 20.2 copy-start.75
  768.9 9.7 collective-permute-start
  778.9 74.2 %copy-start.13 = (bf16[64,2048]{1,0:T(8,128)(2,1)}, bf16[64,2048]{1,0:T(8,128)(2,1)S(1)}, u32[]{:S(2)}) copy-start(bf16[64,2048]{1,0:T(8,128)(2,1)S(1)} %get-tuple-element.59) | copy-start | bytes 786436
  803.8 28.8 copy-start.133
  803.8 28.8 copy-start.106
  836.8 16.4 copy-start.121
  836.8 16.5 copy-start.107
  836.8 16.6 copy-start.130
  836.8 16.6 copy-start.134
  836.8 16.7 copy-start.126
  836.8 16.7 copy-start.143
  836.8 16.7 copy-start.94
  836.8 16.7 copy-start.105
  836.8 18.0 copy-start.41
  836.8 18.0 copy-start.43
  851.5 11.8 copy-start.16
  851.5 11.8 collective-permute-start.1
  864.4 67.9 %copy-start.11 = (bf16[64,2048]{1,0:T(8,128)(2,1)}, bf16[64,2048]{1,0:T(8,128)(2,1)S(1)}, u32[]{:S(2)}) copy-start(bf16[64,2048]{1,0:T(8,128)(2,1)S(1)} %get-tuple-element.55) | copy-start | bytes 786436
  893.0 266.6 %copy-start.2 = (f32[64,2048]{1,0:T(8,128)}, f32[64,2048]{1,0:T(8,128)S(1)}, u32[]{:S(2)}) copy-start(f32[64,2048]{1,0:T(8,128)S(1)} %get-tuple-element.162) | copy-start | bytes 1572868
  922.9 9.7 copy-start.52
  932.6 170.5 %copy-start = (f32[2,64,2048]{2,1,0:T(8,128)}, f32[2,64,2048]{2,1,0:T(8,128)S(1)}, u32[]{:S(2)}) copy-start(f32[2,64,2048]{2,1,0:T(8,128)S(1)} %get-tuple-element.186) | copy-start | bytes 3145732
  951.3 29.5 copy-start.132
  951.4 29.5 copy-start.136
  951.4 29.5 copy-start.128
  951.4 29.5 copy-start.141
  991.9 10.1 copy-start.55
  993.9 9.8 copy-start.44
  1003.7 85.3 %copy-start.56 = (bf16[2,64,8,64]{3,1,2,0:T(8,128)(2,1)}, bf16[2,64,8,64]{3,1,2,0:T(8,128)(2,1)S(1)}, u32[]{:S(2)}) copy-start(bf16[2,64,8,64]{3,1,2,0:T(8,128)(2,1)S(1)} %get-tuple-element.189) | copy-start | bytes 393220
  1008.2 15.0 copy-start.80
  1018.6 9.2 collective-permute-start.2
  1029.6 18.5 copy-start.63
  1093.5 9.6 copy-start.69
  1093.7 14.0 copy-start.81
  1093.7 17.1 copy-start.19
  1093.7 17.1 copy-start.53
  1104.2 6.6 collective-permute-start.3
  1129.8 29.1 copy-start.8
  1129.8 29.8 copy-start.23
  1161.7 9.9 copy-start.24
  1161.7 17.8 copy-start.28
  1171.6 428.1 %reduce-scatter.5.cloned.1.call-start = ((), (), s32[]{:S(2)}) async-start(), calls=%async_computation.8 | async-start | bytes 26738688 | tf_op jit(solution)/shard_map/reduce_scatter | solution.py:323
  1198.8 10.8 copy-start.33
  1209.6 1030.2 %reduce-scatter.11.cloned.1.call-start = ((), (), s32[]{:S(2)}) async-start(), calls=%async_computation.11 | async-start | bytes 71303168 | tf_op jit(solution)/shard_map/reduce_scatter | solution.py:323
  1239.2 2241.0 %reduce-scatter.9.cloned.1.call-start = ((), (), s32[]{:S(2)}) async-start(), calls=%async_computation.10 | async-start | bytes 142606336 | tf_op jit(solution)/shard_map/reduce_scatter | solution.py:323
  1300.0 14.1 copy-start.66
  1300.0 14.1 copy-start.84
  1300.0 14.3 copy-start.62
  1300.0 14.3 copy-start.68
  1300.0 14.3 copy-start.72
  1314.1 10.9 copy-start.86
  1315.6 9.6 copy-start.111
  1376.1 2104.1 %copy-start.82 = (f32[1,128,2048]{2,1,0:T(8,128)}, f32[1,128,2048]{2,1,0:T(8,128)S(1)}, u32[]{:S(2)}) copy-start(f32[1,128,2048]{2,1,0:T(8,128)S(1)} %bitcast_dynamic-update-slice_fusion.2) | copy-start | bytes 3145732
  (95 other events, 402.6 us)
Sparse Core Ops, SparseCore 0:
  9.6 83.6 all-gather.4
  94.8 58.2 all-gather.6
  154.7 392.7 all-gather.8
  548.9 201.5 all-gather.10
  1171.7 180.8 reduce-scatter.6
  1357.1 242.4 reduce-scatter.4
  1604.4 635.3 reduce-scatter.10
  2244.7 1235.5 reduce-scatter.8
where the time goes:
time: 3500 us; the launch traced here: 3490 us
  waiting for transfers between devices  2770 us (79%)
  matrix products  486 us (14%)
  local copies, waits for them, and re-layouts  80.7 us (2%)
  other arithmetic  74.4 us (2%)
  blocking collectives  50.8 us (1%)
    reduce_scatter x4, waiting for transfers between devices, on_device(): lax.psum_scatter(row_terms(left_op, right_op), ('replica', 'shard'), scat...  2100 us
    all_gather x1, waiting for transfers between devices, on_device(): lax.all_gather(gate_up_weight, 'shard', axis=1, tiled=True)  387 us
    all_gather x1, waiting for transfers between devices, on_device(): lax.all_gather(down_weight, 'shard', axis=1, tiled=True)  154 us
    dot_general x3, matrix products, layer_forward(): jnp.dot(normed_two, gate_up_full, preferred_element_type=jnp.float32)  96.1 us
    dot_general x4, matrix products, row_terms(): lax.dot_general(left_op, right_op, (((0,), (0,)), ((), ())), preferred_el...  92.4 us
    dot_general x3, matrix products, layer_backward(): lax.dot_general(grad_gate_up, gate_up_full, CONTRACT_LAST, preferred_elem...  87.6 us
    all_gather x1, waiting for transfers between devices, on_device(): lax.all_gather(qkv_weight, 'shard', axis=1, tiled=True)  74.7 us
  transfers between devices with their start and end apart: 12, of which 9 were waited for; matrix products, arithmetic and copies ran while one was open for 7% of the time, Pallas kernels for 0%

commit v1 on v0

v1 whole, which is shorter than its diff:
```python
import jax
import jax.numpy as jnp
from jax import lax
from jax.sharding import PartitionSpec as P

HEADS = 32
KV_HEADS = 8
HEAD = 64
SEQ = 64
EPSILON = 1e-05
ROPE_BASE = 500000.0
BF = jnp.bfloat16
F32 = jnp.float32
CONTRACT_LAST = (((1,), (1,)), ((), ()))
CONTRACT_FIRST = (((0,), (0,)), ((), ()))


def dot(left, right):
    return jnp.dot(left, right, preferred_element_type=F32)


def dot_rows(left, right):
    return lax.dot_general(left, right, CONTRACT_LAST, preferred_element_type=F32)


def dot_tokens(left, right):
    return lax.dot_general(left, right, CONTRACT_FIRST, preferred_element_type=F32)


def rope_tables(seq_pos):
    half_index = jnp.arange(HEAD // 2, dtype=F32)
    frequency = jnp.power(ROPE_BASE, -2.0 * half_index / HEAD)
    angles = seq_pos.astype(F32)[:, None] * frequency[None, :]
    return (jnp.cos(angles)[:, None, :], jnp.sin(angles)[:, None, :])


def rotate(vectors, cosine, sine):
    first_half = vectors[..., : HEAD // 2]
    second_half = vectors[..., HEAD // 2 :]
    return jnp.concatenate(
        [first_half * cosine - second_half * sine, second_half * cosine + first_half * sine], -1
    )


def visible(seq_pos):
    row_index = jnp.arange(SEQ)[None, :, None]
    col_index = jnp.arange(SEQ)[None, None, :]
    return (col_index <= row_index) & (row_index - col_index <= seq_pos[:, :, None])


def rms_parts(values):
    inverse = lax.rsqrt(jnp.mean(values * values, -1, keepdims=True) + EPSILON)
    return (values * inverse, inverse)


def norm_back(grad_normed, normal_rows, inverse, gain_row):
    scaled = grad_normed * gain_row
    gain_term = jnp.sum(grad_normed * normal_rows, 0)
    grad_rows = inverse * (scaled - normal_rows * jnp.mean(scaled * normal_rows, -1, keepdims=True))
    return (grad_rows, gain_term)


def attention_forward(state, tables, allowed, gain, qkv_full, out_full):
    rows = state.shape[0]
    seqs = rows // SEQ
    width = HEADS * HEAD
    kv_cols = KV_HEADS * HEAD
    normal_one, scale_one = rms_parts(state)
    normed = (normal_one * gain).astype(BF)
    projected = dot(normed, qkv_full)
    cosine, sine = tables
    queries = rotate(projected[:, :width].reshape(rows, HEADS, HEAD), cosine, sine).astype(BF)
    keys_in = rotate(
        projected[:, width : width + kv_cols].reshape(rows, KV_HEADS, HEAD), cosine, sine
    ).astype(BF)
    values_in = projected[:, width + kv_cols :].reshape(rows, KV_HEADS, HEAD).astype(BF)
    grouped = queries.reshape(seqs, SEQ, KV_HEADS, HEADS // KV_HEADS, HEAD)
    keys_in = keys_in.reshape(seqs, SEQ, KV_HEADS, HEAD)
    values_in = values_in.reshape(seqs, SEQ, KV_HEADS, HEAD)
    scores = jnp.einsum(
        "sqgrd,skgd->sgrqk", grouped, keys_in, preferred_element_type=F32
    ) * HEAD ** (-0.5)
    masked = jnp.where(allowed[:, None, None], scores, -1e30)
    top_score = jnp.max(masked, -1, keepdims=True)
    expon = jnp.exp(masked - top_score)
    probs = expon / jnp.sum(expon, -1, keepdims=True)
    attended = (
        jnp.einsum("sgrqk,skgd->sqgrd", probs.astype(BF), values_in, preferred_element_type=F32)
        .reshape(rows, width)
        .astype(BF)
    )
    middle = state + dot(attended, out_full)
    return middle, (normal_one, scale_one, normed, grouped, keys_in, values_in, probs, attended)


def attention_backward(grad_out, grouped, keys_in, values_in, probs, tables):
    rows = grad_out.shape[0]
    seqs = rows // SEQ
    scale_factor = HEAD ** (-0.5)
    grad_grouped = grad_out.reshape(seqs, SEQ, KV_HEADS, HEADS // KV_HEADS, HEAD)
    grad_probs = jnp.einsum("sqgrd,skgd->sgrqk", grad_grouped, values_in, preferred_element_type=F32)
    grad_values = jnp.einsum(
        "sgrqk,sqgrd->skgd", probs.astype(BF), grad_grouped, preferred_element_type=F32
    )
    row_dot = jnp.sum(probs * grad_probs, -1, keepdims=True)
    grad_scores = (probs * (grad_probs - row_dot)).astype(BF)
    grad_queries = (
        jnp.einsum("sgrqk,skgd->sqgrd", grad_scores, keys_in, preferred_element_type=F32)
        * scale_factor
    )
    grad_keys = (
        jnp.einsum("sgrqk,sqgrd->skgd", grad_scores, grouped, preferred_element_type=F32)
        * scale_factor
    )
    cosine, sine = tables
    return jnp.concatenate(
        [
            rotate(grad_queries.reshape(rows, HEADS, HEAD), cosine, -sine).reshape(rows, -1),
            rotate(grad_keys.reshape(rows, KV_HEADS, HEAD), cosine, -sine).reshape(rows, -1),
            grad_values.reshape(rows, -1),
        ],
        1,
    ).astype(BF)


def gather_slice(rows):
    return lax.all_gather(rows, "shard", axis=0, tiled=True)


def gather_section(rows):
    return lax.all_gather(rows, ("replica", "shard"), axis=0, tiled=True)


def scatter_slice(partial):
    return lax.psum_scatter(partial, "shard", scatter_dimension=0, tiled=True)


def feed_forward(normed_rows, gate_up_part):
    gate_up = dot(normed_rows, gate_up_part)
    half = gate_up.shape[1] // 2
    gate = gate_up[:, :half]
    hidden = (gate * jax.nn.sigmoid(gate) * gate_up[:, half:]).astype(BF)
    return gate_up, hidden


def feed_backward(upstream, gate_up, down_part):
    half = gate_up.shape[1] // 2
    gate, up = gate_up[:, :half], gate_up[:, half:]
    grad_hidden = dot_rows(upstream, down_part)
    sigmoid = jax.nn.sigmoid(gate)
    grad_gate = grad_hidden * up * sigmoid * (1.0 + gate * (1.0 - sigmoid))
    grad_up = grad_hidden * gate * sigmoid
    return jnp.concatenate([grad_gate, grad_up], 1).astype(BF)


def on_device(
    tokens_in,
    positions,
    attn_gain,
    qkv_weight,
    out_weight,
    mlp_gain,
    gate_up_weight,
    down_weight,
    cotangent,
):
    sections = lax.axis_size("section")
    replicas = lax.axis_size("replica")
    shards = lax.axis_size("shard")
    section_at = lax.axis_index("section")
    replica_at = lax.axis_index("replica")
    shard_at = lax.axis_index("shard")
    is_first = section_at == 0
    is_last = section_at == sections - 1
    rows, width = tokens_in.shape
    seqs = rows // SEQ
    up_steps = [(at, at + 1) for at in range(sections - 1)]
    down_steps = [(at + 1, at) for at in range(sections - 1)]

    tables = rope_tables(positions)
    allowed = visible(positions.reshape(seqs, SEQ))
    gain_one, gain_two = attn_gain[0], mlp_gain[0]

    qkv_full = lax.all_gather(qkv_weight[0], "shard", axis=0, tiled=True)
    out_full = lax.all_gather(out_weight[0], "shard", axis=0, tiled=True)
    gate_up_local = gate_up_weight[0]
    ff = gate_up_local.shape[1] // 2
    ff_part = ff // shards
    gate_up_part = lax.all_to_all(
        gate_up_local.reshape(-1, 2, shards, ff_part), "shard", 2, 0, tiled=True
    ).reshape(width, 2 * ff_part)
    down_part = down_weight[0]

    received = jnp.zeros((rows, width), BF)
    for tick_at in range(sections):
        state = jnp.where(is_first, tokens_in, received).astype(F32)
        middle, kept = attention_forward(state, tables, allowed, gain_one, qkv_full, out_full)
        normal_two, scale_two = rms_parts(middle)
        normed_two = (normal_two * gain_two).astype(BF)
        gate_up, hidden = feed_forward(gather_slice(normed_two), gate_up_part)
        result = middle + scatter_slice(dot(hidden, down_part).astype(BF)).astype(F32)
        block_out = result.astype(BF)
        if tick_at + 1 < sections:
            received = lax.ppermute(block_out, "section", up_steps)
    normal_one, scale_one, normed, grouped, keys_in, values_in, probs, attended = kept

    received_grad = jnp.zeros((rows, width), BF)
    for tick_at in range(sections):
        upstream = jnp.where(is_last, cotangent, received_grad)
        grad_gate_up = feed_backward(gather_slice(upstream), gate_up, down_part)
        grad_normed_two = scatter_slice(dot_rows(grad_gate_up, gate_up_part).astype(BF)).astype(F32)
        grad_rows, gain_term_two = norm_back(grad_normed_two, normal_two, scale_two, gain_two)
        grad_middle = upstream.astype(F32) + grad_rows
        grad_branch = grad_middle.astype(BF)
        grad_attended = dot_rows(grad_branch, out_full).astype(BF)
        grad_projected = attention_backward(
            grad_attended, grouped, keys_in, values_in, probs, tables
        )
        grad_normed = dot_rows(grad_projected, qkv_full)
        grad_rows, gain_term_one = norm_back(grad_normed, normal_one, scale_one, gain_one)
        grad_state = grad_middle + grad_rows
        grad_low = grad_state.astype(BF)
        if tick_at + 1 < sections:
            received_grad = lax.ppermute(grad_low, "section", down_steps)
    grad_in = jnp.where(is_first, grad_state, grad_low.astype(F32))

    both = ("replica", "shard")
    normed_two_all = gather_section(normed_two)
    upstream_all = gather_section(upstream)
    gate_up_all, hidden_all = feed_forward(normed_two_all, gate_up_part)
    grad_gate_up_all = feed_backward(upstream_all, gate_up_all, down_part)

    slice_rows = width // replicas
    left_rows = lax.dynamic_slice_in_dim(normed_two_all, replica_at * slice_rows, slice_rows, 1)
    gate_up_grad = dot_tokens(left_rows, grad_gate_up_all).astype(BF)
    gate_up_grad = lax.all_to_all(
        gate_up_grad.reshape(slice_rows, 2, 1, ff_part), "shard", 0, 2, tiled=True
    ).reshape(slice_rows // shards, 2 * ff).astype(F32)

    ff_rows = ff // (replicas * shards)
    owner = (replica_at * shards) // replicas
    first_col = (replica_at * shards) % replicas * ff_rows
    hidden_rows = lax.dynamic_slice_in_dim(hidden_all, first_col + shard_at * ff_rows, ff_rows, 1)
    for step in range(1, shards):
        target = lax.rem(shard_at + step, shards)
        part = lax.dynamic_slice_in_dim(hidden_all, first_col + target * ff_rows, ff_rows, 1)
        pairs = []
        for at in range(replicas):
            source = at * shards // replicas
            pairs.append((at * shards + source, at * shards + (source + step) % shards))
        sent = lax.ppermute(part, both, pairs)
        hidden_rows = jnp.where(lax.rem(owner + step, shards) == shard_at, sent, hidden_rows)
    down_grad = dot_tokens(hidden_rows, upstream_all)

    attended_rows = lax.all_to_all(attended, both, 1, 0, tiled=True)
    normed_rows = lax.all_to_all(normed, both, 1, 0, tiled=True)
    out_grad = dot_tokens(attended_rows, gather_section(grad_branch))
    qkv_grad = dot_tokens(normed_rows, gather_section(grad_projected))

    gains = jnp.stack([gain_term_one, gain_term_two])
    gains = jnp.sum(lax.all_gather(gains, both, axis=0), 0)
    return (
        block_out[None],
        grad_in[None],
        gains[0][None],
        qkv_grad[None],
        out_grad[None],
        gains[1][None],
        gate_up_grad[None],
        down_grad[None],
    )


def solution(mesh):
    both = ("replica", "shard")
    return jax.shard_map(
        on_device,
        mesh=mesh,
        in_specs=(
            P(both, None),
            P(both),
            P("section", None),
            P("section", "shard", None),
            P("section", "shard", None),
            P("section", None),
            P("section", "shard", None),
            P("section", "shard", None),
            P(both, None),
        ),
        out_specs=(
            P("section", both, None),
            P("section", both, None),
            P("section", None),
            P("section", both, None),
            P("section", both, None),
            P("section", None),
            P("section", both, None),
            P("section", both, None),
        ),
        check_vma=False,
    )
```

time: 3500 us -> 1130 us (0.32)
  waiting for transfers between devices: 2770 us -> 458 us
  matrix products: 486 us -> 299 us
  local copies, waits for them, and re-layouts: 80.7 us -> 165 us
  blocking collectives: 50.8 us -> 104 us
  other arithmetic: 74.4 us -> 34.3 us
    reduce_scatter x4, waiting for transfers between devices: 2100 us -> 80 us  [scatter_slice(): return lax.psum_scatter(partial, 'shard', scatter_dimension=0, tiled=True)]
    all_gather x4 -> x10, waiting for transfers between devices: 655 us -> 241 us  [the longest x1 83.7 us: on_device(): out_full = lax.all_gather(out_weight[0], 'shard', axis=0, tiled=True)]
    dot_general x49 -> x32, matrix products: 486 us -> 293 us  [the longest x9 119 us: dot_rows(): lax.dot_general(left, right, CONTRACT_LAST, preferred_element_type=F32)]
    all_to_all x0 -> x4, waiting for transfers between devices: none -> 110 us  [the longest x1 110 us: on_device(): lax.all_to_all(gate_up_local.reshape(-1, 2, shards, ff_part), 'shard', 2,...]
    all_gather x0 -> x1, blocking collectives: none -> 104 us  [on_device(): gains = jnp.sum(lax.all_gather(gains, both, axis=0), 0)]
    another operation x17 -> x2, local copies, waits for them, and re-layouts: 7.22 us -> 59.2 us  [on_device(): gate_up_local.reshape(-1, 2, shards, ff_part)]
    select_n x46 -> x2, other arithmetic: 53.5 us -> 1.68 us  [on_device(): upstream = jnp.where(is_last, cotangent, received_grad)]
    psum x1 -> x0, blocking collectives: 50.8 us -> none  [on_device(): total_gains = lax.psum((gain_sums[0], gain_sums[1]), ('replica', 'shard'))]
  transfers between devices with their start and end apart: 12 -> 23, of which waited for: 9 -> 14; matrix products, arithmetic and copies ran while one was open for 7% -> 30% of each run, Pallas kernels for 0% -> 0%
where the time goes in v1:
time: 1130 us; the launch traced here: 1120 us
  waiting for transfers between devices  458 us (41%)
  matrix products  299 us (26%)
  local copies, waits for them, and re-layouts  165 us (15%)
  blocking collectives  104 us (9%)
  starting transfers between devices  46.2 us (4%)
  other arithmetic  34.3 us (3%)
  between operations  15.6 us (1%)
    dot_general x9, matrix products, dot_rows(): lax.dot_general(left, right, CONTRACT_LAST, preferred_element_type=F32)  119 us
    dot_general x9, matrix products, dot(): return jnp.dot(left, right, preferred_element_type=F32)  114 us
    all_to_all x1, waiting for transfers between devices, on_device(): lax.all_to_all(gate_up_local.reshape(-1, 2, shards, ff_part), 'shard', 2,...  110 us
    all_gather x1, blocking collectives, on_device(): gains = jnp.sum(lax.all_gather(gains, both, axis=0), 0)  104 us
    all_gather x1, waiting for transfers between devices, on_device(): out_full = lax.all_gather(out_weight[0], 'shard', axis=0, tiled=True)  83.7 us
    all_gather x4, waiting for transfers between devices, gather_section(): return lax.all_gather(rows, ('replica', 'shard'), axis=0, tiled=True)  80.1 us
    reduce_scatter x4, waiting for transfers between devices, scatter_slice(): return lax.psum_scatter(partial, 'shard', scatter_dimension=0, tiled=True)  80 us
    another operation x2, local copies, waits for them, and re-layouts, on_device(): gate_up_local.reshape(-1, 2, shards, ff_part)  59.2 us
  transfers between devices with their start and end apart: 23, of which 14 were waited for; matrix products, arithmetic and copies ran while one was open for 30% of the time, Pallas kernels for 0%

profile of v1, /device:TPU:11, one launch (start us, length us, event | category | flops | bytes accessed | tf_op | source)
XLA Modules:
  0.0 1123.5 jit_solution(3498594597492272265)
XLA Ops:
  8.7 28.4 %reshape_squeeze.3 = bf16[512,2,4,2048]{3,2,1,0:T(4,128)(2,1)} reshape(bf16[1,512,16384]{2,1,0:T(8,128)(2,1)} %param.15) | data formatting | bytes 33554432 | tf_op jit(solution)/shard_map/reshape;squeeze | solution.py:190
  37.0 30.8 %copy.98 = bf16[512,2,4,2048]{3,1,0,2:T(2,128)(2,1)} copy(bf16[512,2,4,2048]{3,2,1,0:T(4,128)(2,1)} %reshape_squeeze.3) | data formatting | bytes 33554432 | tf_op jit(solution)/shard_map/reshape;squeeze | solution.py:190
  67.9 7.8 all-to-all-start
  77.4 28.5 %all-gather.31.cloned.1.call-done = bf16[1,2048,3072]{2,1,0:T(8,128)(2,1)} async-done(((bf16[1,512,3072]{2,1,0:T(8,128)(2,1)}), bf16[1,2048,3072]{2,1,0:T(8,128)(2,1)}) %all-gather.31.cloned.1.call-update) | async-done | bytes 12582928 | tf_op jit(solution)/shard_map/all_gather | solution.py:184
  105.9 6.5 fusion.12
  118.9 3.9 fusion.186
  127.3 83.7 %all-gather.33.cloned.1.call-done = bf16[1,2048,2048]{2,1,0:T(8,128)(2,1)} async-done(((bf16[1,512,2048]{2,1,0:T(8,128)(2,1)}), bf16[1,2048,2048]{2,1,0:T(8,128)(2,1)}) %all-gather.33.cloned.1.call-update) | async-done | bytes 8388624 | tf_op jit(solution)/shard_map/all_gather | solution.py:185
  211.0 4.8 multiply_reduce_fusion.2
  217.1 109.9 %all-to-all-done = bf16[512,2,4,2048]{3,1,0,2:T(2,128)(2,1)} async-done(((bf16[512,2,4,2048]{3,1,0,2:T(2,128)(2,1)}), bf16[512,2,4,2048]{3,1,0,2:T(2,128)(2,1)}, u32[]{:S(2)}, u32[]{:S(2)}) %all-to-all-start) | async-done | bytes 16777248 | tf_op jit(solution)/shard_map/all_to_all | solution.py:189
  327.0 17.3 %copy.179 = bf16[256,8,2,2048]{3,1,2,0:T(8,128)(2,1)} copy(bf16[256,8,2,2048]{3,2,1,0:T(2,128)(2,1)} %bitcast.76) | data formatting | bytes 33554432
  344.3 12.3 %fusion.190 = f32[512,4096]{1,0:T(8,128)S(1)} fusion(bf16[512,2048]{1,0:T(8,128)(2,1)} %all-gather.15.cloned.1.call-done, bf16[2048,4096]{1,0:T(8,128)(2,1)} %bitcast.267), kind=kOutput, calls=%fused_computation.256 | convolution fusion | flops 8589934592 | bytes 27262976 | tf_op jit(solution)/shard_map/dot_general | solution.py:19
  356.6 9.2 fusion.50
  365.8 31.4 %reduce-scatter.5.cloned.1.call-done = bf16[128,2048]{1,0:T(8,128)(2,1)} async-done(((bf16[512,2048]{1,0:T(8,128)(2,1)}), bf16[128,2048]{1,0:T(8,128)(2,1)}) %reduce-scatter.5.cloned.1.call-update) | async-done | bytes 524304 | tf_op jit(solution)/shard_map/reduce_scatter | solution.py:135
  399.7 13.4 %collective-permute-done = bf16[128,2048]{1,0:T(8,128)(2,1)S(1)} collective-permute-done((bf16[128,2048]{1,0:T(8,128)(2,1)S(1)}, bf16[128,2048]{1,0:T(8,128)(2,1)S(1)}, u32[]{:S(2)}, u32[]{:S(2)}) %collective-permute-start) | collective-permute-done | bytes 524320 | tf_op jit(solution)/shard_map/ppermute | solution.py:204
  413.4 6.7 fusion.10
  426.9 2.5 fusion.189
  429.4 3.2 fusion.96
  432.6 2.6 copy.107
  437.8 5.0 multiply_reduce_fusion.1
  444.8 8.6 reduce-scatter.9.cloned.1.call-start
  453.4 14.5 %all-gather.17.cloned.1.call-done = bf16[512,2048]{1,0:T(8,128)(2,1)} async-done(((bf16[128,2048]{1,0:T(8,128)(2,1)}), bf16[512,2048]{1,0:T(8,128)(2,1)}) %all-gather.17.cloned.1.call-update) | async-done | bytes 2097168 | tf_op jit(solution)/shard_map/all_gather | solution.py:127
  468.0 15.0 %fusion.191 = f32[512,4096]{1,0:T(8,128)} fusion(bf16[512,2048]{1,0:T(8,128)(2,1)} %all-gather.17.cloned.1.call-done, bf16[2048,4096]{1,0:T(8,128)(2,1)} %bitcast.268), kind=kOutput, calls=%fused_computation.257 | convolution fusion | flops 8589934592 | bytes 27262976 | tf_op jit(solution)/shard_map/dot_general | solution.py:19
  482.9 9.7 all-gather.19.cloned.1.call-done
  492.6 11.9 %multiply_convert_fusion.6 = (bf16[512,2048]{1,0:T(8,128)(2,1)S(1)}, bf16[512,2048]{1,0:T(8,128)(2,1)S(1)}) fusion(f32[512,4096]{1,0:T(8,128)} %fusion.191, bf16[512,2048]{1,0:T(8,128)(2,1)} %all-gather.19.cloned.1.call-done, bf16[1,2048,2048]{2,1,0:T(8,128)(2,1)} %param.16), kind=kOutput, calls=%fused_computation.51 | convolution fusion | flops 4308598784 | bytes 23068672 | tf_op jit(solution)/shard_map/dot_general | solution.py:23
  504.6 13.5 %fusion.47 = bf16[512,2048]{1,0:T(8,128)(2,1)} fusion(bf16[2048,4096]{1,0:T(8,128)(2,1)} %bitcast.269, bf16[512,2048]{1,0:T(8,128)(2,1)S(1)} %get-tuple-element.20, bf16[512,2048]{1,0:T(8,128)(2,1)S(1)} %get-tuple-element.19), kind=kOutput, calls=%fused_computation.58 | convolution fusion | flops 8599371776 | bytes 23068672 | tf_op jit(solution)/shard_map/dot_general | solution.py:23
  518.4 30.9 %reduce-scatter.9.cloned.1.call-done = bf16[128,2048]{1,0:T(8,128)(2,1)} async-done(((bf16[512,2048]{1,0:T(8,128)(2,1)}), bf16[128,2048]{1,0:T(8,128)(2,1)}) %reduce-scatter.9.cloned.1.call-update) | async-done | bytes 524304 | tf_op jit(solution)/shard_map/reduce_scatter | solution.py:135
  550.6 7.3 fusion.65
  557.9 3.3 reshape.297
  561.2 2.9 copy.116
  575.1 4.7 copy.112
  579.8 3.7 reshape.298
  585.0 9.1 fusion.115
  596.9 10.5 collective-permute-done.1
  608.4 25.0 %all-gather.21.cloned.1.call-done = bf16[512,2048]{1,0:T(8,128)(2,1)} async-done(((bf16[128,2048]{1,0:T(8,128)(2,1)}), bf16[512,2048]{1,0:T(8,128)(2,1)}) %all-gather.21.cloned.1.call-update) | async-done | bytes 2097168 | tf_op jit(solution)/shard_map/all_gather | solution.py:127
  633.4 11.9 %multiply_convert_fusion.4 = (bf16[512,2048]{1,0:T(8,128)(2,1)S(1)}, bf16[512,2048]{1,0:T(8,128)(2,1)S(1)}) fusion(f32[512,4096]{1,0:T(8,128)} %fusion.191, bf16[512,2048]{1,0:T(8,128)(2,1)} %all-gather.21.cloned.1.call-done, bf16[1,2048,2048]{2,1,0:T(8,128)(2,1)} %param.16), kind=kOutput, calls=%fused_computation.49 | convolution fusion | flops 4308598784 | bytes 23068672 | tf_op jit(solution)/shard_map/dot_general | solution.py:23
  645.3 13.6 %fusion.44 = bf16[512,2048]{1,0:T(8,128)(2,1)} fusion(bf16[2048,4096]{1,0:T(8,128)(2,1)} %bitcast.270, bf16[512,2048]{1,0:T(8,128)(2,1)S(1)} %get-tuple-element.18, bf16[512,2048]{1,0:T(8,128)(2,1)S(1)} %get-tuple-element.17), kind=kOutput, calls=%fused_computation.57 | convolution fusion | flops 8599371776 | bytes 23068672 | tf_op jit(solution)/shard_map/dot_general | solution.py:23
  660.4 12.1 %fusion.53 = bf16[512,2048]{1,0:T(8,128)(2,1)} fusion(bf16[1,2048,2048]{2,1,0:T(8,128)(2,1)} %param.16, f32[512,4096]{1,0:T(8,128)} %fusion.191), kind=kOutput, calls=%fused_computation.60 | convolution fusion | flops 4302307328 | bytes 18874368 | tf_op jit(solution)/shard_map/dot_general | solution.py:19
  672.6 17.6 %reduce-scatter.11.cloned.1.call-done = bf16[128,2048]{1,0:T(8,128)(2,1)} async-done(((bf16[512,2048]{1,0:T(8,128)(2,1)}), bf16[128,2048]{1,0:T(8,128)(2,1)}) %reduce-scatter.11.cloned.1.call-update) | async-done | bytes 524304 | tf_op jit(solution)/shard_map/reduce_scatter | solution.py:135
  694.5 6.5 fusion.68
  712.0 3.0 copy.124
  715.0 2.7 reshape.304
  720.5 5.8 all-to-all-start.2
  726.4 9.6 fusion.6
  738.0 34.9 %all-gather.27.cloned.1.call-done = bf16[2048,2048]{1,0:T(8,128)(2,1)} async-done(((bf16[128,2048]{1,0:T(8,128)(2,1)}), bf16[2048,2048]{1,0:T(8,128)(2,1)}) %all-gather.27.cloned.1.call-update) | async-done | bytes 8388624 | tf_op jit(solution)/shard_map/all_gather | solution.py:131
  772.9 42.7 %fusion.192 = f32[2048,4096]{0,1:T(8,128)} fusion(bf16[2048,2048]{1,0:T(8,128)(2,1)} %all-gather.27.cloned.1.call-done, bf16[2048,4096]{1,0:T(8,128)(2,1)} %bitcast.271), kind=kOutput, calls=%fused_computation.258 | convolution fusion | flops 34359738368 | bytes 58720256 | tf_op jit(solution)/shard_map/dot_general | solution.py:19
  815.6 37.4 %all-gather.29.cloned.1.call-done = bf16[2048,2048]{1,0:T(8,128)(2,1)} async-done(((bf16[128,2048]{1,0:T(8,128)(2,1)}), bf16[2048,2048]{1,0:T(8,128)(2,1)}) %all-gather.29.cloned.1.call-update) | async-done | bytes 8388624 | tf_op jit(solution)/shard_map/all_gather | solution.py:131
  853.0 35.6 %multiply_convert_fusion.2 = (bf16[2048,2048]{0,1:T(8,128)(2,1)}, bf16[2048,2048]{0,1:T(8,128)(2,1)}, bf16[2048,2048]{0,1:T(8,128)(2,1)}) fusion(f32[2048,4096]{0,1:T(8,128)} %fusion.192, bf16[2048,2048]{1,0:T(8,128)(2,1)} %all-gather.29.cloned.1.call-done, bf16[1,2048,2048]{2,1,0:T(8,128)(2,1)} %param.16), kind=kOutput, calls=%fused_computation.8 | convolution fusion | flops 17246978048 | bytes 75497472 | tf_op jit(solution)/shard_map/dot_general | solution.py:23
  888.5 5.7 constant_dynamic-slice_fusion
  894.3 3.4 collective-permute-start.2
  897.7 2.7 collective-permute-start.3
  900.4 2.6 collective-permute-start.4
  903.0 15.7 %fusion.32 = bf16[512,4096]{1,0:T(8,128)(2,1)} fusion(bf16[2048,2048]{0,1:T(8,128)(2,1)} %get-tuple-element.15, bf16[2048,2048]{0,1:T(8,128)(2,1)} %get-tuple-element.14, bf16[2048,2048]{1,0:T(8,128)(2,1)} %all-gather.27.cloned.1.call-done, s32[]{:T(128)S(6)} %select_n.90), kind=kOutput, calls=%fused_computation.37 | convolution fusion | flops 8625586176 | bytes 23068676 | tf_op jit(solution)/shard_map/dot_general | solution.py:27
  918.6 7.9 reshape.309
  926.6 5.1 all-to-all-start.3
  931.8 104.5 %all-gather.3 = f32[16,2,2048]{2,1,0:T(2,128)S(1)} all-gather(f32[1,2,2048]{2,1,0:T(2,128)S(1)} %maximum_bitcast_fusion.7), channel_id=4, replica_groups=mesh['section'=2,'replica'=4,'shard'=4] {'replica','shard'}, dimensions={0}, use_global_device_ids=true | all-gather | bytes 278528 | tf_op jit(solution)/shard_map/all_gather | solution.py:261
  1037.1 2.9 select_bitcast_fusion
  1040.0 10.8 convolution_bitcast_fusion.1
  1050.8 5.7 all-to-all-start.1
  1056.4 10.4 convert_bitcast_fusion
  1066.8 14.9 %copy.138 = f32[128,2,4,1,2048]{4,2,1,0,3:T(4,128)} copy(f32[128,2,4,1,2048]{4,1,0,2,3:T(2,128)} %convert_bitcast_fusion) | data formatting | bytes 16777216 | tf_op jit(solution)/shard_map/convert_element_type | solution.py:238
  1081.7 11.1 reshape.310
  1092.9 5.8 convolution_bitcast_fusion.2
  1098.7 7.8 all-gather.23.cloned.1.call-done
  1106.5 10.0 convolution_bitcast_fusion
  (235 shorter events, 69.2 us)
Async XLA Ops:
  7.2 98.8 %all-gather.31.cloned.1.call-start = ((), (), s32[]{:S(2)}) async-start(), calls=%async_computation.20 | async-start | bytes 15728640 | tf_op jit(solution)/shard_map/all_gather | solution.py:184
  7.9 203.1 %all-gather.33.cloned.1.call-start = ((), (), s32[]{:S(2)}) async-start(), calls=%async_computation.21 | async-start | bytes 10485760 | tf_op jit(solution)/shard_map/all_gather | solution.py:185
  67.9 7.8 copy-start.48
  67.9 8.0 copy-start.6
  67.9 38.1 %copy-start.25 = (f32[1,2048]{1,0:T(1,128)S(1)}, f32[1,2048]{1,0:T(1,128)}, u32[]{:S(2)}) copy-start(f32[1,2048]{1,0:T(1,128)} %param.11) | copy-start | bytes 24580
  67.9 259.1 %all-to-all-start = ((bf16[512,2,4,2048]{3,1,0,2:T(2,128)(2,1)}), bf16[512,2,4,2048]{3,1,0,2:T(2,128)(2,1)}, u32[]{:S(2)}, u32[]{:S(2)}) async-start(bf16[512,2,4,2048]{3,1,0,2:T(2,128)(2,1)} %copy.98), calls=%async_computation | async-start | bytes 33554432 | tf_op jit(solution)/shard_map/all_to_all | solution.py:189
  75.7 268.6 %all-gather.15.cloned.1.call-start = ((), (), s32[]{:S(2)}) async-start(), calls=%async_computation.8 | async-start | bytes 2621440 | tf_op jit(solution)/shard_map/all_gather | solution.py:127
  76.8 36.8 %copy-start.31 = (f32[128,32]{0,1:T(8,128)}, f32[128,32]{0,1:T(8,128)S(1)}, u32[]{:S(2)}) copy-start(f32[128,32]{0,1:T(8,128)S(1)} %get-tuple-element.46) | copy-start | bytes 49156
  127.3 88.5 %copy-start.23 = (f32[1,2048]{1,0:T(1,128)S(1)}, f32[1,2048]{1,0:T(1,128)}, u32[]{:S(2)}) copy-start(f32[1,2048]{1,0:T(1,128)} %param.14) | copy-start | bytes 24580
  216.8 180.5 %reduce-scatter.5.cloned.1.call-start = ((), (), s32[]{:S(2)}) async-start(), calls=%async_computation.9 | async-start | bytes 2621440 | tf_op jit(solution)/shard_map/reduce_scatter | solution.py:135
  365.8 47.7 %copy-start.26 = (f32[1,2048]{1,0:T(1,128)S(1)}, f32[1,2048]{1,0:T(1,128)}, u32[]{:S(2)}) copy-start(f32[1,2048]{1,0:T(1,128)} %param.11) | copy-start | bytes 24580
  365.8 102.2 %all-gather.17.cloned.1.call-start = ((), (), s32[]{:S(2)}) async-start(), calls=%async_computation.10 | async-start | bytes 2621440 | tf_op jit(solution)/shard_map/all_gather | solution.py:127
  398.4 14.7 %collective-permute-start = (bf16[128,2048]{1,0:T(8,128)(2,1)S(1)}, bf16[128,2048]{1,0:T(8,128)(2,1)S(1)}, u32[]{:S(2)}, u32[]{:S(2)}) collective-permute-start(bf16[128,2048]{1,0:T(8,128)(2,1)S(1)} %add_convert_fusion.1), channel_id=1, source_target_pairs={{0,16},{1,17},{2,18},{3,19},{4,20},{5,21},{6,22},{7,23},{8,24},{9,... | collective-permute-start | bytes 1572872 | tf_op jit(solution)/shard_map/ppermute | solution.py:204
  413.4 322.6 %copy-start.2 = (bf16[128,2048]{1,0:T(8,128)(2,1)}, bf16[128,2048]{1,0:T(8,128)(2,1)S(1)}, u32[]{:S(2)}) copy-start(bf16[128,2048]{1,0:T(8,128)(2,1)S(1)} %get-tuple-element.13) | copy-start | bytes 1572868
  413.4 180.7 %copy-start.42 = (f32[128]{0:T(128)}, f32[128]{0:T(128)S(1)}, u32[]{:S(2)}) copy-start(f32[128]{0:T(128)S(1)} %add_rsqrt_fusion.1) | copy-start | bytes 1540
  422.6 4.3 copy-start.41
  425.0 7.6 copy-start.17
  429.4 274.8 %copy-start.35 = (f32[2,8,4,64]{3,2,1,0:T(4,128)}, f32[2,8,4,64]{3,2,1,0:T(4,128)S(1)}, u32[]{:S(2)}) copy-start(f32[2,8,4,64]{3,2,1,0:T(4,128)S(1)} %get-tuple-element.52) | copy-start | bytes 49156
  437.8 6.2 copy-start.14
  442.8 249.4 %copy-start = (f32[128,2048]{1,0:T(8,128)}, f32[128,2048]{1,0:T(8,128)S(1)}, u32[]{:S(2)}) copy-start(f32[128,2048]{1,0:T(8,128)S(1)} %get-tuple-element.55) | copy-start | bytes 3145732
  442.8 249.4 %copy-start.39 = (f32[128]{0:T(128)}, f32[128]{0:T(128)S(1)}, u32[]{:S(2)}) copy-start(f32[128]{0:T(128)S(1)} %add_rsqrt_fusion) | copy-start | bytes 1540
  443.9 48.7 %all-gather.19.cloned.1.call-start = ((), (), s32[]{:S(2)}) async-start(), calls=%async_computation.12 | async-start | bytes 2621440 | tf_op jit(solution)/shard_map/all_gather | solution.py:127
  444.8 104.5 %reduce-scatter.9.cloned.1.call-start = ((), (), s32[]{:S(2)}) async-start(), calls=%async_computation.13 | async-start | bytes 2621440 | tf_op jit(solution)/shard_map/reduce_scatter | solution.py:135
  504.6 46.0 %copy-start.13 = (bf16[128,2048]{1,0:T(8,128)(2,1)S(1)}, bf16[128,2048]{1,0:T(8,128)(2,1)}, u32[]{:S(2)}) copy-start(bf16[128,2048]{1,0:T(8,128)(2,1)} %broadcast_select_fusion.1) | copy-start | bytes 1572868
  518.1 115.3 %all-gather.21.cloned.1.call-start = ((), (), s32[]{:S(2)}) async-start(), calls=%async_computation.14 | async-start | bytes 2621440 | tf_op jit(solution)/shard_map/all_gather | solution.py:127
  564.1 2.8 copy-start.22
  564.1 2.8 copy-start.33
  574.1 9.4 copy-start.29
  575.1 8.4 copy-start.20
  585.0 9.1 copy-start.15
  585.0 9.1 copy-start.16
  594.7 12.8 %collective-permute-start.1 = (bf16[128,2048]{1,0:T(8,128)(2,1)S(1)}, bf16[128,2048]{1,0:T(8,128)(2,1)S(1)}, u32[]{:S(2)}, u32[]{:S(2)}) collective-permute-start(bf16[128,2048]{1,0:T(8,128)(2,1)S(1)} %fusion.119), channel_id=1, source_target_pairs={{16,0},{17,1},{18,2},{19,3},{20,4},{21,5},{22,6},{23,7},{24,8},{25... | collective-permute-start | bytes 1572872 | tf_op jit(solution)/shard_map/ppermute | solution.py:224
  608.3 81.8 %reduce-scatter.11.cloned.1.call-start = ((), (), s32[]{:S(2)}) async-start(), calls=%async_computation.15 | async-start | bytes 2621440 | tf_op jit(solution)/shard_map/reduce_scatter | solution.py:135
  659.0 113.9 %all-gather.27.cloned.1.call-start = ((), (), s32[]{:S(2)}) async-start(), calls=%async_computation.18 | async-start | bytes 8912896 | tf_op jit(solution)/shard_map/all_gather | solution.py:131
  659.6 193.4 %all-gather.29.cloned.1.call-start = ((), (), s32[]{:S(2)}) async-start(), calls=%async_computation.19 | async-start | bytes 8912896 | tf_op jit(solution)/shard_map/all_gather | solution.py:131
  660.3 31.9 %copy-start.4 = (bf16[128,2048]{1,0:T(8,128)(2,1)S(1)}, bf16[128,2048]{1,0:T(8,128)(2,1)}, u32[]{:S(2)}) copy-start(bf16[128,2048]{1,0:T(8,128)(2,1)} %broadcast_select_fusion) | copy-start | bytes 1572868
  660.3 376.7 %reduce-scatter.7.cloned.1.call-start = ((), (), s32[]{:S(2)}) async-start(), calls=%async_computation.11 | async-start | bytes 2621440 | tf_op jit(solution)/shard_map/reduce_scatter | solution.py:135
  672.5 420.3 %all-gather.25.cloned.1.call-start = ((), (), s32[]{:S(2)}) async-start(), calls=%async_computation.17 | async-start | bytes 8912896 | tf_op jit(solution)/shard_map/all_gather | solution.py:131
  692.2 8.7 copy-start.45
  694.4 412.0 %all-gather.23.cloned.1.call-start = ((), (), s32[]{:S(2)}) async-start(), calls=%async_computation.16 | async-start | bytes 13369344 | tf_op jit(solution)/shard_map/all_gather | solution.py:131
  704.2 2.9 copy-start.21
  704.2 2.9 copy-start.34
  712.0 5.7 copy-start.30
  715.0 4.0 copy-start.8
  720.5 206.0 %all-to-all-start.2 = ((bf16[128,16,128]{2,0,1:T(8,128)(2,1)}), bf16[128,16,128]{2,0,1:T(8,128)(2,1)}, u32[]{:S(2)}, u32[]{:S(2)}) async-start(bf16[128,16,128]{2,0,1:T(8,128)(2,1)} %copy.134), calls=%async_computation.6 | async-start | bytes 1048576 | tf_op jit(solution)/shard_map/all_to_all | solution.py:255
  726.3 9.7 copy-start.27
  726.4 9.6 copy-start.43
  894.3 145.7 %collective-permute-start.2 = (bf16[2048,512]{0,1:T(8,128)(2,1)}, bf16[2048,512]{0,1:T(8,128)(2,1)}, u32[]{:S(2)}, u32[]{:S(2)}) collective-permute-start(bf16[2048,512]{0,1:T(8,128)(2,1)} %get-tuple-element.23), channel_id=1, source_target_pairs={{0,3},{5,4},{10,9},{15,14},{16,19},{21,20},{26,25},{31,30}} | collective-permute-start | bytes 6291464 | tf_op jit(solution)/shard_map/ppermute | solution.py:251
  897.7 142.3 %collective-permute-start.3 = (bf16[2048,512]{0,1:T(8,128)(2,1)}, bf16[2048,512]{0,1:T(8,128)(2,1)}, u32[]{:S(2)}, u32[]{:S(2)}) collective-permute-start(bf16[2048,512]{0,1:T(8,128)(2,1)} %get-tuple-element.22), channel_id=1, source_target_pairs={{0,2},{5,7},{10,8},{15,13},{16,18},{21,23},{26,24},{31,29}} | collective-permute-start | bytes 6291464 | tf_op jit(solution)/shard_map/ppermute | solution.py:251
  900.4 139.6 %collective-permute-start.4 = (bf16[2048,512]{0,1:T(8,128)(2,1)}, bf16[2048,512]{0,1:T(8,128)(2,1)}, u32[]{:S(2)}, u32[]{:S(2)}) collective-permute-start(bf16[2048,512]{0,1:T(8,128)(2,1)} %get-tuple-element.21), channel_id=1, source_target_pairs={{0,1},{5,6},{10,11},{15,12},{16,17},{21,22},{26,27},{31,28}} | collective-permute-start | bytes 6291464 | tf_op jit(solution)/shard_map/ppermute | solution.py:251
  926.5 5.3 copy-start.37
  926.5 5.3 copy-start.38
  926.5 109.9 %copy-start.47 = (f32[128]{0:T(128)S(1)}, f32[128]{0:T(128)}, u32[]{:S(2)}) copy-start(f32[128]{0:T(128)} %get-tuple-element.9) | copy-start | bytes 1540
  926.5 110.5 %copy-start.1 = (f32[128,2048]{1,0:T(8,128)S(1)}, f32[128,2048]{1,0:T(8,128)}, u32[]{:S(2)}) copy-start(f32[128,2048]{1,0:T(8,128)} %copy-done) | copy-start | bytes 3145732
  926.5 110.5 %copy-start.3 = (bf16[128,2048]{1,0:T(8,128)(2,1)S(1)}, bf16[128,2048]{1,0:T(8,128)(2,1)}, u32[]{:S(2)}) copy-start(bf16[128,2048]{1,0:T(8,128)(2,1)} %copy-done.2) | copy-start | bytes 1572868
  926.5 110.5 %copy-start.5 = (bf16[128,2048]{1,0:T(8,128)(2,1)S(1)}, bf16[128,2048]{1,0:T(8,128)(2,1)}, u32[]{:S(2)}) copy-start(bf16[128,2048]{1,0:T(8,128)(2,1)} %broadcast_select_fusion) | copy-start | bytes 1572868
  926.5 110.5 %copy-start.10 = (f32[128,2048]{1,0:T(8,128)S(1)}, f32[128,2048]{1,0:T(8,128)}, u32[]{:S(2)}) copy-start(f32[128,2048]{1,0:T(8,128)} %copy-done.9) | copy-start | bytes 3145732
  926.6 110.5 %copy-start.24 = (f32[1,2048]{1,0:T(1,128)S(1)}, f32[1,2048]{1,0:T(1,128)}, u32[]{:S(2)}) copy-start(f32[1,2048]{1,0:T(1,128)} %param.14) | copy-start | bytes 24580
  926.6 110.5 %copy-start.28 = (f32[1,2048]{1,0:T(1,128)S(1)}, f32[1,2048]{1,0:T(1,128)}, u32[]{:S(2)}) copy-start(f32[1,2048]{1,0:T(1,128)} %param.11) | copy-start | bytes 24580
  926.6 110.5 %copy-start.40 = (f32[128]{0:T(128)S(1)}, f32[128]{0:T(128)}, u32[]{:S(2)}) copy-start(f32[128]{0:T(128)} %copy-done.39) | copy-start | bytes 1540
  926.6 110.5 %copy-start.44 = (f32[128]{0:T(128)S(1)}, f32[128]{0:T(128)}, u32[]{:S(2)}) copy-start(f32[128]{0:T(128)} %copy-done.42) | copy-start | bytes 1540
  926.6 110.5 %copy-start.46 = (f32[128]{0:T(128)S(1)}, f32[128]{0:T(128)}, u32[]{:S(2)}) copy-start(f32[128]{0:T(128)} %copy-done.45) | copy-start | bytes 1540
  926.6 124.2 %all-to-all-start.3 = ((bf16[512,2,1,2048]{3,1,2,0:T(2,128)(2,1)}), bf16[512,2,1,2048]{3,1,2,0:T(2,128)(2,1)}, u32[]{:S(2)}, u32[]{:S(2)}) async-start(bf16[512,2,1,2048]{3,1,2,0:T(2,128)(2,1)} %bitcast.272), calls=%async_computation.7 | async-start | bytes 8388608 | tf_op jit(solution)/shard_map/all_to_all | solution.py:236
  1050.8 47.9 %all-to-all-start.1 = ((bf16[128,16,128]{2,0,1:T(8,128)(2,1)}), bf16[128,16,128]{2,0,1:T(8,128)(2,1)S(1)}, u32[]{:S(2)}, u32[]{:S(2)}) async-start(bf16[128,16,128]{2,0,1:T(8,128)(2,1)} %bitcast.266), calls=%async_computation.5 | async-start | bytes 1048576 | tf_op jit(solution)/shard_map/all_to_all | solution.py:256
  (8 other events, 14.4 us)
Sparse Core Ops, SparseCore 0:
  9.6 96.3 all-gather.30
  107.5 103.4 all-gather.32
  216.9 33.9 all-gather.14
  365.9 31.3 reduce-scatter.4
  444.0 23.8 all-gather.16
  470.0 22.5 all-gather.18
  518.3 31.0 reduce-scatter.8
  608.5 24.8 all-gather.20
  659.1 31.0 reduce-scatter.10
  692.4 80.4 all-gather.26
  775.9 77.0 all-gather.28
  855.5 29.8 reduce-scatter.6
  887.5 95.1 all-gather.24
  984.7 121.7 all-gather.22

commit v2 on v1

v2 whole, which is shorter than its diff:
```python
import functools

import jax
import jax.numpy as jnp
from jax import lax
from jax.experimental import pallas as pl
from jax.experimental.pallas import tpu as pltpu
from jax.sharding import PartitionSpec as P

HEADS = 32
KV_HEADS = 8
HEAD = 64
SEQ = 64
EPSILON = 1e-05
ROPE_BASE = 500000.0
BF = jnp.bfloat16
F32 = jnp.float32
CONTRACT_LAST = (((1,), (1,)), ((), ()))
CONTRACT_FIRST = (((0,), (0,)), ((), ()))


MESH = pl.DeviceIdType.MESH
VMEM_LIMIT = 60 * 2**20
TILE = 128


def dot(left, right):
    return jnp.dot(left, right, preferred_element_type=F32)


def dot_rows(left, right):
    return lax.dot_general(left, right, CONTRACT_LAST, preferred_element_type=F32)


def dot_tokens(left, right):
    return lax.dot_general(left, right, CONTRACT_FIRST, preferred_element_type=F32)


def rope_tables(seq_pos):
    half_index = jnp.arange(HEAD // 2, dtype=F32)
    frequency = jnp.power(ROPE_BASE, -2.0 * half_index / HEAD)
    angles = seq_pos.astype(F32)[:, None] * frequency[None, :]
    cosine, sine = jnp.cos(angles), jnp.sin(angles)
    return (
        jnp.concatenate([cosine] * 4, 1),
        jnp.concatenate([-sine, sine, -sine, sine], 1),
    )


def visible(seq_pos):
    rows = seq_pos.shape[0]
    row_index = jnp.arange(rows)[:, None]
    col_index = jnp.arange(rows)[None, :]
    same = row_index // SEQ == col_index // SEQ
    seen = (col_index <= row_index) & (row_index - col_index <= seq_pos[:, None])
    return jnp.where(same & seen, 1.0, 0.0).astype(F32)


def lanes(rows):
    return lax.broadcasted_iota(jnp.int32, (rows, TILE), 1)


def swap_halves(tile, lane):
    return jnp.where(lane % HEAD < HEAD // 2, pltpu.roll(tile, TILE - HEAD // 2, 1), pltpu.roll(tile, HEAD // 2, 1))


def spread(tile, odd, lane):
    turned = pltpu.roll(tile, HEAD, 1)
    lower, upper = (turned, tile) if odd else (tile, turned)
    return jnp.concatenate(
        [jnp.where(lane < HEAD, lower, 0.0), jnp.where(lane < HEAD, 0.0, upper)], 0
    ).astype(BF)


def softmax_pair(queries, spread_keys, allowed):
    scores = dot_rows(queries, spread_keys) * HEAD ** (-0.5)
    halves = []
    for side in range(2):
        masked = jnp.where(allowed > 0.5, scores[:, side * TILE : (side + 1) * TILE], -1e30)
        expon = jnp.exp(masked - jnp.max(masked, -1, keepdims=True))
        halves.append(expon / jnp.sum(expon, -1, keepdims=True))
    return halves


def attend_forward(
    tokens_ref, received_ref, gain_one_ref, gain_two_ref, cos_ref, sin_ref, allowed_ref, qkv_hbm, out_hbm,
    middle_ref, normed_two_ref, normed_ref, rotated_ref, attended_ref,
    qkv_ref, out_ref, sems,
):
    rows, width = tokens_ref.shape
    cols = qkv_hbm.shape[1]
    step = 512
    copies = [
        pltpu.make_async_copy(
            qkv_hbm.at[:, pl.ds(at, step)], qkv_ref.at[:, pl.ds(at, step)], sems.at[at // step]
        )
        for at in range(0, cols, step)
    ]
    out_copies = [
        pltpu.make_async_copy(
            out_hbm.at[:, pl.ds(at, step)], out_ref.at[:, pl.ds(at, step)], sems.at[(cols + at) // step]
        )
        for at in range(0, width, step)
    ]
    for copy in copies + out_copies:
        copy.start()
    first = lax.axis_index("section") == 0
    state = jnp.where(first, tokens_ref[...], received_ref[...]).astype(F32)
    inverse = lax.rsqrt(jnp.mean(state * state, -1, keepdims=True) + EPSILON)
    normed_ref[...] = (state * inverse * gain_one_ref[...]).astype(BF)
    lane = lanes(rows)
    cosine, sine, allowed = cos_ref[...], sin_ref[...], allowed_ref[...]
    rope_cols = (HEADS + KV_HEADS) * HEAD
    for at in range(0, cols, step):
        copies[at // step].wait()
        projected = dot(normed_ref[...], qkv_ref[:, at : at + step])
        for tile_at in range(0, step, TILE):
            tile = projected[:, tile_at : tile_at + TILE]
            if at + tile_at < rope_cols:
                tile = tile * cosine + swap_halves(tile, lane) * sine
            rotated_ref[:, at + tile_at : at + tile_at + TILE] = tile.astype(BF)
    for group in range(KV_HEADS):
        key_at = width + group // 2 * TILE
        value_at = rope_cols + group // 2 * TILE
        keys = spread(rotated_ref[:, key_at : key_at + TILE].astype(F32), group % 2, lane)
        values = spread(rotated_ref[:, value_at : value_at + TILE].astype(F32), group % 2, lane)
        for pair in range(2):
            at = (group * 2 + pair) * TILE
            halves = softmax_pair(rotated_ref[:, at : at + TILE], keys, allowed)
            probs = jnp.concatenate([half.astype(BF) for half in halves], 1)
            attended_ref[:, at : at + TILE] = dot(probs, values).astype(BF)
    total = jnp.zeros((rows, 1), F32)
    for at in range(0, width, step):
        out_copies[at // step].wait()
        state = jnp.where(first, tokens_ref[:, at : at + step], received_ref[:, at : at + step]).astype(F32)
        middle = state + dot(attended_ref[...], out_ref[:, at : at + step])
        middle_ref[:, at : at + step] = middle
        total += jnp.sum(middle * middle, -1, keepdims=True)
    inverse = lax.rsqrt(total / width + EPSILON)
    normed_two_ref[...] = (middle_ref[...] * inverse * gain_two_ref[...]).astype(BF)


def attend_backward(
    grad_ref, cotangent_ref, received_ref, middle_ref, tokens_ref, state_ref, rotated_ref,
    gain_one_ref, gain_two_ref, cos_ref, sin_ref, allowed_ref, qkv_hbm, out_hbm,
    grad_state_ref, grad_low_ref, grad_branch_ref, grad_projected_ref, gain_terms_ref,
    qkv_ref, out_ref, grad_out_ref, middle_grad_ref, sems,
):
    rows, width = middle_ref.shape
    cols = qkv_hbm.shape[1]
    step = 512
    steps = width // step
    out_copies = [
        pltpu.make_async_copy(out_hbm.at[pl.ds(at * step, step)], out_ref.at[pl.ds(at * step, step)], sems.at[at])
        for at in range(steps)
    ]
    copies = [
        pltpu.make_async_copy(
            qkv_hbm.at[pl.ds(at * step, step)], qkv_ref.at[pl.ds(at * step, step)], sems.at[steps + at]
        )
        for at in range(steps)
    ]
    for copy in out_copies + copies:
        copy.start()
    first = lax.axis_index("section") == 0
    last = lax.axis_index("section") == lax.axis_size("section") - 1

    def norm_back(grad, values, gain):
        inverse = lax.rsqrt(jnp.mean(values * values, -1, keepdims=True) + EPSILON)
        normal = values * inverse
        term = jnp.sum(grad * normal, 0, keepdims=True)
        scaled = grad * gain
        return inverse * (scaled - normal * jnp.mean(scaled * normal, -1, keepdims=True)), term

    upstream = jnp.where(last, cotangent_ref[...], received_ref[...]).astype(F32)
    back, term = norm_back(grad_ref[...], middle_ref[...], gain_two_ref[...])
    gain_terms_ref[1:2, :] = term
    middle_grad_ref[...] = upstream + back
    grad_branch_ref[...] = middle_grad_ref[...].astype(BF)
    for at in range(steps):
        out_copies[at].wait()
        grad_out_ref[:, at * step : (at + 1) * step] = dot_rows(
            grad_branch_ref[...], out_ref[at * step : (at + 1) * step, :]
        ).astype(BF)
    lane = lanes(rows)
    cosine, sine, allowed = cos_ref[...], sin_ref[...], allowed_ref[...]
    rope_cols = (HEADS + KV_HEADS) * HEAD
    scale = HEAD ** (-0.5)

    def unrotate(tile):
        return tile * cosine - swap_halves(tile, lane) * sine

    for group_pair in range(KV_HEADS // 2):
        key_at = width + group_pair * TILE
        value_at = rope_cols + group_pair * TILE
        sums = []
        for odd in range(2):
            keys = spread(rotated_ref[:, key_at : key_at + TILE].astype(F32), odd, lane)
            values = spread(rotated_ref[:, value_at : value_at + TILE].astype(F32), odd, lane)
            key_sum = jnp.zeros((rows, TILE), F32)
            value_sum = jnp.zeros((rows, TILE), F32)
            for pair in range(2):
                at = ((group_pair * 2 + odd) * 2 + pair) * TILE
                queries = rotated_ref[:, at : at + TILE]
                grad_out = grad_out_ref[:, at : at + TILE]
                halves = softmax_pair(queries, keys, allowed)
                grad_probs = dot_rows(grad_out, values)
                grad_halves = []
                for side in range(2):
                    grad = grad_probs[:, side * TILE : (side + 1) * TILE]
                    row_dot = jnp.sum(halves[side] * grad, -1, keepdims=True)
                    grad_halves.append((halves[side] * (grad - row_dot)).astype(BF))
                grad_scores = jnp.concatenate(grad_halves, 1)
                probs = jnp.concatenate([half.astype(BF) for half in halves], 1)
                grad_projected_ref[:, at : at + TILE] = unrotate(dot(grad_scores, keys) * scale).astype(BF)
                key_terms = dot_tokens(grad_scores, queries)
                value_terms = dot_tokens(probs, grad_out)
                key_sum += jnp.where(lane < HEAD, key_terms[:rows], key_terms[rows:])
                value_sum += jnp.where(lane < HEAD, value_terms[:rows], value_terms[rows:])
            sums.append((key_sum + pltpu.roll(key_sum, HEAD, 1), value_sum + pltpu.roll(value_sum, HEAD, 1)))
        keys_grad = jnp.where(lane < HEAD, sums[0][0], sums[1][0]) * scale
        grad_projected_ref[:, key_at : key_at + TILE] = unrotate(keys_grad).astype(BF)
        grad_projected_ref[:, value_at : value_at + TILE] = jnp.where(
            lane < HEAD, sums[0][1], sums[1][1]
        ).astype(BF)
    for at in range(steps):
        copies[at].wait()
        grad_state_ref[:, at * step : (at + 1) * step] = dot_rows(
            grad_projected_ref[...], qkv_ref[at * step : (at + 1) * step, :]
        )
    state = jnp.where(first, tokens_ref[...], state_ref[...]).astype(F32)
    back, term = norm_back(grad_state_ref[...], state, gain_one_ref[...])
    gain_terms_ref[0:1, :] = term
    grad_state = middle_grad_ref[...] + back
    grad_low = grad_state.astype(BF)
    grad_low_ref[...] = grad_low
    grad_state_ref[...] = jnp.where(first, grad_state, grad_low.astype(F32))


def call_attend_forward(*operands):
    rows, width = operands[0].shape
    cols = operands[7].shape[1]
    specs = [pl.BlockSpec(memory_space=pltpu.VMEM)] * 7 + [pl.BlockSpec(memory_space=pl.ANY)] * 2
    return pl.pallas_call(
        attend_forward,
        out_shape=(
            jax.ShapeDtypeStruct((rows, width), F32),
            jax.ShapeDtypeStruct((rows, width), BF),
            jax.ShapeDtypeStruct((rows, width), BF),
            jax.ShapeDtypeStruct((rows, cols), BF),
            jax.ShapeDtypeStruct((rows, width), BF),
        ),
        in_specs=specs,
        out_specs=[pl.BlockSpec(memory_space=pltpu.VMEM)] * 5,
        scratch_shapes=[
            pltpu.VMEM((width, cols), BF),
            pltpu.VMEM((width, width), BF),
            pltpu.SemaphoreType.DMA(((cols + width) // 512,)),
        ],
        compiler_params=pltpu.CompilerParams(vmem_limit_bytes=VMEM_LIMIT),
        name="attend_forward",
    )(*operands)


def call_attend_backward(*operands):
    rows, width = operands[3].shape
    cols = operands[12].shape[1]
    specs = [pl.BlockSpec(memory_space=pltpu.VMEM)] * 12 + [pl.BlockSpec(memory_space=pl.ANY)] * 2
    return pl.pallas_call(
        attend_backward,
        out_shape=(
            jax.ShapeDtypeStruct((rows, width), F32),
            jax.ShapeDtypeStruct((rows, width), BF),
            jax.ShapeDtypeStruct((rows, width), BF),
            jax.ShapeDtypeStruct((rows, cols), BF),
            jax.ShapeDtypeStruct((2, width), F32),
        ),
        in_specs=specs,
        out_specs=[pl.BlockSpec(memory_space=pltpu.VMEM)] * 5,
        scratch_shapes=[
            pltpu.VMEM((width, cols), BF),
            pltpu.VMEM((width, width), BF),
            pltpu.VMEM((rows, width), BF),
            pltpu.VMEM((rows, width), F32),
            pltpu.SemaphoreType.DMA((2 * width // 512,)),
        ],
        compiler_params=pltpu.CompilerParams(vmem_limit_bytes=VMEM_LIMIT),
        name="attend_backward",
    )(*operands)


CHUNK = 512


def feed_kernel(backward, rows, *refs):
    if backward:
        (cotangent_ref, received_ref, gate_up_ref, first_hbm, second_hbm, result_ref, all_ref, mid_ref,
         first_ref, second_ref, part_ref, take_ref, sent_ref, land_ref, own_ref, own_take_ref,
         load_sems, send_sems, recv_sems) = refs
    else:
        (mine_ref, middle_ref, first_hbm, second_hbm, result_ref, all_ref, gate_up_ref,
         mid_ref, first_ref, second_ref, part_ref, take_ref, sent_ref, land_ref, own_ref, own_take_ref,
         load_sems, send_sems, recv_sems) = refs
    shard = lax.axis_index("shard")
    chip, core = shard // 2, shard % 2
    beside = chip * 2 + (1 - core)
    across = (1 - chip) * 2 + core
    half = rows // 2
    width = all_ref.shape[1]
    ff = second_ref.shape[0] if not backward else first_ref.shape[0]
    first_steps = ff // CHUNK
    second_steps = width // CHUNK

    def load_first(at):
        if backward:
            place = (pl.ds(pl.multiple_of(at * CHUNK, CHUNK), CHUNK), slice(None))
            return [pltpu.make_async_copy(first_hbm.at[place], first_ref.at[place], load_sems.at[0, at])]
        places = [
            (slice(None), pl.ds(pl.multiple_of(side * ff + at * CHUNK, CHUNK), CHUNK)) for side in range(2)
        ]
        return [
            pltpu.make_async_copy(first_hbm.at[place], first_ref.at[place], load_sems.at[side, at])
            for side, place in enumerate(places)
        ]

    def load_second(at):
        span = pl.ds(pl.multiple_of(at * CHUNK, CHUNK), CHUNK)
        place = (span, slice(None)) if backward else (slice(None), span)
        return pltpu.make_async_copy(second_hbm.at[place], second_ref.at[place], load_sems.at[2, at])

    for at in range(first_steps):
        for copy in load_first(at):
            copy.start()
    for at in range(second_steps):
        load_second(at).start()

    def remote(source, target, at, device):
        return pltpu.make_async_remote_copy(
            source, target, send_sems.at[at], recv_sems.at[at], device_id={"shard": device}, device_id_type=MESH
        )

    def owned(owner, offset, count):
        return all_ref.at[pl.ds(pl.multiple_of(owner * rows + offset, half), count)]

    barrier = pltpu.get_barrier_semaphore()
    for device in (beside, across):
        pl.semaphore_signal(barrier, inc=1, device_id={"shard": device}, device_id_type=MESH)
    pl.semaphore_wait(barrier, 2)

    place = pl.ds(pl.multiple_of(shard * rows, rows), rows)
    if backward:
        last = lax.axis_index("section") == lax.axis_size("section") - 1
        all_ref[place, :] = jnp.where(last, cotangent_ref[...], received_ref[...])
    else:
        all_ref[place, :] = mine_ref[...]
    across_copies = [remote(owned(shard, at * half, half), owned(shard, at * half, half), 1 + at, across) for at in range(2)]
    beside_copy = remote(owned(shard, 0, rows), owned(shard, 0, rows), 0, beside)
    relays = [remote(owned(across, at * half, half), owned(across, at * half, half), 3 + at, beside) for at in range(2)]
    for copy in across_copies:
        copy.start()
    beside_copy.start()

    def first_product(block, waits):
        span = pl.ds(pl.multiple_of(block * 2 * rows, 2 * rows), 2 * rows)

        def step(at, carry):
            cols = pl.ds(pl.multiple_of(at * CHUNK, CHUNK), CHUNK)
            high = pl.ds(pl.multiple_of(ff + at * CHUNK, CHUNK), CHUNK)
            if waits:
                for copy in load_first(at):
                    copy.wait()
            if backward:
                grad_hidden = dot_rows(all_ref[span, :], first_ref[cols, :])
                gate = gate_up_ref[span, cols].astype(F32)
                up = gate_up_ref[span, high].astype(F32)
                sigmoid = jax.nn.sigmoid(gate)
                mid_ref[span, cols] = (grad_hidden * up * sigmoid * (1.0 + gate * (1.0 - sigmoid))).astype(BF)
                mid_ref[span, high] = (grad_hidden * gate * sigmoid).astype(BF)
            else:
                gate = dot(all_ref[span, :], first_ref[:, cols])
                up = dot(all_ref[span, :], first_ref[:, high])
                gate_up_ref[span, cols] = gate.astype(BF)
                gate_up_ref[span, high] = up.astype(BF)
                mid_ref[span, cols] = (gate * jax.nn.sigmoid(gate) * up).astype(BF)
            return carry

        lax.fori_loop(0, first_steps, step, 0)

    def second_product(block, at, target_ref):
        span = pl.ds(pl.multiple_of(block * 2 * rows, 2 * rows), 2 * rows)
        cols = pl.ds(pl.multiple_of(at * CHUNK, CHUNK), CHUNK)
        if backward:
            partial = dot_rows(mid_ref[span, :], second_ref[cols, :])
        else:
            partial = dot(mid_ref[span, :], second_ref[:, cols])
        target_ref[at, 0] = partial[:rows].astype(BF)
        target_ref[at, 1] = partial[rows:].astype(BF)

    def give(at):
        return remote(part_ref.at[at, 1 - core], take_ref.at[at], 5 + at, beside)

    def cross(at):
        return remote(sent_ref.at[at], land_ref.at[at], 5 + second_steps + at, across)

    def give_own(at):
        return remote(own_ref.at[at, 1 - core], own_take_ref.at[at], 5 + 2 * second_steps + at, beside)

    def pass_on(at):
        give(at).wait_recv()
        sent_ref[at] = (part_ref[at, core].astype(F32) + take_ref[at].astype(F32)).astype(BF)
        cross(at).start()

    beside_copy.wait_recv()
    first_product(chip, True)
    for at in range(2):
        across_copies[at].wait_recv()
        relays[at].start()
    for at in range(2):
        relays[at].wait_recv()
    first_product(1 - chip, False)

    def other_step(at, carry):
        load_second(at).wait()
        second_product(1 - chip, at, part_ref)
        give(at).start()

        @pl.when(at > 0)
        def _():
            pass_on(at - 1)

        return carry

    lax.fori_loop(0, second_steps, other_step, 0)

    def own_step(at, carry):
        @pl.when(at == 0)
        def _():
            pass_on(second_steps - 1)

        second_product(chip, at, own_ref)
        give_own(at).start()
        return carry

    lax.fori_loop(0, second_steps, own_step, 0)
    for at in range(second_steps):
        give_own(at).wait_recv()
        cross(at).wait_recv()
        cols = slice(at * CHUNK, (at + 1) * CHUNK)
        total = own_ref[at, core].astype(F32) + own_take_ref[at].astype(F32) + land_ref[at].astype(F32)
        if backward:
            result_ref[:, cols] = total
        else:
            result_ref[:, cols] = (middle_ref[:, cols] + total).astype(BF)
    for copy in [beside_copy] + across_copies + relays:
        copy.wait_send()
    for at in range(second_steps):
        give(at).wait_send()
        cross(at).wait_send()
        give_own(at).wait_send()


def call_feed(backward, operands, collective):
    first, second = operands[-2], operands[-1]
    rows, width = operands[0].shape
    shards = lax.axis_size("shard")
    ff = first.shape[0] if backward else second.shape[0]
    every = shards * rows
    steps = width // CHUNK
    out_shape = [
        jax.ShapeDtypeStruct((rows, width), F32 if backward else BF),
        jax.ShapeDtypeStruct((every, width), BF),
        jax.ShapeDtypeStruct((every, 2 * ff), BF),
    ]
    copies = 5 + 3 * steps
    piece = pltpu.VMEM((steps, rows, CHUNK), BF)
    pair = pltpu.VMEM((steps, 2, rows, CHUNK), BF)
    scratch = [pltpu.VMEM(first.shape, BF), pltpu.VMEM(second.shape, BF), pair, piece, piece, piece, pair, piece]
    if not backward:
        scratch.insert(0, pltpu.VMEM((every, ff), BF))
    scratch += [
        pltpu.SemaphoreType.DMA((3, max(ff // CHUNK, steps))),
        pltpu.SemaphoreType.DMA((copies,)),
        pltpu.SemaphoreType.DMA((copies,)),
    ]
    return pl.pallas_call(
        functools.partial(feed_kernel, backward, rows),
        out_shape=out_shape,
        in_specs=[pl.BlockSpec(memory_space=pltpu.VMEM)] * (len(operands) - 2)
        + [pl.BlockSpec(memory_space=pl.ANY)] * 2,
        out_specs=[pl.BlockSpec(memory_space=pltpu.VMEM)] * 3,
        scratch_shapes=scratch,
        compiler_params=pltpu.CompilerParams(
            collective_id=collective, has_side_effects=True, vmem_limit_bytes=VMEM_LIMIT
        ),
        name="feed_backward" if backward else "feed_forward",
    )(*operands)


def gather_section(rows):
    return lax.all_gather(rows, ("replica", "shard"), axis=0, tiled=True)


def on_device(
    tokens_in,
    positions,
    attn_gain,
    qkv_weight,
    out_weight,
    mlp_gain,
    gate_up_weight,
    down_weight,
    cotangent,
):
    sections = lax.axis_size("section")
    replicas = lax.axis_size("replica")
    shards = lax.axis_size("shard")
    replica_at = lax.axis_index("replica")
    shard_at = lax.axis_index("shard")
    rows, width = tokens_in.shape
    up_steps = [(at, at + 1) for at in range(sections - 1)]
    down_steps = [(at + 1, at) for at in range(sections - 1)]

    cosine, sine = rope_tables(positions)
    allowed = visible(positions)

    qkv_full = lax.all_gather(qkv_weight[0], "shard", axis=0, tiled=True)
    out_full = lax.all_gather(out_weight[0], "shard", axis=0, tiled=True)
    gate_up_local = gate_up_weight[0]
    ff = gate_up_local.shape[1] // 2
    ff_part = ff // shards
    gate_up_part = lax.all_to_all(
        gate_up_local.reshape(-1, 2, shards, ff_part), "shard", 2, 0, tiled=True
    ).reshape(width, 2 * ff_part)
    down_part = down_weight[0]

    received = jnp.zeros((rows, width), BF)
    for tick_at in range(sections):
        state = received
        middle, normed_two, normed, rotated, attended = call_attend_forward(
            tokens_in, state, attn_gain, mlp_gain, cosine, sine, allowed, qkv_full, out_full
        )
        block_out, normed_two_slice, gate_up = call_feed(
            False, (normed_two, middle, gate_up_part, down_part), 1
        )
        if tick_at + 1 < sections:
            received = lax.ppermute(block_out, "section", up_steps)

    received_grad = jnp.zeros((rows, width), BF)
    for tick_at in range(sections):
        grad_normed_two, upstream_slice, grad_gate_up = call_feed(
            True, (cotangent, received_grad, gate_up, down_part, gate_up_part), 2
        )
        grad_in, grad_low, grad_branch, grad_projected, gains = call_attend_backward(
            grad_normed_two, cotangent, received_grad, middle, tokens_in, state, rotated,
            attn_gain, mlp_gain, cosine, sine, allowed, qkv_full, out_full,
        )
        upstream = jnp.where(lax.axis_index("section") == sections - 1, cotangent, received_grad)
        if tick_at + 1 < sections:
            received_grad = lax.ppermute(grad_low, "section", down_steps)

    both = ("replica", "shard")
    normed_two_all = gather_section(normed_two)
    upstream_all = gather_section(upstream)
    gate_up_all = dot(normed_two_all, gate_up_part)
    gate_all, up_all = gate_up_all[:, :ff_part], gate_up_all[:, ff_part:]
    sigmoid = jax.nn.sigmoid(gate_all)
    hidden_all = (gate_all * sigmoid * up_all).astype(BF)
    grad_hidden = dot_rows(upstream_all, down_part)
    grad_gate = grad_hidden * up_all * sigmoid * (1.0 + gate_all * (1.0 - sigmoid))
    grad_up = grad_hidden * gate_all * sigmoid
    grad_gate_up_all = jnp.concatenate([grad_gate, grad_up], 1).astype(BF)

    slice_rows = width // replicas
    left_rows = lax.dynamic_slice_in_dim(normed_two_all, replica_at * slice_rows, slice_rows, 1)
    gate_up_grad = dot_tokens(left_rows, grad_gate_up_all).astype(BF)
    gate_up_grad = lax.all_to_all(
        gate_up_grad.reshape(slice_rows, 2, 1, ff_part), "shard", 0, 2, tiled=True
    ).reshape(slice_rows // shards, 2 * ff).astype(F32)

    ff_rows = ff // (replicas * shards)
    owner = (replica_at * shards) // replicas
    first_col = (replica_at * shards) % replicas * ff_rows
    hidden_rows = lax.dynamic_slice_in_dim(hidden_all, first_col + shard_at * ff_rows, ff_rows, 1)
    for step in range(1, shards):
        target = lax.rem(shard_at + step, shards)
        part = lax.dynamic_slice_in_dim(hidden_all, first_col + target * ff_rows, ff_rows, 1)
        pairs = []
        for at in range(replicas):
            source = at * shards // replicas
            pairs.append((at * shards + source, at * shards + (source + step) % shards))
        sent = lax.ppermute(part, both, pairs)
        hidden_rows = jnp.where(lax.rem(owner + step, shards) == shard_at, sent, hidden_rows)
    down_grad = dot_tokens(hidden_rows, upstream_all)

    attended_rows = lax.all_to_all(attended, both, 1, 0, tiled=True)
    normed_rows = lax.all_to_all(normed, both, 1, 0, tiled=True)
    out_grad = dot_tokens(attended_rows, gather_section(grad_branch))
    qkv_grad = dot_tokens(normed_rows, gather_section(grad_projected))

    gains = jnp.sum(lax.all_gather(gains, both, axis=0), 0)
    return (
        block_out[None],
        grad_in[None],
        gains[0][None],
        qkv_grad[None],
        out_grad[None],
        gains[1][None],
        gate_up_grad[None],
        down_grad[None],
    )


def solution(mesh):
    both = ("replica", "shard")
    return jax.shard_map(
        on_device,
        mesh=mesh,
        in_specs=(
            P(both, None),
            P(both),
            P("section", None),
            P("section", "shard", None),
            P("section", "shard", None),
            P("section", None),
            P("section", "shard", None),
            P("section", "shard", None),
            P(both, None),
        ),
        out_specs=(
            P("section", both, None),
            P("section", both, None),
            P("section", None),
            P("section", both, None),
            P("section", both, None),
            P("section", None),
            P("section", both, None),
            P("section", both, None),
        ),
        check_vma=False,
    )
```

time: 1130 us -> 961 us (0.85)
  Pallas kernels: 0 us -> 258 us
  waiting for transfers between devices: 458 us -> 274 us
  matrix products: 299 us -> 117 us
  local copies, waits for them, and re-layouts: 165 us -> 121 us
  other arithmetic: 34.3 us -> 13.2 us
    pallas_call x0 -> x8, Pallas kernels: none -> 258 us  [the longest x4 188 us: call_feed(): pl.pallas_call(functools.partial(feed_kernel, backward, rows), out_shape=...]
    all_to_all x1, waiting for transfers between devices: 110 us -> 248 us  [on_device(): lax.all_to_all(gate_up_local.reshape(-1, 2, shards, ff_part), 'shard', 2,...]
    dot_general x9 -> x1, matrix products: 119 us -> 35 us  [dot_rows(): lax.dot_general(left, right, CONTRACT_LAST, preferred_element_type=F32)]
    all_gather x1, waiting for transfers between devices: 83.7 us -> 0.01 us  [on_device(): out_full = lax.all_gather(out_weight[0], 'shard', axis=0, tiled=True)]
    all_gather x4, waiting for transfers between devices: 80.1 us -> 0.02 us  [gather_section(): return lax.all_gather(rows, ('replica', 'shard'), axis=0, tiled=True)]
    reduce_scatter x4 -> x0, waiting for transfers between devices: 80 us -> none  [scatter_slice(): return lax.psum_scatter(partial, 'shard', scatter_dimension=0, tiled=True)]
    dot_general x9 -> x1, matrix products: 114 us -> 42.9 us  [dot(): return jnp.dot(left, right, preferred_element_type=F32)]
    all_gather x4 -> x0, waiting for transfers between devices: 49.2 us -> none  [gather_slice(): return lax.all_gather(rows, 'shard', axis=0, tiled=True)]
  transfers between devices with their start and end apart: 23 -> 15, of which waited for: 14 -> 3; matrix products, arithmetic and copies ran while one was open for 30% -> 26% of each run, Pallas kernels for 0% -> 21%
where the time goes in v2:
time: 961 us; the launch traced here: 946 us
  waiting for transfers between devices  274 us (29%)
  Pallas kernels  258 us (27%)
  local copies, waits for them, and re-layouts  121 us (13%)
  matrix products  117 us (12%)
  blocking collectives  111 us (12%)
  starting transfers between devices  37.6 us (4%)
  between operations  14.6 us (2%)
  other arithmetic  13.2 us (1%)
    all_to_all x1, waiting for transfers between devices, on_device(): lax.all_to_all(gate_up_local.reshape(-1, 2, shards, ff_part), 'shard', 2,...  248 us
    pallas_call x4, Pallas kernels, call_feed(): pl.pallas_call(functools.partial(feed_kernel, backward, rows), out_shape=...  188 us
    all_gather x1, blocking collectives, on_device(): gains = jnp.sum(lax.all_gather(gains, both, axis=0), 0)  111 us
    another operation x2, local copies, waits for them, and re-layouts, on_device(): gate_up_local.reshape(-1, 2, shards, ff_part)  58.9 us
    pallas_call x2, Pallas kernels, call_attend_backward(): pl.pallas_call(attend_backward, out_shape=(jax.ShapeDtypeStruct((rows, wi...  45.2 us
    dot_general x1, matrix products, dot(): return jnp.dot(left, right, preferred_element_type=F32)  42.9 us
    dot_general x4, matrix products, dot_tokens(): lax.dot_general(left, right, CONTRACT_FIRST, preferred_element_type=F32)  39.3 us
    dot_general x1, matrix products, dot_rows(): lax.dot_general(left, right, CONTRACT_LAST, preferred_element_type=F32)  35 us
  transfers between devices with their start and end apart: 15, of which 3 were waited for; matrix products, arithmetic and copies ran while one was open for 26% of the time, Pallas kernels for 21%

profile of v2, /device:TPU:11, one launch (start us, length us, event | category | flops | bytes accessed | tf_op | source)
XLA Modules:
  0.0 945.7 jit_solution(16349547296200724116)
XLA Ops:
  7.2 0.0 all-gather.21.cloned.1.call-start
  7.2 0.7 all-gather.21.cloned.1.call-update
  7.9 0.0 all-gather.19.cloned.1.call-start
  7.9 0.7 all-gather.19.cloned.1.call-update
  8.7 28.1 %reshape_squeeze.3 = bf16[512,2,4,2048]{3,2,1,0:T(4,128)(2,1)} reshape(bf16[1,512,16384]{2,1,0:T(8,128)(2,1)} %param.15) | data formatting | bytes 33554432 | tf_op jit(solution)/shard_map/reshape;squeeze | solution.py:532
  36.8 30.8 %copy.35 = bf16[512,2,4,2048]{3,1,0,2:T(2,128)(2,1)} copy(bf16[512,2,4,2048]{3,2,1,0:T(4,128)(2,1)} %reshape_squeeze.3) | data formatting | bytes 33554432 | tf_op jit(solution)/shard_map/reshape;squeeze | solution.py:532
  67.6 7.9 all-to-all-start
  75.5 0.3 fusion.18
  75.8 0.8 pad_maximum_fusion
  76.7 0.7 fusion.17.allowed_ref
  77.4 247.8 %all-to-all-done = bf16[512,2,4,2048]{3,1,0,2:T(2,128)(2,1)} async-done(((bf16[512,2,4,2048]{3,1,0,2:T(2,128)(2,1)}), bf16[512,2,4,2048]{3,1,0,2:T(2,128)(2,1)}, u32[]{:S(2)}, u32[]{:S(2)}) %all-to-all-start) | async-done | bytes 16777248 | tf_op jit(solution)/shard_map/all_to_all | solution.py:531
  325.1 17.3 %copy.45 = bf16[256,8,2,2048]{3,1,2,0:T(8,128)(2,1)} copy(bf16[256,8,2,2048]{3,2,1,0:T(2,128)(2,1)} %bitcast.28) | data formatting | bytes 33554432
  342.4 0.8 broadcast_3_received_ref_refs_1_.2.received_ref.refs_1_
  343.3 12.0 %attend_forward.2 = (f32[128,2048]{1,0:T(8,128)}, bf16[128,2048]{1,0:T(8,128)(2,1)}, bf16[128,2048]{1,0:T(8,128)(2,1)}, bf16[128,3072]{1,0:T(8,128)(2,1)}, bf16[128,2048]{1,0:T(8,128)(2,1)}) custom-call(bf16[128,2048]{1,0:T(8,128)(2,1)} %tokens_ref.7, bf16[128,2048]{1,0:T(8,128)(2,1)} %broadcast_3_received_ref_refs_1_.2.received_ref.refs_1_, ...), custom_call_target="tpu_custom_call" | custom-call | tf_op jit(solution)/shard_map/attend_forward/pallas_call | solution.py:244
  355.3 39.2 %feed_forward.2 = (bf16[128,2048]{1,0:T(8,128)(2,1)}, bf16[512,2048]{1,0:T(8,128)(2,1)}, bf16[512,4096]{1,0:T(8,128)(2,1)}) custom-call(bf16[128,2048]{1,0:T(8,128)(2,1)} %get-tuple-element.25.refs_0_, f32[128,2048]{1,0:T(8,128)} %get-tuple-element.26.refs_1_, bf16[2048,4096]{1,0:T(8,128)(2,1)} %bitcast.54, bf16[2048,2048]{1,0:T(8,128)(2,1)} %bitcast.63), custom_call_target="tpu_custom_call" | custom-call | tf_op jit(solution)/shard_map/feed_forward/pallas_call | solution.py:485
  394.5 1.8 collective-permute-start
  396.2 12.6 %collective-permute-done.received_ref.state_ref = bf16[128,2048]{1,0:T(8,128)(2,1)S(1)} collective-permute-done((bf16[128,2048]{1,0:T(8,128)(2,1)}, bf16[128,2048]{1,0:T(8,128)(2,1)S(1)}, u32[]{:S(2)}, u32[]{:S(2)}) %collective-permute-start) | collective-permute-done | bytes 524320 | tf_op jit(solution)/shard_map/ppermute | solution.py:546
  408.8 0.8 copy-done.1
  409.6 12.0 %attend_forward.3 = (f32[128,2048]{1,0:T(8,128)}, bf16[128,2048]{1,0:T(8,128)(2,1)}, bf16[128,2048]{1,0:T(8,128)(2,1)}, bf16[128,3072]{1,0:T(8,128)(2,1)}, bf16[128,2048]{1,0:T(8,128)(2,1)}) custom-call(bf16[128,2048]{1,0:T(8,128)(2,1)} %tokens_ref.7, bf16[128,2048]{1,0:T(8,128)(2,1)} %copy-done.1, f32[1,2048]{1,0:T(1,128)} %gain_one_ref.7, ...), custom_call_target="tpu_custom_call" | custom-call | tf_op jit(solution)/shard_map/attend_forward/pallas_call | solution.py:244
  421.6 0.0 all-gather.15.cloned.1.call-update
  421.6 0.0 all-gather.17.cloned.1.call-start
  421.7 48.0 %feed_forward.3 = (bf16[128,2048]{1,0:T(8,128)(2,1)}, bf16[512,2048]{1,0:T(8,128)(2,1)}, bf16[512,4096]{1,0:T(8,128)(2,1)}) custom-call(bf16[128,2048]{1,0:T(8,128)(2,1)} %get-tuple-element.28.refs_0_, f32[128,2048]{1,0:T(8,128)} %get-tuple-element.29.refs_1_.middle_ref, bf16[2048,4096]{1,0:T(8,128)(2,1)} %bitcast.55, bf16[2048,2048]{1,0:T(8,128)(2,1)} %bitcast.64), custom_call_target="tpu_custom_call" | custom-call | tf_op jit(solution)/shard_map/feed_forward/pallas_call | solution.py:485
  469.7 52.3 %feed_backward.2 = (f32[128,2048]{1,0:T(8,128)}, bf16[512,2048]{1,0:T(8,128)(2,1)}, bf16[512,4096]{1,0:T(8,128)(2,1)}) custom-call(bf16[128,2048]{1,0:T(8,128)(2,1)} %cotangent_ref.3, bf16[128,2048]{1,0:T(8,128)(2,1)} %broadcast_3_received_ref_refs_1_.2.received_ref.refs_1_, bf16[512,4096]{1,0:T(8,128)(2,1)} %get-tuple-element.31.refs_2_, ...), custom_call_target="tpu_custom_call" | custom-call | tf_op jit(solution)/shard_map/feed_backward/pallas_call | solution.py:485
  522.0 0.0 copy-start
  522.0 22.7 %attend_backward.2 = (f32[128,2048]{1,0:T(8,128)}, bf16[128,2048]{1,0:T(8,128)(2,1)}, bf16[128,2048]{1,0:T(8,128)(2,1)}, bf16[128,3072]{1,0:T(8,128)(2,1)}, f32[2,2048]{1,0:T(2,128)}) custom-call(f32[128,2048]{1,0:T(8,128)} %get-tuple-element.32.grad_ref, bf16[128,2048]{1,0:T(8,128)(2,1)} %cotangent_ref.3, ...), custom_call_target="tpu_custom_call" | custom-call | tf_op jit(solution)/shard_map/attend_backward/pallas_call | solution.py:269
  544.7 1.3 collective-permute-start.1
  546.0 11.2 %collective-permute-done.1.refs_1_.received_ref = bf16[128,2048]{1,0:T(8,128)(2,1)S(1)} collective-permute-done((bf16[128,2048]{1,0:T(8,128)(2,1)}, bf16[128,2048]{1,0:T(8,128)(2,1)S(1)}, u32[]{:S(2)}, u32[]{:S(2)}) %collective-permute-start.1) | collective-permute-done | bytes 524320 | tf_op jit(solution)/shard_map/ppermute | solution.py:559
  557.2 0.9 broadcast_select_fusion
  558.1 0.0 all-gather.17.cloned.1.call-update
  558.1 0.0 all-gather.13.cloned.1.call-start
  558.2 48.9 %feed_backward.3 = (f32[128,2048]{1,0:T(8,128)}, bf16[512,2048]{1,0:T(8,128)(2,1)}, bf16[512,4096]{1,0:T(8,128)(2,1)}) custom-call(bf16[128,2048]{1,0:T(8,128)(2,1)} %cotangent_ref.3, bf16[128,2048]{1,0:T(8,128)(2,1)} %copy-done.2, bf16[512,4096]{1,0:T(8,128)(2,1)} %get-tuple-element.31.refs_2_, bf16[2048,2048]{1,0:T(8,128)(2,1)} %bitcast.66, ...), custom_call_target="tpu_custom_call" | custom-call | tf_op jit(solution)/shard_map/feed_backward/pallas_call | solution.py:485
  607.2 22.5 %attend_backward.3 = (f32[128,2048]{1,0:T(8,128)}, bf16[128,2048]{1,0:T(8,128)(2,1)}, bf16[128,2048]{1,0:T(8,128)(2,1)}, bf16[128,3072]{1,0:T(8,128)(2,1)}, f32[2,2048]{1,0:T(2,128)}) custom-call(f32[128,2048]{1,0:T(8,128)} %get-tuple-element.35.grad_ref, bf16[128,2048]{1,0:T(8,128)(2,1)} %cotangent_ref.3, bf16[128,2048]{1,0:T(8,128)(2,1)} %copy-done.2, ...), custom_call_target="tpu_custom_call" | custom-call | tf_op jit(solution)/shard_map/attend_backward/pallas_call | solution.py:269
  629.7 0.0 all-gather.13.cloned.1.call-update
  629.7 0.0 all-gather.11.cloned.1.call-start
  629.8 0.5 all-gather.11.cloned.1.call-update
  630.3 0.9 copy_bitcast_fusion
  631.3 6.2 all-to-all-start.2
  637.4 0.0 all-gather.15.cloned.1.call-done
  637.5 42.9 %fusion.25 = f32[2048,4096]{0,1:T(8,128)} fusion(bf16[2048,2048]{1,0:T(8,128)(2,1)} %all-gather.15.cloned.1.call-done, bf16[2048,4096]{1,0:T(8,128)(2,1)} %bitcast.58), kind=kOutput, calls=%fused_computation.48 | convolution fusion | flops 34359738368 | bytes 58720256 | tf_op jit(solution)/shard_map/dot_general | solution.py:28
  680.3 35.0 %multiply_convert_fusion.2 = (bf16[2048,2048]{0,1:T(8,128)(2,1)}, bf16[2048,2048]{0,1:T(8,128)(2,1)}, bf16[2048,2048]{0,1:T(8,128)(2,1)}) fusion(f32[2048,4096]{0,1:T(8,128)} %fusion.25, bf16[2048,2048]{1,0:T(8,128)(2,1)} %all-gather.17.cloned.1.call-done, bf16[1,2048,2048]{2,1,0:T(8,128)(2,1)} %param.16), kind=kOutput, calls=%fused_computation.6 | convolution fusion | flops 17246978048 | bytes 75497472 | tf_op jit(solution)/shard_map/dot_general | solution.py:32
  715.3 6.0 constant_dynamic-slice_fusion
  721.3 3.4 collective-permute-start.2
  724.7 3.4 collective-permute-start.3
  728.1 2.6 collective-permute-start.4
  730.8 15.5 %fusion.4 = bf16[512,4096]{1,0:T(8,128)(2,1)} fusion(bf16[2048,2048]{0,1:T(8,128)(2,1)} %get-tuple-element.43, bf16[2048,2048]{0,1:T(8,128)(2,1)} %get-tuple-element.42, bf16[2048,2048]{1,0:T(8,128)(2,1)} %all-gather.15.cloned.1.call-done, s32[]{:T(128)S(6)} %select_n.78), kind=kOutput, calls=%fused_computation.9 | convolution fusion | flops 8625586176 | bytes 23068676 | tf_op jit(solution)/shard_map/dot_general | solution.py:36
  746.2 7.9 reshape.127
  754.1 0.0 all-to-all-done.2
  754.1 4.8 all-to-all-start.3
  759.0 0.9 copy_bitcast_fusion.1
  759.9 111.0 %all-gather.3 = f32[16,2,2048]{2,1,0:T(2,128)S(1)} all-gather(f32[1,2,2048]{2,1,0:T(2,128)S(1)} %bitcast.75), channel_id=4, replica_groups=mesh['section'=2,'replica'=4,'shard'=4] {'replica','shard'}, dimensions={0}, use_global_device_ids=true | all-gather | bytes 278528 | tf_op jit(solution)/shard_map/all_gather | solution.py:600
  870.9 0.1 reduce_sum.9
  871.0 0.6 fusion.24
  871.6 5.6 convolution_bitcast_fusion.2
  877.3 0.0 collective-permute-done.2
  877.3 0.0 collective-permute-done.3
  877.3 10.6 %convolution_bitcast_fusion.1 = f32[1,512,2048]{2,1,0:T(8,128)} fusion(bf16[2048,2048]{1,0:T(8,128)(2,1)} %all-gather.17.cloned.1.call-done, bf16[2048,512]{0,1:T(8,128)(2,1)} %collective-permute-done.2, bf16[2048,512]{0,1:T(8,128)(2,1)} %collective-permute-done.3, bf16[2048,512]{0,1:T(8,128)(2,1)} %collective-permute-done.4, ...), kind=kOutput, calls=%fused_computation.11 | convolution fusion | flops 4298113024 | bytes 20971528 | tf_op jit(solution)/shard_map/dot_general | solution.py:36
  887.9 0.0 all-to-all-done.3
  887.9 6.0 all-to-all-start.1
  894.0 10.3 %convert_bitcast_fusion = f32[128,2,4,1,2048]{4,1,0,2,3:T(2,128)} fusion(bf16[4,128,2,1,2048]{4,2,1,0,3:T(2,128)(2,1)} %bitcast.21), kind=kLoop, calls=%fused_computation.8 | loop fusion | flops 2097152 | bytes 12582912 | tf_op jit(solution)/shard_map/convert_element_type | solution.py:578
  904.3 14.9 %copy.41 = f32[128,2,4,1,2048]{4,2,1,0,3:T(4,128)} copy(f32[128,2,4,1,2048]{4,1,0,2,3:T(2,128)} %convert_bitcast_fusion) | data formatting | bytes 16777216 | tf_op jit(solution)/shard_map/convert_element_type | solution.py:578
  919.2 11.0 %reshape.128 = f32[1,128,16384]{2,1,0:T(8,128)} reshape(f32[128,2,4,1,2048]{4,2,1,0,3:T(4,128)} %copy.41) | data formatting | bytes 16777216 | tf_op jit(solution)/shard_map/convert_element_type | solution.py:578
  930.3 0.0 all-to-all-done.1
  930.3 7.6 convolution_bitcast_fusion
  937.9 0.8 copy.49
  (24 shorter events, 0.1 us)
Async XLA Ops:
  7.2 335.3 %all-gather.21.cloned.1.call-start = ((), (), s32[]{:S(2)}) async-start(), calls=%async_computation.9 | async-start | bytes 10485760 | tf_op jit(solution)/shard_map/all_gather | solution.py:527
  7.9 334.5 %all-gather.19.cloned.1.call-start = ((), (), s32[]{:S(2)}) async-start(), calls=%async_computation.8 | async-start | bytes 15728640 | tf_op jit(solution)/shard_map/all_gather | solution.py:526
  67.6 7.9 copy-start.7
  67.6 257.5 %all-to-all-start = ((bf16[512,2,4,2048]{3,1,0,2:T(2,128)(2,1)}), bf16[512,2,4,2048]{3,1,0,2:T(2,128)(2,1)}, u32[]{:S(2)}, u32[]{:S(2)}) async-start(bf16[512,2,4,2048]{3,1,0,2:T(2,128)(2,1)} %copy.35), calls=%async_computation | async-start | bytes 33554432 | tf_op jit(solution)/shard_map/all_to_all | solution.py:531
  75.5 562.0 %all-gather.15.cloned.1.call-start = ((), (), s32[]{:S(2)}) async-start(), calls=%async_computation.6 | async-start | bytes 8912896 | tf_op jit(solution)/shard_map/all_gather | solution.py:500
  394.5 14.3 %collective-permute-start = (bf16[128,2048]{1,0:T(8,128)(2,1)}, bf16[128,2048]{1,0:T(8,128)(2,1)S(1)}, u32[]{:S(2)}, u32[]{:S(2)}) collective-permute-start(bf16[128,2048]{1,0:T(8,128)(2,1)} %get-tuple-element.27), channel_id=1, source_target_pairs={{0,16},{1,17},{2,18},{3,19},{4,20},{5,21},{6,22},{7,23},{8,24},{9,... | collective-permute-start | bytes 1572872 | tf_op jit(solution)/shard_map/ppermute | solution.py:546
  408.8 0.8 copy-start.1
  421.6 258.7 %all-gather.17.cloned.1.call-start = ((), (), s32[]{:S(2)}) async-start(), calls=%async_computation.7 | async-start | bytes 8912896 | tf_op jit(solution)/shard_map/all_gather | solution.py:500
  522.0 35.2 %copy-start = (bf16[128,2048]{1,0:T(8,128)(2,1)S(1)}, bf16[128,2048]{1,0:T(8,128)(2,1)}, u32[]{:S(2)}) copy-start(bf16[128,2048]{1,0:T(8,128)(2,1)} %cotangent_ref.3) | copy-start | bytes 1572868
  544.7 12.5 %collective-permute-start.1 = (bf16[128,2048]{1,0:T(8,128)(2,1)}, bf16[128,2048]{1,0:T(8,128)(2,1)S(1)}, u32[]{:S(2)}, u32[]{:S(2)}) collective-permute-start(bf16[128,2048]{1,0:T(8,128)(2,1)} %get-tuple-element.34), channel_id=1, source_target_pairs={{16,0},{17,1},{18,2},{19,3},{20,4},{21,5},{22,6},{23,7},{24,8},{25... | collective-permute-start | bytes 1572872 | tf_op jit(solution)/shard_map/ppermute | solution.py:559
  557.2 1.0 copy-start.2
  558.1 313.5 %all-gather.13.cloned.1.call-start = ((), (), s32[]{:S(2)}) async-start(), calls=%async_computation.5 | async-start | bytes 8912896 | tf_op jit(solution)/shard_map/all_gather | solution.py:500
  607.1 23.2 %copy-start.5 = (bf16[128,2048]{1,0:T(8,128)(2,1)S(1)}, bf16[128,2048]{1,0:T(8,128)(2,1)}, u32[]{:S(2)}) copy-start(bf16[128,2048]{1,0:T(8,128)(2,1)} %get-tuple-element.40) | copy-start | bytes 1572868
  629.7 300.6 %all-gather.11.cloned.1.call-start = ((), (), s32[]{:S(2)}) async-start(), calls=%async_computation.4 | async-start | bytes 13369344 | tf_op jit(solution)/shard_map/all_gather | solution.py:500
  631.3 122.8 %all-to-all-start.2 = ((bf16[128,16,128]{2,0,1:T(8,128)(2,1)}), bf16[128,16,128]{2,0,1:T(8,128)(2,1)S(1)}, u32[]{:S(2)}, u32[]{:S(2)}) async-start(bf16[128,16,128]{2,0,1:T(8,128)(2,1)} %copy_bitcast_fusion), calls=%async_computation.2 | async-start | bytes 1048576 | tf_op jit(solution)/shard_map/all_to_all | solution.py:595
  721.3 156.0 %collective-permute-start.2 = (bf16[2048,512]{0,1:T(8,128)(2,1)}, bf16[2048,512]{0,1:T(8,128)(2,1)}, u32[]{:S(2)}, u32[]{:S(2)}) collective-permute-start(bf16[2048,512]{0,1:T(8,128)(2,1)} %get-tuple-element.47), channel_id=1, source_target_pairs={{0,3},{5,4},{10,9},{15,14},{16,19},{21,20},{26,25},{31,30}} | collective-permute-start | bytes 6291464 | tf_op jit(solution)/shard_map/ppermute | solution.py:591
  724.7 152.6 %collective-permute-start.3 = (bf16[2048,512]{0,1:T(8,128)(2,1)}, bf16[2048,512]{0,1:T(8,128)(2,1)}, u32[]{:S(2)}, u32[]{:S(2)}) collective-permute-start(bf16[2048,512]{0,1:T(8,128)(2,1)} %get-tuple-element.46), channel_id=1, source_target_pairs={{0,2},{5,7},{10,8},{15,13},{16,18},{21,23},{26,24},{31,29}} | collective-permute-start | bytes 6291464 | tf_op jit(solution)/shard_map/ppermute | solution.py:591
  728.1 149.2 %collective-permute-start.4 = (bf16[2048,512]{0,1:T(8,128)(2,1)S(1)}, bf16[2048,512]{0,1:T(8,128)(2,1)}, u32[]{:S(2)}, u32[]{:S(2)}) collective-permute-start(bf16[2048,512]{0,1:T(8,128)(2,1)S(1)} %get-tuple-element.45), channel_id=1, source_target_pairs={{0,1},{5,6},{10,11},{15,12},{16,17},{21,22},{26,27},{31,28}} | collective-permute-start | bytes 6291464 | tf_op jit(solution)/shard_map/ppermute | solution.py:591
  746.2 12.8 %copy-start.4 = (bf16[128,2048]{1,0:T(8,128)(2,1)S(1)}, bf16[128,2048]{1,0:T(8,128)(2,1)}, u32[]{:S(2)}) copy-start(bf16[128,2048]{1,0:T(8,128)(2,1)} %get-tuple-element.38) | copy-start | bytes 1572868
  746.2 13.7 %copy-start.6 = (f32[2,2048]{1,0:T(2,128)S(1)}, f32[2,2048]{1,0:T(2,128)}, u32[]{:S(2)}) copy-start(f32[2,2048]{1,0:T(2,128)} %get-tuple-element.37) | copy-start | bytes 49156
  754.1 133.8 %all-to-all-start.3 = ((bf16[512,2,1,2048]{3,1,2,0:T(2,128)(2,1)}), bf16[512,2,1,2048]{3,1,2,0:T(2,128)(2,1)}, u32[]{:S(2)}, u32[]{:S(2)}) async-start(bf16[512,2,1,2048]{3,1,2,0:T(2,128)(2,1)} %bitcast.71), calls=%async_computation.3 | async-start | bytes 8388608 | tf_op jit(solution)/shard_map/all_to_all | solution.py:576
  887.9 42.4 %all-to-all-start.1 = ((bf16[128,16,128]{2,0,1:T(8,128)(2,1)}), bf16[128,16,128]{2,0,1:T(8,128)(2,1)S(1)}, u32[]{:S(2)}, u32[]{:S(2)}) async-start(bf16[128,16,128]{2,0,1:T(8,128)(2,1)} %copy_bitcast_fusion.1), calls=%async_computation.1 | async-start | bytes 1048576 | tf_op jit(solution)/shard_map/all_to_all | solution.py:596
  930.3 7.6 copy-start.3
Sparse Core Ops, SparseCore 0:
  9.6 59.8 all-gather.20
  71.0 149.6 all-gather.18
  421.8 91.8 all-gather.14
  558.3 82.1 all-gather.16
  642.5 76.5 all-gather.12
  721.2 132.6 all-gather.10

commit v3 on v2

--- a/solution.py
+++ b/solution.py
@@ -83,11 +83,11 @@
 
 
 def attend_forward(
-    tokens_ref, received_ref, gain_one_ref, gain_two_ref, cos_ref, sin_ref, allowed_ref, qkv_hbm, out_hbm,
+    state_ref, gain_one_ref, gain_two_ref, cos_ref, sin_ref, allowed_ref, qkv_hbm, out_hbm,
     middle_ref, normed_two_ref, normed_ref, rotated_ref, attended_ref,
     qkv_ref, out_ref, sems,
 ):
-    rows, width = tokens_ref.shape
+    rows, width = state_ref.shape
     cols = qkv_hbm.shape[1]
     step = 512
     copies = [
@@ -104,8 +104,7 @@
     ]
     for copy in copies + out_copies:
         copy.start()
-    first = lax.axis_index("section") == 0
-    state = jnp.where(first, tokens_ref[...], received_ref[...]).astype(F32)
+    state = state_ref[...].astype(F32)
     inverse = lax.rsqrt(jnp.mean(state * state, -1, keepdims=True) + EPSILON)
     normed_ref[...] = (state * inverse * gain_one_ref[...]).astype(BF)
     lane = lanes(rows)
@@ -132,8 +131,7 @@
     total = jnp.zeros((rows, 1), F32)
     for at in range(0, width, step):
         out_copies[at // step].wait()
-        state = jnp.where(first, tokens_ref[:, at : at + step], received_ref[:, at : at + step]).astype(F32)
-        middle = state + dot(attended_ref[...], out_ref[:, at : at + step])
+        middle = state_ref[:, at : at + step].astype(F32) + dot(attended_ref[...], out_ref[:, at : at + step])
         middle_ref[:, at : at + step] = middle
         total += jnp.sum(middle * middle, -1, keepdims=True)
     inverse = lax.rsqrt(total / width + EPSILON)
@@ -141,7 +139,7 @@
 
 
 def attend_backward(
-    grad_ref, cotangent_ref, received_ref, middle_ref, tokens_ref, state_ref, rotated_ref,
+    rounds, grad_ref, upstream_ref, middle_ref, state_ref, rotated_ref,
     gain_one_ref, gain_two_ref, cos_ref, sin_ref, allowed_ref, qkv_hbm, out_hbm,
     grad_state_ref, grad_low_ref, grad_branch_ref, grad_projected_ref, gain_terms_ref,
     qkv_ref, out_ref, grad_out_ref, middle_grad_ref, sems,
@@ -162,8 +160,6 @@
     ]
     for copy in out_copies + copies:
         copy.start()
-    first = lax.axis_index("section") == 0
-    last = lax.axis_index("section") == lax.axis_size("section") - 1
 
     def norm_back(grad, values, gain):
         inverse = lax.rsqrt(jnp.mean(values * values, -1, keepdims=True) + EPSILON)
@@ -172,7 +168,7 @@
         scaled = grad * gain
         return inverse * (scaled - normal * jnp.mean(scaled * normal, -1, keepdims=True)), term
 
-    upstream = jnp.where(last, cotangent_ref[...], received_ref[...]).astype(F32)
+    upstream = upstream_ref[...].astype(F32)
     back, term = norm_back(grad_ref[...], middle_ref[...], gain_two_ref[...])
     gain_terms_ref[1:2, :] = term
     middle_grad_ref[...] = upstream + back
@@ -228,21 +224,30 @@
         grad_state_ref[:, at * step : (at + 1) * step] = dot_rows(
             grad_projected_ref[...], qkv_ref[at * step : (at + 1) * step, :]
         )
-    state = jnp.where(first, tokens_ref[...], state_ref[...]).astype(F32)
+    state = state_ref[...].astype(F32)
     back, term = norm_back(grad_state_ref[...], state, gain_one_ref[...])
     gain_terms_ref[0:1, :] = term
     grad_state = middle_grad_ref[...] + back
     grad_low = grad_state.astype(BF)
     grad_low_ref[...] = grad_low
-    grad_state_ref[...] = jnp.where(first, grad_state, grad_low.astype(F32))
-
-
-def call_attend_forward(*operands):
+    grad_state_ref[...] = grad_low.astype(F32) if rounds else grad_state
+
+
+def gated(section, body):
+    def kernel(*refs):
+        @pl.when(lax.axis_index("section") == section)
+        def _():
+            body(*refs)
+
+    return kernel
+
+
+def call_attend_forward(section, *operands):
     rows, width = operands[0].shape
-    cols = operands[7].shape[1]
-    specs = [pl.BlockSpec(memory_space=pltpu.VMEM)] * 7 + [pl.BlockSpec(memory_space=pl.ANY)] * 2
+    cols = operands[6].shape[1]
+    specs = [pl.BlockSpec(memory_space=pltpu.VMEM)] * 6 + [pl.BlockSpec(memory_space=pl.ANY)] * 2
     return pl.pallas_call(
-        attend_forward,
+        gated(section, attend_forward),
         out_shape=(
             jax.ShapeDtypeStruct((rows, width), F32),
             jax.ShapeDtypeStruct((rows, width), BF),
@@ -262,12 +267,12 @@
     )(*operands)
 
 
-def call_attend_backward(*operands):
-    rows, width = operands[3].shape
-    cols = operands[12].shape[1]
-    specs = [pl.BlockSpec(memory_space=pltpu.VMEM)] * 12 + [pl.BlockSpec(memory_space=pl.ANY)] * 2
+def call_attend_backward(section, *operands):
+    rows, width = operands[2].shape
+    cols = operands[10].shape[1]
+    specs = [pl.BlockSpec(memory_space=pltpu.VMEM)] * 10 + [pl.BlockSpec(memory_space=pl.ANY)] * 2
     return pl.pallas_call(
-        attend_backward,
+        gated(section, functools.partial(attend_backward, section > 0)),
         out_shape=(
             jax.ShapeDtypeStruct((rows, width), F32),
             jax.ShapeDtypeStruct((rows, width), BF),
@@ -294,7 +299,7 @@
 
 def feed_kernel(backward, rows, *refs):
     if backward:
-        (cotangent_ref, received_ref, gate_up_ref, first_hbm, second_hbm, result_ref, all_ref, mid_ref,
+        (mine_ref, gate_up_ref, first_hbm, second_hbm, result_ref, all_ref, mid_ref,
          first_ref, second_ref, part_ref, take_ref, sent_ref, land_ref, own_ref, own_take_ref,
          load_sems, send_sems, recv_sems) = refs
     else:
@@ -348,11 +353,7 @@
     pl.semaphore_wait(barrier, 2)
 
     place = pl.ds(pl.multiple_of(shard * rows, rows), rows)
-    if backward:
-        last = lax.axis_index("section") == lax.axis_size("section") - 1
-        all_ref[place, :] = jnp.where(last, cotangent_ref[...], received_ref[...])
-    else:
-        all_ref[place, :] = mine_ref[...]
+    all_ref[place, :] = mine_ref[...]
     across_copies = [remote(owned(shard, at * half, half), owned(shard, at * half, half), 1 + at, across) for at in range(2)]
     beside_copy = remote(owned(shard, 0, rows), owned(shard, 0, rows), 0, beside)
     relays = [remote(owned(across, at * half, half), owned(across, at * half, half), 3 + at, beside) for at in range(2)]
@@ -459,7 +460,7 @@
         give_own(at).wait_send()
 
 
-def call_feed(backward, operands, collective):
+def call_feed(section, backward, operands, collective):
     first, second = operands[-2], operands[-1]
     rows, width = operands[0].shape
     shards = lax.axis_size("shard")
@@ -483,7 +484,7 @@
         pltpu.SemaphoreType.DMA((copies,)),
     ]
     return pl.pallas_call(
-        functools.partial(feed_kernel, backward, rows),
+        gated(section, functools.partial(feed_kernel, backward, rows)),
         out_shape=out_shape,
         in_specs=[pl.BlockSpec(memory_space=pltpu.VMEM)] * (len(operands) - 2)
         + [pl.BlockSpec(memory_space=pl.ANY)] * 2,
@@ -496,8 +497,679 @@
     )(*operands)
 
 
-def gather_section(rows):
-    return lax.all_gather(rows, ("replica", "shard"), axis=0, tiled=True)
+def weights_kernel(
+    qkv_ref, out_ref, gate_up_ref, qkv_full, out_full, gate_up_part, qkv_hold, out_hold, gate_up_hold, local_sems, send_sems,
+    recv_sems,
+):
+    shard, replica = lax.axis_index("shard"), lax.axis_index("replica")
+    chip, core = shard // 2, shard % 2
+    beside = {"shard": chip * 2 + (1 - core)}
+    across = {"shard": (1 - chip) * 2 + core}
+    diagonal = {"shard": (1 - chip) * 2 + (1 - core)}
+    mine = replica % 2
+    partner = {"replica": replica + 1 - 2 * mine}
+    rows = qkv_ref.shape[0]
+    half = rows // 2
+    ff = gate_up_ref.shape[1] // 2
+    part = gate_up_part.shape[1] // 2
+
+    def remote(source, target, at, device):
+        return pltpu.make_async_remote_copy(
+            source, target, send_sems.at[at], recv_sems.at[at], device_id=device, device_id_type=MESH
+        )
+
+    def span(start, count):
+        return pl.ds(pl.multiple_of(start, count), count)
+
+    sides = [pl.ds(side * part, part) for side in range(2)]
+    loads = [
+        pltpu.make_async_copy(qkv_ref, qkv_hold, local_sems.at[0]),
+        pltpu.make_async_copy(out_ref, out_hold, local_sems.at[1]),
+    ] + [
+        pltpu.make_async_copy(
+            gate_up_ref.at[:, span(side * ff + shard * part, part)], gate_up_hold.at[side], local_sems.at[2 + side]
+        )
+        for side in range(2)
+    ]
+    own_rows = span(shard * rows, rows)
+    stores = [
+        pltpu.make_async_copy(qkv_hold, qkv_full.at[own_rows], local_sems.at[4]),
+        pltpu.make_async_copy(out_hold, out_full.at[own_rows], local_sems.at[5]),
+    ] + [
+        pltpu.make_async_copy(gate_up_hold.at[side], gate_up_part.at[own_rows, sides[side]], local_sems.at[6 + side])
+        for side in range(2)
+    ]
+    for copy in loads:
+        copy.start()
+
+    pieces = []
+    for source, whole, count in ((qkv_ref, qkv_full, 64), (out_ref, out_full, 128)):
+        for offset in range(0, half, count):
+
+            def place(owner, part_of, whole=whole, offset=offset, count=count):
+                return whole.at[span(owner["shard"] * rows + part_of * half + offset, count)]
+
+            own = source.at[span(mine * half + offset, count)]
+            pieces.append((own, place, across, True))
+    for offset in range(0, half, 128):
+        for side in range(2):
+            for device in (across, diagonal):
+
+                def place(owner, part_of, offset=offset, side=side):
+                    return gate_up_part.at[
+                        span(owner["shard"] * rows + part_of * half + offset, 128), pl.ds(side * part, part)
+                    ]
+
+                own = gate_up_ref.at[
+                    span(mine * half + offset, 128), span(side * ff + device["shard"] * part, part)
+                ]
+                pieces.append((own, place, device, False))
+    count = len(pieces)
+    me = {"shard": shard}
+    over = [remote(own, place(me, mine), at, device) for at, (own, place, device, _) in enumerate(pieces)]
+    passed = [
+        remote(place(device, mine), place(device, mine), count + at, partner)
+        for at, (_, place, device, _) in enumerate(pieces)
+    ]
+    relays = [
+        [
+            remote(place(across, which), place(across, which), (2 + turn) * count + at, beside)
+            if relayed
+            else None
+            for at, (_, place, _, relayed) in enumerate(pieces)
+        ]
+        for turn, which in enumerate((mine, 1 - mine))
+    ]
+    direct = [
+        remote(qkv_ref, qkv_full.at[span(shard * rows, rows)], 4 * count, beside),
+        remote(out_ref, out_full.at[span(shard * rows, rows)], 4 * count + 1, beside),
+    ]
+    for side in range(2):
+        direct.append(
+            remote(
+                gate_up_ref.at[:, span(side * ff + beside["shard"] * part, part)],
+                gate_up_part.at[span(shard * rows, rows), pl.ds(side * part, part)],
+                4 * count + 2 + side,
+                beside,
+            )
+        )
+
+    barrier = pltpu.get_barrier_semaphore()
+    for device in (beside, across, diagonal, partner):
+        pl.semaphore_signal(barrier, inc=1, device_id=device, device_id_type=MESH)
+    pl.semaphore_wait(barrier, 4)
+
+    started = []
+
+    def start(copy):
+        copy.start()
+        started.append(copy)
+
+    ahead = 3
+    for copy in over[:ahead]:
+        start(copy)
+    for copy in direct:
+        start(copy)
+    for load, store in zip(loads, stores):
+        load.wait()
+        store.start()
+    for at in range(count + 1):
+        if at < count:
+            over[at].wait_recv()
+            start(passed[at])
+            if relays[0][at] is not None:
+                start(relays[0][at])
+            if at + ahead < count:
+                over[at].wait_send()
+                started[:] = [copy for copy in started if copy is not over[at]]
+                start(over[at + ahead])
+        if at > 0:
+            passed[at - 1].wait_recv()
+            if relays[1][at - 1] is not None:
+                start(relays[1][at - 1])
+    for copies in relays:
+        for copy in copies:
+            if copy is not None:
+                copy.wait_recv()
+    for copy in direct:
+        copy.wait_recv()
+    for copy in stores:
+        copy.wait()
+    for copy in started:
+        copy.wait_send()
+
+
+def call_weights(qkv_weight, out_weight, gate_up_weight, collective):
+    shards = lax.axis_size("shard")
+    rows = qkv_weight.shape[0]
+    count = 4 + 2 + 8
+    anywhere = pl.BlockSpec(memory_space=pl.ANY)
+    return pl.pallas_call(
+        weights_kernel,
+        out_shape=[
+            jax.ShapeDtypeStruct((shards * rows, qkv_weight.shape[1]), BF),
+            jax.ShapeDtypeStruct((shards * rows, out_weight.shape[1]), BF),
+            jax.ShapeDtypeStruct((shards * rows, gate_up_weight.shape[1] // shards), BF),
+        ],
+        in_specs=[anywhere] * 3,
+        out_specs=[anywhere] * 3,
+        scratch_shapes=[
+            pltpu.VMEM(qkv_weight.shape, BF),
+            pltpu.VMEM(out_weight.shape, BF),
+            pltpu.VMEM((2, rows, gate_up_weight.shape[1] // (2 * shards)), BF),
+            pltpu.SemaphoreType.DMA((8,)),
+            pltpu.SemaphoreType.DMA((4 * count + 4,)),
+            pltpu.SemaphoreType.DMA((4 * count + 4,)),
+        ],
+        compiler_params=pltpu.CompilerParams(
+            collective_id=collective, has_side_effects=True, vmem_limit_bytes=VMEM_LIMIT
+        ),
+        name="weights",
+    )(qkv_weight, out_weight, gate_up_weight)
+
+
+def slice_peers():
+    shard = lax.axis_index("shard")
+    chip, core = shard // 2, shard % 2
+    return shard, chip * 2 + (1 - core), (1 - chip) * 2 + core, (1 - chip) * 2 + (1 - core)
+
+
+def slice_barrier(devices, replicas=1):
+    barrier = pltpu.get_barrier_semaphore()
+    for device in devices:
+        pl.semaphore_signal(barrier, inc=1, device_id={"shard": device}, device_id_type=MESH)
+    for turn in range(1, replicas):
+        target = lax.rem(lax.axis_index("replica") + turn, replicas)
+        pl.semaphore_signal(barrier, inc=1, device_id={"replica": target}, device_id_type=MESH)
+    pl.semaphore_wait(barrier, len(devices) + replicas - 1)
+
+
+def replica_copy(source, target, turn, send_sems, recv_sems, base):
+    replicas = lax.axis_size("replica")
+    device = lax.rem(lax.axis_index("replica") + replicas - turn, replicas)
+    return pltpu.make_async_remote_copy(
+        source, target, send_sems.at[base + turn], recv_sems.at[base + turn],
+        device_id={"replica": device}, device_id_type=MESH,
+    )
+
+
+def attend_grads_kernel(
+    projected_ref, branch_ref, left_qkv_ref, left_out_ref, upstream_ref, qkv_part_ref, out_part_ref, others_hbm,
+    all_ref, send_sems, recv_sems,
+):
+    shard, beside, across, _ = slice_peers()
+    replica, replicas = lax.axis_index("replica"), lax.axis_size("replica")
+    rows, cols = projected_ref.shape
+    pieces = all_ref.shape[0]
+    step = all_ref.shape[2]
+    slice_barrier((beside, across), replicas)
+    spread_copies = [
+        replica_copy(upstream_ref, others_hbm.at[replica], turn, send_sems, recv_sems, 3 * pieces)
+        for turn in range(1, replicas)
+    ]
+
+    def remote(owner, piece, at, device):
+        place = all_ref.at[piece, pl.ds(pl.multiple_of(owner * rows, rows), rows)]
+        return pltpu.make_async_remote_copy(
+            place, place, send_sems.at[at], recv_sems.at[at], device_id={"shard": device}, device_id_type=MESH
+        )
+
+    own = pl.ds(pl.multiple_of(shard * rows, rows), rows)
+    over = [remote(shard, piece, piece, across) for piece in range(pieces)]
+    direct = [remote(shard, piece, pieces + piece, beside) for piece in range(pieces)]
+    relays = [remote(across, piece, 2 * pieces + piece, beside) for piece in range(pieces)]
+    for piece in range(pieces):
+        at = piece * step
+        all_ref[piece, own, :] = (
+            projected_ref[:, at : at + step] if at < cols else branch_ref[:, at - cols : at - cols + step]
+        )
+        over[piece].start()
+        direct[piece].start()
+    for copy in spread_copies:
+        copy.start()
+    for piece in range(pieces):
+        over[piece].wait_recv()
+        relays[piece].start()
+    for piece in range(pieces):
+        direct[piece].wait_recv()
+        relays[piece].wait_recv()
+        at = piece * step
+        if at < cols:
+            qkv_part_ref[:, at : at + step] = dot(left_qkv_ref[...], all_ref[piece]).astype(BF)
+        else:
+            out_part_ref[:, at - cols : at - cols + step] = dot(left_out_ref[...], all_ref[piece]).astype(BF)
+    for copy in over + direct + relays:
+        copy.wait_send()
+    for copy in spread_copies:
+        copy.wait()
+
+
+def call_attend_grads(projected, branch, left_qkv, left_out, upstream, collective):
+    replicas = lax.axis_size("replica")
+    rows, cols = projected.shape
+    width = branch.shape[1]
+    every, tokens = left_qkv.shape
+    pieces = (cols + width) // CHUNK
+    return pl.pallas_call(
+        attend_grads_kernel,
+        out_shape=[
+            jax.ShapeDtypeStruct((every, cols), BF),
+            jax.ShapeDtypeStruct((every, width), BF),
+            jax.ShapeDtypeStruct((replicas,) + upstream.shape, BF),
+        ],
+        in_specs=[pl.BlockSpec(memory_space=pltpu.VMEM)] * 5,
+        out_specs=[pl.BlockSpec(memory_space=pltpu.VMEM)] * 2 + [pl.BlockSpec(memory_space=pl.ANY)],
+        scratch_shapes=[
+            pltpu.VMEM((pieces, tokens, CHUNK), BF),
+            pltpu.SemaphoreType.DMA((3 * pieces + replicas,)),
+            pltpu.SemaphoreType.DMA((3 * pieces + replicas,)),
+        ],
+        compiler_params=pltpu.CompilerParams(
+            collective_id=collective, has_side_effects=True, vmem_limit_bytes=VMEM_LIMIT
+        ),
+        name="attend_grads",
+    )(projected, branch, left_qkv, left_out, upstream)
+
+
+def feed_grads_kernel(
+    upstream_ref, left_ref, hidden_ref, others_hbm, gate_up_hbm, down_hbm,
+    gate_up_grad_ref, down_grad_ref, gathered_hbm,
+    down_ref, block_ref, gate_up_ref, mid_ref, sum_ref, stage_ref,
+    load_sems, block_sems, send_sems, recv_sems,
+):
+    shard, beside, across, diagonal = slice_peers()
+    replica, replicas = lax.axis_index("replica"), lax.axis_size("replica")
+    rows = others_hbm.shape[1]
+    every, width = upstream_ref.shape
+    part = down_ref.shape[0]
+    ff = gate_up_grad_ref.shape[1] // 2
+    steps = part // CHUNK
+    wide = width // CHUNK
+    out_rows = gate_up_grad_ref.shape[0]
+
+    load_down = pltpu.make_async_copy(down_hbm, down_ref, load_sems.at[0])
+    load_down.start()
+
+    def block_at(turn):
+        return lax.rem(replica + turn, replicas)
+
+    def load_gate_up(turn):
+        source = gate_up_hbm.at[pl.ds(pl.multiple_of(block_at(turn) * every, every), every)]
+        return pltpu.make_async_copy(source, gate_up_ref.at[turn % 2], block_sems.at[0, turn % 2])
+
+    def load_block(turn):
+        return pltpu.make_async_copy(gathered_hbm.at[turn], block_ref.at[turn % 2], block_sems.at[1, turn % 2])
+
+    load_gate_up(0).start()
+
+    def remote(source, target, at, device):
+        return pltpu.make_async_remote_copy(
+            source, target, send_sems.at[at], recv_sems.at[at], device_id={"shard": device}, device_id_type=MESH
+        )
+
+    def landing(turn, owner):
+        return gathered_hbm.at[turn, pl.ds(pl.multiple_of(owner * rows, rows), rows)]
+
+    def over(turn):
+        return remote(others_hbm.at[block_at(turn)], landing(turn, shard), 3 * turn, across)
+
+    def direct(turn):
+        return remote(others_hbm.at[block_at(turn)], landing(turn, shard), 3 * turn + 1, beside)
+
+    def relay(turn):
+        return remote(landing(turn, across), landing(turn, across), 3 * turn + 2, beside)
+
+    def keep(turn):
+        return pltpu.make_async_copy(others_hbm.at[block_at(turn)], landing(turn, shard), load_sems.at[turn])
+
+    slice_barrier((beside, across, diagonal))
+    for turn in range(1, replicas):
+        keep(turn).start()
+    for turn in range(1, min(3, replicas)):
+        over(turn).start()
+        direct(turn).start()
+    sum_ref[...] = jnp.zeros_like(sum_ref)
+    down_grad_ref[...] = jnp.zeros_like(down_grad_ref)
+    load_down.wait()
+
+    def send_grad(at, peer, device):
+        cols = pl.ds(pl.multiple_of(at * CHUNK, CHUNK), CHUNK)
+        side, offset = at // steps, at % steps
+        target = pl.ds(pl.multiple_of(side * ff + shard * part + offset * CHUNK, CHUNK), CHUNK)
+        return remote(
+            stage_ref.at[pl.ds(pl.multiple_of(device * out_rows, out_rows), out_rows), cols],
+            gate_up_grad_ref.at[:, target],
+            3 * replicas + peer * 2 * steps + at,
+            device,
+        )
+
+    def work(turn, grad_rows):
+        slot = turn % 2
+        load_gate_up(turn).wait()
+        tokens = pl.ds(pl.multiple_of(block_at(turn) * every, every), every)
+
+        def products(at, carry):
+            cols = pl.ds(pl.multiple_of(at * CHUNK, CHUNK), CHUNK)
+            high = pl.ds(pl.multiple_of(part + at * CHUNK, CHUNK), CHUNK)
+            grad_hidden = dot_rows(grad_rows[...], down_ref[cols, :])
+            gate = gate_up_ref[slot, :, cols].astype(F32)
+            up = gate_up_ref[slot, :, high].astype(F32)
+            sigmoid = jax.nn.sigmoid(gate)
+            mid_ref[:, cols] = (grad_hidden * up * sigmoid * (1.0 + gate * (1.0 - sigmoid))).astype(BF)
+            mid_ref[:, high] = (grad_hidden * gate * sigmoid).astype(BF)
+            return carry
+
+        lax.fori_loop(0, steps, products, 0)
+
+        def sums(at, carry):
+            cols = pl.ds(pl.multiple_of(at * CHUNK, CHUNK), CHUNK)
+            total = sum_ref[:, cols] + dot(left_ref[:, tokens], mid_ref[:, cols])
+            if turn < replicas - 1:
+                sum_ref[:, cols] = total
+            else:
+                stage_ref[:, cols] = total.astype(BF)
+                for peer, device in enumerate((across, diagonal, beside)):
+                    send_grad(at, peer, device).start()
+            return carry
+
+        lax.fori_loop(0, 2 * steps, sums, 0)
+
+        def down_sums(at, carry):
+            cols = pl.ds(pl.multiple_of(at * CHUNK, CHUNK), CHUNK)
+            down_grad_ref[:, cols] += dot(hidden_ref[:, tokens], grad_rows[:, cols])
+            return carry
+
+        lax.fori_loop(0, wide, down_sums, 0)
+
+    for turn in range(replicas):
+        if turn + 1 < replicas:
+            load_gate_up(turn + 1).start()
+        if turn == 0:
+            work(0, upstream_ref)
+        else:
+            work(turn, block_ref.at[turn % 2])
+        after = turn + 1
+        if after < replicas:
+            over(after).wait_recv()
+            relay(after).start()
+            direct(after).wait_recv()
+            keep(after).wait()
+            relay(after).wait_recv()
+            load_block(after).start()
+            if after + 2 < replicas:
+                over(after).wait_send()
+                direct(after).wait_send()
+                over(after + 2).start()
+                direct(after + 2).start()
+            load_block(after).wait()
+    own = pl.ds(pl.multiple_of(shard * out_rows, out_rows), out_rows)
+
+    def store_own(at, carry):
+        cols = pl.ds(pl.multiple_of(at * CHUNK, CHUNK), CHUNK)
+        target = pl.ds(
+            pl.multiple_of((at // steps) * ff + shard * part + (at % steps) * CHUNK, CHUNK), CHUNK
+        )
+        gate_up_grad_ref[:, target] = stage_ref[own, cols]
+        return carry
+
+    lax.fori_loop(0, 2 * steps, store_own, 0)
+
+    def finish(at, carry):
+        for peer, device in enumerate((across, diagonal, beside)):
+            send_grad(at, peer, device).wait_recv()
+            send_grad(at, peer, device).wait_send()
+        return carry
+
+    lax.fori_loop(0, 2 * steps, finish, 0)
+    for turn in range(1, replicas):
+        relay(turn).wait_send()
+        if turn + 2 >= replicas:
+            over(turn).wait_send()
+            direct(turn).wait_send()
+
+
+def call_feed_grads(upstream, left, hidden, others, gate_up, down, collective):
+    every, width = upstream.shape
+    replicas, rows, _ = others.shape
+    shards = lax.axis_size("shard")
+    part = down.shape[0]
+    out_rows = left.shape[0] // shards
+    vmem, anywhere = pl.BlockSpec(memory_space=pltpu.VMEM), pl.BlockSpec(memory_space=pl.ANY)
+    copies = 3 * replicas + 3 * 2 * (part // CHUNK)
+    return pl.pallas_call(
+        feed_grads_kernel,
+        out_shape=[
+            jax.ShapeDtypeStruct((out_rows, 2 * part * shards), BF),
+            jax.ShapeDtypeStruct((hidden.shape[0], width), F32),
+            jax.ShapeDtypeStruct((replicas, every, width), BF),
+        ],
+        in_specs=[vmem] * 3 + [anywhere] * 3,
+        out_specs=[vmem, vmem, anywhere],
+        scratch_shapes=[
+            pltpu.VMEM(down.shape, BF),
+            pltpu.VMEM((2, every, width), BF),
+            pltpu.VMEM((2, every, 2 * part), BF),
+            pltpu.VMEM((every, 2 * part), BF),
+            pltpu.VMEM((left.shape[0], 2 * part), F32),
+            pltpu.VMEM((left.shape[0], 2 * part), BF),
+            pltpu.SemaphoreType.DMA((max(replicas, 2),)),
+            pltpu.SemaphoreType.DMA((2, 2)),
+            pltpu.SemaphoreType.DMA((copies,)),
+            pltpu.SemaphoreType.DMA((copies,)),
+        ],
+        compiler_params=pltpu.CompilerParams(
+            collective_id=collective, has_side_effects=True, vmem_limit_bytes=VMEM_LIMIT
+        ),
+        name="feed_grads",
+    )(upstream, left, hidden, others, gate_up, down)
+
+
+def prepare_kernel(
+    normed_two_ref, lefts_ref, gate_up_hbm, gathered_hbm, gate_up_all_hbm, hidden_hbm, left_hbm,
+    weight_ref, block_ref, gate_up_ref, hidden_ref,
+    load_sems, store_sems, keep_sems, send_sems, recv_sems,
+):
+    shard, beside, across, diagonal = slice_peers()
+    peers = (across, diagonal, beside)
+    replica, replicas = lax.axis_index("replica"), lax.axis_size("replica")
+    shards = lax.axis_size("shard")
+    rows, width = normed_two_ref.shape
+    every = rows * shards
+    part = hidden_ref.shape[2]
+    ff_rows = hidden_hbm.shape[1]
+    steps = part // CHUNK
+    kinds, groups, _, _, sub_rows = lefts_ref.shape
+    owner = (replica * shards) // replicas
+    first_col = lax.rem(replica * shards, replicas) * ff_rows
+
+    def load_weight(side, at):
+        place = (slice(None), pl.ds(pl.multiple_of(side * part + at * CHUNK, CHUNK), CHUNK))
+        return pltpu.make_async_copy(gate_up_hbm.at[place], weight_ref.at[place], load_sems.at[side, at])
+
+    for at in range(steps):
+        for side in range(2):
+            load_weight(side, at).start()
+
+    def remote(source, target, at, device):
+        return pltpu.make_async_remote_copy(
+            source, target, send_sems.at[at], recv_sems.at[at], device_id={"shard": device}, device_id_type=MESH
+        )
+
+    def block_at(turn):
+        return lax.rem(replica + turn, replicas)
+
+    def landing(turn, who):
+        return gathered_hbm.at[block_at(turn), pl.ds(pl.multiple_of(who * rows, rows), rows)]
+
+    def over(turn):
+        return remote(landing(turn, shard) if turn else normed_two_ref, landing(turn, shard), 3 * turn, across)
+
+    def direct(turn):
+        return remote(landing(turn, shard) if turn else normed_two_ref, landing(turn, shard), 3 * turn + 1, beside)
+
+    def relay(turn):
+        return remote(landing(turn, across), landing(turn, across), 3 * turn + 2, beside)
+
+    def from_replica(turn):
+        return replica_copy(normed_two_ref, landing(0, shard), turn, send_sems, recv_sems, 3 * replicas)
+
+    def tokens(turn):
+        return pl.ds(pl.multiple_of(block_at(turn) * every, every), every)
+
+    def load_block(turn):
+        return pltpu.make_async_copy(gathered_hbm.at[block_at(turn)], block_ref.at[turn % 2], store_sems.at[0, turn % 2])
+
+    def store_block(turn):
+        return pltpu.make_async_copy(gate_up_ref.at[turn % 2], gate_up_all_hbm.at[tokens(turn)], store_sems.at[1, turn % 2])
+
+    def hidden_cols(turn, device):
+        return hidden_ref.at[turn % 2, :, pl.ds(pl.multiple_of(first_col + device * ff_rows, ff_rows), ff_rows)]
+
+    def hand_hidden(turn, peer):
+        device = peers[peer]
+        return remote(hidden_cols(turn, device), hidden_hbm.at[tokens(turn)], 4 * replicas + 3 * turn + peer, device)
+
+    def keep_hidden(turn):
+        return pltpu.make_async_copy(hidden_cols(turn, shard), hidden_hbm.at[tokens(turn)], store_sems.at[2, turn % 2])
+
+    own_rows = pl.ds(pl.multiple_of(shard * rows, rows), rows)
+
+    def hand_left(kind, group, peer):
+        device = peers[peer]
+        return remote(
+            lefts_ref.at[kind, group, device],
+            left_hbm.at[kind, group, own_rows],
+            7 * replicas + (kind * groups + group) * 3 + peer,
+            device,
+        )
+
+    def keep_left(kind, group):
+        return pltpu.make_async_copy(
+            lefts_ref.at[kind, group, shard], left_hbm.at[kind, group, own_rows], keep_sems.at[1 + kind * groups + group]
+        )
+
+    keep_own = pltpu.make_async_copy(normed_two_ref, landing(0, shard), keep_sems.at[0])
+    slice_barrier(peers, replicas)
+    over(0).start()
+    direct(0).start()
+    for turn in range(1, replicas):
+        from_replica(turn).start()
+    keep_own.start()
+    for kind in range(kinds):
+        for group in range(groups):
+            keep_left(kind, group).start()
+            for peer in range(3):
+                hand_left(kind, group, peer).start()
+
+    for turn in range(replicas):
+        over(turn).wait_recv()
+        relay(turn).start()
+        if turn + 1 < replicas:
+            from_replica(turn + 1).wait_recv()
+            over(turn + 1).start()
+            direct(turn + 1).start()
+        direct(turn).wait_recv()
+        if turn == 0:
+            keep_own.wait()
+        relay(turn).wait_recv()
+        load_block(turn).start()
+        load_block(turn).wait()
+        if turn > 1:
+            store_block(turn - 2).wait()
+
+            @pl.when(shard == owner)
+            def _(turn=turn):
+                keep_hidden(turn - 2).wait()
+                for peer in range(3):
+                    hand_hidden(turn - 2, peer).wait_send()
+
+        def products(at, carry, turn=turn):
+            slot = turn % 2
+            cols = pl.ds(pl.multiple_of(at * CHUNK, CHUNK), CHUNK)
+            high = pl.ds(pl.multiple_of(part + at * CHUNK, CHUNK), CHUNK)
+            if turn == 0:
+                load_weight(0, at).wait()
+                load_weight(1, at).wait()
+            gate = dot(block_ref[slot], weight_ref[:, cols])
+            up = dot(block_ref[slot], weight_ref[:, high])
+            gate_up_ref[slot, :, cols] = gate.astype(BF)
+            gate_up_ref[slot, :, high] = up.astype(BF)
+            hidden_ref[slot, :, cols] = (gate * jax.nn.sigmoid(gate) * up).astype(BF)
+            return carry
+
+        lax.fori_loop(0, steps, products, 0)
+        store_block(turn).start()
+
+        @pl.when(shard == owner)
+        def _(turn=turn):
+            keep_hidden(turn).start()
+            for peer in range(3):
+                hand_hidden(turn, peer).start()
+
+    for turn in range(max(0, replicas - 2), replicas):
+        store_block(turn).wait()
+
+        @pl.when(shard == owner)
+        def _(turn=turn):
+            keep_hidden(turn).wait()
+            for peer in range(3):
+                hand_hidden(turn, peer).wait_send()
+
+    for turn in range(replicas):
+        for peer in range(3):
+
+            @pl.when(peers[peer] == owner)
+            def _(turn=turn, peer=peer):
+                hand_hidden(turn, peer).wait_recv()
+
+        over(turn).wait_send()
+        direct(turn).wait_send()
+        relay(turn).wait_send()
+        if turn:
+            from_replica(turn).wait_send()
+    for kind in range(kinds):
+        for group in range(groups):
+            keep_left(kind, group).wait()
+            for peer in range(3):
+                hand_left(kind, group, peer).wait()
+
+
+def call_prepare(normed_two, normed, attended, gate_up_part, collective):
+    rows, width = normed_two.shape
+    shards, replicas = lax.axis_size("shard"), lax.axis_size("replica")
+    part = gate_up_part.shape[1] // 2
+    every = rows * shards
+    sub_rows = width // (replicas * shards)
+    ff_rows = part // replicas
+    lefts = jnp.stack([normed, attended]).reshape(2, rows, replicas, shards, sub_rows).transpose(0, 2, 3, 1, 4)
+    vmem, anywhere = pl.BlockSpec(memory_space=pltpu.VMEM), pl.BlockSpec(memory_space=pl.ANY)
+    copies = 7 * replicas + 2 * replicas * 3
+    return pl.pallas_call(
+        prepare_kernel,
+        out_shape=[
+            jax.ShapeDtypeStruct((replicas, every, width), BF),
+            jax.ShapeDtypeStruct((replicas * every, 2 * part), BF),
+            jax.ShapeDtypeStruct((replicas * every, ff_rows), BF),
+            jax.ShapeDtypeStruct((2, replicas, every, sub_rows), BF),
+        ],
+        in_specs=[vmem, vmem, anywhere],
+        out_specs=[anywhere] * 4,
+        scratch_shapes=[
+            pltpu.VMEM(gate_up_part.shape, BF),
+            pltpu.VMEM((2, every, width), BF),
+            pltpu.VMEM((2, every, 2 * part), BF),
+            pltpu.VMEM((2, every, part), BF),
+            pltpu.SemaphoreType.DMA((2, part // CHUNK)),
+            pltpu.SemaphoreType.DMA((3, 2)),
+            pltpu.SemaphoreType.DMA((1 + 2 * replicas,)),
+            pltpu.SemaphoreType.DMA((copies,)),
+            pltpu.SemaphoreType.DMA((copies,)),
+        ],
+        compiler_params=pltpu.CompilerParams(
+            collective_id=collective, has_side_effects=True, vmem_limit_bytes=VMEM_LIMIT
+        ),
+        name="prepare",
+    )(normed_two, lefts, gate_up_part)
 
 
 def on_device(
@@ -515,7 +1187,6 @@
     replicas = lax.axis_size("replica")
     shards = lax.axis_size("shard")
     replica_at = lax.axis_index("replica")
-    shard_at = lax.axis_index("shard")
     rows, width = tokens_in.shape
     up_steps = [(at, at + 1) for at in range(sections - 1)]
     down_steps = [(at + 1, at) for at in range(sections - 1)]
@@ -523,80 +1194,74 @@
     cosine, sine = rope_tables(positions)
     allowed = visible(positions)
 
-    qkv_full = lax.all_gather(qkv_weight[0], "shard", axis=0, tiled=True)
-    out_full = lax.all_gather(out_weight[0], "shard", axis=0, tiled=True)
-    gate_up_local = gate_up_weight[0]
-    ff = gate_up_local.shape[1] // 2
-    ff_part = ff // shards
-    gate_up_part = lax.all_to_all(
-        gate_up_local.reshape(-1, 2, shards, ff_part), "shard", 2, 0, tiled=True
-    ).reshape(width, 2 * ff_part)
+    qkv_full, out_full, gate_up_part = call_weights(qkv_weight[0], out_weight[0], gate_up_weight[0], 3)
     down_part = down_weight[0]
 
-    received = jnp.zeros((rows, width), BF)
-    for tick_at in range(sections):
-        state = received
+    forward = []
+    state = tokens_in
+    for section in range(sections):
         middle, normed_two, normed, rotated, attended = call_attend_forward(
-            tokens_in, state, attn_gain, mlp_gain, cosine, sine, allowed, qkv_full, out_full
-        )
-        block_out, normed_two_slice, gate_up = call_feed(
-            False, (normed_two, middle, gate_up_part, down_part), 1
-        )
-        if tick_at + 1 < sections:
-            received = lax.ppermute(block_out, "section", up_steps)
-
-    received_grad = jnp.zeros((rows, width), BF)
-    for tick_at in range(sections):
-        grad_normed_two, upstream_slice, grad_gate_up = call_feed(
-            True, (cotangent, received_grad, gate_up, down_part, gate_up_part), 2
+            section, state, attn_gain, mlp_gain, cosine, sine, allowed, qkv_full, out_full
+        )
+        block_out, _, gate_up = call_feed(
+            section, False, (normed_two, middle, gate_up_part, down_part), 8 + section
+        )
+        forward.append((state, middle, rotated, gate_up, normed_two, normed, attended, block_out))
+        if section + 1 < sections:
+            state = lax.ppermute(block_out, "section", up_steps)
+
+    def pick(values):
+        chosen = values[-1]
+        for section in range(sections - 1):
+            chosen = jnp.where(lax.axis_index("section") == section, values[section], chosen)
+        return chosen
+
+    normed_two, normed, attended, block_out = [pick(values) for values in list(zip(*forward))[4:]]
+    both = ("replica", "shard")
+    slice_rows = width // replicas
+
+    backward = []
+    upstream = cotangent
+    for section in reversed(range(sections)):
+        state, middle, rotated, gate_up = forward[section][:4]
+        grad_normed_two, upstream_slice, _ = call_feed(
+            section, True, (upstream, gate_up, down_part, gate_up_part), 8 + sections + section
         )
         grad_in, grad_low, grad_branch, grad_projected, gains = call_attend_backward(
-            grad_normed_two, cotangent, received_grad, middle, tokens_in, state, rotated,
+            section, grad_normed_two, upstream, middle, state, rotated,
             attn_gain, mlp_gain, cosine, sine, allowed, qkv_full, out_full,
         )
-        upstream = jnp.where(lax.axis_index("section") == sections - 1, cotangent, received_grad)
-        if tick_at + 1 < sections:
-            received_grad = lax.ppermute(grad_low, "section", down_steps)
-
-    both = ("replica", "shard")
-    normed_two_all = gather_section(normed_two)
-    upstream_all = gather_section(upstream)
-    gate_up_all = dot(normed_two_all, gate_up_part)
-    gate_all, up_all = gate_up_all[:, :ff_part], gate_up_all[:, ff_part:]
-    sigmoid = jax.nn.sigmoid(gate_all)
-    hidden_all = (gate_all * sigmoid * up_all).astype(BF)
-    grad_hidden = dot_rows(upstream_all, down_part)
-    grad_gate = grad_hidden * up_all * sigmoid * (1.0 + gate_all * (1.0 - sigmoid))
-    grad_up = grad_hidden * gate_all * sigmoid
-    grad_gate_up_all = jnp.concatenate([grad_gate, grad_up], 1).astype(BF)
-
-    slice_rows = width // replicas
-    left_rows = lax.dynamic_slice_in_dim(normed_two_all, replica_at * slice_rows, slice_rows, 1)
-    gate_up_grad = dot_tokens(left_rows, grad_gate_up_all).astype(BF)
-    gate_up_grad = lax.all_to_all(
-        gate_up_grad.reshape(slice_rows, 2, 1, ff_part), "shard", 0, 2, tiled=True
-    ).reshape(slice_rows // shards, 2 * ff).astype(F32)
-
-    ff_rows = ff // (replicas * shards)
-    owner = (replica_at * shards) // replicas
-    first_col = (replica_at * shards) % replicas * ff_rows
-    hidden_rows = lax.dynamic_slice_in_dim(hidden_all, first_col + shard_at * ff_rows, ff_rows, 1)
-    for step in range(1, shards):
-        target = lax.rem(shard_at + step, shards)
-        part = lax.dynamic_slice_in_dim(hidden_all, first_col + target * ff_rows, ff_rows, 1)
-        pairs = []
-        for at in range(replicas):
-            source = at * shards // replicas
-            pairs.append((at * shards + source, at * shards + (source + step) % shards))
-        sent = lax.ppermute(part, both, pairs)
-        hidden_rows = jnp.where(lax.rem(owner + step, shards) == shard_at, sent, hidden_rows)
-    down_grad = dot_tokens(hidden_rows, upstream_all)
-
-    attended_rows = lax.all_to_all(attended, both, 1, 0, tiled=True)
-    normed_rows = lax.all_to_all(normed, both, 1, 0, tiled=True)
-    out_grad = dot_tokens(attended_rows, gather_section(grad_branch))
-    qkv_grad = dot_tokens(normed_rows, gather_section(grad_projected))
-
+        backward.insert(0, (upstream, upstream_slice, grad_in, grad_branch, grad_projected, gains))
+        if section == sections - 1:
+            normed_two, normed, attended, grad_low = lax.optimization_barrier(
+                (normed_two, normed, attended, grad_low)
+            )
+        if section > 0:
+            upstream = lax.ppermute(grad_low, "section", down_steps)
+        if section == sections - 1:
+            normed_two_all, gate_up_all, hidden_rows, lefts = call_prepare(
+                normed_two, normed, attended, gate_up_part, 6
+            )
+            left_rows = lax.dynamic_slice_in_dim(normed_two_all, replica_at * slice_rows, slice_rows, 2)
+            left_rows = left_rows.reshape(-1, slice_rows).T
+            hidden_rows = hidden_rows.T
+            lefts = jnp.swapaxes(lefts, 2, 3).reshape(2, width // shards, shards * rows)
+            upstream, gate_up_all, left_rows, hidden_rows, lefts = lax.optimization_barrier(
+                (upstream, gate_up_all, left_rows, hidden_rows, lefts)
+            )
+
+    upstream, upstream_slice, grad_in, grad_branch, grad_projected, gains = [
+        pick(values) for values in zip(*backward)
+    ]
+    qkv_grad, out_grad, upstream_all = call_attend_grads(
+        grad_projected, grad_branch, lefts[0], lefts[1], upstream, 4
+    )
+    qkv_grad = lax.psum_scatter(qkv_grad, "replica", scatter_dimension=0, tiled=True).astype(F32)
+    out_grad = lax.psum_scatter(out_grad, "replica", scatter_dimension=0, tiled=True).astype(F32)
+    gate_up_grad, down_grad, _ = call_feed_grads(
+        upstream_slice, left_rows, hidden_rows, upstream_all, gate_up_all, down_part, 5
+    )
+    gate_up_grad = gate_up_grad.astype(F32)
     gains = jnp.sum(lax.all_gather(gains, both, axis=0), 0)
     return (
         block_out[None],

time: 961 us -> 736 us (0.77)
  Pallas kernels: 258 us -> 588 us
  waiting for transfers between devices: 274 us -> 56.3 us
  matrix products: 117 us -> 0 us
  local copies, waits for them, and re-layouts: 121 us -> 19.5 us
  blocking collectives: 111 us -> 19.9 us
  starting transfers between devices: 37.6 us -> 3.1 us
  other arithmetic: 13.2 us -> 23.6 us
    pallas_call x8 -> x12, Pallas kernels: 258 us -> 588 us  [the longest x1 163 us: call_weights(): pl.pallas_call(weights_kernel, out_shape=[jax.ShapeDtypeStruct((shards *...]
    all_to_all x4 -> x0, waiting for transfers between devices: 248 us -> none  [the longest x1 248 us: on_device(): lax.all_to_all(gate_up_local.reshape(-1, 2, shards, ff_part), 'shard', 2,...]
    dot_general x6 -> x0, matrix products: 117 us -> none  [the longest x1 42.9 us: dot(): return jnp.dot(left, right, preferred_element_type=F32)]
    all_gather x1, blocking collectives: 111 us -> 19.9 us  [on_device(): gains = jnp.sum(lax.all_gather(gains, both, axis=0), 0)]
    another operation x3 -> x4, local copies, waits for them, and re-layouts: 59.8 us -> 1.01 us  [call_prepare(): jnp.stack([normed, attended]).reshape(2, rows, replicas, shards, sub_rows)]
    ppermute x5 -> x2, waiting for transfers between devices: 23.8 us -> 56.2 us  [the longest x1 56.2 us: on_device(): state = lax.ppermute(block_out, 'section', up_steps)]
    convert_element_type x2 -> x0, local copies, waits for them, and re-layouts: 26 us -> none  [on_device(): gate_up_grad = lax.all_to_all(gate_up_grad.reshape(slice_rows, 2, 1, ff_p...]
    all_to_all x4 -> x0, starting transfers between devices: 24.9 us -> none  [the longest x1 7.89 us: on_device(): lax.all_to_all(gate_up_local.reshape(-1, 2, shards, ff_part), 'shard', 2,...]
  transfers between devices with their start and end apart: 15 -> 4, of which waited for: 3 -> 1; matrix products, arithmetic and copies ran while one was open for 26% -> 3% of each run, Pallas kernels for 21% -> 31%
where the time goes in v3:
time: 736 us; the launch traced here: 725 us
  Pallas kernels  588 us (80%)
  waiting for transfers between devices  56.3 us (8%)
  other arithmetic  23.6 us (3%)
  blocking collectives  19.9 us (3%)
  local copies, waits for them, and re-layouts  19.5 us (3%)
  between operations  14.7 us (2%)
    pallas_call x1, Pallas kernels, call_weights(): pl.pallas_call(weights_kernel, out_shape=[jax.ShapeDtypeStruct((shards *...  163 us
    pallas_call x1, Pallas kernels, call_feed_grads(): pl.pallas_call(feed_grads_kernel, out_shape=[jax.ShapeDtypeStruct((out_ro...  112 us
    pallas_call x1, Pallas kernels, call_prepare(): pl.pallas_call(prepare_kernel, out_shape=[jax.ShapeDtypeStruct((replicas,...  111 us
    pallas_call x4, Pallas kernels, call_feed(): pl.pallas_call(gated(section, functools.partial(feed_kernel, backward, ro...  91.4 us
    ppermute x1, waiting for transfers between devices, on_device(): state = lax.ppermute(block_out, 'section', up_steps)  56.2 us
    pallas_call x1, Pallas kernels, call_attend_grads(): pl.pallas_call(attend_grads_kernel, out_shape=[jax.ShapeDtypeStruct((ever...  50.2 us
    pallas_call x2, Pallas kernels, call_attend_backward(): pl.pallas_call(gated(section, functools.partial(attend_backward, section...  43.9 us
    all_gather x1, blocking collectives, on_device(): gains = jnp.sum(lax.all_gather(gains, both, axis=0), 0)  19.9 us
  transfers between devices with their start and end apart: 4, of which 1 were waited for; matrix products, arithmetic and copies ran while one was open for 3% of the time, Pallas kernels for 31%

profile of v3, /device:TPU:11, one launch (start us, length us, event | category | flops | bytes accessed | tf_op | source)
XLA Modules:
  0.0 724.9 jit_solution(11877471231071041526)
XLA Ops:
  7.2 0.0 reduce-scatter.5.cloned.1.call-start
  7.2 0.7 convert_element_type.2
  7.9 1.4 fusion.2.refs_5_.refs_9_
  9.3 0.3 fusion.3
  9.6 0.8 pad_maximum_fusion
  10.4 163.5 %weights.1 = (bf16[2048,3072]{1,0:T(8,128)(2,1)}, bf16[2048,2048]{1,0:T(8,128)(2,1)}, bf16[2048,4096]{1,0:T(8,128)(2,1)}) custom-call(bf16[512,3072]{1,0:T(8,128)(2,1)} %bitcast.42, bf16[512,2048]{1,0:T(8,128)(2,1)} %bitcast.43, bf16[512,16384]{1,0:T(8,128)(2,1)} %bitcast.36), custom_call_target="tpu_custom_call" | custom-call | tf_op jit(solution)/shard_map/weights/pallas_call | solution.py:647
  173.9 2.9 attend_forward.2
  176.8 4.6 feed_forward.2
  181.4 1.3 collective-permute-start
  182.7 0.0 copy-start.5
  182.8 56.2 %collective-permute-done.refs_0_.refs_3_ = bf16[128,2048]{1,0:T(8,128)(2,1)S(1)} collective-permute-done((bf16[128,2048]{1,0:T(8,128)(2,1)}, bf16[128,2048]{1,0:T(8,128)(2,1)S(1)}, u32[]{:S(2)}, u32[]{:S(2)}) %collective-permute-start) | collective-permute-done | bytes 524320 | tf_op jit(solution)/shard_map/ppermute | solution.py:1211
  239.0 0.8 copy-done.4
  239.8 12.5 %attend_forward.3 = (f32[128,2048]{1,0:T(8,128)}, bf16[128,2048]{1,0:T(8,128)(2,1)}, bf16[128,2048]{1,0:T(8,128)(2,1)}, bf16[128,3072]{1,0:T(8,128)(2,1)}, bf16[128,2048]{1,0:T(8,128)(2,1)}) custom-call(bf16[128,2048]{1,0:T(8,128)(2,1)} %copy-done.4, f32[1,2048]{1,0:T(1,128)} %refs_5_.3, f32[1,2048]{1,0:T(1,128)} %refs_6_.3, ...), custom_call_target="tpu_custom_call" | custom-call | tf_op jit(solution)/shard_map/attend_forward/pallas_call | solution.py:249
  252.3 0.0 copy-done.5
  252.3 2.0 broadcast_select_fusion.6.normed_two_ref
  254.3 40.3 %feed_forward.3 = (bf16[128,2048]{1,0:T(8,128)(2,1)}, bf16[512,2048]{1,0:T(8,128)(2,1)}, bf16[512,4096]{1,0:T(8,128)(2,1)}) custom-call(bf16[128,2048]{1,0:T(8,128)(2,1)} %get-tuple-element.62.refs_0_, f32[128,2048]{1,0:T(8,128)} %get-tuple-element.63.refs_1_.refs_2_, bf16[2048,4096]{1,0:T(8,128)(2,1)} %get-tuple-element.60.refs_2_.refs_3_.gate_up_hbm, ...), custom_call_target="tpu_custom_call" | custom-call | tf_op jit(solution)/shard_map/feed_forward/pallas_call | solution.py:486
  294.6 0.0 copy-done.13
  294.6 0.0 copy-done.15
  294.6 0.1 broadcast_select_fusion.5
  294.6 0.0 copy-done.12
  294.7 0.0 copy-done.14
  294.7 0.1 broadcast_select_fusion.4
  294.7 40.8 %feed_backward.2 = (f32[128,2048]{1,0:T(8,128)}, bf16[512,2048]{1,0:T(8,128)(2,1)}, bf16[512,4096]{1,0:T(8,128)(2,1)}) custom-call(bf16[128,2048]{1,0:T(8,128)(2,1)} %refs_1_.5, bf16[512,4096]{1,0:T(8,128)(2,1)} %get-tuple-element.69.refs_1_, bf16[2048,2048]{1,0:T(8,128)(2,1)} %bitcast.33, bf16[2048,4096]{1,0:T(8,128)(2,1)} %get-tuple-element.60.refs_2_.refs_3_.gate_up_hbm), custom_call_target="tpu_custom_call" | custom-call | tf_op jit(solution)/shard_map/feed_backward/pallas_call | solution.py:486
  335.5 30.4 %attend_backward.2 = (f32[128,2048]{1,0:T(8,128)}, bf16[128,2048]{1,0:T(8,128)(2,1)}, bf16[128,2048]{1,0:T(8,128)(2,1)}, bf16[128,3072]{1,0:T(8,128)(2,1)}, f32[2,2048]{1,0:T(2,128)}) custom-call(f32[128,2048]{1,0:T(8,128)} %get-tuple-element.70.refs_0_, bf16[128,2048]{1,0:T(8,128)(2,1)} %refs_1_.5, f32[128,2048]{1,0:T(8,128)} %get-tuple-element.63.refs_1_.refs_2_, ...), custom_call_target="tpu_custom_call" | custom-call | tf_op jit(solution)/shard_map/attend_backward/pallas_call | solution.py:274
  365.9 1.7 collective-permute-start.1
  367.6 0.4 stack.9
  368.0 0.1 copy.28
  368.1 0.4 stack.10
  368.5 0.1 copy.29
  368.6 1.1 maximum_bitcast_fusion.lefts_ref
  369.7 111.2 %prepare.1 = (bf16[4,512,2048]{2,1,0:T(8,128)(2,1)}, bf16[2048,4096]{1,0:T(8,128)(2,1)}, bf16[2048,512]{1,0:T(8,128)(2,1)}, bf16[2,4,512,128]{3,2,1,0:T(8,128)(2,1)}) custom-call(bf16[128,2048]{1,0:T(8,128)(2,1)} %broadcast_select_fusion.6.normed_two_ref, bf16[2,4,4,128,128]{4,3,2,1,0:T(8,128)(2,1)} %maximum_bitcast_fusion.lefts_ref, ...), custom_call_target="tpu_custom_call" | custom-call | tf_op jit(solution)/shard_map/prepare/pallas_call | solution.py:1147
  480.9 2.3 copy.32
  483.1 1.7 constant_dynamic-slice_fusion
  484.9 2.4 copy.33
  487.3 4.0 copy.31
  491.2 0.0 collective-permute-done.1.refs_0_.refs_1_
  491.3 0.0 copy-done
  491.3 0.9 broadcast_select_fusion.2.upstream_ref
  492.2 0.1 copy-done.1
  492.2 5.8 feed_backward.3
  498.0 1.1 slice_bitcast_fusion
  499.1 13.6 %attend_backward.3 = (f32[128,2048]{1,0:T(8,128)}, bf16[128,2048]{1,0:T(8,128)(2,1)}, bf16[128,2048]{1,0:T(8,128)(2,1)}, bf16[128,3072]{1,0:T(8,128)(2,1)}, f32[2,2048]{1,0:T(2,128)}) custom-call(f32[128,2048]{1,0:T(8,128)} %get-tuple-element.83.refs_0_, bf16[128,2048]{1,0:T(8,128)(2,1)} %copy-done.1, f32[128,2048]{1,0:T(8,128)} %get-tuple-element.59.refs_1_.refs_2_, ...), custom_call_target="tpu_custom_call" | custom-call | tf_op jit(solution)/shard_map/attend_backward/pallas_call | solution.py:274
  512.7 0.9 broadcast_select_fusion.3.branch_ref
  513.6 1.0 broadcast_select_fusion.1.projected_ref
  514.5 50.2 %attend_grads.1 = (bf16[512,3072]{1,0:T(8,128)(2,1)}, bf16[512,2048]{1,0:T(8,128)(2,1)}, bf16[4,128,2048]{2,1,0:T(8,128)(2,1)}) custom-call(bf16[128,3072]{1,0:T(8,128)(2,1)} %broadcast_select_fusion.1.projected_ref, bf16[128,2048]{1,0:T(8,128)(2,1)} %broadcast_select_fusion.3.branch_ref, bf16[512,512]{1,0:T(8,128)(2,1)} %get-tuple-element.105.left_qkv_ref, ...), custom_call_target="tpu_custom_call" | custom-call | tf_op jit(solution)/shard_map/attend_grads/pallas_call | solution.py:753
  564.7 0.0 copy-start.3
  564.8 0.0 reduce-scatter.5.cloned.1.call-update
  564.8 0.0 reduce-scatter.3.cloned.1.call-start
  564.8 0.0 copy-done.9
  564.8 0.0 copy-done.10
  564.8 0.9 select_bitcast_fusion.1
  565.7 0.0 reduce-scatter.3.cloned.1.call-update
  565.7 0.8 copy-done.3
  566.5 1.5 broadcast_select_fusion.upstream_ref
  568.1 112.1 %feed_grads.1 = (bf16[128,16384]{1,0:T(8,128)(2,1)}, f32[512,2048]{1,0:T(8,128)}, bf16[4,512,2048]{2,1,0:T(8,128)(2,1)}) custom-call(bf16[512,2048]{1,0:T(8,128)(2,1)} %broadcast_select_fusion.upstream_ref, bf16[512,2048]{1,0:T(8,128)(2,1)} %bitcast.37, bf16[512,2048]{1,0:T(8,128)(2,1)} %bitcast.38, bf16[4,128,2048]{2,1,0:T(8,128)(2,1)} %get-tuple-element.100.others_hbm, ...), custom_call_target="tpu_custom_call" | custom-call | tf_op jit(solution)/shard_map/feed_grads/pallas_call | solution.py:939
  680.2 19.9 %all-gather.1 = f32[16,2,2048]{2,1,0:T(2,128)S(1)} all-gather(f32[1,2,2048]{2,1,0:T(2,128)S(1)} %select_bitcast_fusion.2), channel_id=2, replica_groups=mesh['section'=2,'replica'=4,'shard'=4] {'replica','shard'}, dimensions={0}, use_global_device_ids=true | all-gather | bytes 278528 | tf_op jit(solution)/shard_map/all_gather | solution.py:1265
  700.2 0.1 reduce_sum.9
  700.3 0.6 fusion.4
  700.9 0.0 copy-done.6
  700.9 1.1 select_bitcast_fusion
  702.0 6.4 bitcast_convert_fusion
  708.4 2.1 bitcast_convert_fusion.2
  710.5 2.4 bitcast_convert_fusion.1
  713.0 4.7 copy.35
  (27 shorter events, 0.1 us)
Async XLA Ops:
  7.2 701.2 %reduce-scatter.5.cloned.1.call-start = ((), (), s32[]{:S(2)}) async-start(), calls=%async_computation.3 | async-start | bytes 2621440 | tf_op jit(solution)/shard_map/reduce_scatter | solution.py:1260
  181.4 57.5 %collective-permute-start = (bf16[128,2048]{1,0:T(8,128)(2,1)}, bf16[128,2048]{1,0:T(8,128)(2,1)S(1)}, u32[]{:S(2)}, u32[]{:S(2)}) collective-permute-start(bf16[128,2048]{1,0:T(8,128)(2,1)} %get-tuple-element.61), channel_id=1, source_target_pairs={{0,16},{1,17},{2,18},{3,19},{4,20},{5,21},{6,22},{7,23},{8,24},{9,... | collective-permute-start | bytes 1572872 | tf_op jit(solution)/shard_map/ppermute | solution.py:1211
  182.7 69.6 %copy-start.5 = (bf16[128,2048]{1,0:T(8,128)(2,1)S(1)}, bf16[128,2048]{1,0:T(8,128)(2,1)}, u32[]{:S(2)}) copy-start(bf16[128,2048]{1,0:T(8,128)(2,1)} %get-tuple-element.58.refs_0_) | copy-start | bytes 1572868
  239.0 0.8 copy-start.4
  254.3 40.3 %copy-start.13 = (bf16[128,2048]{1,0:T(8,128)(2,1)S(1)}, bf16[128,2048]{1,0:T(8,128)(2,1)}, u32[]{:S(2)}) copy-start(bf16[128,2048]{1,0:T(8,128)(2,1)} %get-tuple-element.65) | copy-start | bytes 1572868
  254.3 40.3 %copy-start.15 = (bf16[128,2048]{1,0:T(8,128)(2,1)S(1)}, bf16[128,2048]{1,0:T(8,128)(2,1)}, u32[]{:S(2)}) copy-start(bf16[128,2048]{1,0:T(8,128)(2,1)} %get-tuple-element.66) | copy-start | bytes 1572868
  254.3 40.4 %copy-start.12 = (bf16[128,2048]{1,0:T(8,128)(2,1)S(1)}, bf16[128,2048]{1,0:T(8,128)(2,1)}, u32[]{:S(2)}) copy-start(bf16[128,2048]{1,0:T(8,128)(2,1)} %get-tuple-element.67) | copy-start | bytes 1572868
  254.3 40.4 %copy-start.14 = (bf16[128,2048]{1,0:T(8,128)(2,1)S(1)}, bf16[128,2048]{1,0:T(8,128)(2,1)}, u32[]{:S(2)}) copy-start(bf16[128,2048]{1,0:T(8,128)(2,1)} %get-tuple-element.68) | copy-start | bytes 1572868
  365.9 125.4 %collective-permute-start.1 = (bf16[128,2048]{1,0:T(8,128)(2,1)}, bf16[128,2048]{1,0:T(8,128)(2,1)S(1)}, u32[]{:S(2)}, u32[]{:S(2)}) collective-permute-start(bf16[128,2048]{1,0:T(8,128)(2,1)} %get-tuple-element.73), channel_id=1, source_target_pairs={{16,0},{17,1},{18,2},{19,3},{20,4},{21,5},{22,6},{23,7},{24,8},{25... | collective-permute-start | bytes 1572872 | tf_op jit(solution)/shard_map/ppermute | solution.py:1240
  487.3 4.0 copy-start
  491.3 1.0 copy-start.1
  492.2 5.8 copy-start.2
  499.1 13.6 %copy-start.11 = (bf16[128,2048]{1,0:T(8,128)(2,1)S(1)}, bf16[128,2048]{1,0:T(8,128)(2,1)}, u32[]{:S(2)}) copy-start(bf16[128,2048]{1,0:T(8,128)(2,1)} %get-tuple-element.92) | copy-start | bytes 1572868
  499.1 14.5 %copy-start.8 = (bf16[128,3072]{1,0:T(8,128)(2,1)S(1)}, bf16[128,3072]{1,0:T(8,128)(2,1)}, u32[]{:S(2)}) copy-start(bf16[128,3072]{1,0:T(8,128)(2,1)} %get-tuple-element.90) | copy-start | bytes 2359300
  513.6 51.3 %copy-start.9 = (bf16[128,2048]{1,0:T(8,128)(2,1)S(1)}, bf16[128,2048]{1,0:T(8,128)(2,1)}, u32[]{:S(2)}) copy-start(bf16[128,2048]{1,0:T(8,128)(2,1)} %get-tuple-element.61) | copy-start | bytes 1572868
  513.6 51.3 %copy-start.10 = (bf16[128,2048]{1,0:T(8,128)(2,1)S(1)}, bf16[128,2048]{1,0:T(8,128)(2,1)}, u32[]{:S(2)}) copy-start(bf16[128,2048]{1,0:T(8,128)(2,1)} %get-tuple-element.64) | copy-start | bytes 1572868
  564.7 1.8 copy-start.3
  564.8 145.7 %reduce-scatter.3.cloned.1.call-start = ((), (), s32[]{:S(2)}) async-start(), calls=%async_computation.2 | async-start | bytes 3932160 | tf_op jit(solution)/shard_map/reduce_scatter | solution.py:1259
  568.1 112.1 %copy-start.16 = (f32[2,2048]{1,0:T(2,128)S(1)}, f32[2,2048]{1,0:T(2,128)}, u32[]{:S(2)}) copy-start(f32[2,2048]{1,0:T(2,128)} %get-tuple-element.88) | copy-start | bytes 49156
  568.1 112.1 %copy-start.17 = (f32[2,2048]{1,0:T(2,128)S(1)}, f32[2,2048]{1,0:T(2,128)}, u32[]{:S(2)}) copy-start(f32[2,2048]{1,0:T(2,128)} %get-tuple-element.87) | copy-start | bytes 49156
  568.1 132.8 %copy-start.6 = (f32[128,2048]{1,0:T(8,128)S(1)}, f32[128,2048]{1,0:T(8,128)}, u32[]{:S(2)}) copy-start(f32[128,2048]{1,0:T(8,128)} %get-tuple-element.86) | copy-start | bytes 3145732
  568.1 132.8 %copy-start.7 = (f32[128,2048]{1,0:T(8,128)S(1)}, f32[128,2048]{1,0:T(8,128)}, u32[]{:S(2)}) copy-start(f32[128,2048]{1,0:T(8,128)} %get-tuple-element.85) | copy-start | bytes 3145732
Sparse Core Ops, SparseCore 0:
  564.9 42.4 reduce-scatter.4
  609.8 61.5 reduce-scatter.2

commit v4 on v3

--- a/solution.py
+++ b/solution.py
@@ -186,19 +186,19 @@
     def unrotate(tile):
         return tile * cosine - swap_halves(tile, lane) * sine
 
-    for group_pair in range(KV_HEADS // 2):
-        key_at = width + group_pair * TILE
-        value_at = rope_cols + group_pair * TILE
+    def group_step(group_pair, carry):
+        key_at = pl.multiple_of(width + group_pair * TILE, TILE)
+        value_at = pl.multiple_of(rope_cols + group_pair * TILE, TILE)
         sums = []
         for odd in range(2):
-            keys = spread(rotated_ref[:, key_at : key_at + TILE].astype(F32), odd, lane)
-            values = spread(rotated_ref[:, value_at : value_at + TILE].astype(F32), odd, lane)
+            keys = spread(rotated_ref[:, pl.ds(key_at, TILE)].astype(F32), odd, lane)
+            values = spread(rotated_ref[:, pl.ds(value_at, TILE)].astype(F32), odd, lane)
             key_sum = jnp.zeros((rows, TILE), F32)
             value_sum = jnp.zeros((rows, TILE), F32)
             for pair in range(2):
-                at = ((group_pair * 2 + odd) * 2 + pair) * TILE
-                queries = rotated_ref[:, at : at + TILE]
-                grad_out = grad_out_ref[:, at : at + TILE]
+                at = pl.multiple_of(((group_pair * 2 + odd) * 2 + pair) * TILE, TILE)
+                queries = rotated_ref[:, pl.ds(at, TILE)]
+                grad_out = grad_out_ref[:, pl.ds(at, TILE)]
                 halves = softmax_pair(queries, keys, allowed)
                 grad_probs = dot_rows(grad_out, values)
                 grad_halves = []
@@ -208,17 +208,20 @@
                     grad_halves.append((halves[side] * (grad - row_dot)).astype(BF))
                 grad_scores = jnp.concatenate(grad_halves, 1)
                 probs = jnp.concatenate([half.astype(BF) for half in halves], 1)
-                grad_projected_ref[:, at : at + TILE] = unrotate(dot(grad_scores, keys) * scale).astype(BF)
+                grad_projected_ref[:, pl.ds(at, TILE)] = unrotate(dot(grad_scores, keys) * scale).astype(BF)
                 key_terms = dot_tokens(grad_scores, queries)
                 value_terms = dot_tokens(probs, grad_out)
                 key_sum += jnp.where(lane < HEAD, key_terms[:rows], key_terms[rows:])
                 value_sum += jnp.where(lane < HEAD, value_terms[:rows], value_terms[rows:])
             sums.append((key_sum + pltpu.roll(key_sum, HEAD, 1), value_sum + pltpu.roll(value_sum, HEAD, 1)))
         keys_grad = jnp.where(lane < HEAD, sums[0][0], sums[1][0]) * scale
-        grad_projected_ref[:, key_at : key_at + TILE] = unrotate(keys_grad).astype(BF)
-        grad_projected_ref[:, value_at : value_at + TILE] = jnp.where(
+        grad_projected_ref[:, pl.ds(key_at, TILE)] = unrotate(keys_grad).astype(BF)
+        grad_projected_ref[:, pl.ds(value_at, TILE)] = jnp.where(
             lane < HEAD, sums[0][1], sums[1][1]
         ).astype(BF)
+        return carry
+
+    lax.fori_loop(0, KV_HEADS // 2, group_step, 0)
     for at in range(steps):
         copies[at].wait()
         grad_state_ref[:, at * step : (at + 1) * step] = dot_rows(
@@ -294,12 +297,38 @@
     )(*operands)
 
 
+def slice_peers():
+    shard = lax.axis_index("shard")
+    chip, core = shard // 2, shard % 2
+    return shard, chip * 2 + (1 - core), (1 - chip) * 2 + core, (1 - chip) * 2 + (1 - core)
+
+
+def slice_barrier(devices, turns=()):
+    barrier = pltpu.get_barrier_semaphore()
+    replicas = lax.axis_size("replica")
+    for device in devices:
+        pl.semaphore_signal(barrier, inc=1, device_id={"shard": device}, device_id_type=MESH)
+    for turn in turns:
+        target = lax.rem(lax.axis_index("replica") + turn, replicas)
+        pl.semaphore_signal(barrier, inc=1, device_id={"replica": target}, device_id_type=MESH)
+    pl.semaphore_wait(barrier, len(devices) + len(turns))
+
+
+def replica_copy(source, target, turn, send_sems, recv_sems, base):
+    replicas = lax.axis_size("replica")
+    device = lax.rem(lax.axis_index("replica") + replicas - turn, replicas)
+    return pltpu.make_async_remote_copy(
+        source, target, send_sems.at[base + turn], recv_sems.at[base + turn],
+        device_id={"replica": device}, device_id_type=MESH,
+    )
+
+
 CHUNK = 512
 
 
 def feed_kernel(backward, rows, *refs):
     if backward:
-        (mine_ref, gate_up_ref, first_hbm, second_hbm, result_ref, all_ref, mid_ref,
+        (mine_ref, gate_up_ref, first_hbm, second_hbm, result_ref, all_ref, mid_ref, others_hbm,
          first_ref, second_ref, part_ref, take_ref, sent_ref, land_ref, own_ref, own_take_ref,
          load_sems, send_sems, recv_sems) = refs
     else:
@@ -347,11 +376,8 @@
     def owned(owner, offset, count):
         return all_ref.at[pl.ds(pl.multiple_of(owner * rows + offset, half), count)]
 
-    barrier = pltpu.get_barrier_semaphore()
-    for device in (beside, across):
-        pl.semaphore_signal(barrier, inc=1, device_id={"shard": device}, device_id_type=MESH)
-    pl.semaphore_wait(barrier, 2)
-
+    turns = range(1, lax.axis_size("replica"), 2) if backward else ()
+    slice_barrier((beside, across), turns)
     place = pl.ds(pl.multiple_of(shard * rows, rows), rows)
     all_ref[place, :] = mine_ref[...]
     across_copies = [remote(owned(shard, at * half, half), owned(shard, at * half, half), 1 + at, across) for at in range(2)]
@@ -360,6 +386,12 @@
     for copy in across_copies:
         copy.start()
     beside_copy.start()
+    spread_copies = [
+        replica_copy(mine_ref, others_hbm.at[lax.axis_index("replica")], turn, send_sems, recv_sems, 5 + 3 * second_steps)
+        for turn in turns
+    ]
+    for copy in spread_copies:
+        copy.start()
 
     def first_product(block, waits):
         span = pl.ds(pl.multiple_of(block * 2 * rows, 2 * rows), 2 * rows)
@@ -454,6 +486,8 @@
             result_ref[:, cols] = (middle_ref[:, cols] + total).astype(BF)
     for copy in [beside_copy] + across_copies + relays:
         copy.wait_send()
+    for copy in spread_copies:
+        copy.wait()
     for at in range(second_steps):
         give(at).wait_send()
         cross(at).wait_send()
@@ -473,6 +507,10 @@
         jax.ShapeDtypeStruct((every, 2 * ff), BF),
     ]
     copies = 5 + 3 * steps
+    if backward:
+        replicas = lax.axis_size("replica")
+        out_shape.append(jax.ShapeDtypeStruct((replicas, rows, width), BF))
+        copies += replicas
     piece = pltpu.VMEM((steps, rows, CHUNK), BF)
     pair = pltpu.VMEM((steps, 2, rows, CHUNK), BF)
     scratch = [pltpu.VMEM(first.shape, BF), pltpu.VMEM(second.shape, BF), pair, piece, piece, piece, pair, piece]
@@ -488,7 +526,7 @@
         out_shape=out_shape,
         in_specs=[pl.BlockSpec(memory_space=pltpu.VMEM)] * (len(operands) - 2)
         + [pl.BlockSpec(memory_space=pl.ANY)] * 2,
-        out_specs=[pl.BlockSpec(memory_space=pltpu.VMEM)] * 3,
+        out_specs=[pl.BlockSpec(memory_space=pltpu.VMEM)] * 3 + [pl.BlockSpec(memory_space=pl.ANY)] * backward,
         scratch_shapes=scratch,
         compiler_params=pltpu.CompilerParams(
             collective_id=collective, has_side_effects=True, vmem_limit_bytes=VMEM_LIMIT
@@ -668,43 +706,23 @@
     )(qkv_weight, out_weight, gate_up_weight)
 
 
-def slice_peers():
-    shard = lax.axis_index("shard")
-    chip, core = shard // 2, shard % 2
-    return shard, chip * 2 + (1 - core), (1 - chip) * 2 + core, (1 - chip) * 2 + (1 - core)
-
-
-def slice_barrier(devices, replicas=1):
-    barrier = pltpu.get_barrier_semaphore()
-    for device in devices:
-        pl.semaphore_signal(barrier, inc=1, device_id={"shard": device}, device_id_type=MESH)
-    for turn in range(1, replicas):
-        target = lax.rem(lax.axis_index("replica") + turn, replicas)
-        pl.semaphore_signal(barrier, inc=1, device_id={"replica": target}, device_id_type=MESH)
-    pl.semaphore_wait(barrier, len(devices) + replicas - 1)
-
-
-def replica_copy(source, target, turn, send_sems, recv_sems, base):
-    replicas = lax.axis_size("replica")
-    device = lax.rem(lax.axis_index("replica") + replicas - turn, replicas)
-    return pltpu.make_async_remote_copy(
-        source, target, send_sems.at[base + turn], recv_sems.at[base + turn],
-        device_id={"replica": device}, device_id_type=MESH,
-    )
-
-
 def attend_grads_kernel(
-    projected_ref, branch_ref, left_qkv_ref, left_out_ref, upstream_ref, qkv_part_ref, out_part_ref, others_hbm,
-    all_ref, send_sems, recv_sems,
+    projected_ref, branch_ref, left_ref, upstream_ref, gains_ref, terms_ref, gain_sum_ref, others_hbm,
+    all_ref, gains_land_ref, send_sems, recv_sems,
 ):
     shard, beside, across, _ = slice_peers()
     replica, replicas = lax.axis_index("replica"), lax.axis_size("replica")
     rows, cols = projected_ref.shape
     pieces = all_ref.shape[0]
     step = all_ref.shape[2]
-    slice_barrier((beside, across), replicas)
+    sub_rows = terms_ref.shape[1]
+    slice_barrier((beside, across), range(1, replicas))
     spread_copies = [
         replica_copy(upstream_ref, others_hbm.at[replica], turn, send_sems, recv_sems, 3 * pieces)
+        for turn in range(2, replicas, 2)
+    ]
+    gain_copies = [
+        replica_copy(gains_ref, gains_land_ref.at[replica], turn, send_sems, recv_sems, 3 * pieces + replicas)
         for turn in range(1, replicas)
     ]
 
@@ -725,82 +743,135 @@
         )
         over[piece].start()
         direct[piece].start()
-    for copy in spread_copies:
+    gains_land_ref[replica] = gains_ref[...]
+    for copy in gain_copies + spread_copies:
         copy.start()
+
+    def product(piece):
+        direct[piece].wait_recv()
+        relays[piece].wait_recv()
+        at = piece * step
+        total = dot(left_ref[0 if at < cols else 1], all_ref[piece]).astype(BF)
+        for group in range(replicas):
+            terms_ref[group, :, at : at + step] = total[group * sub_rows : (group + 1) * sub_rows]
+
     for piece in range(pieces):
         over[piece].wait_recv()
         relays[piece].start()
-    for piece in range(pieces):
-        direct[piece].wait_recv()
-        relays[piece].wait_recv()
-        at = piece * step
-        if at < cols:
-            qkv_part_ref[:, at : at + step] = dot(left_qkv_ref[...], all_ref[piece]).astype(BF)
-        else:
-            out_part_ref[:, at - cols : at - cols + step] = dot(left_out_ref[...], all_ref[piece]).astype(BF)
+        if piece:
+            product(piece - 1)
+    product(pieces - 1)
+    for copy in gain_copies:
+        copy.wait()
+    gain_sum_ref[...] = jnp.sum(gains_land_ref[...], 0)
     for copy in over + direct + relays:
         copy.wait_send()
     for copy in spread_copies:
         copy.wait()
 
 
-def call_attend_grads(projected, branch, left_qkv, left_out, upstream, collective):
+def call_attend_grads(projected, branch, left, upstream, gains, collective):
     replicas = lax.axis_size("replica")
     rows, cols = projected.shape
     width = branch.shape[1]
-    every, tokens = left_qkv.shape
+    _, every, tokens = left.shape
     pieces = (cols + width) // CHUNK
+    copies = 3 * pieces + 2 * replicas
+    vmem = pl.BlockSpec(memory_space=pltpu.VMEM)
     return pl.pallas_call(
         attend_grads_kernel,
         out_shape=[
-            jax.ShapeDtypeStruct((every, cols), BF),
-            jax.ShapeDtypeStruct((every, width), BF),
+            jax.ShapeDtypeStruct((replicas, every // replicas, cols + width), BF),
+            jax.ShapeDtypeStruct(gains.shape, F32),
             jax.ShapeDtypeStruct((replicas,) + upstream.shape, BF),
         ],
-        in_specs=[pl.BlockSpec(memory_space=pltpu.VMEM)] * 5,
-        out_specs=[pl.BlockSpec(memory_space=pltpu.VMEM)] * 2 + [pl.BlockSpec(memory_space=pl.ANY)],
+        in_specs=[vmem] * 5,
+        out_specs=[vmem] * 2 + [pl.BlockSpec(memory_space=pl.ANY)],
         scratch_shapes=[
             pltpu.VMEM((pieces, tokens, CHUNK), BF),
-            pltpu.SemaphoreType.DMA((3 * pieces + replicas,)),
-            pltpu.SemaphoreType.DMA((3 * pieces + replicas,)),
+            pltpu.VMEM((replicas,) + gains.shape, F32),
+            pltpu.SemaphoreType.DMA((copies,)),
+            pltpu.SemaphoreType.DMA((copies,)),
         ],
         compiler_params=pltpu.CompilerParams(
             collective_id=collective, has_side_effects=True, vmem_limit_bytes=VMEM_LIMIT
         ),
         name="attend_grads",
-    )(projected, branch, left_qkv, left_out, upstream)
+    )(projected, branch, left, upstream, gains)
 
 
 def feed_grads_kernel(
-    upstream_ref, left_ref, hidden_ref, others_hbm, gate_up_hbm, down_hbm,
-    gate_up_grad_ref, down_grad_ref, gathered_hbm,
-    down_ref, block_ref, gate_up_ref, mid_ref, sum_ref, stage_ref,
-    load_sems, block_sems, send_sems, recv_sems,
+    left_ref, hidden_ref, terms_ref, gains_ref, upstream_hbm, odd_hbm, even_hbm, early_hbm, gate_up_hbm, down_hbm,
+    gate_up_grad_ref, down_grad_ref, attend_grad_ref, gain_sum_ref, gathered_hbm,
+    down_ref, block_ref, gate_up_ref, mid_ref, sum_ref, stage_ref, chain_ref, gains_land_ref,
+    load_sems, block_sems, keep_sem, send_sems, recv_sems,
 ):
     shard, beside, across, diagonal = slice_peers()
+    peers = (across, diagonal, beside)
     replica, replicas = lax.axis_index("replica"), lax.axis_size("replica")
-    rows = others_hbm.shape[1]
-    every, width = upstream_ref.shape
+    early = lax.axis_index("section") == lax.axis_size("section") - 1
+    late = lax.axis_index("section") < lax.axis_size("section") - 1
+    rows = odd_hbm.shape[1]
+    every, width = upstream_hbm.shape
     part = down_ref.shape[0]
+    half_part = part // 2
     ff = gate_up_grad_ref.shape[1] // 2
-    steps = part // CHUNK
+    steps = half_part // CHUNK
     wide = width // CHUNK
     out_rows = gate_up_grad_ref.shape[0]
-
-    load_down = pltpu.make_async_copy(down_hbm, down_ref, load_sems.at[0])
+    grad_base = 3 * replicas
+    chain_base = grad_base + 2 * 2 * steps * 3
+    gain_base = chain_base + 2 * replicas
+
+    load_down = pltpu.make_async_copy(down_hbm, down_ref, load_sems.at[3, 0])
     load_down.start()
 
     def block_at(turn):
         return lax.rem(replica + turn, replicas)
 
-    def load_gate_up(turn):
-        source = gate_up_hbm.at[pl.ds(pl.multiple_of(block_at(turn) * every, every), every)]
-        return pltpu.make_async_copy(source, gate_up_ref.at[turn % 2], block_sems.at[0, turn % 2])
+    def tokens(turn):
+        return pl.ds(pl.multiple_of(block_at(turn) * every, every), every)
+
+    def load_gate_up(half, turn, side):
+        cols = pl.ds(side * part + half * half_part, half_part)
+        slot = lax.rem(turn, 2)
+        return pltpu.make_async_copy(
+            gate_up_hbm.at[tokens(turn), cols], gate_up_ref.at[slot, side], load_sems.at[side, slot]
+        )
+
+    def block_copies(turn, source):
+        slot = lax.rem(turn, 2)
+        copies = []
+        for at, owner in enumerate(peers + (shard,)):
+            place = pl.ds(pl.multiple_of(owner * rows, rows), rows)
+            if source is early_hbm:
+                own = early_hbm.at[turn, place]
+            else:
+                own = gathered_hbm.at[turn, place] if source is None or at < 3 else source.at[block_at(turn)]
+            copies.append(pltpu.make_async_copy(own, block_ref.at[slot, place], block_sems.at[slot, at]))
+        return copies
 
     def load_block(turn):
-        return pltpu.make_async_copy(gathered_hbm.at[turn], block_ref.at[turn % 2], block_sems.at[1, turn % 2])
-
-    load_gate_up(0).start()
+        @pl.when(early & (turn > 0))
+        def _():
+            for copy in block_copies(turn, early_hbm):
+                copy.start()
+
+        @pl.when(late | (turn == 0))
+        def _():
+            for copy in block_copies(turn, None)[:3]:
+                copy.start()
+
+        cases = ((turn == 0, None), (late & (turn > 0) & (turn % 2 == 0), even_hbm), (late & (turn % 2 == 1), odd_hbm))
+        for case, source in cases:
+
+            @pl.when(case)
+            def _(source=source):
+                block_copies(turn, source)[3].start()
+
+    def wait_block(turn):
+        for copy in block_copies(turn, None):
+            copy.wait()
 
     def remote(source, target, at, device):
         return pltpu.make_async_remote_copy(
@@ -810,150 +881,337 @@
     def landing(turn, owner):
         return gathered_hbm.at[turn, pl.ds(pl.multiple_of(owner * rows, rows), rows)]
 
-    def over(turn):
-        return remote(others_hbm.at[block_at(turn)], landing(turn, shard), 3 * turn, across)
-
-    def direct(turn):
-        return remote(others_hbm.at[block_at(turn)], landing(turn, shard), 3 * turn + 1, beside)
+    def over(turn, source):
+        return remote(source.at[block_at(turn)], landing(turn, shard), 3 * turn, across)
+
+    def direct(turn, source):
+        return remote(source.at[block_at(turn)], landing(turn, shard), 3 * turn + 1, beside)
 
     def relay(turn):
         return remote(landing(turn, across), landing(turn, across), 3 * turn + 2, beside)
 
-    def keep(turn):
-        return pltpu.make_async_copy(others_hbm.at[block_at(turn)], landing(turn, shard), load_sems.at[turn])
-
-    slice_barrier((beside, across, diagonal))
-    for turn in range(1, replicas):
-        keep(turn).start()
-    for turn in range(1, min(3, replicas)):
-        over(turn).start()
-        direct(turn).start()
-    sum_ref[...] = jnp.zeros_like(sum_ref)
-    down_grad_ref[...] = jnp.zeros_like(down_grad_ref)
+    def send_block(turn):
+        for parity, source in ((0, even_hbm), (1, odd_hbm)):
+
+            @pl.when(lax.rem(turn, 2) == parity)
+            def _(source=source):
+                over(turn, source).start()
+                direct(turn, source).start()
+
+    def chain_slot(block, at):
+        return replicas - (replicas - block) * ((at - block + replicas - 1) // replicas)
+
+    def chain_up(block):
+        return pltpu.make_async_remote_copy(
+            chain_ref.at[block], chain_ref.at[block], send_sems.at[chain_base + block],
+            recv_sems.at[chain_base + block], device_id={"replica": replica + 1}, device_id_type=MESH,
+        )
+
+    def chain_down(block):
+        return pltpu.make_async_remote_copy(
+            chain_ref.at[block], chain_ref.at[chain_slot(block, replica - 1)],
+            send_sems.at[chain_base + replicas + block],
+            recv_sems.at[chain_base + replicas + block], device_id={"replica": replica - 1}, device_id_type=MESH,
+        )
+
+    def add_terms(block):
+        chain_ref[block] = (chain_ref[block].astype(F32) + terms_ref[block].astype(F32)).astype(BF)
+
+    def chain_step(step):
+        high = replicas - 1 - step + replica
+
+        @pl.when((replica > 0) & (step >= replica))
+        def _():
+            chain_up(high).wait_recv()
+
+            @pl.when(step < replicas - 1)
+            def _():
+                add_terms(high)
+                chain_up(high).start()
+
+        low = step - (replicas - 1 - replica)
+
+        @pl.when((replica < replicas - 1) & (step >= replicas - 1 - replica))
+        def _():
+            chain_down(low).wait_recv()
+
+            @pl.when(step < replicas - 1)
+            def _():
+                add_terms(low)
+                chain_down(low).start()
+
+    def gain_copy(peer):
+        return remote(
+            gains_ref, gains_land_ref.at[shard], gain_base + peer, peers[peer]
+        )
+
+    barrier = pltpu.get_barrier_semaphore()
+    for device in peers:
+        pl.semaphore_signal(barrier, inc=1, device_id={"shard": device}, device_id_type=MESH)
+
+    @pl.when(replica > 0)
+    def _():
+        pl.semaphore_signal(barrier, inc=1, device_id={"replica": replica - 1}, device_id_type=MESH)
+
+    @pl.when(replica < replicas - 1)
+    def _():
+        pl.semaphore_signal(barrier, inc=1, device_id={"replica": replica + 1}, device_id_type=MESH)
+
+    below = (replica + replicas - 1) // replicas
+    above = (2 * replicas - 2 - replica) // replicas
+    pl.semaphore_wait(barrier, 3 + below + above)
+
+    @pl.when(late)
+    def _():
+        for turn in range(1, min(3, replicas)):
+            send_block(turn)
+
+    for block in reversed(range(1, replicas)):
+
+        @pl.when(replica == 0)
+        def _(block=block):
+            chain_ref[block] = terms_ref[block]
+            chain_up(block).start()
+
+    for block in range(replicas - 1):
+
+        @pl.when(replica == replicas - 1)
+        def _(block=block):
+            chain_ref[block] = terms_ref[block]
+            chain_down(block).start()
+
+    for peer in range(3):
+        gain_copy(peer).start()
+    gains_land_ref[shard] = gains_ref[...]
+    load_own = pltpu.make_async_copy(upstream_hbm, block_ref.at[0], load_sems.at[2, 0])
+    load_own.start()
+    load_own.wait()
+    keep_own = pltpu.make_async_copy(block_ref.at[0], gathered_hbm.at[0], keep_sem)
+    keep_own.start()
     load_down.wait()
-
-    def send_grad(at, peer, device):
-        cols = pl.ds(pl.multiple_of(at * CHUNK, CHUNK), CHUNK)
-        side, offset = at // steps, at % steps
-        target = pl.ds(pl.multiple_of(side * ff + shard * part + offset * CHUNK, CHUNK), CHUNK)
-        return remote(
-            stage_ref.at[pl.ds(pl.multiple_of(device * out_rows, out_rows), out_rows), cols],
-            gate_up_grad_ref.at[:, target],
-            3 * replicas + peer * 2 * steps + at,
-            device,
-        )
-
-    def work(turn, grad_rows):
-        slot = turn % 2
-        load_gate_up(turn).wait()
-        tokens = pl.ds(pl.multiple_of(block_at(turn) * every, every), every)
-
-        def products(at, carry):
-            cols = pl.ds(pl.multiple_of(at * CHUNK, CHUNK), CHUNK)
-            high = pl.ds(pl.multiple_of(part + at * CHUNK, CHUNK), CHUNK)
-            grad_hidden = dot_rows(grad_rows[...], down_ref[cols, :])
-            gate = gate_up_ref[slot, :, cols].astype(F32)
-            up = gate_up_ref[slot, :, high].astype(F32)
-            sigmoid = jax.nn.sigmoid(gate)
-            mid_ref[:, cols] = (grad_hidden * up * sigmoid * (1.0 + gate * (1.0 - sigmoid))).astype(BF)
-            mid_ref[:, high] = (grad_hidden * gate * sigmoid).astype(BF)
-            return carry
-
-        lax.fori_loop(0, steps, products, 0)
-
-        def sums(at, carry):
-            cols = pl.ds(pl.multiple_of(at * CHUNK, CHUNK), CHUNK)
-            total = sum_ref[:, cols] + dot(left_ref[:, tokens], mid_ref[:, cols])
-            if turn < replicas - 1:
-                sum_ref[:, cols] = total
-            else:
-                stage_ref[:, cols] = total.astype(BF)
-                for peer, device in enumerate((across, diagonal, beside)):
-                    send_grad(at, peer, device).start()
-            return carry
-
-        lax.fori_loop(0, 2 * steps, sums, 0)
-
-        def down_sums(at, carry):
-            cols = pl.ds(pl.multiple_of(at * CHUNK, CHUNK), CHUNK)
-            down_grad_ref[:, cols] += dot(hidden_ref[:, tokens], grad_rows[:, cols])
-            return carry
-
-        lax.fori_loop(0, wide, down_sums, 0)
-
-    for turn in range(replicas):
-        if turn + 1 < replicas:
-            load_gate_up(turn + 1).start()
-        if turn == 0:
-            work(0, upstream_ref)
-        else:
-            work(turn, block_ref.at[turn % 2])
-        after = turn + 1
-        if after < replicas:
-            over(after).wait_recv()
-            relay(after).start()
-            direct(after).wait_recv()
-            keep(after).wait()
-            relay(after).wait_recv()
-            load_block(after).start()
-            if after + 2 < replicas:
-                over(after).wait_send()
-                direct(after).wait_send()
-                over(after + 2).start()
-                direct(after + 2).start()
-            load_block(after).wait()
-    own = pl.ds(pl.multiple_of(shard * out_rows, out_rows), out_rows)
-
-    def store_own(at, carry):
+    keep_own.wait()
+
+    def send_grad(half, at, peer):
+        device = peers[peer]
         cols = pl.ds(pl.multiple_of(at * CHUNK, CHUNK), CHUNK)
         target = pl.ds(
-            pl.multiple_of((at // steps) * ff + shard * part + (at % steps) * CHUNK, CHUNK), CHUNK
-        )
-        gate_up_grad_ref[:, target] = stage_ref[own, cols]
+            pl.multiple_of(
+                (at // steps) * ff + shard * part + half * half_part + (at % steps) * CHUNK, CHUNK
+            ),
+            CHUNK,
+        )
+        return remote(
+            stage_ref.at[half, pl.ds(pl.multiple_of(device * out_rows, out_rows), out_rows), cols],
+            gate_up_grad_ref.at[:, target],
+            grad_base + (half * 2 * steps + at) * 3 + peer,
+            device,
+        )
+
+    def half_pass(half):
+        for side in range(2):
+            load_gate_up(half, 0, side).start()
+        sum_ref[...] = jnp.zeros_like(sum_ref)
+
+        def work(turn, carry):
+            slot = lax.rem(turn, 2)
+            later = lax.rem(turn + 1, replicas)
+            for side in range(2):
+                load_gate_up(half, turn, side).wait()
+
+            @pl.when(turn + 1 < replicas)
+            def _():
+                for side in range(2):
+                    load_gate_up(half, later, side).start()
+
+            if half:
+
+                @pl.when(turn + 1 < replicas)
+                def _():
+                    load_block(later)
+
+            def products(at, inner):
+                cols = pl.ds(pl.multiple_of(at * CHUNK, CHUNK), CHUNK)
+                high = pl.ds(pl.multiple_of(half_part + at * CHUNK, CHUNK), CHUNK)
+                down_rows = pl.ds(pl.multiple_of(half * half_part + at * CHUNK, CHUNK), CHUNK)
+                grad_hidden = dot_rows(block_ref[slot], down_ref[down_rows, :])
+                gate = gate_up_ref[slot, 0, :, cols].astype(F32)
+                up = gate_up_ref[slot, 1, :, cols].astype(F32)
+                sigmoid = jax.nn.sigmoid(gate)
+                mid_ref[:, cols] = (grad_hidden * up * sigmoid * (1.0 + gate * (1.0 - sigmoid))).astype(BF)
+                mid_ref[:, high] = (grad_hidden * gate * sigmoid).astype(BF)
+                return inner
+
+            lax.fori_loop(0, steps, products, 0)
+
+            def sums(at, inner):
+                cols = pl.ds(pl.multiple_of(at * CHUNK, CHUNK), CHUNK)
+                total = sum_ref[:, cols] + dot(left_ref[:, tokens(turn)], mid_ref[:, cols])
+
+                @pl.when(turn < replicas - 1)
+                def _():
+                    sum_ref[:, cols] = total
+
+                @pl.when(turn == replicas - 1)
+                def _():
+                    stage_ref[half, :, cols] = total.astype(BF)
+                    for peer in range(3):
+                        send_grad(half, at, peer).start()
+
+                return inner
+
+            lax.fori_loop(0, 2 * steps, sums, 0)
+
+            @pl.when(turn + 1 < replicas)
+            def _():
+                if half:
+                    wait_block(later)
+                else:
+
+                    @pl.when(late)
+                    def _():
+                        over(later, even_hbm).wait_recv()
+                        relay(later).start()
+                        direct(later, even_hbm).wait_recv()
+                        relay(later).wait_recv()
+
+                    load_block(later)
+
+                    @pl.when(late & (turn + 3 < replicas))
+                    def _():
+                        send_block(turn + 3)
+
+                    wait_block(later)
+
+            return carry
+
+        return work
+
+    first = half_pass(0)
+    lax.fori_loop(0, replicas - 1, first, 0)
+    chain_step(1)
+    first(replicas - 1, 0)
+    load_block(0)
+    wait_block(0)
+    second = half_pass(1)
+    lax.fori_loop(0, replicas - 1, second, 0)
+    if replicas > 2:
+        chain_step(2)
+    second(replicas - 1, 0)
+    load_block(0)
+    wait_block(0)
+    down_grad_ref[...] = jnp.zeros_like(down_grad_ref)
+
+    def down_work(turn, carry):
+        slot = lax.rem(turn, 2)
+        later = lax.rem(turn + 1, replicas)
+
+        @pl.when(turn + 1 < replicas)
+        def _():
+            load_block(later)
+
+        def down_sums(at, inner):
+            cols = pl.ds(pl.multiple_of(at * CHUNK, CHUNK), CHUNK)
+            down_grad_ref[:, cols] += dot(hidden_ref[:, tokens(turn)], block_ref[slot, :, cols])
+            return inner
+
+        lax.fori_loop(0, wide, down_sums, 0)
+
+        @pl.when(turn + 1 < replicas)
+        def _():
+            wait_block(later)
+
         return carry
 
-    lax.fori_loop(0, 2 * steps, store_own, 0)
-
-    def finish(at, carry):
-        for peer, device in enumerate((across, diagonal, beside)):
-            send_grad(at, peer, device).wait_recv()
-            send_grad(at, peer, device).wait_send()
-        return carry
-
-    lax.fori_loop(0, 2 * steps, finish, 0)
-    for turn in range(1, replicas):
-        relay(turn).wait_send()
-        if turn + 2 >= replicas:
-            over(turn).wait_send()
-            direct(turn).wait_send()
-
-
-def call_feed_grads(upstream, left, hidden, others, gate_up, down, collective):
+    lax.fori_loop(0, replicas, down_work, 0)
+    for peer in range(3):
+        gain_copy(peer).wait()
+    gain_sum_ref[...] = jnp.sum(gains_land_ref[...], 0)
+    own = pl.ds(pl.multiple_of(shard * out_rows, out_rows), out_rows)
+    for half in range(2):
+
+        def store_own(at, carry, half=half):
+            cols = pl.ds(pl.multiple_of(at * CHUNK, CHUNK), CHUNK)
+            target = pl.ds(
+                pl.multiple_of(
+                    (at // steps) * ff + shard * part + half * half_part + (at % steps) * CHUNK, CHUNK
+                ),
+                CHUNK,
+            )
+            gate_up_grad_ref[:, target] = stage_ref[half, own, cols]
+            return carry
+
+        lax.fori_loop(0, 2 * steps, store_own, 0)
+    for step in range(3, replicas):
+        chain_step(step)
+    attend_grad_ref[...] = terms_ref[replica].astype(F32)
+
+    @pl.when(replica > 0)
+    def _():
+        attend_grad_ref[...] += chain_ref[replica].astype(F32)
+
+    @pl.when(replica < replicas - 1)
+    def _():
+        attend_grad_ref[...] += chain_ref[replicas].astype(F32)
+
+    for half in range(2):
+
+        def finish(at, carry, half=half):
+            for peer in range(3):
+                send_grad(half, at, peer).wait()
+            return carry
+
+        lax.fori_loop(0, 2 * steps, finish, 0)
+    @pl.when(late)
+    def _():
+        for turn in range(1, replicas):
+            over(turn, even_hbm).wait_send()
+            direct(turn, even_hbm).wait_send()
+            relay(turn).wait_send()
+
+    for block in range(1, replicas):
+
+        @pl.when(replica < block)
+        def _(block=block):
+            chain_up(block).wait_send()
+
+    for block in range(replicas - 1):
+
+        @pl.when(replica > block)
+        def _(block=block):
+            chain_down(block).wait_send()
+
+
+def call_feed_grads(left, hidden, terms, gains, upstream, odd, even, early, gate_up, down, collective):
     every, width = upstream.shape
-    replicas, rows, _ = others.shape
+    replicas = odd.shape[0]
     shards = lax.axis_size("shard")
     part = down.shape[0]
     out_rows = left.shape[0] // shards
     vmem, anywhere = pl.BlockSpec(memory_space=pltpu.VMEM), pl.BlockSpec(memory_space=pl.ANY)
-    copies = 3 * replicas + 3 * 2 * (part // CHUNK)
+    copies = 5 * replicas + 3 * 2 * (part // CHUNK) + 3
     return pl.pallas_call(
         feed_grads_kernel,
         out_shape=[
             jax.ShapeDtypeStruct((out_rows, 2 * part * shards), BF),
             jax.ShapeDtypeStruct((hidden.shape[0], width), F32),
+            jax.ShapeDtypeStruct(terms.shape[1:], F32),
+            jax.ShapeDtypeStruct(gains.shape, F32),
             jax.ShapeDtypeStruct((replicas, every, width), BF),
         ],
-        in_specs=[vmem] * 3 + [anywhere] * 3,
-        out_specs=[vmem, vmem, anywhere],
+        in_specs=[vmem] * 4 + [anywhere] * 6,
+        out_specs=[vmem] * 4 + [anywhere],
         scratch_shapes=[
             pltpu.VMEM(down.shape, BF),
             pltpu.VMEM((2, every, width), BF),
-            pltpu.VMEM((2, every, 2 * part), BF),
-            pltpu.VMEM((every, 2 * part), BF),
-            pltpu.VMEM((left.shape[0], 2 * part), F32),
-            pltpu.VMEM((left.shape[0], 2 * part), BF),
-            pltpu.SemaphoreType.DMA((max(replicas, 2),)),
-            pltpu.SemaphoreType.DMA((2, 2)),
+            pltpu.VMEM((2, 2, every, part // 2), BF),
+            pltpu.VMEM((every, part), BF),
+            pltpu.VMEM((left.shape[0], part), F32),
+            pltpu.VMEM((2, left.shape[0], part), BF),
+            pltpu.VMEM((replicas + 1,) + terms.shape[1:], BF),
+            pltpu.VMEM((shards,) + gains.shape, F32),
+            pltpu.SemaphoreType.DMA((4, 2)),
+            pltpu.SemaphoreType.DMA((2, 4)),
+            pltpu.SemaphoreType.DMA,
             pltpu.SemaphoreType.DMA((copies,)),
             pltpu.SemaphoreType.DMA((copies,)),
         ],
@@ -961,24 +1219,31 @@
             collective_id=collective, has_side_effects=True, vmem_limit_bytes=VMEM_LIMIT
         ),
         name="feed_grads",
-    )(upstream, left, hidden, others, gate_up, down)
+    )(left, hidden, terms, gains, upstream, odd, even, early, gate_up, down)
+
+
+def turn_order(replicas):
+    return [0] + list(range(1, replicas, 2)) + list(range(2, replicas, 2))
 
 
 def prepare_kernel(
-    normed_two_ref, lefts_ref, gate_up_hbm, gathered_hbm, gate_up_all_hbm, hidden_hbm, left_hbm,
-    weight_ref, block_ref, gate_up_ref, hidden_ref,
-    load_sems, store_sems, keep_sems, send_sems, recv_sems,
+    sections, normed_two_ref, lefts_ref, gate_up_hbm, *refs
 ):
+    slices = refs[:sections]
+    (gathered_hbm, gate_up_all_hbm, hidden_hbm, left_hbm, left_rows_ref,
+     weight_ref, block_ref, gate_up_ref, hidden_ref, turned_ref,
+     load_sems, store_sems, keep_sems, send_sems, recv_sems) = refs[sections:]
     shard, beside, across, diagonal = slice_peers()
     peers = (across, diagonal, beside)
     replica, replicas = lax.axis_index("replica"), lax.axis_size("replica")
     shards = lax.axis_size("shard")
     rows, width = normed_two_ref.shape
     every = rows * shards
-    part = hidden_ref.shape[2]
-    ff_rows = hidden_hbm.shape[1]
+    part = hidden_ref.shape[1]
+    ff_rows = hidden_hbm.shape[0]
     steps = part // CHUNK
-    kinds, groups, _, _, sub_rows = lefts_ref.shape
+    slice_rows = left_rows_ref.shape[0]
+    kinds, groups = lefts_ref.shape[:2]
     owner = (replica * shards) // replicas
     first_col = lax.rem(replica * shards, replicas) * ff_rows
 
@@ -995,42 +1260,40 @@
             source, target, send_sems.at[at], recv_sems.at[at], device_id={"shard": device}, device_id_type=MESH
         )
 
-    def block_at(turn):
-        return lax.rem(replica + turn, replicas)
-
     def landing(turn, who):
-        return gathered_hbm.at[block_at(turn), pl.ds(pl.multiple_of(who * rows, rows), rows)]
+        return gathered_hbm.at[turn, pl.ds(pl.multiple_of(who * rows, rows), rows)]
 
     def over(turn):
-        return remote(landing(turn, shard) if turn else normed_two_ref, landing(turn, shard), 3 * turn, across)
+        return remote(landing(turn, shard), landing(turn, shard), 3 * turn, across)
 
     def direct(turn):
-        return remote(landing(turn, shard) if turn else normed_two_ref, landing(turn, shard), 3 * turn + 1, beside)
+        return remote(landing(turn, shard), landing(turn, shard), 3 * turn + 1, beside)
 
     def relay(turn):
         return remote(landing(turn, across), landing(turn, across), 3 * turn + 2, beside)
 
     def from_replica(turn):
-        return replica_copy(normed_two_ref, landing(0, shard), turn, send_sems, recv_sems, 3 * replicas)
+        return replica_copy(normed_two_ref, landing(turn, shard), turn, send_sems, recv_sems, 3 * replicas)
 
     def tokens(turn):
-        return pl.ds(pl.multiple_of(block_at(turn) * every, every), every)
-
-    def load_block(turn):
-        return pltpu.make_async_copy(gathered_hbm.at[block_at(turn)], block_ref.at[turn % 2], store_sems.at[0, turn % 2])
-
-    def store_block(turn):
-        return pltpu.make_async_copy(gate_up_ref.at[turn % 2], gate_up_all_hbm.at[tokens(turn)], store_sems.at[1, turn % 2])
-
-    def hidden_cols(turn, device):
-        return hidden_ref.at[turn % 2, :, pl.ds(pl.multiple_of(first_col + device * ff_rows, ff_rows), ff_rows)]
-
-    def hand_hidden(turn, peer):
+        return pl.ds(pl.multiple_of(lax.rem(replica + turn, replicas) * every, every), every)
+
+    def load_block(turn, slot):
+        return pltpu.make_async_copy(gathered_hbm.at[turn], block_ref.at[slot], store_sems.at[0, slot])
+
+    def store_block(turn, slot):
+        return pltpu.make_async_copy(gate_up_ref.at[slot], gate_up_all_hbm.at[tokens(turn)], store_sems.at[1, slot])
+
+    def hand_hidden(turn, slot, peer):
         device = peers[peer]
-        return remote(hidden_cols(turn, device), hidden_hbm.at[tokens(turn)], 4 * replicas + 3 * turn + peer, device)
-
-    def keep_hidden(turn):
-        return pltpu.make_async_copy(hidden_cols(turn, shard), hidden_hbm.at[tokens(turn)], store_sems.at[2, turn % 2])
+        return remote(
+            turned_ref.at[slot, device], hidden_hbm.at[:, tokens(turn)], 4 * replicas + 3 * turn + peer, device
+        )
+
+    def keep_hidden(turn, slot):
+        return pltpu.make_async_copy(
+            turned_ref.at[slot, shard], hidden_hbm.at[:, tokens(turn)], store_sems.at[2, slot]
+        )
 
     own_rows = pl.ds(pl.multiple_of(shard * rows, rows), rows)
 
@@ -1038,94 +1301,111 @@
         device = peers[peer]
         return remote(
             lefts_ref.at[kind, group, device],
-            left_hbm.at[kind, group, own_rows],
+            left_hbm.at[kind, group, :, own_rows],
             7 * replicas + (kind * groups + group) * 3 + peer,
             device,
         )
 
     def keep_left(kind, group):
         return pltpu.make_async_copy(
-            lefts_ref.at[kind, group, shard], left_hbm.at[kind, group, own_rows], keep_sems.at[1 + kind * groups + group]
-        )
-
-    keep_own = pltpu.make_async_copy(normed_two_ref, landing(0, shard), keep_sems.at[0])
-    slice_barrier(peers, replicas)
-    over(0).start()
-    direct(0).start()
-    for turn in range(1, replicas):
-        from_replica(turn).start()
-    keep_own.start()
+            lefts_ref.at[kind, group, shard], left_hbm.at[kind, group, :, own_rows],
+            keep_sems.at[kind * groups + group],
+        )
+
+    for section in range(sections):
+
+        @pl.when(lax.axis_index("section") == section)
+        def _(section=section):
+            pltpu.make_async_copy(slices[section], block_ref.at[0], store_sems.at[0, 0]).start()
+
+    slice_barrier(peers, range(1, replicas))
+    order = turn_order(replicas)
+    if replicas > 1:
+        from_replica(order[1]).start()
     for kind in range(kinds):
         for group in range(groups):
             keep_left(kind, group).start()
             for peer in range(3):
                 hand_left(kind, group, peer).start()
 
-    for turn in range(replicas):
-        over(turn).wait_recv()
-        relay(turn).start()
-        if turn + 1 < replicas:
-            from_replica(turn + 1).wait_recv()
-            over(turn + 1).start()
-            direct(turn + 1).start()
-        direct(turn).wait_recv()
-        if turn == 0:
-            keep_own.wait()
-        relay(turn).wait_recv()
-        load_block(turn).start()
-        load_block(turn).wait()
-        if turn > 1:
-            store_block(turn - 2).wait()
-
-            @pl.when(shard == owner)
-            def _(turn=turn):
-                keep_hidden(turn - 2).wait()
-                for peer in range(3):
-                    hand_hidden(turn - 2, peer).wait_send()
-
-        def products(at, carry, turn=turn):
-            slot = turn % 2
-            cols = pl.ds(pl.multiple_of(at * CHUNK, CHUNK), CHUNK)
-            high = pl.ds(pl.multiple_of(part + at * CHUNK, CHUNK), CHUNK)
-            if turn == 0:
-                load_weight(0, at).wait()
-                load_weight(1, at).wait()
+    for at, turn in enumerate(order):
+        later = order[at + 1] if at + 1 < replicas else None
+        slot = at % 2
+        if later is not None:
+            from_replica(later).wait_recv()
+            over(later).start()
+            direct(later).start()
+            if at + 2 < replicas:
+                from_replica(later).wait_send()
+                from_replica(order[at + 2]).start()
+        load_block(turn, slot).wait()
+        if at > 1:
+            store_block(order[at - 2], slot).wait()
+
+        def products(step, carry, at=at, slot=slot):
+            cols = pl.ds(pl.multiple_of(step * CHUNK, CHUNK), CHUNK)
+            high = pl.ds(pl.multiple_of(part + step * CHUNK, CHUNK), CHUNK)
+            if at == 0:
+                load_weight(0, step).wait()
+                load_weight(1, step).wait()
             gate = dot(block_ref[slot], weight_ref[:, cols])
             up = dot(block_ref[slot], weight_ref[:, high])
             gate_up_ref[slot, :, cols] = gate.astype(BF)
             gate_up_ref[slot, :, high] = up.astype(BF)
-            hidden_ref[slot, :, cols] = (gate * jax.nn.sigmoid(gate) * up).astype(BF)
+            hidden_ref[:, cols] = (gate * jax.nn.sigmoid(gate) * up).astype(BF)
             return carry
 
         lax.fori_loop(0, steps, products, 0)
-        store_block(turn).start()
+        store_block(turn, slot).start()
+        if later is not None:
+            over(later).wait_recv()
+            relay(later).start()
 
         @pl.when(shard == owner)
-        def _(turn=turn):
-            keep_hidden(turn).start()
+        def _(at=at, turn=turn, slot=slot):
+            if at > 1:
+                keep_hidden(order[at - 2], slot).wait()
+                for peer in range(3):
+                    hand_hidden(order[at - 2], slot, peer).wait_send()
+
+            def turn_over(device, carry):
+                cols = pl.ds(pl.multiple_of(first_col + device * ff_rows, ff_rows), ff_rows)
+                turned_ref[slot, device] = hidden_ref[:, cols].T
+                return carry
+
+            lax.fori_loop(0, shards, turn_over, 0)
+            keep_hidden(turn, slot).start()
             for peer in range(3):
-                hand_hidden(turn, peer).start()
-
-    for turn in range(max(0, replicas - 2), replicas):
-        store_block(turn).wait()
+                hand_hidden(turn, slot, peer).start()
+
+        slice_cols = pl.ds(pl.multiple_of(replica * slice_rows, slice_rows), slice_rows)
+        left_rows_ref[:, tokens(turn)] = block_ref[slot, :, slice_cols].T
+        if later is not None:
+            direct(later).wait_recv()
+            relay(later).wait_recv()
+            load_block(later, 1 - slot).start()
+
+    for at in range(max(0, replicas - 2), replicas):
+        store_block(order[at], at % 2).wait()
 
         @pl.when(shard == owner)
-        def _(turn=turn):
-            keep_hidden(turn).wait()
+        def _(at=at):
+            keep_hidden(order[at], at % 2).wait()
             for peer in range(3):
-                hand_hidden(turn, peer).wait_send()
+                hand_hidden(order[at], at % 2, peer).wait_send()
 
     for turn in range(replicas):
         for peer in range(3):
 
             @pl.when(peers[peer] == owner)
             def _(turn=turn, peer=peer):
-                hand_hidden(turn, peer).wait_recv()
-
-        over(turn).wait_send()
-        direct(turn).wait_send()
-        relay(turn).wait_send()
+                hand_hidden(turn, 0, peer).wait_recv()
+
         if turn:
+            over(turn).wait_send()
+            direct(turn).wait_send()
+            relay(turn).wait_send()
+        if turn and turn == order[-1]:
             from_replica(turn).wait_send()
     for kind in range(kinds):
         for group in range(groups):
@@ -1134,34 +1414,37 @@
                 hand_left(kind, group, peer).wait()
 
 
-def call_prepare(normed_two, normed, attended, gate_up_part, collective):
+def call_prepare(normed_two, normed, attended, gate_up_part, slices, collective):
     rows, width = normed_two.shape
     shards, replicas = lax.axis_size("shard"), lax.axis_size("replica")
     part = gate_up_part.shape[1] // 2
     every = rows * shards
-    sub_rows = width // (replicas * shards)
+    slice_rows = width // replicas
+    sub_rows = slice_rows // shards
     ff_rows = part // replicas
-    lefts = jnp.stack([normed, attended]).reshape(2, rows, replicas, shards, sub_rows).transpose(0, 2, 3, 1, 4)
+    lefts = jnp.stack([normed.T, attended.T]).reshape(2, replicas, shards, sub_rows, rows)
     vmem, anywhere = pl.BlockSpec(memory_space=pltpu.VMEM), pl.BlockSpec(memory_space=pl.ANY)
     copies = 7 * replicas + 2 * replicas * 3
-    return pl.pallas_call(
-        prepare_kernel,
+    outs = pl.pallas_call(
+        functools.partial(prepare_kernel, len(slices)),
         out_shape=[
             jax.ShapeDtypeStruct((replicas, every, width), BF),
             jax.ShapeDtypeStruct((replicas * every, 2 * part), BF),
-            jax.ShapeDtypeStruct((replicas * every, ff_rows), BF),
-            jax.ShapeDtypeStruct((2, replicas, every, sub_rows), BF),
+            jax.ShapeDtypeStruct((ff_rows, replicas * every), BF),
+            jax.ShapeDtypeStruct((2, replicas, sub_rows, every), BF),
+            jax.ShapeDtypeStruct((slice_rows, replicas * every), BF),
         ],
-        in_specs=[vmem, vmem, anywhere],
-        out_specs=[anywhere] * 4,
+        in_specs=[vmem, vmem, anywhere] + [anywhere] * len(slices),
+        out_specs=[anywhere] * 4 + [vmem],
         scratch_shapes=[
             pltpu.VMEM(gate_up_part.shape, BF),
             pltpu.VMEM((2, every, width), BF),
             pltpu.VMEM((2, every, 2 * part), BF),
-            pltpu.VMEM((2, every, part), BF),
+            pltpu.VMEM((every, part), BF),
+            pltpu.VMEM((2, shards, ff_rows, every), BF),
             pltpu.SemaphoreType.DMA((2, part // CHUNK)),
             pltpu.SemaphoreType.DMA((3, 2)),
-            pltpu.SemaphoreType.DMA((1 + 2 * replicas,)),
+            pltpu.SemaphoreType.DMA((2 * replicas,)),
             pltpu.SemaphoreType.DMA((copies,)),
             pltpu.SemaphoreType.DMA((copies,)),
         ],
@@ -1169,7 +1452,68 @@
             collective_id=collective, has_side_effects=True, vmem_limit_bytes=VMEM_LIMIT
         ),
         name="prepare",
-    )(normed_two, lefts, gate_up_part)
+    )(normed_two, lefts, gate_up_part, *slices)
+    _, gate_up_all, hidden_rows, lefts, left_rows = outs
+    return gate_up_all, hidden_rows, lefts.reshape(2, replicas * sub_rows, every), left_rows
+
+
+def gather_kernel(mine_ref, gathered_hbm, send_sems, recv_sems):
+    shard, beside, across, _ = slice_peers()
+    replicas = lax.axis_size("replica")
+    rows = mine_ref.shape[0]
+
+    def remote(owner, turn, at, device):
+        place = gathered_hbm.at[turn, pl.ds(pl.multiple_of(owner * rows, rows), rows)]
+        return pltpu.make_async_remote_copy(
+            place, place, send_sems.at[at], recv_sems.at[at], device_id={"shard": device}, device_id_type=MESH
+        )
+
+    own_rows = pl.ds(pl.multiple_of(shard * rows, rows), rows)
+    slice_barrier((beside, across), range(1, replicas))
+    order = turn_order(replicas)[1:]
+    spread_copies = [
+        replica_copy(mine_ref, gathered_hbm.at[turn, own_rows], turn, send_sems, recv_sems, 3 * replicas)
+        for turn in order
+    ]
+    over = [remote(shard, turn, 3 * turn, across) for turn in order]
+    direct = [remote(shard, turn, 3 * turn + 1, beside) for turn in order]
+    relays = [remote(across, turn, 3 * turn + 2, beside) for turn in order]
+    spread_copies[0].start()
+    for at in range(replicas - 1):
+        spread_copies[at].wait_recv()
+        over[at].start()
+        direct[at].start()
+        spread_copies[at].wait_send()
+        if at + 2 < replicas:
+            spread_copies[at + 1].start()
+        if at:
+            over[at - 1].wait_recv()
+            relays[at - 1].start()
+    over[-1].wait_recv()
+    relays[-1].start()
+    for copy in direct + relays:
+        copy.wait_recv()
+    for copy in over + direct + relays:
+        copy.wait_send()
+
+
+def call_gather(section, mine, collective):
+    replicas, shards = lax.axis_size("replica"), lax.axis_size("shard")
+    rows, width = mine.shape
+    return pl.pallas_call(
+        gated(section, gather_kernel),
+        out_shape=jax.ShapeDtypeStruct((replicas, shards * rows, width), BF),
+        in_specs=[pl.BlockSpec(memory_space=pltpu.VMEM)],
+        out_specs=pl.BlockSpec(memory_space=pl.ANY),
+        scratch_shapes=[
+            pltpu.SemaphoreType.DMA((4 * replicas,)),
+            pltpu.SemaphoreType.DMA((4 * replicas,)),
+        ],
+        compiler_params=pltpu.CompilerParams(
+            collective_id=collective, has_side_effects=True, vmem_limit_bytes=VMEM_LIMIT
+        ),
+        name="gather",
+    )(mine)
 
 
 def on_device(
@@ -1184,9 +1528,6 @@
     cotangent,
 ):
     sections = lax.axis_size("section")
-    replicas = lax.axis_size("replica")
-    shards = lax.axis_size("shard")
-    replica_at = lax.axis_index("replica")
     rows, width = tokens_in.shape
     up_steps = [(at, at + 1) for at in range(sections - 1)]
     down_steps = [(at + 1, at) for at in range(sections - 1)]
@@ -1203,12 +1544,16 @@
         middle, normed_two, normed, rotated, attended = call_attend_forward(
             section, state, attn_gain, mlp_gain, cosine, sine, allowed, qkv_full, out_full
         )
-        block_out, _, gate_up = call_feed(
+        block_out, normed_two_slice, gate_up = call_feed(
             section, False, (normed_two, middle, gate_up_part, down_part), 8 + section
         )
-        forward.append((state, middle, rotated, gate_up, normed_two, normed, attended, block_out))
+        forward.append((state, middle, rotated, gate_up, normed_two_slice, normed_two, normed, attended, block_out))
         if section + 1 < sections:
             state = lax.ppermute(block_out, "section", up_steps)
+        if section + 2 == sections:
+            held, _ = lax.optimization_barrier((cotangent, block_out))
+            early = call_gather(sections - 1, held, 7)
+            state, early = lax.optimization_barrier((state, early))
 
     def pick(values):
         chosen = values[-1]
@@ -1216,22 +1561,19 @@
             chosen = jnp.where(lax.axis_index("section") == section, values[section], chosen)
         return chosen
 
-    normed_two, normed, attended, block_out = [pick(values) for values in list(zip(*forward))[4:]]
-    both = ("replica", "shard")
-    slice_rows = width // replicas
-
+    normed_two, normed, attended, block_out = [pick(values) for values in list(zip(*forward))[5:]]
     backward = []
     upstream = cotangent
     for section in reversed(range(sections)):
         state, middle, rotated, gate_up = forward[section][:4]
-        grad_normed_two, upstream_slice, _ = call_feed(
+        grad_normed_two, upstream_slice, _, odd = call_feed(
             section, True, (upstream, gate_up, down_part, gate_up_part), 8 + sections + section
         )
         grad_in, grad_low, grad_branch, grad_projected, gains = call_attend_backward(
             section, grad_normed_two, upstream, middle, state, rotated,
             attn_gain, mlp_gain, cosine, sine, allowed, qkv_full, out_full,
         )
-        backward.insert(0, (upstream, upstream_slice, grad_in, grad_branch, grad_projected, gains))
+        backward.insert(0, (upstream, upstream_slice, odd, grad_in, grad_branch, grad_projected, gains))
         if section == sections - 1:
             normed_two, normed, attended, grad_low = lax.optimization_barrier(
                 (normed_two, normed, attended, grad_low)
@@ -1239,30 +1581,23 @@
         if section > 0:
             upstream = lax.ppermute(grad_low, "section", down_steps)
         if section == sections - 1:
-            normed_two_all, gate_up_all, hidden_rows, lefts = call_prepare(
-                normed_two, normed, attended, gate_up_part, 6
+            gate_up_all, hidden_rows, lefts, left_rows = call_prepare(
+                normed_two, normed, attended, gate_up_part, [values[4] for values in forward], 6
             )
-            left_rows = lax.dynamic_slice_in_dim(normed_two_all, replica_at * slice_rows, slice_rows, 2)
-            left_rows = left_rows.reshape(-1, slice_rows).T
-            hidden_rows = hidden_rows.T
-            lefts = jnp.swapaxes(lefts, 2, 3).reshape(2, width // shards, shards * rows)
             upstream, gate_up_all, left_rows, hidden_rows, lefts = lax.optimization_barrier(
                 (upstream, gate_up_all, left_rows, hidden_rows, lefts)
             )
 
-    upstream, upstream_slice, grad_in, grad_branch, grad_projected, gains = [
+    upstream, upstream_slice, odd, grad_in, grad_branch, grad_projected, gains = [
         pick(values) for values in zip(*backward)
     ]
-    qkv_grad, out_grad, upstream_all = call_attend_grads(
-        grad_projected, grad_branch, lefts[0], lefts[1], upstream, 4
-    )
-    qkv_grad = lax.psum_scatter(qkv_grad, "replica", scatter_dimension=0, tiled=True).astype(F32)
-    out_grad = lax.psum_scatter(out_grad, "replica", scatter_dimension=0, tiled=True).astype(F32)
-    gate_up_grad, down_grad, _ = call_feed_grads(
-        upstream_slice, left_rows, hidden_rows, upstream_all, gate_up_all, down_part, 5
+    terms, gains, even = call_attend_grads(grad_projected, grad_branch, lefts, upstream, gains, 4)
+    gate_up_grad, down_grad, attend_grad, gains, _ = call_feed_grads(
+        left_rows, hidden_rows, terms, gains, upstream_slice, odd, even, early, gate_up_all, down_part, 5
     )
     gate_up_grad = gate_up_grad.astype(F32)
-    gains = jnp.sum(lax.all_gather(gains, both, axis=0), 0)
+    qkv_cols = grad_projected.shape[1]
+    qkv_grad, out_grad = attend_grad[:, :qkv_cols], attend_grad[:, qkv_cols:]
     return (
         block_out[None],
         grad_in[None],

time: 736 us -> 652 us (0.89)
  waiting for transfers between devices: 56.3 us -> 0.01 us
  Pallas kernels: 588 us -> 608 us
  blocking collectives: 19.9 us -> 0 us
  between operations: 14.7 us -> 1.49 us
  local copies, waits for them, and re-layouts: 19.5 us -> 9.22 us
    ppermute x1, waiting for transfers between devices: 56.2 us -> 0.01 us  [on_device(): state = lax.ppermute(block_out, 'section', up_steps)]
    pallas_call x2 -> x3, Pallas kernels: 161 us -> 198 us  [the longest x1 99.4 us: call_prepare(): pl.pallas_call(functools.partial(prepare_kernel, len(slices)), out_shape=...]
    all_gather x1 -> x0, blocking collectives: 19.9 us -> none  [on_device(): gains = jnp.sum(lax.all_gather(gains, both, axis=0), 0)]
    pallas_call x2, Pallas kernels: 43.9 us -> 27.9 us  [call_attend_backward(): pl.pallas_call(gated(section, functools.partial(attend_backward, section...]
    pallas_call x1, Pallas kernels: 112 us -> 99.9 us  [call_feed_grads(): pl.pallas_call(feed_grads_kernel, out_shape=[jax.ShapeDtypeStruct((out_ro...]
    pallas_call x4, Pallas kernels: 91.4 us -> 103 us  [call_feed(): pl.pallas_call(gated(section, functools.partial(feed_kernel, backward, ro...]
  transfers between devices with their start and end apart: 4 -> 2, of which waited for: 1 -> 0; matrix products, arithmetic and copies ran while one was open for 3% -> 0% of each run, Pallas kernels for 31% -> 25%
where the time goes in v4:
time: 652 us; the launch traced here: 641 us
  Pallas kernels  608 us (93%)
  other arithmetic  19.4 us (3%)
  local copies, waits for them, and re-layouts  9.22 us (1%)
    pallas_call x1, Pallas kernels, call_weights(): pl.pallas_call(weights_kernel, out_shape=[jax.ShapeDtypeStruct((shards *...  163 us
    pallas_call x4, Pallas kernels, call_feed(): pl.pallas_call(gated(section, functools.partial(feed_kernel, backward, ro...  103 us
    pallas_call x1, Pallas kernels, call_feed_grads(): pl.pallas_call(feed_grads_kernel, out_shape=[jax.ShapeDtypeStruct((out_ro...  99.9 us
    pallas_call x1, Pallas kernels, call_prepare(): pl.pallas_call(functools.partial(prepare_kernel, len(slices)), out_shape=...  99.4 us
    pallas_call x1, Pallas kernels, call_gather(): pl.pallas_call(gated(section, gather_kernel), out_shape=jax.ShapeDtypeStr...  57.7 us
    pallas_call x1, Pallas kernels, call_attend_grads(): pl.pallas_call(attend_grads_kernel, out_shape=[jax.ShapeDtypeStruct((repl...  41.1 us
    pallas_call x2, Pallas kernels, call_attend_backward(): pl.pallas_call(gated(section, functools.partial(attend_backward, section...  27.9 us
    pallas_call x2, Pallas kernels, call_attend_forward(): pl.pallas_call(gated(section, attend_forward), out_shape=(jax.ShapeDtypeS...  15.4 us
  transfers between devices with their start and end apart: 2, of which 0 were waited for; matrix products, arithmetic and copies ran while one was open for 0% of the time, Pallas kernels for 25%

profile of v4, /device:TPU:11, one launch (start us, length us, event | category | flops | bytes accessed | tf_op | source)
XLA Modules:
  0.0 641.1 jit_solution(1774830575063941270)
XLA Ops:
  0.7 0.7 convert_element_type.4
  1.3 1.4 fusion.2.refs_5_.refs_9_
  2.7 0.3 fusion.3
  3.0 0.8 pad_maximum_fusion.1
  3.8 163.5 %weights.1 = (bf16[2048,3072]{1,0:T(8,128)(2,1)}, bf16[2048,2048]{1,0:T(8,128)(2,1)}, bf16[2048,4096]{1,0:T(8,128)(2,1)}) custom-call(bf16[512,3072]{1,0:T(8,128)(2,1)} %bitcast.28, bf16[512,2048]{1,0:T(8,128)(2,1)} %bitcast.33, bf16[512,16384]{1,0:T(8,128)(2,1)} %bitcast.26), custom_call_target="tpu_custom_call" | custom-call | tf_op jit(solution)/shard_map/weights/pallas_call | solution.py:685
  167.3 2.9 attend_forward.2
  170.3 4.6 feed_forward.2
  174.9 1.3 collective-permute-start
  176.2 57.7 %gather.1.early_hbm = bf16[4,512,2048]{2,1,0:T(8,128)(2,1)} custom-call(bf16[128,2048]{1,0:T(8,128)(2,1)} %refs_1_.5), custom_call_target="tpu_custom_call" | custom-call | tf_op jit(solution)/shard_map/gather/pallas_call | solution.py:1503
  234.0 0.0 copy-start.8
  234.0 0.0 collective-permute-done.refs_0_.refs_3_
  234.0 0.0 copy-start.7
  234.0 0.8 copy-done.7
  234.8 12.5 %attend_forward.3 = (f32[128,2048]{1,0:T(8,128)}, bf16[128,2048]{1,0:T(8,128)(2,1)}, bf16[128,2048]{1,0:T(8,128)(2,1)}, bf16[128,3072]{1,0:T(8,128)(2,1)}, bf16[128,2048]{1,0:T(8,128)(2,1)}) custom-call(bf16[128,2048]{1,0:T(8,128)(2,1)} %copy-done.7, f32[1,2048]{1,0:T(1,128)} %refs_5_.3, f32[1,2048]{1,0:T(1,128)} %refs_6_.3, ...), custom_call_target="tpu_custom_call" | custom-call | tf_op jit(solution)/shard_map/attend_forward/pallas_call | solution.py:252
  247.2 0.0 copy-done.8
  247.3 1.9 broadcast_select_fusion.7.normed_two_ref
  249.2 38.6 %feed_forward.3 = (bf16[128,2048]{1,0:T(8,128)(2,1)}, bf16[512,2048]{1,0:T(8,128)(2,1)}, bf16[512,4096]{1,0:T(8,128)(2,1)}) custom-call(bf16[128,2048]{1,0:T(8,128)(2,1)} %get-tuple-element.73.refs_0_, f32[128,2048]{1,0:T(8,128)} %get-tuple-element.74.refs_1_.refs_2_, bf16[2048,4096]{1,0:T(8,128)(2,1)} %get-tuple-element.69.refs_2_.refs_3_.gate_up_hbm, ...), custom_call_target="tpu_custom_call" | custom-call | tf_op jit(solution)/shard_map/feed_forward/pallas_call | solution.py:524
  287.7 0.0 copy-start.15
  287.7 0.0 copy-start.18
  287.8 0.0 copy-start.14
  287.8 0.0 copy-start.17
  287.8 54.0 %feed_backward.2 = (f32[128,2048]{1,0:T(8,128)}, bf16[512,2048]{1,0:T(8,128)(2,1)}, bf16[512,4096]{1,0:T(8,128)(2,1)}, bf16[4,128,2048]{2,1,0:T(8,128)(2,1)}) custom-call(bf16[128,2048]{1,0:T(8,128)(2,1)} %refs_1_.5, bf16[512,4096]{1,0:T(8,128)(2,1)} %get-tuple-element.80.refs_1_, bf16[2048,2048]{1,0:T(8,128)(2,1)} %bitcast.23, ...), custom_call_target="tpu_custom_call" | custom-call | tf_op jit(solution)/shard_map/feed_backward/pallas_call | solution.py:524
  341.7 0.0 copy-done.15
  341.7 0.0 copy-done.18
  341.8 0.1 broadcast_select_fusion.6
  341.8 0.0 copy-done.14
  341.8 0.0 copy-done.17
  341.8 0.1 broadcast_select_fusion.5
  341.9 23.3 %attend_backward.2 = (f32[128,2048]{1,0:T(8,128)}, bf16[128,2048]{1,0:T(8,128)(2,1)}, bf16[128,2048]{1,0:T(8,128)(2,1)}, bf16[128,3072]{1,0:T(8,128)(2,1)}, f32[2,2048]{1,0:T(2,128)}) custom-call(f32[128,2048]{1,0:T(8,128)} %get-tuple-element.81.refs_0_, bf16[128,2048]{1,0:T(8,128)(2,1)} %refs_1_.5, f32[128,2048]{1,0:T(8,128)} %get-tuple-element.74.refs_1_.refs_2_, ...), custom_call_target="tpu_custom_call" | custom-call | tf_op jit(solution)/shard_map/attend_backward/pallas_call | solution.py:277
  365.2 0.3 copy.22
  365.5 0.3 copy.23
  365.8 1.5 collective-permute-start.1
  367.3 1.1 pad_maximum_fusion.lefts_ref
  368.3 99.4 %prepare.1 = (bf16[4,512,2048]{2,1,0:T(8,128)(2,1)}, bf16[2048,4096]{1,0:T(8,128)(2,1)}, bf16[512,2048]{1,0:T(8,128)(2,1)}, bf16[2,4,128,512]{3,2,1,0:T(8,128)(2,1)}, bf16[512,2048]{1,0:T(8,128)(2,1)}) custom-call(bf16[128,2048]{1,0:T(8,128)(2,1)} %broadcast_select_fusion.7.normed_two_ref, bf16[2,4,4,128,128]{4,3,2,1,0:T(8,128)(2,1)} %pad_maximum_fusion.lefts_ref, ...), custom_call_target="tpu_custom_call" | custom-call | tf_op jit(solution)/shard_map/prepare/pallas_call | solution.py:1428
  467.7 0.0 copy-done.12
  467.7 0.0 copy-done.16
  467.7 0.9 select_bitcast_fusion.1
  468.6 0.0 collective-permute-done.1.refs_0_.refs_1_
  468.6 0.0 copy-done
  468.6 0.9 broadcast_select_fusion.3.upstream_ref
  469.5 0.0 copy-done.1
  469.5 6.2 feed_backward.3
  475.7 0.0 copy-done.5
  475.7 1.5 broadcast_select_fusion.odd_hbm
  477.3 4.6 attend_backward.3
  481.9 0.0 copy-start.4
  481.9 0.6 broadcast_select_fusion.8.gains_ref
  482.5 0.0 copy-done.13
  482.5 0.9 broadcast_select_fusion.4.branch_ref
  483.4 0.0 copy-done.11
  483.4 1.0 broadcast_select_fusion.2.projected_ref
  484.3 0.0 copy-done.6
  484.3 1.5 broadcast_select_fusion.1.upstream_hbm
  485.9 41.1 %attend_grads.1 = (bf16[4,128,5120]{2,1,0:T(8,128)(2,1)}, f32[2,2048]{1,0:T(2,128)}, bf16[4,128,2048]{2,1,0:T(8,128)(2,1)}) custom-call(bf16[128,3072]{1,0:T(8,128)(2,1)} %broadcast_select_fusion.2.projected_ref, bf16[128,2048]{1,0:T(8,128)(2,1)} %broadcast_select_fusion.4.branch_ref, bf16[2,512,512]{2,1,0:T(8,128)(2,1)} %bitcast.34, ...), custom_call_target="tpu_custom_call" | custom-call | tf_op jit(solution)/shard_map/attend_grads/pallas_call | solution.py:781
  527.0 99.9 %feed_grads.1 = (bf16[128,16384]{1,0:T(8,128)(2,1)}, f32[512,2048]{1,0:T(8,128)}, f32[128,5120]{1,0:T(8,128)}, f32[2,2048]{1,0:T(2,128)}, bf16[4,512,2048]{2,1,0:T(8,128)(2,1)}) custom-call(bf16[512,2048]{1,0:T(8,128)(2,1)} %get-tuple-element.100.left_ref, bf16[512,2048]{1,0:T(8,128)(2,1)} %get-tuple-element.101.hidden_ref, ...), custom_call_target="tpu_custom_call" | custom-call | tf_op jit(solution)/shard_map/feed_grads/pallas_call | solution.py:1192
  626.9 2.4 slice_bitcast_fusion.1
  629.3 2.7 slice_bitcast_fusion
  632.0 0.0 copy-done.20
  632.0 0.6 fusion.4
  632.6 0.0 copy-done.2
  632.6 4.8 bitcast_convert_fusion
  637.4 0.0 copy-done.9
  637.4 1.1 select_bitcast_fusion
  638.5 2.0 copy.25
  (20 shorter events, 0.0 us)
Async XLA Ops:
  174.9 59.0 %collective-permute-start = (bf16[128,2048]{1,0:T(8,128)(2,1)}, bf16[128,2048]{1,0:T(8,128)(2,1)S(1)}, u32[]{:S(2)}, u32[]{:S(2)}) collective-permute-start(bf16[128,2048]{1,0:T(8,128)(2,1)} %get-tuple-element.70), channel_id=1, source_target_pairs={{0,16},{1,17},{2,18},{3,19},{4,20},{5,21},{6,22},{7,23},{8,24},{9,... | collective-permute-start | bytes 1572872 | tf_op jit(solution)/shard_map/ppermute | solution.py:1552
  234.0 13.3 %copy-start.8 = (bf16[128,2048]{1,0:T(8,128)(2,1)S(1)}, bf16[128,2048]{1,0:T(8,128)(2,1)}, u32[]{:S(2)}) copy-start(bf16[128,2048]{1,0:T(8,128)(2,1)} %get-tuple-element.67.refs_0_) | copy-start | bytes 1572868
  234.0 0.8 copy-start.7
  287.7 54.0 %copy-start.15 = (bf16[128,2048]{1,0:T(8,128)(2,1)S(1)}, bf16[128,2048]{1,0:T(8,128)(2,1)}, u32[]{:S(2)}) copy-start(bf16[128,2048]{1,0:T(8,128)(2,1)} %get-tuple-element.76) | copy-start | bytes 1572868
  287.7 54.0 %copy-start.18 = (bf16[128,2048]{1,0:T(8,128)(2,1)S(1)}, bf16[128,2048]{1,0:T(8,128)(2,1)}, u32[]{:S(2)}) copy-start(bf16[128,2048]{1,0:T(8,128)(2,1)} %get-tuple-element.77) | copy-start | bytes 1572868
  287.8 54.1 %copy-start.14 = (bf16[128,2048]{1,0:T(8,128)(2,1)S(1)}, bf16[128,2048]{1,0:T(8,128)(2,1)}, u32[]{:S(2)}) copy-start(bf16[128,2048]{1,0:T(8,128)(2,1)} %get-tuple-element.78) | copy-start | bytes 1572868
  287.8 54.1 %copy-start.17 = (bf16[128,2048]{1,0:T(8,128)(2,1)S(1)}, bf16[128,2048]{1,0:T(8,128)(2,1)}, u32[]{:S(2)}) copy-start(bf16[128,2048]{1,0:T(8,128)(2,1)} %get-tuple-element.79) | copy-start | bytes 1572868
  365.8 102.8 %collective-permute-start.1 = (bf16[128,2048]{1,0:T(8,128)(2,1)}, bf16[128,2048]{1,0:T(8,128)(2,1)S(1)}, u32[]{:S(2)}, u32[]{:S(2)}) collective-permute-start(bf16[128,2048]{1,0:T(8,128)(2,1)} %get-tuple-element.84), channel_id=1, source_target_pairs={{16,0},{17,1},{18,2},{19,3},{20,4},{21,5},{22,6},{23,7},{24,8},{25... | collective-permute-start | bytes 1572872 | tf_op jit(solution)/shard_map/ppermute | solution.py:1582
  368.3 99.4 %copy-start.12 = (bf16[128,2048]{1,0:T(8,128)(2,1)S(1)}, bf16[128,2048]{1,0:T(8,128)(2,1)}, u32[]{:S(2)}) copy-start(bf16[128,2048]{1,0:T(8,128)(2,1)} %get-tuple-element.70) | copy-start | bytes 1572868
  368.3 99.4 %copy-start.16 = (bf16[128,2048]{1,0:T(8,128)(2,1)S(1)}, bf16[128,2048]{1,0:T(8,128)(2,1)}, u32[]{:S(2)}) copy-start(bf16[128,2048]{1,0:T(8,128)(2,1)} %get-tuple-element.75) | copy-start | bytes 1572868
  368.3 100.2 %copy-start = (bf16[128,2048]{1,0:T(8,128)(2,1)S(1)}, bf16[128,2048]{1,0:T(8,128)(2,1)}, u32[]{:S(2)}) copy-start(bf16[128,2048]{1,0:T(8,128)(2,1)} %refs_1_.5) | copy-start | bytes 1572868
  468.6 1.0 copy-start.1
  469.5 6.2 copy-start.5
  477.3 4.6 copy-start.19
  477.3 5.2 copy-start.13
  477.3 6.1 copy-start.11
  477.3 7.1 %copy-start.6 = (bf16[512,2048]{1,0:T(8,128)(2,1)S(1)}, bf16[512,2048]{1,0:T(8,128)(2,1)}, u32[]{:S(2)}) copy-start(bf16[512,2048]{1,0:T(8,128)(2,1)} %get-tuple-element.111) | copy-start | bytes 6291460
  481.9 2.5 copy-start.4
  626.8 5.2 copy-start.20
  626.8 5.8 copy-start.2
  632.6 4.8 copy-start.9
  632.6 4.8 copy-start.10
  632.6 5.9 copy-start.3

commit v5 on v4

--- a/solution.py
+++ b/solution.py
@@ -82,67 +82,88 @@
     return halves
 
 
-def attend_forward(
+def attend_parts(
     state_ref, gain_one_ref, gain_two_ref, cos_ref, sin_ref, allowed_ref, qkv_hbm, out_hbm,
-    middle_ref, normed_two_ref, normed_ref, rotated_ref, attended_ref,
-    qkv_ref, out_ref, sems,
+    middle_ref, normed_two_ref, rotated_ref, lefts_ref,
+    qkv_ref, out_ref, normed_ref, attended_ref, sems,
 ):
     rows, width = state_ref.shape
     cols = qkv_hbm.shape[1]
     step = 512
-    copies = [
-        pltpu.make_async_copy(
-            qkv_hbm.at[:, pl.ds(at, step)], qkv_ref.at[:, pl.ds(at, step)], sems.at[at // step]
-        )
-        for at in range(0, cols, step)
-    ]
-    out_copies = [
-        pltpu.make_async_copy(
+    rope_cols = (HEADS + KV_HEADS) * HEAD
+
+    def qkv_copy(at):
+        return pltpu.make_async_copy(qkv_hbm.at[:, pl.ds(at, step)], qkv_ref.at[:, pl.ds(at, step)], sems.at[at // step])
+
+    def out_copy(at):
+        return pltpu.make_async_copy(
             out_hbm.at[:, pl.ds(at, step)], out_ref.at[:, pl.ds(at, step)], sems.at[(cols + at) // step]
         )
-        for at in range(0, width, step)
-    ]
-    for copy in copies + out_copies:
-        copy.start()
-    state = state_ref[...].astype(F32)
-    inverse = lax.rsqrt(jnp.mean(state * state, -1, keepdims=True) + EPSILON)
-    normed_ref[...] = (state * inverse * gain_one_ref[...]).astype(BF)
-    lane = lanes(rows)
-    cosine, sine, allowed = cos_ref[...], sin_ref[...], allowed_ref[...]
-    rope_cols = (HEADS + KV_HEADS) * HEAD
-    for at in range(0, cols, step):
-        copies[at // step].wait()
+
+    def begin():
+        for at in range(0, cols, step):
+            qkv_copy(at).start()
+        state = state_ref[...].astype(F32)
+        inverse = lax.rsqrt(jnp.mean(state * state, -1, keepdims=True) + EPSILON)
+        normed_ref[...] = (state * inverse * gain_one_ref[...]).astype(BF)
+
+    def project(at):
+        qkv_copy(at).wait()
+        lane = lanes(rows)
         projected = dot(normed_ref[...], qkv_ref[:, at : at + step])
         for tile_at in range(0, step, TILE):
             tile = projected[:, tile_at : tile_at + TILE]
             if at + tile_at < rope_cols:
-                tile = tile * cosine + swap_halves(tile, lane) * sine
+                tile = tile * cos_ref[...] + swap_halves(tile, lane) * sin_ref[...]
             rotated_ref[:, at + tile_at : at + tile_at + TILE] = tile.astype(BF)
-    for group in range(KV_HEADS):
+
+    def attend(group):
+        lane = lanes(rows)
         key_at = width + group // 2 * TILE
         value_at = rope_cols + group // 2 * TILE
         keys = spread(rotated_ref[:, key_at : key_at + TILE].astype(F32), group % 2, lane)
         values = spread(rotated_ref[:, value_at : value_at + TILE].astype(F32), group % 2, lane)
         for pair in range(2):
             at = (group * 2 + pair) * TILE
-            halves = softmax_pair(rotated_ref[:, at : at + TILE], keys, allowed)
+            halves = softmax_pair(rotated_ref[:, at : at + TILE], keys, allowed_ref[...])
             probs = jnp.concatenate([half.astype(BF) for half in halves], 1)
             attended_ref[:, at : at + TILE] = dot(probs, values).astype(BF)
-    total = jnp.zeros((rows, 1), F32)
-    for at in range(0, width, step):
-        out_copies[at // step].wait()
+
+    def load_out():
+        for at in range(0, width, step):
+            out_copy(at).start()
+
+    def leave(at):
+        out_copy(at).wait()
         middle = state_ref[:, at : at + step].astype(F32) + dot(attended_ref[...], out_ref[:, at : at + step])
         middle_ref[:, at : at + step] = middle
-        total += jnp.sum(middle * middle, -1, keepdims=True)
-    inverse = lax.rsqrt(total / width + EPSILON)
-    normed_two_ref[...] = (middle_ref[...] * inverse * gain_two_ref[...]).astype(BF)
+
+    def finish():
+        middle = middle_ref[...]
+        inverse = lax.rsqrt(jnp.mean(middle * middle, -1, keepdims=True) + EPSILON)
+        normed_two_ref[...] = (middle * inverse * gain_two_ref[...]).astype(BF)
+        lefts_ref[0] = normed_ref[...].T
+        lefts_ref[1] = attended_ref[...].T
+
+    first = [begin] + [functools.partial(project, at) for at in range(0, cols, step)]
+    first += [functools.partial(attend, group) for group in range(KV_HEADS)]
+    second = [functools.partial(leave, at) for at in range(0, width, step)] + [finish]
+    return first, load_out, second
+
+
+def attend_forward(*refs):
+    first, load_out, second = attend_parts(*refs)
+    first[0]()
+    load_out()
+    for part in first[1:] + second:
+        part()
 
 
 def attend_backward(
     rounds, grad_ref, upstream_ref, middle_ref, state_ref, rotated_ref,
     gain_one_ref, gain_two_ref, cos_ref, sin_ref, allowed_ref, qkv_hbm, out_hbm,
-    grad_state_ref, grad_low_ref, grad_branch_ref, grad_projected_ref, gain_terms_ref,
-    qkv_ref, out_ref, grad_out_ref, middle_grad_ref, sems,
+    grad_state_ref, grad_low_ref, grad_projected_ref, gain_terms_ref, branch_hbm,
+    qkv_ref, out_ref, grad_branch_ref, grad_out_ref, middle_grad_ref, sems, keep_sems, send_sems, recv_sems,
 ):
     rows, width = middle_ref.shape
     cols = qkv_hbm.shape[1]
@@ -160,6 +181,23 @@
     ]
     for copy in out_copies + copies:
         copy.start()
+    shard, beside, across, _ = slice_peers()
+    slice_barrier((beside, across))
+
+    def branch_rows(owner, at):
+        return branch_hbm.at[at, pl.ds(pl.multiple_of(owner * rows, rows), rows)]
+
+    def remote(source, owner, at, kind, device):
+        return pltpu.make_async_remote_copy(
+            source, branch_rows(owner, at), send_sems.at[kind, at], recv_sems.at[kind, at],
+            device_id={"shard": device}, device_id_type=MESH,
+        )
+
+    branch = [grad_branch_ref.at[:, pl.ds(at * step, step)] for at in range(steps)]
+    over = [remote(branch[at], shard, at, 0, across) for at in range(steps)]
+    direct = [remote(branch[at], shard, at, 1, beside) for at in range(steps)]
+    relays = [remote(branch_rows(across, at), across, at, 2, beside) for at in range(steps)]
+    keeps = [pltpu.make_async_copy(branch[at], branch_rows(shard, at), keep_sems.at[at]) for at in range(steps)]
 
     def norm_back(grad, values, gain):
         inverse = lax.rsqrt(jnp.mean(values * values, -1, keepdims=True) + EPSILON)
@@ -173,6 +211,8 @@
     gain_terms_ref[1:2, :] = term
     middle_grad_ref[...] = upstream + back
     grad_branch_ref[...] = middle_grad_ref[...].astype(BF)
+    for copy in over + direct + keeps:
+        copy.start()
     for at in range(steps):
         out_copies[at].wait()
         grad_out_ref[:, at * step : (at + 1) * step] = dot_rows(
@@ -223,6 +263,9 @@
 
     lax.fori_loop(0, KV_HEADS // 2, group_step, 0)
     for at in range(steps):
+        over[at].wait_recv()
+        relays[at].start()
+    for at in range(steps):
         copies[at].wait()
         grad_state_ref[:, at * step : (at + 1) * step] = dot_rows(
             grad_projected_ref[...], qkv_ref[at * step : (at + 1) * step, :]
@@ -234,6 +277,12 @@
     grad_low = grad_state.astype(BF)
     grad_low_ref[...] = grad_low
     grad_state_ref[...] = grad_low.astype(F32) if rounds else grad_state
+    for copy in direct + relays:
+        copy.wait()
+    for copy in over:
+        copy.wait_send()
+    for copy in keeps:
+        copy.wait()
 
 
 def gated(section, body):
@@ -245,56 +294,77 @@
     return kernel
 
 
+def attend_shapes(rows, width, cols):
+    return [
+        jax.ShapeDtypeStruct((rows, width), F32),
+        jax.ShapeDtypeStruct((rows, width), BF),
+        jax.ShapeDtypeStruct((rows, cols), BF),
+        jax.ShapeDtypeStruct((2, width, rows), BF),
+    ], [
+        pltpu.VMEM((width, cols), BF),
+        pltpu.VMEM((width, width), BF),
+        pltpu.VMEM((rows, width), BF),
+        pltpu.VMEM((rows, width), BF),
+        pltpu.SemaphoreType.DMA(((cols + width) // 512,)),
+    ]
+
+
 def call_attend_forward(section, *operands):
     rows, width = operands[0].shape
-    cols = operands[6].shape[1]
+    out_shape, scratch = attend_shapes(rows, width, operands[6].shape[1])
     specs = [pl.BlockSpec(memory_space=pltpu.VMEM)] * 6 + [pl.BlockSpec(memory_space=pl.ANY)] * 2
     return pl.pallas_call(
         gated(section, attend_forward),
-        out_shape=(
-            jax.ShapeDtypeStruct((rows, width), F32),
-            jax.ShapeDtypeStruct((rows, width), BF),
-            jax.ShapeDtypeStruct((rows, width), BF),
-            jax.ShapeDtypeStruct((rows, cols), BF),
-            jax.ShapeDtypeStruct((rows, width), BF),
-        ),
+        out_shape=out_shape,
         in_specs=specs,
-        out_specs=[pl.BlockSpec(memory_space=pltpu.VMEM)] * 5,
-        scratch_shapes=[
-            pltpu.VMEM((width, cols), BF),
-            pltpu.VMEM((width, width), BF),
-            pltpu.SemaphoreType.DMA(((cols + width) // 512,)),
-        ],
+        out_specs=[pl.BlockSpec(memory_space=pltpu.VMEM)] * 4,
+        scratch_shapes=scratch,
         compiler_params=pltpu.CompilerParams(vmem_limit_bytes=VMEM_LIMIT),
         name="attend_forward",
     )(*operands)
 
 
-def call_attend_backward(section, *operands):
+def call_attend_backward(section, collective, *operands):
     rows, width = operands[2].shape
     cols = operands[10].shape[1]
-    specs = [pl.BlockSpec(memory_space=pltpu.VMEM)] * 10 + [pl.BlockSpec(memory_space=pl.ANY)] * 2
+    steps = width // 512
+    every = lax.axis_size("shard") * rows
+    vmem, anywhere = pl.BlockSpec(memory_space=pltpu.VMEM), pl.BlockSpec(memory_space=pl.ANY)
     return pl.pallas_call(
         gated(section, functools.partial(attend_backward, section > 0)),
         out_shape=(
             jax.ShapeDtypeStruct((rows, width), F32),
             jax.ShapeDtypeStruct((rows, width), BF),
-            jax.ShapeDtypeStruct((rows, width), BF),
             jax.ShapeDtypeStruct((rows, cols), BF),
             jax.ShapeDtypeStruct((2, width), F32),
+            jax.ShapeDtypeStruct((steps, every, 512), BF),
         ),
-        in_specs=specs,
-        out_specs=[pl.BlockSpec(memory_space=pltpu.VMEM)] * 5,
+        in_specs=[vmem] * 10 + [anywhere] * 2,
+        out_specs=[vmem] * 4 + [anywhere],
         scratch_shapes=[
             pltpu.VMEM((width, cols), BF),
             pltpu.VMEM((width, width), BF),
             pltpu.VMEM((rows, width), BF),
+            pltpu.VMEM((rows, width), BF),
             pltpu.VMEM((rows, width), F32),
-            pltpu.SemaphoreType.DMA((2 * width // 512,)),
+            pltpu.SemaphoreType.DMA((2 * steps,)),
+            pltpu.SemaphoreType.DMA((steps,)),
+            pltpu.SemaphoreType.DMA((3, steps)),
+            pltpu.SemaphoreType.DMA((3, steps)),
         ],
-        compiler_params=pltpu.CompilerParams(vmem_limit_bytes=VMEM_LIMIT),
+        compiler_params=pltpu.CompilerParams(
+            collective_id=collective, has_side_effects=True, vmem_limit_bytes=VMEM_LIMIT
+        ),
         name="attend_backward",
     )(*operands)
+
+
+def start_own(copies):
+    for section, copy in enumerate(copies):
+
+        @pl.when(lax.axis_index("section") == section)
+        def _(copy=copy):
+            copy.start()
 
 
 def slice_peers():
@@ -328,22 +398,21 @@
 
 def feed_kernel(backward, rows, *refs):
     if backward:
-        (mine_ref, gate_up_ref, first_hbm, second_hbm, result_ref, all_ref, mid_ref, others_hbm,
-         first_ref, second_ref, part_ref, take_ref, sent_ref, land_ref, own_ref, own_take_ref,
-         load_sems, send_sems, recv_sems) = refs
+        (mine_ref, gate_up_hbm, first_hbm, second_hbm, result_ref, all_hbm, others_hbm,
+         mid_ref, all_ref, gate_up_ref, first_ref, second_ref, part_ref, take_ref, sent_ref, land_ref, own_ref,
+         own_take_ref, load_sems, keep_sems, hold_sems, send_sems, recv_sems) = refs
     else:
-        (mine_ref, middle_ref, first_hbm, second_hbm, result_ref, all_ref, gate_up_ref,
-         mid_ref, first_ref, second_ref, part_ref, take_ref, sent_ref, land_ref, own_ref, own_take_ref,
-         load_sems, send_sems, recv_sems) = refs
-    shard = lax.axis_index("shard")
+        (mine_ref, middle_hbm, first_hbm, second_hbm, result_ref, all_hbm, gate_up_hbm,
+         mid_ref, all_ref, gate_up_ref, first_ref, second_ref, part_ref, take_ref, sent_ref, land_ref, own_ref,
+         own_take_ref, middle_ref, load_sems, keep_sems, hold_sems, send_sems, recv_sems) = refs
+    shard, beside, across, _ = slice_peers()
     chip, core = shard // 2, shard % 2
-    beside = chip * 2 + (1 - core)
-    across = (1 - chip) * 2 + core
     half = rows // 2
+    parts, spans, _, piece, span_cols = part_ref.shape
+    block = 2 * piece
     width = all_ref.shape[1]
-    ff = second_ref.shape[0] if not backward else first_ref.shape[0]
+    ff = first_ref.shape[0] if backward else second_ref.shape[0]
     first_steps = ff // CHUNK
-    second_steps = width // CHUNK
 
     def load_first(at):
         if backward:
@@ -358,43 +427,67 @@
         ]
 
     def load_second(at):
-        span = pl.ds(pl.multiple_of(at * CHUNK, CHUNK), CHUNK)
+        span = pl.ds(pl.multiple_of(at * span_cols, span_cols), span_cols)
         place = (span, slice(None)) if backward else (slice(None), span)
         return pltpu.make_async_copy(second_hbm.at[place], second_ref.at[place], load_sems.at[2, at])
 
+    load_extra = []
+    if backward:
+        for at in range(2 * lax.axis_size("shard")):
+            group, part, owner = at // 4, at // 2 % 2, at % 2
+            source = pl.ds(at * half, half)
+            target = pl.ds(group * 2 * rows + owner * rows + part * half, half)
+            load_extra.append(pltpu.make_async_copy(gate_up_hbm.at[source], gate_up_ref.at[target], hold_sems.at[at]))
+    else:
+        load_extra.append(pltpu.make_async_copy(middle_hbm, middle_ref, hold_sems.at[0]))
+    if backward:
+        for copy in load_extra:
+            copy.start()
     for at in range(first_steps):
         for copy in load_first(at):
             copy.start()
-    for at in range(second_steps):
+    for at in range(spans):
         load_second(at).start()
+    if not backward:
+        load_extra[0].start()
 
     def remote(source, target, at, device):
         return pltpu.make_async_remote_copy(
             source, target, send_sems.at[at], recv_sems.at[at], device_id={"shard": device}, device_id_type=MESH
         )
 
-    def owned(owner, offset, count):
-        return all_ref.at[pl.ds(pl.multiple_of(owner * rows + offset, half), count)]
+    def place_of(owner, part):
+        start = part * block + (owner % 2) * piece if parts == 2 else (owner % 2) * piece + part * half
+        return pl.ds(pl.multiple_of((owner // 2) * 2 * rows + start, half), half)
+
+    def owned(owner, part):
+        return all_ref.at[place_of(owner, part)]
 
     turns = range(1, lax.axis_size("replica"), 2) if backward else ()
     slice_barrier((beside, across), turns)
-    place = pl.ds(pl.multiple_of(shard * rows, rows), rows)
-    all_ref[place, :] = mine_ref[...]
-    across_copies = [remote(owned(shard, at * half, half), owned(shard, at * half, half), 1 + at, across) for at in range(2)]
-    beside_copy = remote(owned(shard, 0, rows), owned(shard, 0, rows), 0, beside)
-    relays = [remote(owned(across, at * half, half), owned(across, at * half, half), 3 + at, beside) for at in range(2)]
-    for copy in across_copies:
+
+    def across_copy(part):
+        return remote(owned(shard, part), owned(shard, part), part, across)
+
+    def relay(part):
+        return remote(owned(across, part), owned(across, part), 4 + part, beside)
+
+    beside_copies = [remote(owned(shard, part), owned(shard, part), 2 + part, beside) for part in range(2)]
+    for part in range(2):
+        all_ref[place_of(shard, part), :] = mine_ref[part * half : (part + 1) * half, :]
+        across_copy(part).start()
+    for copy in beside_copies:
         copy.start()
-    beside_copy.start()
+    base = 6 + (2 * parts + 1) * spans
     spread_copies = [
-        replica_copy(mine_ref, others_hbm.at[lax.axis_index("replica")], turn, send_sems, recv_sems, 5 + 3 * second_steps)
+        replica_copy(mine_ref, others_hbm.at[lax.axis_index("replica")], turn, send_sems, recv_sems, base)
         for turn in turns
     ]
     for copy in spread_copies:
         copy.start()
 
-    def first_product(block, waits):
-        span = pl.ds(pl.multiple_of(block * 2 * rows, 2 * rows), 2 * rows)
+    def first_product(start, count, waits):
+        span = pl.ds(pl.multiple_of(start, count), count)
 
         def step(at, carry):
             cols = pl.ds(pl.multiple_of(at * CHUNK, CHUNK), CHUNK)
@@ -419,114 +512,192 @@
 
         lax.fori_loop(0, first_steps, step, 0)
 
-    def second_product(block, at, target_ref):
-        span = pl.ds(pl.multiple_of(block * 2 * rows, 2 * rows), 2 * rows)
-        cols = pl.ds(pl.multiple_of(at * CHUNK, CHUNK), CHUNK)
-        if backward:
-            partial = dot_rows(mid_ref[span, :], second_ref[cols, :])
+    def second_product(start, count, at, store):
+        span = pl.ds(pl.multiple_of(start, count), count)
+
+        def step(inner, carry):
+            cols = pl.ds(pl.multiple_of(at * span_cols + inner * CHUNK, CHUNK), CHUNK)
+            if backward:
+                partial = dot_rows(mid_ref[span, :], second_ref[cols, :])
+            else:
+                partial = dot(mid_ref[span, :], second_ref[:, cols])
+            store(pl.ds(pl.multiple_of(inner * CHUNK, CHUNK), CHUNK), partial.astype(BF))
+            return carry
+
+        lax.fori_loop(0, span_cols // CHUNK, step, 0)
+
+    def give(part, at):
+        return remote(part_ref.at[part, at, 1 - core], take_ref.at[part, at], 6 + part * spans + at, beside)
+
+    def cross(part, at):
+        return remote(sent_ref.at[part, at], land_ref.at[part, at], 6 + (parts + part) * spans + at, across)
+
+    def give_own(at):
+        return remote(own_ref.at[at, 1 - core], own_take_ref.at[at], 6 + 2 * parts * spans + at, beside)
+
+    def pass_on(part, at):
+        give(part, at).wait_recv()
+        sent_ref[part, at] = (part_ref[part, at, core].astype(F32) + take_ref[part, at].astype(F32)).astype(BF)
+        cross(part, at).start()
+
+    own_start = chip * 2 * rows
+    other_start = (1 - chip) * 2 * rows
+    stores = []
+    for copy in beside_copies:
+        copy.wait_recv()
+    if backward:
+        for copy in load_extra:
+            copy.wait()
+    first_product(own_start, 2 * rows, True)
+    if not backward:
+        own_place = pl.ds(pl.multiple_of(own_start, 2 * rows), 2 * rows)
+        stores.append(pltpu.make_async_copy(gate_up_ref.at[own_place], gate_up_hbm.at[own_place], keep_sems.at[1]))
+        stores[-1].start()
+
+    def store_part(part):
+        place = pl.ds(pl.multiple_of(other_start + part * block, block), block)
+        return pltpu.make_async_copy(gate_up_ref.at[place], gate_up_hbm.at[place], keep_sems.at[2 + part])
+
+    def arrive(part):
+        across_copy(part).wait_recv()
+        relay(part).start()
+
+    if parts == 1:
+        for part in range(2):
+            arrive(part)
+
+    def other_part(part, carry):
+        if parts == 1:
+            for late in range(2):
+                relay(late).wait_recv()
         else:
-            partial = dot(mid_ref[span, :], second_ref[:, cols])
-        target_ref[at, 0] = partial[:rows].astype(BF)
-        target_ref[at, 1] = partial[rows:].astype(BF)
-
-    def give(at):
-        return remote(part_ref.at[at, 1 - core], take_ref.at[at], 5 + at, beside)
-
-    def cross(at):
-        return remote(sent_ref.at[at], land_ref.at[at], 5 + second_steps + at, across)
-
-    def give_own(at):
-        return remote(own_ref.at[at, 1 - core], own_take_ref.at[at], 5 + 2 * second_steps + at, beside)
-
-    def pass_on(at):
-        give(at).wait_recv()
-        sent_ref[at] = (part_ref[at, core].astype(F32) + take_ref[at].astype(F32)).astype(BF)
-        cross(at).start()
-
-    beside_copy.wait_recv()
-    first_product(chip, True)
-    for at in range(2):
-        across_copies[at].wait_recv()
-        relays[at].start()
-    for at in range(2):
-        relays[at].wait_recv()
-    first_product(1 - chip, False)
-
-    def other_step(at, carry):
-        load_second(at).wait()
-        second_product(1 - chip, at, part_ref)
-        give(at).start()
-
-        @pl.when(at > 0)
-        def _():
-            pass_on(at - 1)
-
+            arrive(part)
+            relay(part).wait_recv()
+        start = other_start + part * block
+        first_product(start, block, False)
+        if not backward:
+            store_part(part).start()
+
+        def span_step(at, inner):
+            @pl.when(part == 0)
+            def _():
+                load_second(at).wait()
+
+            def store(cols, partial):
+                part_ref[part, at, 0, :, cols] = partial[:piece]
+                part_ref[part, at, 1, :, cols] = partial[piece:]
+
+            second_product(start, block, at, store)
+            give(part, at).start()
+
+            @pl.when(at > 0)
+            def _():
+                pass_on(part, at - 1)
+
+            return inner
+
+        lax.fori_loop(0, spans, span_step, 0)
+        pass_on(part, spans - 1)
         return carry
 
-    lax.fori_loop(0, second_steps, other_step, 0)
+    lax.fori_loop(0, parts, other_part, 0)
+    if not backward:
+        stores += [store_part(part) for part in range(parts)]
+    for owner in range(lax.axis_size("shard")):
+        for part in range(2):
+            at = owner * 2 + part
+            copy = pltpu.make_async_copy(
+                all_ref.at[place_of(owner, part)], all_hbm.at[pl.ds(owner * rows + part * half, half)],
+                keep_sems.at[4 + at],
+            )
+            copy.start()
+            stores.append(copy)
 
     def own_step(at, carry):
-        @pl.when(at == 0)
-        def _():
-            pass_on(second_steps - 1)
-
-        second_product(chip, at, own_ref)
+        def store(cols, partial):
+            for part in range(parts):
+                for owner in range(2):
+                    first_row = part * block + owner * piece
+                    own_ref[at, owner, part * piece : (part + 1) * piece, cols] = partial[first_row : first_row + piece]
+
+        second_product(own_start, 2 * rows, at, store)
         give_own(at).start()
         return carry
 
-    lax.fori_loop(0, second_steps, own_step, 0)
-    for at in range(second_steps):
+    lax.fori_loop(0, spans, own_step, 0)
+    if not backward:
+        load_extra[0].wait()
+    for at in range(spans):
         give_own(at).wait_recv()
-        cross(at).wait_recv()
-        cols = slice(at * CHUNK, (at + 1) * CHUNK)
-        total = own_ref[at, core].astype(F32) + own_take_ref[at].astype(F32) + land_ref[at].astype(F32)
-        if backward:
-            result_ref[:, cols] = total
-        else:
-            result_ref[:, cols] = (middle_ref[:, cols] + total).astype(BF)
-    for copy in [beside_copy] + across_copies + relays:
-        copy.wait_send()
-    for copy in spread_copies:
+        cols = slice(at * span_cols, (at + 1) * span_cols)
+        for part in range(parts):
+            cross(part, at).wait_recv()
+            place = slice(part * piece, (part + 1) * piece)
+            total = (
+                own_ref[at, core, place].astype(F32)
+                + own_take_ref[at, place].astype(F32)
+                + land_ref[part, at].astype(F32)
+            )
+            if backward:
+                result_ref[place, cols] = total
+            else:
+                result_ref[place, cols] = (middle_ref[place, cols] + total).astype(BF)
+    for part in range(2):
+        beside_copies[part].wait_send()
+        across_copy(part).wait_send()
+        relay(part).wait_send()
+    for copy in spread_copies + stores:
         copy.wait()
-    for at in range(second_steps):
-        give(at).wait_send()
-        cross(at).wait_send()
+    for at in range(spans):
         give_own(at).wait_send()
+        for part in range(parts):
+            give(part, at).wait_send()
+            cross(part, at).wait_send()
 
 
 def call_feed(section, backward, operands, collective):
     first, second = operands[-2], operands[-1]
     rows, width = operands[0].shape
-    shards = lax.axis_size("shard")
+    shards, replicas = lax.axis_size("shard"), lax.axis_size("replica")
     ff = first.shape[0] if backward else second.shape[0]
     every = shards * rows
-    steps = width // CHUNK
+    parts, span_cols = (1, CHUNK) if backward else (2, 2 * CHUNK)
+    spans, piece_rows = width // span_cols, rows // parts
+    vmem, anywhere = pl.BlockSpec(memory_space=pltpu.VMEM), pl.BlockSpec(memory_space=pl.ANY)
     out_shape = [
         jax.ShapeDtypeStruct((rows, width), F32 if backward else BF),
         jax.ShapeDtypeStruct((every, width), BF),
-        jax.ShapeDtypeStruct((every, 2 * ff), BF),
+        jax.ShapeDtypeStruct((replicas, rows, width) if backward else (every, 2 * ff), BF),
     ]
-    copies = 5 + 3 * steps
-    if backward:
-        replicas = lax.axis_size("replica")
-        out_shape.append(jax.ShapeDtypeStruct((replicas, rows, width), BF))
-        copies += replicas
-    piece = pltpu.VMEM((steps, rows, CHUNK), BF)
-    pair = pltpu.VMEM((steps, 2, rows, CHUNK), BF)
-    scratch = [pltpu.VMEM(first.shape, BF), pltpu.VMEM(second.shape, BF), pair, piece, piece, piece, pair, piece]
+    copies = 6 + (2 * parts + 1) * spans + (replicas if backward else 0)
+    piece = pltpu.VMEM((parts, spans, piece_rows, span_cols), BF)
+    scratch = [
+        pltpu.VMEM((every, 2 * ff if backward else ff), BF),
+        pltpu.VMEM((every, width), BF),
+        pltpu.VMEM((every, 2 * ff), BF),
+        pltpu.VMEM(first.shape, BF),
+        pltpu.VMEM(second.shape, BF),
+        pltpu.VMEM((parts, spans, 2, piece_rows, span_cols), BF),
+        piece,
+        piece,
+        piece,
+        pltpu.VMEM((spans, 2, rows, span_cols), BF),
+        pltpu.VMEM((spans, rows, span_cols), BF),
+    ]
     if not backward:
-        scratch.insert(0, pltpu.VMEM((every, ff), BF))
+        scratch.append(pltpu.VMEM((rows, width), F32))
     scratch += [
-        pltpu.SemaphoreType.DMA((3, max(ff // CHUNK, steps))),
+        pltpu.SemaphoreType.DMA((3, max(ff // CHUNK, spans))),
+        pltpu.SemaphoreType.DMA((4 + 2 * shards,)),
+        pltpu.SemaphoreType.DMA((2 * shards,)),
         pltpu.SemaphoreType.DMA((copies,)),
         pltpu.SemaphoreType.DMA((copies,)),
     ]
     return pl.pallas_call(
         gated(section, functools.partial(feed_kernel, backward, rows)),
         out_shape=out_shape,
-        in_specs=[pl.BlockSpec(memory_space=pltpu.VMEM)] * (len(operands) - 2)
-        + [pl.BlockSpec(memory_space=pl.ANY)] * 2,
-        out_specs=[pl.BlockSpec(memory_space=pltpu.VMEM)] * 3 + [pl.BlockSpec(memory_space=pl.ANY)] * backward,
+        in_specs=[vmem] + [anywhere] * 3,
+        out_specs=[vmem] + [anywhere] * 2,
         scratch_shapes=scratch,
         compiler_params=pltpu.CompilerParams(
             collective_id=collective, has_side_effects=True, vmem_limit_bytes=VMEM_LIMIT
@@ -536,8 +707,10 @@
 
 
 def weights_kernel(
-    qkv_ref, out_ref, gate_up_ref, qkv_full, out_full, gate_up_part, qkv_hold, out_hold, gate_up_hold, local_sems, send_sems,
-    recv_sems,
+    qkv_ref, out_ref, gate_up_ref, state_ref, gain_one_ref, gain_two_ref, cos_ref, sin_ref, allowed_ref,
+    qkv_full, out_full, gate_up_part, middle_ref, normed_two_ref, rotated_ref, lefts_ref,
+    qkv_hold, out_hold, gate_up_hold, qkv_work, out_work, normed_ref, attended_ref, work_sems,
+    local_sems, send_sems, recv_sems,
 ):
     shard, replica = lax.axis_index("shard"), lax.axis_index("replica")
     chip, core = shard // 2, shard % 2
@@ -581,7 +754,7 @@
         copy.start()
 
     pieces = []
-    for source, whole, count in ((qkv_ref, qkv_full, 64), (out_ref, out_full, 128)):
+    for source, whole, count in ((qkv_ref, qkv_full, 64), (out_ref, out_full, 64)):
         for offset in range(0, half, count):
 
             def place(owner, part_of, whole=whole, offset=offset, count=count):
@@ -651,6 +824,28 @@
     for load, store in zip(loads, stores):
         load.wait()
         store.start()
+    first, load_out, second = attend_parts(
+        state_ref, gain_one_ref, gain_two_ref, cos_ref, sin_ref, allowed_ref, qkv_full, out_full,
+        middle_ref, normed_two_ref, rotated_ref, lefts_ref,
+        qkv_work, out_work, normed_ref, attended_ref, work_sems,
+    )
+    qkv_last = half // 64 - 1
+    out_last = qkv_last + half // 64
+    arrived = [0]
+
+    def wait_relays(last):
+        for at in range(arrived[0], last + 1):
+            for copies in relays:
+                copies[at].wait_recv()
+        arrived[0] = last + 1
+
+    def work(parts):
+        @pl.when(lax.axis_index("section") == 0)
+        def _():
+            for part in parts:
+                part()
+
+    ready = list(first)
     for at in range(count + 1):
         if at < count:
             over[at].wait_recv()
@@ -665,22 +860,34 @@
             passed[at - 1].wait_recv()
             if relays[1][at - 1] is not None:
                 start(relays[1][at - 1])
-    for copies in relays:
-        for copy in copies:
-            if copy is not None:
-                copy.wait_recv()
-    for copy in direct:
+        if at == qkv_last + 2:
+            wait_relays(qkv_last)
+            direct[0].wait_recv()
+            stores[0].wait()
+        if at == out_last + 2:
+            wait_relays(out_last)
+            direct[1].wait_recv()
+            stores[1].wait()
+            work([load_out])
+            ready += second
+        if at >= qkv_last + 2:
+            work(ready[:3])
+            ready = ready[3:]
+    work(ready)
+    for copy in direct[2:]:
         copy.wait_recv()
-    for copy in stores:
+    for copy in stores[2:]:
         copy.wait()
     for copy in started:
         copy.wait_send()
 
 
-def call_weights(qkv_weight, out_weight, gate_up_weight, collective):
+def call_weights(qkv_weight, out_weight, gate_up_weight, operands, collective):
     shards = lax.axis_size("shard")
     rows = qkv_weight.shape[0]
-    count = 4 + 2 + 8
+    count = 2 * (rows // 128) + rows // 64
+    out_shape, scratch = attend_shapes(*operands[0].shape, qkv_weight.shape[1])
+    vmem = pl.BlockSpec(memory_space=pltpu.VMEM)
     anywhere = pl.BlockSpec(memory_space=pl.ANY)
     return pl.pallas_call(
         weights_kernel,
@@ -688,13 +895,14 @@
             jax.ShapeDtypeStruct((shards * rows, qkv_weight.shape[1]), BF),
             jax.ShapeDtypeStruct((shards * rows, out_weight.shape[1]), BF),
             jax.ShapeDtypeStruct((shards * rows, gate_up_weight.shape[1] // shards), BF),
-        ],
-        in_specs=[anywhere] * 3,
-        out_specs=[anywhere] * 3,
+        ] + out_shape,
+        in_specs=[anywhere] * 3 + [vmem] * len(operands),
+        out_specs=[anywhere] * 3 + [vmem] * len(out_shape),
         scratch_shapes=[
             pltpu.VMEM(qkv_weight.shape, BF),
             pltpu.VMEM(out_weight.shape, BF),
             pltpu.VMEM((2, rows, gate_up_weight.shape[1] // (2 * shards)), BF),
+            *scratch,
             pltpu.SemaphoreType.DMA((8,)),
             pltpu.SemaphoreType.DMA((4 * count + 4,)),
             pltpu.SemaphoreType.DMA((4 * count + 4,)),
@@ -703,20 +911,45 @@
             collective_id=collective, has_side_effects=True, vmem_limit_bytes=VMEM_LIMIT
         ),
         name="weights",
-    )(qkv_weight, out_weight, gate_up_weight)
-
-
-def attend_grads_kernel(
-    projected_ref, branch_ref, left_ref, upstream_ref, gains_ref, terms_ref, gain_sum_ref, others_hbm,
-    all_ref, gains_land_ref, send_sems, recv_sems,
-):
-    shard, beside, across, _ = slice_peers()
+    )(qkv_weight, out_weight, gate_up_weight, *operands)
+
+
+def attend_grads_kernel(sections, *refs):
+    sources = [refs[at * sections : (at + 1) * sections] for at in range(5)]
+    (terms_ref, gain_sum_ref, others_hbm, all_ref, projected_ref, upstream_ref, gains_ref, gains_land_ref,
+     lefts_ref, left_ref, load_sems, send_sems, recv_sems) = refs[5 * sections :]
+    shard, beside, across, diagonal = slice_peers()
+    peers = (across, diagonal, beside)
     replica, replicas = lax.axis_index("replica"), lax.axis_size("replica")
     rows, cols = projected_ref.shape
-    pieces = all_ref.shape[0]
-    step = all_ref.shape[2]
+    every, step = all_ref.shape[1:]
+    pieces = cols // step
     sub_rows = terms_ref.shape[1]
-    slice_barrier((beside, across), range(1, replicas))
+    loads = []
+    for at, target in enumerate((projected_ref, gains_ref, upstream_ref)):
+        loads.append([pltpu.make_async_copy(source, target, load_sems.at[at]) for source in sources[at]])
+    loads.append(
+        [
+            pltpu.make_async_copy(source, all_ref.at[pl.ds(pieces, all_ref.shape[0] - pieces)], load_sems.at[3])
+            for source in sources[3]
+        ]
+    )
+    loads.append([pltpu.make_async_copy(source, lefts_ref, load_sems.at[4]) for source in sources[4]])
+    for copies in loads:
+        start_own(copies)
+    slice_barrier(peers, range(1, replicas))
+    kinds, groups = lefts_ref.shape[:2]
+    left_base = 3 * pieces + 2 * replicas
+
+    def hand_left(kind, group, peer):
+        own_cols = pl.ds(pl.multiple_of(shard * rows, rows), rows)
+        return pltpu.make_async_remote_copy(
+            lefts_ref.at[kind, group, peers[peer]], left_ref.at[kind, group, :, own_cols],
+            send_sems.at[left_base + (kind * groups + group) * 3 + peer],
+            recv_sems.at[left_base + (kind * groups + group) * 3 + peer],
+            device_id={"shard": peers[peer]}, device_id_type=MESH,
+        )
+
     spread_copies = [
         replica_copy(upstream_ref, others_hbm.at[replica], turn, send_sems, recv_sems, 3 * pieces)
         for turn in range(2, replicas, 2)
@@ -736,60 +969,87 @@
     over = [remote(shard, piece, piece, across) for piece in range(pieces)]
     direct = [remote(shard, piece, pieces + piece, beside) for piece in range(pieces)]
     relays = [remote(across, piece, 2 * pieces + piece, beside) for piece in range(pieces)]
+    lefts = [(kind, group, peer) for kind in reversed(range(kinds)) for group in range(groups) for peer in range(3)]
+    loads[4][0].wait()
+    for place in lefts:
+        hand_left(*place).start()
+    for kind in range(kinds):
+        for group in range(groups):
+            left_ref[kind, group, :, own] = lefts_ref[kind, group, shard]
+    loads[0][0].wait()
     for piece in range(pieces):
-        at = piece * step
-        all_ref[piece, own, :] = (
-            projected_ref[:, at : at + step] if at < cols else branch_ref[:, at - cols : at - cols + step]
-        )
+        all_ref[piece, own, :] = projected_ref[:, piece * step : (piece + 1) * step]
         over[piece].start()
         direct[piece].start()
+    loads[1][0].wait()
     gains_land_ref[replica] = gains_ref[...]
+    loads[2][0].wait()
     for copy in gain_copies + spread_copies:
         copy.start()
 
     def product(piece):
-        direct[piece].wait_recv()
-        relays[piece].wait_recv()
         at = piece * step
-        total = dot(left_ref[0 if at < cols else 1], all_ref[piece]).astype(BF)
-        for group in range(replicas):
+        kind = 0 if at < cols else 1
+        left = jnp.concatenate([left_ref[kind, group] for group in range(groups)], 0)
+        total = dot(left, all_ref[piece]).astype(BF)
+        for group in range(groups):
             terms_ref[group, :, at : at + step] = total[group * sub_rows : (group + 1) * sub_rows]
 
+    loads[3][0].wait()
+    for place in lefts:
+        hand_left(*place).wait_recv()
+    for piece in range(pieces, all_ref.shape[0]):
+        product(piece)
     for piece in range(pieces):
         over[piece].wait_recv()
         relays[piece].start()
         if piece:
+            direct[piece - 1].wait_recv()
+            relays[piece - 1].wait_recv()
             product(piece - 1)
+    direct[pieces - 1].wait_recv()
+    relays[pieces - 1].wait_recv()
     product(pieces - 1)
     for copy in gain_copies:
         copy.wait()
     gain_sum_ref[...] = jnp.sum(gains_land_ref[...], 0)
     for copy in over + direct + relays:
         copy.wait_send()
+    for place in lefts:
+        hand_left(*place).wait_send()
     for copy in spread_copies:
         copy.wait()
 
 
-def call_attend_grads(projected, branch, left, upstream, gains, collective):
-    replicas = lax.axis_size("replica")
-    rows, cols = projected.shape
-    width = branch.shape[1]
-    _, every, tokens = left.shape
-    pieces = (cols + width) // CHUNK
-    copies = 3 * pieces + 2 * replicas
-    vmem = pl.BlockSpec(memory_space=pltpu.VMEM)
+def call_attend_grads(lefts, projected, gains, upstream, branch, collective):
+    replicas, sections = lax.axis_size("replica"), len(projected)
+    rows, cols = projected[0].shape
+    width = upstream[0].shape[1]
+    shards = lax.axis_size("shard")
+    every, tokens = width // shards, shards * rows
+    sub_rows = every // replicas
+    lefts = [values.reshape(2, replicas, shards, sub_rows, rows) for values in lefts]
+    pieces = cols // CHUNK
+    copies = 3 * pieces + 2 * replicas + 2 * replicas * 3
+    vmem, anywhere = pl.BlockSpec(memory_space=pltpu.VMEM), pl.BlockSpec(memory_space=pl.ANY)
     return pl.pallas_call(
-        attend_grads_kernel,
+        functools.partial(attend_grads_kernel, sections),
         out_shape=[
             jax.ShapeDtypeStruct((replicas, every // replicas, cols + width), BF),
-            jax.ShapeDtypeStruct(gains.shape, F32),
-            jax.ShapeDtypeStruct((replicas,) + upstream.shape, BF),
+            jax.ShapeDtypeStruct(gains[0].shape, F32),
+            jax.ShapeDtypeStruct((replicas, rows, width), BF),
         ],
-        in_specs=[vmem] * 5,
-        out_specs=[vmem] * 2 + [pl.BlockSpec(memory_space=pl.ANY)],
+        in_specs=[anywhere] * 5 * sections,
+        out_specs=[vmem] * 2 + [anywhere],
         scratch_shapes=[
-            pltpu.VMEM((pieces, tokens, CHUNK), BF),
-            pltpu.VMEM((replicas,) + gains.shape, F32),
+            pltpu.VMEM(((cols + width) // CHUNK, tokens, CHUNK), BF),
+            pltpu.VMEM((rows, cols), BF),
+            pltpu.VMEM((rows, width), BF),
+            pltpu.VMEM(gains[0].shape, F32),
+            pltpu.VMEM((replicas,) + gains[0].shape, F32),
+            pltpu.VMEM(lefts[0].shape, BF),
+            pltpu.VMEM((2, replicas, sub_rows, tokens), BF),
+            pltpu.SemaphoreType.DMA((5,)),
             pltpu.SemaphoreType.DMA((copies,)),
             pltpu.SemaphoreType.DMA((copies,)),
         ],
@@ -797,22 +1057,22 @@
             collective_id=collective, has_side_effects=True, vmem_limit_bytes=VMEM_LIMIT
         ),
         name="attend_grads",
-    )(projected, branch, left, upstream, gains)
-
-
-def feed_grads_kernel(
-    left_ref, hidden_ref, terms_ref, gains_ref, upstream_hbm, odd_hbm, even_hbm, early_hbm, gate_up_hbm, down_hbm,
-    gate_up_grad_ref, down_grad_ref, attend_grad_ref, gain_sum_ref, gathered_hbm,
-    down_ref, block_ref, gate_up_ref, mid_ref, sum_ref, stage_ref, chain_ref, gains_land_ref,
-    load_sems, block_sems, keep_sem, send_sems, recv_sems,
-):
+    )(*projected, *gains, *upstream, *branch, *lefts)
+
+
+def feed_grads_kernel(sections, left_ref, hidden_ref, terms_ref, gains_ref, *refs):
+    upstream = refs[:sections]
+    (odd_hbm, even_hbm, early_hbm, gate_up_hbm, down_hbm,
+     gate_up_grad_ref, down_grad_ref, qkv_grad_ref, out_grad_ref, gain_sum_ref, gathered_hbm,
+     down_ref, block_ref, gate_up_ref, mid_ref, sum_ref, stage_ref, chain_ref, gains_land_ref,
+     load_sems, block_sems, keep_sem, send_sems, recv_sems) = refs[sections:]
     shard, beside, across, diagonal = slice_peers()
     peers = (across, diagonal, beside)
     replica, replicas = lax.axis_index("replica"), lax.axis_size("replica")
     early = lax.axis_index("section") == lax.axis_size("section") - 1
     late = lax.axis_index("section") < lax.axis_size("section") - 1
     rows = odd_hbm.shape[1]
-    every, width = upstream_hbm.shape
+    every, width = upstream[0].shape
     part = down_ref.shape[0]
     half_part = part // 2
     ff = gate_up_grad_ref.shape[1] // 2
@@ -852,17 +1112,17 @@
         return copies
 
     def load_block(turn):
-        @pl.when(early & (turn > 0))
+        @pl.when(early & (turn % 2 == 1))
         def _():
             for copy in block_copies(turn, early_hbm):
                 copy.start()
 
-        @pl.when(late | (turn == 0))
+        @pl.when(late | (turn % 2 == 0))
         def _():
             for copy in block_copies(turn, None)[:3]:
                 copy.start()
 
-        cases = ((turn == 0, None), (late & (turn > 0) & (turn % 2 == 0), even_hbm), (late & (turn % 2 == 1), odd_hbm))
+        cases = ((turn == 0, None), ((turn > 0) & (turn % 2 == 0), even_hbm), (late & (turn % 2 == 1), odd_hbm))
         for case, source in cases:
 
             @pl.when(case)
@@ -893,7 +1153,7 @@
     def send_block(turn):
         for parity, source in ((0, even_hbm), (1, odd_hbm)):
 
-            @pl.when(lax.rem(turn, 2) == parity)
+            @pl.when((lax.rem(turn, 2) == 1) & late if parity else lax.rem(turn, 2) == 0)
             def _(source=source):
                 over(turn, source).start()
                 direct(turn, source).start()
@@ -961,10 +1221,8 @@
     above = (2 * replicas - 2 - replica) // replicas
     pl.semaphore_wait(barrier, 3 + below + above)
 
-    @pl.when(late)
-    def _():
-        for turn in range(1, min(3, replicas)):
-            send_block(turn)
+    for turn in range(1, min(3, replicas)):
+        send_block(turn)
 
     for block in reversed(range(1, replicas)):
 
@@ -983,9 +1241,9 @@
     for peer in range(3):
         gain_copy(peer).start()
     gains_land_ref[shard] = gains_ref[...]
-    load_own = pltpu.make_async_copy(upstream_hbm, block_ref.at[0], load_sems.at[2, 0])
-    load_own.start()
-    load_own.wait()
+    load_own = [pltpu.make_async_copy(source, block_ref.at[0], load_sems.at[2, 0]) for source in upstream]
+    start_own(load_own)
+    load_own[0].wait()
     keep_own = pltpu.make_async_copy(block_ref.at[0], gathered_hbm.at[0], keep_sem)
     keep_own.start()
     load_down.wait()
@@ -1067,7 +1325,7 @@
                     wait_block(later)
                 else:
 
-                    @pl.when(late)
+                    @pl.when(late | (later % 2 == 0))
                     def _():
                         over(later, even_hbm).wait_recv()
                         relay(later).start()
@@ -1076,7 +1334,7 @@
 
                     load_block(later)
 
-                    @pl.when(late & (turn + 3 < replicas))
+                    @pl.when(turn + 3 < replicas)
                     def _():
                         send_block(turn + 3)
 
@@ -1143,15 +1401,17 @@
         lax.fori_loop(0, 2 * steps, store_own, 0)
     for step in range(3, replicas):
         chain_step(step)
-    attend_grad_ref[...] = terms_ref[replica].astype(F32)
-
-    @pl.when(replica > 0)
-    def _():
-        attend_grad_ref[...] += chain_ref[replica].astype(F32)
-
-    @pl.when(replica < replicas - 1)
-    def _():
-        attend_grad_ref[...] += chain_ref[replicas].astype(F32)
+    cut = qkv_grad_ref.shape[1]
+    for grad_ref, cols in ((qkv_grad_ref, slice(0, cut)), (out_grad_ref, slice(cut, None))):
+        grad_ref[...] = terms_ref[replica, :, cols].astype(F32)
+
+        @pl.when(replica > 0)
+        def _(grad_ref=grad_ref, cols=cols):
+            grad_ref[...] += chain_ref[replica, :, cols].astype(F32)
+
+        @pl.when(replica < replicas - 1)
+        def _(grad_ref=grad_ref, cols=cols):
+            grad_ref[...] += chain_ref[replicas, :, cols].astype(F32)
 
     for half in range(2):
 
@@ -1161,9 +1421,10 @@
             return carry
 
         lax.fori_loop(0, 2 * steps, finish, 0)
-    @pl.when(late)
-    def _():
-        for turn in range(1, replicas):
+    for turn in range(1, replicas):
+
+        @pl.when(late | (turn % 2 == 0))
+        def _(turn=turn):
             over(turn, even_hbm).wait_send()
             direct(turn, even_hbm).wait_send()
             relay(turn).wait_send()
@@ -1181,8 +1442,9 @@
             chain_down(block).wait_send()
 
 
-def call_feed_grads(left, hidden, terms, gains, upstream, odd, even, early, gate_up, down, collective):
-    every, width = upstream.shape
+def call_feed_grads(left, hidden, terms, gains, upstream, odd, even, early, gate_up, down, qkv_cols, collective):
+    every, width = upstream[0].shape
+    sub_rows, attend_cols = terms.shape[1:]
     replicas = odd.shape[0]
     shards = lax.axis_size("shard")
     part = down.shape[0]
@@ -1190,16 +1452,17 @@
     vmem, anywhere = pl.BlockSpec(memory_space=pltpu.VMEM), pl.BlockSpec(memory_space=pl.ANY)
     copies = 5 * replicas + 3 * 2 * (part // CHUNK) + 3
     return pl.pallas_call(
-        feed_grads_kernel,
+        functools.partial(feed_grads_kernel, len(upstream)),
         out_shape=[
             jax.ShapeDtypeStruct((out_rows, 2 * part * shards), BF),
             jax.ShapeDtypeStruct((hidden.shape[0], width), F32),
-            jax.ShapeDtypeStruct(terms.shape[1:], F32),
+            jax.ShapeDtypeStruct((sub_rows, qkv_cols), F32),
+            jax.ShapeDtypeStruct((sub_rows, attend_cols - qkv_cols), F32),
             jax.ShapeDtypeStruct(gains.shape, F32),
             jax.ShapeDtypeStruct((replicas, every, width), BF),
         ],
-        in_specs=[vmem] * 4 + [anywhere] * 6,
-        out_specs=[vmem] * 4 + [anywhere],
+        in_specs=[vmem] * 4 + [anywhere] * (5 + len(upstream)),
+        out_specs=[vmem] * 5 + [anywhere],
         scratch_shapes=[
             pltpu.VMEM(down.shape, BF),
             pltpu.VMEM((2, every, width), BF),
@@ -1219,20 +1482,18 @@
             collective_id=collective, has_side_effects=True, vmem_limit_bytes=VMEM_LIMIT
         ),
         name="feed_grads",
-    )(left, hidden, terms, gains, upstream, odd, even, early, gate_up, down)
+    )(left, hidden, terms, gains, *upstream, odd, even, early, gate_up, down)
 
 
 def turn_order(replicas):
     return [0] + list(range(1, replicas, 2)) + list(range(2, replicas, 2))
 
 
-def prepare_kernel(
-    sections, normed_two_ref, lefts_ref, gate_up_hbm, *refs
-):
-    slices = refs[:sections]
-    (gathered_hbm, gate_up_all_hbm, hidden_hbm, left_hbm, left_rows_ref,
-     weight_ref, block_ref, gate_up_ref, hidden_ref, turned_ref,
-     load_sems, store_sems, keep_sems, send_sems, recv_sems) = refs[sections:]
+def prepare_kernel(sections, gate_up_hbm, *refs):
+    slices, normed_two = refs[:sections], refs[sections : 2 * sections]
+    (gathered_hbm, gate_up_all_hbm, hidden_hbm, left_rows_ref,
+     normed_two_ref, weight_ref, block_ref, gate_up_ref, hidden_ref, turned_ref,
+     load_sems, store_sems, start_sems, send_sems, recv_sems) = refs[2 * sections :]
     shard, beside, across, diagonal = slice_peers()
     peers = (across, diagonal, beside)
     replica, replicas = lax.axis_index("replica"), lax.axis_size("replica")
@@ -1243,7 +1504,6 @@
     ff_rows = hidden_hbm.shape[0]
     steps = part // CHUNK
     slice_rows = left_rows_ref.shape[0]
-    kinds, groups = lefts_ref.shape[:2]
     owner = (replica * shards) // replicas
     first_col = lax.rem(replica * shards, replicas) * ff_rows
 
@@ -1295,38 +1555,20 @@
             turned_ref.at[slot, shard], hidden_hbm.at[:, tokens(turn)], store_sems.at[2, slot]
         )
 
-    own_rows = pl.ds(pl.multiple_of(shard * rows, rows), rows)
-
-    def hand_left(kind, group, peer):
-        device = peers[peer]
-        return remote(
-            lefts_ref.at[kind, group, device],
-            left_hbm.at[kind, group, :, own_rows],
-            7 * replicas + (kind * groups + group) * 3 + peer,
-            device,
-        )
-
-    def keep_left(kind, group):
-        return pltpu.make_async_copy(
-            lefts_ref.at[kind, group, shard], left_hbm.at[kind, group, :, own_rows],
-            keep_sems.at[kind * groups + group],
-        )
-
-    for section in range(sections):
-
-        @pl.when(lax.axis_index("section") == section)
-        def _(section=section):
-            pltpu.make_async_copy(slices[section], block_ref.at[0], store_sems.at[0, 0]).start()
-
+    loads = [
+        [pltpu.make_async_copy(source, target, sem) for source in sources]
+        for sources, target, sem in (
+            (normed_two, normed_two_ref, start_sems.at[0]),
+            (slices, block_ref.at[0], store_sems.at[0, 0]),
+        )
+    ]
+    for copies in loads:
+        start_own(copies)
     slice_barrier(peers, range(1, replicas))
     order = turn_order(replicas)
+    loads[0][0].wait()
     if replicas > 1:
         from_replica(order[1]).start()
-    for kind in range(kinds):
-        for group in range(groups):
-            keep_left(kind, group).start()
-            for peer in range(3):
-                hand_left(kind, group, peer).start()
 
     for at, turn in enumerate(order):
         later = order[at + 1] if at + 1 < replicas else None
@@ -1407,36 +1649,29 @@
             relay(turn).wait_send()
         if turn and turn == order[-1]:
             from_replica(turn).wait_send()
-    for kind in range(kinds):
-        for group in range(groups):
-            keep_left(kind, group).wait()
-            for peer in range(3):
-                hand_left(kind, group, peer).wait()
-
-
-def call_prepare(normed_two, normed, attended, gate_up_part, slices, collective):
-    rows, width = normed_two.shape
+
+
+def call_prepare(normed_two, gate_up_part, slices, collective):
+    rows, width = normed_two[0].shape
     shards, replicas = lax.axis_size("shard"), lax.axis_size("replica")
     part = gate_up_part.shape[1] // 2
     every = rows * shards
     slice_rows = width // replicas
-    sub_rows = slice_rows // shards
     ff_rows = part // replicas
-    lefts = jnp.stack([normed.T, attended.T]).reshape(2, replicas, shards, sub_rows, rows)
     vmem, anywhere = pl.BlockSpec(memory_space=pltpu.VMEM), pl.BlockSpec(memory_space=pl.ANY)
-    copies = 7 * replicas + 2 * replicas * 3
+    copies = 7 * replicas
     outs = pl.pallas_call(
         functools.partial(prepare_kernel, len(slices)),
         out_shape=[
             jax.ShapeDtypeStruct((replicas, every, width), BF),
             jax.ShapeDtypeStruct((replicas * every, 2 * part), BF),
             jax.ShapeDtypeStruct((ff_rows, replicas * every), BF),
-            jax.ShapeDtypeStruct((2, replicas, sub_rows, every), BF),
             jax.ShapeDtypeStruct((slice_rows, replicas * every), BF),
         ],
-        in_specs=[vmem, vmem, anywhere] + [anywhere] * len(slices),
-        out_specs=[anywhere] * 4 + [vmem],
+        in_specs=[anywhere] * (1 + 2 * len(slices)),
+        out_specs=[anywhere] * 3 + [vmem],
         scratch_shapes=[
+            pltpu.VMEM((rows, width), BF),
             pltpu.VMEM(gate_up_part.shape, BF),
             pltpu.VMEM((2, every, width), BF),
             pltpu.VMEM((2, every, 2 * part), BF),
@@ -1444,7 +1679,7 @@
             pltpu.VMEM((2, shards, ff_rows, every), BF),
             pltpu.SemaphoreType.DMA((2, part // CHUNK)),
             pltpu.SemaphoreType.DMA((3, 2)),
-            pltpu.SemaphoreType.DMA((2 * replicas,)),
+            pltpu.SemaphoreType.DMA((1,)),
             pltpu.SemaphoreType.DMA((copies,)),
             pltpu.SemaphoreType.DMA((copies,)),
         ],
@@ -1452,9 +1687,8 @@
             collective_id=collective, has_side_effects=True, vmem_limit_bytes=VMEM_LIMIT
         ),
         name="prepare",
-    )(normed_two, lefts, gate_up_part, *slices)
-    _, gate_up_all, hidden_rows, lefts, left_rows = outs
-    return gate_up_all, hidden_rows, lefts.reshape(2, replicas * sub_rows, every), left_rows
+    )(gate_up_part, *slices, *normed_two)
+    return outs[1:]
 
 
 def gather_kernel(mine_ref, gathered_hbm, send_sems, recv_sems):
@@ -1469,8 +1703,8 @@
         )
 
     own_rows = pl.ds(pl.multiple_of(shard * rows, rows), rows)
-    slice_barrier((beside, across), range(1, replicas))
-    order = turn_order(replicas)[1:]
+    slice_barrier((beside, across), range(1, replicas, 2))
+    order = list(range(1, replicas, 2))
     spread_copies = [
         replica_copy(mine_ref, gathered_hbm.at[turn, own_rows], turn, send_sems, recv_sems, 3 * replicas)
         for turn in order
@@ -1479,12 +1713,12 @@
     direct = [remote(shard, turn, 3 * turn + 1, beside) for turn in order]
     relays = [remote(across, turn, 3 * turn + 2, beside) for turn in order]
     spread_copies[0].start()
-    for at in range(replicas - 1):
+    for at in range(len(order)):
         spread_copies[at].wait_recv()
         over[at].start()
         direct[at].start()
         spread_copies[at].wait_send()
-        if at + 2 < replicas:
+        if at + 1 < len(order):
             spread_copies[at + 1].start()
         if at:
             over[at - 1].wait_recv()
@@ -1535,19 +1769,22 @@
     cosine, sine = rope_tables(positions)
     allowed = visible(positions)
 
-    qkv_full, out_full, gate_up_part = call_weights(qkv_weight[0], out_weight[0], gate_up_weight[0], 3)
+    tables = (attn_gain, mlp_gain, cosine, sine, allowed)
+    qkv_full, out_full, gate_up_part, *attend_first = call_weights(
+        qkv_weight[0], out_weight[0], gate_up_weight[0], (tokens_in,) + tables, 3
+    )
     down_part = down_weight[0]
 
     forward = []
     state = tokens_in
     for section in range(sections):
-        middle, normed_two, normed, rotated, attended = call_attend_forward(
-            section, state, attn_gain, mlp_gain, cosine, sine, allowed, qkv_full, out_full
+        middle, normed_two, rotated, lefts = (
+            call_attend_forward(section, state, *tables, qkv_full, out_full) if section else attend_first
         )
         block_out, normed_two_slice, gate_up = call_feed(
             section, False, (normed_two, middle, gate_up_part, down_part), 8 + section
         )
-        forward.append((state, middle, rotated, gate_up, normed_two_slice, normed_two, normed, attended, block_out))
+        forward.append((state, middle, rotated, gate_up, normed_two_slice, normed_two, lefts, block_out))
         if section + 1 < sections:
             state = lax.ppermute(block_out, "section", up_steps)
         if section + 2 == sections:
@@ -1561,43 +1798,38 @@
             chosen = jnp.where(lax.axis_index("section") == section, values[section], chosen)
         return chosen
 
-    normed_two, normed, attended, block_out = [pick(values) for values in list(zip(*forward))[5:]]
+    slices, normed_two, lefts, block_out = list(zip(*forward))[4:]
+    block_out = pick(block_out)
     backward = []
     upstream = cotangent
     for section in reversed(range(sections)):
         state, middle, rotated, gate_up = forward[section][:4]
-        grad_normed_two, upstream_slice, _, odd = call_feed(
+        grad_normed_two, upstream_slice, odd = call_feed(
             section, True, (upstream, gate_up, down_part, gate_up_part), 8 + sections + section
         )
-        grad_in, grad_low, grad_branch, grad_projected, gains = call_attend_backward(
-            section, grad_normed_two, upstream, middle, state, rotated,
-            attn_gain, mlp_gain, cosine, sine, allowed, qkv_full, out_full,
-        )
-        backward.insert(0, (upstream, upstream_slice, odd, grad_in, grad_branch, grad_projected, gains))
+        grad_in, grad_low, grad_projected, gains, grad_branch = call_attend_backward(
+            section, 8 + 2 * sections + section, grad_normed_two, upstream, middle, state, rotated,
+            *tables, qkv_full, out_full,
+        )
+        backward.insert(0, (upstream, upstream_slice, odd, grad_in, grad_projected, gains, grad_branch))
         if section == sections - 1:
-            normed_two, normed, attended, grad_low = lax.optimization_barrier(
-                (normed_two, normed, attended, grad_low)
-            )
+            normed_two, grad_low = lax.optimization_barrier((normed_two, grad_low))
         if section > 0:
             upstream = lax.ppermute(grad_low, "section", down_steps)
         if section == sections - 1:
-            gate_up_all, hidden_rows, lefts, left_rows = call_prepare(
-                normed_two, normed, attended, gate_up_part, [values[4] for values in forward], 6
+            gate_up_all, hidden_rows, left_rows = call_prepare(normed_two, gate_up_part, slices, 6)
+            upstream, gate_up_all, left_rows, hidden_rows = lax.optimization_barrier(
+                (upstream, gate_up_all, left_rows, hidden_rows)
             )
-            upstream, gate_up_all, left_rows, hidden_rows, lefts = lax.optimization_barrier(
-                (upstream, gate_up_all, left_rows, hidden_rows, lefts)
-            )
-
-    upstream, upstream_slice, odd, grad_in, grad_branch, grad_projected, gains = [
-        pick(values) for values in zip(*backward)
-    ]
-    terms, gains, even = call_attend_grads(grad_projected, grad_branch, lefts, upstream, gains, 4)
-    gate_up_grad, down_grad, attend_grad, gains, _ = call_feed_grads(
-        left_rows, hidden_rows, terms, gains, upstream_slice, odd, even, early, gate_up_all, down_part, 5
+
+    upstream, upstream_slice, odd, grad_in, grad_projected, gains, grad_branch = zip(*backward)
+    grad_in = pick(grad_in)
+    terms, gains, even = call_attend_grads(lefts, grad_projected, gains, upstream, grad_branch, 4)
+    gate_up_grad, down_grad, qkv_grad, out_grad, gains, _ = call_feed_grads(
+        left_rows, hidden_rows, terms, gains, upstream_slice, pick(odd[:-1]), even, early, gate_up_all, down_part,
+        grad_projected[0].shape[1], 5,
     )
     gate_up_grad = gate_up_grad.astype(F32)
-    qkv_cols = grad_projected.shape[1]
-    qkv_grad, out_grad = attend_grad[:, :qkv_cols], attend_grad[:, qkv_cols:]
     return (
         block_out[None],
         grad_in[None],

time: 652 us -> 605 us (0.928)
  Pallas kernels: 608 us -> 570 us
  other arithmetic: 19.4 us -> 11.7 us
    pallas_call x4, Pallas kernels: 103 us -> 76.6 us  [call_feed(): pl.pallas_call(gated(section, functools.partial(feed_kernel, backward, ro...]
    pallas_call x1, Pallas kernels: 57.7 us -> 44.7 us  [call_gather(): pl.pallas_call(gated(section, gather_kernel), out_shape=jax.ShapeDtypeStr...]
    select_n x9 -> x0, other arithmetic: 8.46 us -> none  [pick(): jnp.where(lax.axis_index('section') == section, values[section], chosen)]
    pallas_call x4 -> x3, Pallas kernels: 156 us -> 154 us  [the longest x1 101 us: call_feed_grads(): pl.pallas_call(functools.partial(feed_grads_kernel, len(upstream)), out_s...]
  transfers between devices with their start and end apart: 2 -> 2, of which waited for: 0 -> 0; matrix products, arithmetic and copies ran while one was open for 0% -> 0% of each run, Pallas kernels for 25% -> 24%
where the time goes in v5:
time: 605 us; the launch traced here: 593 us
  Pallas kernels  570 us (94%)
  other arithmetic  11.7 us (2%)
  local copies, waits for them, and re-layouts  7.85 us (1%)
    pallas_call x1, Pallas kernels, call_weights(): pl.pallas_call(weights_kernel, out_shape=[jax.ShapeDtypeStruct((shards *...  167 us
    pallas_call x1, Pallas kernels, call_feed_grads(): pl.pallas_call(functools.partial(feed_grads_kernel, len(upstream)), out_s...  101 us
    pallas_call x1, Pallas kernels, call_prepare(): pl.pallas_call(functools.partial(prepare_kernel, len(slices)), out_shape=...  99.9 us
    pallas_call x4, Pallas kernels, call_feed(): pl.pallas_call(gated(section, functools.partial(feed_kernel, backward, ro...  76.6 us
    pallas_call x1, Pallas kernels, call_gather(): pl.pallas_call(gated(section, gather_kernel), out_shape=jax.ShapeDtypeStr...  44.7 us
    pallas_call x1, Pallas kernels, call_attend_grads(): pl.pallas_call(functools.partial(attend_grads_kernel, sections), out_shap...  40.5 us
    pallas_call x2, Pallas kernels, call_attend_backward(): pl.pallas_call(gated(section, functools.partial(attend_backward, section...  28.1 us
    pallas_call x1, Pallas kernels, call_attend_forward(): pl.pallas_call(gated(section, attend_forward), out_shape=out_shape, in_sp...  12.2 us
  transfers between devices with their start and end apart: 2, of which 0 were waited for; matrix products, arithmetic and copies ran while one was open for 0% of the time, Pallas kernels for 24%

profile of v5, /device:TPU:11, one launch (start us, length us, event | category | flops | bytes accessed | tf_op | source)
XLA Modules:
  0.0 593.4 jit_solution(9720315631447021267)
XLA Ops:
  0.7 0.7 convert_element_type.4
  1.3 1.4 fusion.2.allowed_ref.refs_5_.refs_9_
  2.7 0.3 fusion.3
  3.0 0.8 pad_maximum_fusion
  3.8 166.5 %weights.1 = (bf16[2048,3072]{1,0:T(8,128)(2,1)}, bf16[2048,2048]{1,0:T(8,128)(2,1)}, bf16[2048,4096]{1,0:T(8,128)(2,1)}, f32[128,2048]{1,0:T(8,128)}, bf16[128,...) custom-call(bf16[512,3072]{1,0:T(8,128)(2,1)} %bitcast.23, bf16[512,2048]{1,0:T(8,128)(2,1)} %bitcast.24, ...), custom_call_target="tpu_custom_call" | custom-call | tf_op jit(solution)/shard_map/weights/pallas_call | solution.py:892
  170.4 2.4 feed_forward.2
  172.8 1.3 collective-permute-start
  174.1 44.7 %gather.1.refs_4_ = bf16[4,512,2048]{2,1,0:T(8,128)(2,1)} custom-call(bf16[128,2048]{1,0:T(8,128)(2,1)} %refs_5_.5), custom_call_target="tpu_custom_call" | custom-call | tf_op jit(solution)/shard_map/gather/pallas_call | solution.py:1737
  218.8 0.0 collective-permute-done.refs_0_.refs_3_
  218.8 0.0 copy-start.2
  218.8 0.8 copy-done.2
  219.6 12.2 %attend_forward.1 = (f32[128,2048]{1,0:T(8,128)}, bf16[128,2048]{1,0:T(8,128)(2,1)}, bf16[128,3072]{1,0:T(8,128)(2,1)}, bf16[2,2048,128]{2,1,0:T(8,128)(2,1)}) custom-call(bf16[128,2048]{1,0:T(8,128)(2,1)} %copy-done.2, f32[1,2048]{1,0:T(1,128)} %refs_5_.4, f32[1,2048]{1,0:T(1,128)} %refs_6_.3, f32[128,128]{1,0:T(8,128)} %get-tuple-element.117.cos_ref.refs_3_.refs_7_, ...), custom_call_target="tpu_custom_call" | custom-call | tf_op jit(solution)/shard_map/attend_forward/pallas_call | solution.py:316
  231.8 31.5 %feed_forward.3 = (bf16[128,2048]{1,0:T(8,128)(2,1)}, bf16[512,2048]{1,0:T(8,128)(2,1)}, bf16[512,4096]{1,0:T(8,128)(2,1)}) custom-call(bf16[128,2048]{1,0:T(8,128)(2,1)} %get-tuple-element.79.refs_0_.refs_3_, f32[128,2048]{1,0:T(8,128)} %get-tuple-element.69.refs_1_.refs_2_, bf16[2048,4096]{1,0:T(8,128)(2,1)} %get-tuple-element.62.refs_2_.refs_3_.gate_up_hbm, ...), custom_call_target="tpu_custom_call" | custom-call | tf_op jit(solution)/shard_map/feed_forward/pallas_call | solution.py:696
  263.3 40.0 %feed_backward.2 = (f32[128,2048]{1,0:T(8,128)}, bf16[512,2048]{1,0:T(8,128)(2,1)}, bf16[4,128,2048]{2,1,0:T(8,128)(2,1)}) custom-call(bf16[128,2048]{1,0:T(8,128)(2,1)} %refs_5_.5, bf16[512,4096]{1,0:T(8,128)(2,1)} %get-tuple-element.71.refs_1_, bf16[2048,2048]{1,0:T(8,128)(2,1)} %bitcast.18, bf16[2048,4096]{1,0:T(8,128)(2,1)} %get-tuple-element.62.refs_2_.refs_3_.gate_up_hbm), custom_call_target="tpu_custom_call" | custom-call | tf_op jit(solution)/shard_map/feed_backward/pallas_call | solution.py:696
  303.4 24.0 %attend_backward.2 = (f32[128,2048]{1,0:T(8,128)}, bf16[128,2048]{1,0:T(8,128)(2,1)}, bf16[128,3072]{1,0:T(8,128)(2,1)}, f32[2,2048]{1,0:T(2,128)}, bf16[4,512,512]{2,1,0:T(8,128)(2,1)}) custom-call(f32[128,2048]{1,0:T(8,128)} %get-tuple-element.72.refs_0_, bf16[128,2048]{1,0:T(8,128)(2,1)} %refs_5_.5, f32[128,2048]{1,0:T(8,128)} %get-tuple-element.69.refs_1_.refs_2_, ...), custom_call_target="tpu_custom_call" | custom-call | tf_op jit(solution)/shard_map/attend_backward/pallas_call | solution.py:333
  327.3 1.5 collective-permute-start.1
  328.9 0.0 copy-start.7
  328.9 0.0 copy-start.8
  328.9 99.9 %prepare.1 = (bf16[4,512,2048]{2,1,0:T(8,128)(2,1)}, bf16[2048,4096]{1,0:T(8,128)(2,1)}, bf16[512,2048]{1,0:T(8,128)(2,1)}, bf16[512,2048]{1,0:T(8,128)(2,1)}) custom-call(bf16[2048,4096]{1,0:T(8,128)(2,1)} %get-tuple-element.62.refs_2_.refs_3_.gate_up_hbm, bf16[512,2048]{1,0:T(8,128)(2,1)} %get-tuple-element.76.refs_0_, ...), custom_call_target="tpu_custom_call" | custom-call | tf_op jit(solution)/shard_map/prepare/pallas_call | solution.py:1663
  428.8 0.0 copy-done.7
  428.8 0.0 copy-done.8
  428.8 0.9 select_bitcast_fusion.1
  429.7 0.0 collective-permute-done.1.refs_0_.refs_1_.refs_4_
  429.7 0.0 copy-start
  429.7 0.8 copy-done
  430.5 2.7 feed_backward.3
  433.2 4.2 attend_backward.3
  437.4 40.5 %attend_grads.1 = (bf16[4,128,5120]{2,1,0:T(8,128)(2,1)}, f32[2,2048]{1,0:T(2,128)}, bf16[4,128,2048]{2,1,0:T(8,128)(2,1)}) custom-call(bf16[128,3072]{1,0:T(8,128)(2,1)} %get-tuple-element.91.refs_0_, bf16[128,3072]{1,0:T(8,128)(2,1)} %get-tuple-element.92.refs_1_, f32[2,2048]{1,0:T(2,128)} %get-tuple-element.93.refs_2_, ...), custom_call_target="tpu_custom_call" | custom-call | tf_op jit(solution)/shard_map/attend_grads/pallas_call | solution.py:1035
  477.9 101.1 %feed_grads.1 = (bf16[128,16384]{1,0:T(8,128)(2,1)}, f32[512,2048]{1,0:T(8,128)}, f32[128,3072]{1,0:T(8,128)}, f32[128,2048]{1,0:T(8,128)}, f32[2,2048]{1,0:T(2,128)}, /*index=5*/bf16[4,512,2048]{2,1,0:T(8,128)(2,1)}) custom-call(bf16[512,2048]{1,0:T(8,128)(2,1)} %get-tuple-element.89.left_ref, bf16[512,2048]{1,0:T(8,128)(2,1)} %get-tuple-element.90.hidden_ref, ...), custom_call_target="tpu_custom_call" | custom-call | tf_op jit(solution)/shard_map/feed_grads/pallas_call | solution.py:1454
  579.0 1.4 fusion.4
  580.4 0.0 copy-start.4
  580.4 0.0 copy-start.5
  580.4 6.6 %bitcast_convert_fusion = f32[1,128,16384]{2,1,0:T(8,128)} fusion(bf16[128,16384]{1,0:T(8,128)(2,1)} %get-tuple-element.110), kind=kLoop, calls=%fused_computation | loop fusion | flops 2097152 | bytes 12582912 | tf_op jit(solution)/shard_map/broadcast_in_dim | solution.py:1840
  587.0 0.0 copy-start.3
  587.0 0.0 copy-start.6
  587.0 0.0 copy-done.4
  587.0 0.0 copy-done.5
  587.0 0.0 copy-start.1
  587.0 1.1 select_bitcast_fusion
  588.1 0.7 copy-done.3
  588.8 1.1 copy.21
  589.9 0.0 copy-done.6
  589.9 1.0 copy.22
  590.9 0.0 copy-done.1
  590.9 2.0 copy.23
  (2 shorter events, 0.0 us)
Async XLA Ops:
  172.8 46.0 %collective-permute-start = (bf16[128,2048]{1,0:T(8,128)(2,1)}, bf16[128,2048]{1,0:T(8,128)(2,1)S(1)}, u32[]{:S(2)}, u32[]{:S(2)}) collective-permute-start(bf16[128,2048]{1,0:T(8,128)(2,1)} %get-tuple-element.63), channel_id=1, source_target_pairs={{0,16},{1,17},{2,18},{3,19},{4,20},{5,21},{6,22},{7,23},{8,24},{9,... | collective-permute-start | bytes 1572872 | tf_op jit(solution)/shard_map/ppermute | solution.py:1789
  218.8 0.8 copy-start.2
  327.3 102.3 %collective-permute-start.1 = (bf16[128,2048]{1,0:T(8,128)(2,1)}, bf16[128,2048]{1,0:T(8,128)(2,1)S(1)}, u32[]{:S(2)}, u32[]{:S(2)}) collective-permute-start(bf16[128,2048]{1,0:T(8,128)(2,1)} %get-tuple-element.75), channel_id=1, source_target_pairs={{16,0},{17,1},{18,2},{19,3},{20,4},{21,5},{22,6},{23,7},{24,8},{25... | collective-permute-start | bytes 1572872 | tf_op jit(solution)/shard_map/ppermute | solution.py:1818
  328.9 100.0 %copy-start.7 = (bf16[128,2048]{1,0:T(8,128)(2,1)S(1)}, bf16[128,2048]{1,0:T(8,128)(2,1)}, u32[]{:S(2)}) copy-start(bf16[128,2048]{1,0:T(8,128)(2,1)} %get-tuple-element.63) | copy-start | bytes 1572868
  328.9 100.0 %copy-start.8 = (bf16[128,2048]{1,0:T(8,128)(2,1)S(1)}, bf16[128,2048]{1,0:T(8,128)(2,1)}, u32[]{:S(2)}) copy-start(bf16[128,2048]{1,0:T(8,128)(2,1)} %get-tuple-element.70) | copy-start | bytes 1572868
  429.7 0.8 copy-start
  580.4 6.6 %copy-start.4 = (f32[128,2048]{1,0:T(8,128)S(1)}, f32[128,2048]{1,0:T(8,128)}, u32[]{:S(2)}) copy-start(f32[128,2048]{1,0:T(8,128)} %get-tuple-element.88) | copy-start | bytes 3145732
  580.4 6.6 %copy-start.5 = (f32[128,2048]{1,0:T(8,128)S(1)}, f32[128,2048]{1,0:T(8,128)}, u32[]{:S(2)}) copy-start(f32[128,2048]{1,0:T(8,128)} %get-tuple-element.87) | copy-start | bytes 3145732
  587.0 1.8 copy-start.3
  587.0 2.9 copy-start.6
  587.0 3.9 copy-start.1

commit v6 on v5

--- a/solution.py
+++ b/solution.py
@@ -373,7 +373,7 @@
     return shard, chip * 2 + (1 - core), (1 - chip) * 2 + core, (1 - chip) * 2 + (1 - core)
 
 
-def slice_barrier(devices, turns=()):
+def slice_barrier(devices, turns=(), more=0):
     barrier = pltpu.get_barrier_semaphore()
     replicas = lax.axis_size("replica")
     for device in devices:
@@ -381,7 +381,7 @@
     for turn in turns:
         target = lax.rem(lax.axis_index("replica") + turn, replicas)
         pl.semaphore_signal(barrier, inc=1, device_id={"replica": target}, device_id_type=MESH)
-    pl.semaphore_wait(barrier, len(devices) + len(turns))
+    pl.semaphore_wait(barrier, len(devices) + len(turns) + more)
 
 
 def replica_copy(source, target, turn, send_sems, recv_sems, base):
@@ -396,13 +396,13 @@
 CHUNK = 512
 
 
-def feed_kernel(backward, rows, *refs):
+def feed_kernel(backward, rows, target, *refs):
     if backward:
         (mine_ref, gate_up_hbm, first_hbm, second_hbm, result_ref, all_hbm, others_hbm,
          mid_ref, all_ref, gate_up_ref, first_ref, second_ref, part_ref, take_ref, sent_ref, land_ref, own_ref,
          own_take_ref, load_sems, keep_sems, hold_sems, send_sems, recv_sems) = refs
     else:
-        (mine_ref, middle_hbm, first_hbm, second_hbm, result_ref, all_hbm, gate_up_hbm,
+        (mine_ref, middle_hbm, first_hbm, second_hbm, result_ref, all_hbm, gate_up_hbm, others_hbm, next_hbm,
          mid_ref, all_ref, gate_up_ref, first_ref, second_ref, part_ref, take_ref, sent_ref, land_ref, own_ref,
          own_take_ref, middle_ref, load_sems, keep_sems, hold_sems, send_sems, recv_sems) = refs
     shard, beside, across, _ = slice_peers()
@@ -436,8 +436,8 @@
         for at in range(2 * lax.axis_size("shard")):
             group, part, owner = at // 4, at // 2 % 2, at % 2
             source = pl.ds(at * half, half)
-            target = pl.ds(group * 2 * rows + owner * rows + part * half, half)
-            load_extra.append(pltpu.make_async_copy(gate_up_hbm.at[source], gate_up_ref.at[target], hold_sems.at[at]))
+            place = pl.ds(group * 2 * rows + owner * rows + part * half, half)
+            load_extra.append(pltpu.make_async_copy(gate_up_hbm.at[source], gate_up_ref.at[place], hold_sems.at[at]))
     else:
         load_extra.append(pltpu.make_async_copy(middle_hbm, middle_ref, hold_sems.at[0]))
     if backward:
@@ -463,8 +463,16 @@
     def owned(owner, part):
         return all_ref.at[place_of(owner, part)]
 
-    turns = range(1, lax.axis_size("replica"), 2) if backward else ()
-    slice_barrier((beside, across), turns)
+    turns = range(1, lax.axis_size("replica"), 2)
+    base = 6 + (2 * parts + 1) * spans
+    slice_barrier((beside, across), turns, 0 if target is None else 1)
+
+    def hand_on(part, at):
+        place = (pl.ds(part * piece, piece), pl.ds(at * span_cols, span_cols))
+        return section_copy(
+            result_ref.at[place], next_hbm.at[place], part * spans + at + base + lax.axis_size("replica"),
+            send_sems, recv_sems, target,
+        )
 
     def across_copy(part):
         return remote(owned(shard, part), owned(shard, part), part, across)
@@ -478,7 +486,6 @@
         across_copy(part).start()
     for copy in beside_copies:
         copy.start()
-    base = 6 + (2 * parts + 1) * spans
     spread_copies = [
         replica_copy(mine_ref, others_hbm.at[lax.axis_index("replica")], turn, send_sems, recv_sems, base)
         for turn in turns
@@ -642,17 +649,49 @@
                 result_ref[place, cols] = total
             else:
                 result_ref[place, cols] = (middle_ref[place, cols] + total).astype(BF)
+                if target is not None:
+                    hand_on(part, at).start()
     for part in range(2):
         beside_copies[part].wait_send()
         across_copy(part).wait_send()
         relay(part).wait_send()
     for copy in spread_copies + stores:
         copy.wait()
+    if target is not None:
+        for part in range(parts):
+            for at in range(spans):
+                hand_on(part, at).wait_send()
     for at in range(spans):
         give_own(at).wait_send()
         for part in range(parts):
             give(part, at).wait_send()
             cross(part, at).wait_send()
+
+
+def section_copy(source, target, at, send_sems, recv_sems, section):
+    return pltpu.make_async_remote_copy(
+        source, target, send_sems.at[at], recv_sems.at[at], device_id={"section": section}, device_id_type=MESH
+    )
+
+
+def feed_forward_kernel(section, last, parts, spans, rows, *refs):
+    @pl.when(lax.axis_index("section") == section)
+    def _():
+        feed_kernel(False, rows, None if last else section + 1, *refs)
+
+    if not last:
+
+        @pl.when(lax.axis_index("section") == section + 1)
+        def _():
+            barrier = pltpu.get_barrier_semaphore()
+            pl.semaphore_signal(barrier, inc=1, device_id={"section": section}, device_id_type=MESH)
+            next_hbm, send_sems, recv_sems = refs[8], refs[-2], refs[-1]
+            base = 6 + (2 * parts + 1) * spans + lax.axis_size("replica")
+            high, wide = rows // parts, next_hbm.shape[1] // spans
+            for part in range(parts):
+                for at in range(spans):
+                    place = next_hbm.at[pl.ds(part * high, high), pl.ds(at * wide, wide)]
+                    section_copy(place, place, base + part * spans + at, send_sems, recv_sems, section).wait_recv()
 
 
 def call_feed(section, backward, operands, collective):
@@ -667,9 +706,12 @@
     out_shape = [
         jax.ShapeDtypeStruct((rows, width), F32 if backward else BF),
         jax.ShapeDtypeStruct((every, width), BF),
-        jax.ShapeDtypeStruct((replicas, rows, width) if backward else (every, 2 * ff), BF),
+        jax.ShapeDtypeStruct((replicas, rows, width), BF),
     ]
-    copies = 6 + (2 * parts + 1) * spans + (replicas if backward else 0)
+    if not backward:
+        out_shape.insert(2, jax.ShapeDtypeStruct((every, 2 * ff), BF))
+        out_shape.append(jax.ShapeDtypeStruct((rows, width), BF))
+    copies = 6 + (3 * parts + 1) * spans + replicas
     piece = pltpu.VMEM((parts, spans, piece_rows, span_cols), BF)
     scratch = [
         pltpu.VMEM((every, 2 * ff if backward else ff), BF),
@@ -694,10 +736,12 @@
         pltpu.SemaphoreType.DMA((copies,)),
     ]
     return pl.pallas_call(
-        gated(section, functools.partial(feed_kernel, backward, rows)),
+        gated(section, functools.partial(feed_kernel, True, rows, None))
+        if backward
+        else functools.partial(feed_forward_kernel, section, section == lax.axis_size("section") - 1, parts, spans, rows),
         out_shape=out_shape,
         in_specs=[vmem] + [anywhere] * 3,
-        out_specs=[vmem] + [anywhere] * 2,
+        out_specs=[vmem] + [anywhere] * (len(out_shape) - 1),
         scratch_shapes=scratch,
         compiler_params=pltpu.CompilerParams(
             collective_id=collective, has_side_effects=True, vmem_limit_bytes=VMEM_LIMIT
@@ -914,177 +958,90 @@
     )(qkv_weight, out_weight, gate_up_weight, *operands)
 
 
-def attend_grads_kernel(sections, *refs):
-    sources = [refs[at * sections : (at + 1) * sections] for at in range(5)]
-    (terms_ref, gain_sum_ref, others_hbm, all_ref, projected_ref, upstream_ref, gains_ref, gains_land_ref,
-     lefts_ref, left_ref, load_sems, send_sems, recv_sems) = refs[5 * sections :]
+def repeat(first, last, body):
+    def step(at, carry):
+        body(at)
+        return carry
+
+    if first < last:
+        lax.fori_loop(first, last, step, 0)
+
+
+def by_chunk(count, body):
+    repeat(0, count, lambda at: body(pl.ds(pl.multiple_of(at * CHUNK, CHUNK), CHUNK)))
+
+
+def weight_grads_kernel(sections, left_rows_ref, hidden_ref, *refs):
+    sources = [refs[at * sections : (at + 1) * sections] for at in range(7)]
+    (gate_up_hbm, down_hbm,
+     gate_up_grad_ref, down_grad_ref, qkv_grad_ref, out_grad_ref, gain_sum_ref, gathered_hbm, even_hbm,
+     projected_ref, upstream_ref, gains_ref, gains_land_ref, gain_part_ref, gains_last_ref, lefts_ref, left_ref,
+     extra_ref, terms_ref, chain_ref, down_ref, block_ref, gate_up_ref, mid_ref, sum_ref, stage_ref,
+     start_sems, load_sems, block_sems, keep_sem, send_sems, recv_sems) = refs[7 * sections :]
     shard, beside, across, diagonal = slice_peers()
     peers = (across, diagonal, beside)
     replica, replicas = lax.axis_index("replica"), lax.axis_size("replica")
+    here = [lax.axis_index("section") == section for section in range(sections)]
     rows, cols = projected_ref.shape
-    every, step = all_ref.shape[1:]
-    pieces = cols // step
-    sub_rows = terms_ref.shape[1]
-    loads = []
-    for at, target in enumerate((projected_ref, gains_ref, upstream_ref)):
-        loads.append([pltpu.make_async_copy(source, target, load_sems.at[at]) for source in sources[at]])
-    loads.append(
-        [
-            pltpu.make_async_copy(source, all_ref.at[pl.ds(pieces, all_ref.shape[0] - pieces)], load_sems.at[3])
-            for source in sources[3]
-        ]
-    )
-    loads.append([pltpu.make_async_copy(source, lefts_ref, load_sems.at[4]) for source in sources[4]])
-    for copies in loads:
-        start_own(copies)
-    slice_barrier(peers, range(1, replicas))
-    kinds, groups = lefts_ref.shape[:2]
-    left_base = 3 * pieces + 2 * replicas
-
-    def hand_left(kind, group, peer):
-        own_cols = pl.ds(pl.multiple_of(shard * rows, rows), rows)
-        return pltpu.make_async_remote_copy(
-            lefts_ref.at[kind, group, peers[peer]], left_ref.at[kind, group, :, own_cols],
-            send_sems.at[left_base + (kind * groups + group) * 3 + peer],
-            recv_sems.at[left_base + (kind * groups + group) * 3 + peer],
-            device_id={"shard": peers[peer]}, device_id_type=MESH,
-        )
-
-    spread_copies = [
-        replica_copy(upstream_ref, others_hbm.at[replica], turn, send_sems, recv_sems, 3 * pieces)
-        for turn in range(2, replicas, 2)
-    ]
-    gain_copies = [
-        replica_copy(gains_ref, gains_land_ref.at[replica], turn, send_sems, recv_sems, 3 * pieces + replicas)
-        for turn in range(1, replicas)
-    ]
-
-    def remote(owner, piece, at, device):
-        place = all_ref.at[piece, pl.ds(pl.multiple_of(owner * rows, rows), rows)]
-        return pltpu.make_async_remote_copy(
-            place, place, send_sems.at[at], recv_sems.at[at], device_id={"shard": device}, device_id_type=MESH
-        )
-
-    own = pl.ds(pl.multiple_of(shard * rows, rows), rows)
-    over = [remote(shard, piece, piece, across) for piece in range(pieces)]
-    direct = [remote(shard, piece, pieces + piece, beside) for piece in range(pieces)]
-    relays = [remote(across, piece, 2 * pieces + piece, beside) for piece in range(pieces)]
-    lefts = [(kind, group, peer) for kind in reversed(range(kinds)) for group in range(groups) for peer in range(3)]
-    loads[4][0].wait()
-    for place in lefts:
-        hand_left(*place).start()
-    for kind in range(kinds):
-        for group in range(groups):
-            left_ref[kind, group, :, own] = lefts_ref[kind, group, shard]
-    loads[0][0].wait()
-    for piece in range(pieces):
-        all_ref[piece, own, :] = projected_ref[:, piece * step : (piece + 1) * step]
-        over[piece].start()
-        direct[piece].start()
-    loads[1][0].wait()
-    gains_land_ref[replica] = gains_ref[...]
-    loads[2][0].wait()
-    for copy in gain_copies + spread_copies:
-        copy.start()
-
-    def product(piece):
-        at = piece * step
-        kind = 0 if at < cols else 1
-        left = jnp.concatenate([left_ref[kind, group] for group in range(groups)], 0)
-        total = dot(left, all_ref[piece]).astype(BF)
-        for group in range(groups):
-            terms_ref[group, :, at : at + step] = total[group * sub_rows : (group + 1) * sub_rows]
-
-    loads[3][0].wait()
-    for place in lefts:
-        hand_left(*place).wait_recv()
-    for piece in range(pieces, all_ref.shape[0]):
-        product(piece)
-    for piece in range(pieces):
-        over[piece].wait_recv()
-        relays[piece].start()
-        if piece:
-            direct[piece - 1].wait_recv()
-            relays[piece - 1].wait_recv()
-            product(piece - 1)
-    direct[pieces - 1].wait_recv()
-    relays[pieces - 1].wait_recv()
-    product(pieces - 1)
-    for copy in gain_copies:
-        copy.wait()
-    gain_sum_ref[...] = jnp.sum(gains_land_ref[...], 0)
-    for copy in over + direct + relays:
-        copy.wait_send()
-    for place in lefts:
-        hand_left(*place).wait_send()
-    for copy in spread_copies:
-        copy.wait()
-
-
-def call_attend_grads(lefts, projected, gains, upstream, branch, collective):
-    replicas, sections = lax.axis_size("replica"), len(projected)
-    rows, cols = projected[0].shape
-    width = upstream[0].shape[1]
-    shards = lax.axis_size("shard")
-    every, tokens = width // shards, shards * rows
-    sub_rows = every // replicas
-    lefts = [values.reshape(2, replicas, shards, sub_rows, rows) for values in lefts]
-    pieces = cols // CHUNK
-    copies = 3 * pieces + 2 * replicas + 2 * replicas * 3
-    vmem, anywhere = pl.BlockSpec(memory_space=pltpu.VMEM), pl.BlockSpec(memory_space=pl.ANY)
-    return pl.pallas_call(
-        functools.partial(attend_grads_kernel, sections),
-        out_shape=[
-            jax.ShapeDtypeStruct((replicas, every // replicas, cols + width), BF),
-            jax.ShapeDtypeStruct(gains[0].shape, F32),
-            jax.ShapeDtypeStruct((replicas, rows, width), BF),
-        ],
-        in_specs=[anywhere] * 5 * sections,
-        out_specs=[vmem] * 2 + [anywhere],
-        scratch_shapes=[
-            pltpu.VMEM(((cols + width) // CHUNK, tokens, CHUNK), BF),
-            pltpu.VMEM((rows, cols), BF),
-            pltpu.VMEM((rows, width), BF),
-            pltpu.VMEM(gains[0].shape, F32),
-            pltpu.VMEM((replicas,) + gains[0].shape, F32),
-            pltpu.VMEM(lefts[0].shape, BF),
-            pltpu.VMEM((2, replicas, sub_rows, tokens), BF),
-            pltpu.SemaphoreType.DMA((5,)),
-            pltpu.SemaphoreType.DMA((copies,)),
-            pltpu.SemaphoreType.DMA((copies,)),
-        ],
-        compiler_params=pltpu.CompilerParams(
-            collective_id=collective, has_side_effects=True, vmem_limit_bytes=VMEM_LIMIT
-        ),
-        name="attend_grads",
-    )(*projected, *gains, *upstream, *branch, *lefts)
-
-
-def feed_grads_kernel(sections, left_ref, hidden_ref, terms_ref, gains_ref, *refs):
-    upstream = refs[:sections]
-    (odd_hbm, even_hbm, early_hbm, gate_up_hbm, down_hbm,
-     gate_up_grad_ref, down_grad_ref, qkv_grad_ref, out_grad_ref, gain_sum_ref, gathered_hbm,
-     down_ref, block_ref, gate_up_ref, mid_ref, sum_ref, stage_ref, chain_ref, gains_land_ref,
-     load_sems, block_sems, keep_sem, send_sems, recv_sems) = refs[sections:]
-    shard, beside, across, diagonal = slice_peers()
-    peers = (across, diagonal, beside)
-    replica, replicas = lax.axis_index("replica"), lax.axis_size("replica")
-    early = lax.axis_index("section") == lax.axis_size("section") - 1
-    late = lax.axis_index("section") < lax.axis_size("section") - 1
-    rows = odd_hbm.shape[1]
-    every, width = upstream[0].shape
+    every, width = sources[5][0].shape
+    pieces, all_pieces = cols // CHUNK, (cols + width) // CHUNK
+    staged = stage_ref.shape[2] // CHUNK
+    kinds, groups, _, sub_rows, _ = lefts_ref.shape
     part = down_ref.shape[0]
     half_part = part // 2
     ff = gate_up_grad_ref.shape[1] // 2
     steps = half_part // CHUNK
     wide = width // CHUNK
     out_rows = gate_up_grad_ref.shape[0]
-    grad_base = 3 * replicas
-    chain_base = grad_base + 2 * 2 * steps * 3
-    gain_base = chain_base + 2 * replicas
-
+    piece_base = 3 * replicas
+    spread_base = piece_base + 3 * pieces
+    gain_base = spread_base + replicas
+    left_base = gain_base + replicas
+    chain_base = left_base + kinds * groups * 3
+    last_base = chain_base + 2 * replicas
+    grad_base = last_base + 3
+
+    def remote(source, target, at, device):
+        return pltpu.make_async_remote_copy(
+            source, target, send_sems.at[at], recv_sems.at[at], device_id={"shard": device}, device_id_type=MESH
+        )
+
+    def owned(owner):
+        return pl.ds(pl.multiple_of(owner * rows, rows), rows)
+
+    def piece_place(piece, place=None):
+        if piece < 2 * staged:
+            place = pl.ds(0, every) if place is None else place
+            return stage_ref.at[piece // staged, place, pl.ds(piece % staged * CHUNK, CHUNK)]
+        return extra_ref.at[piece - 2 * staged] if place is None else extra_ref.at[piece - 2 * staged, place]
+
+    def piece_copy(owner, piece, kind, device):
+        place = piece_place(piece, owned(owner))
+        return remote(place, place, piece_base + kind * pieces + piece, device)
+
+    over = [piece_copy(shard, piece, 0, across) for piece in range(pieces)]
+    direct = [piece_copy(shard, piece, 1, beside) for piece in range(pieces)]
+    relays = [piece_copy(across, piece, 2, beside) for piece in range(pieces)]
+
+    def hand_left(kind, group, peer):
+        return remote(
+            lefts_ref.at[kind, group, peers[peer]], left_ref.at[kind, group, :, owned(shard)],
+            left_base + (kind * groups + group) * 3 + peer, peers[peer],
+        )
+
+    lefts = [(kind, group, peer) for kind in reversed(range(kinds)) for group in range(groups) for peer in range(3)]
+    loads = []
+    for at, target in enumerate((lefts_ref, projected_ref, gains_ref, upstream_ref)):
+        loads.append([pltpu.make_async_copy(source, target, start_sems.at[at]) for source in sources[at]])
+    load_branch = [
+        [
+            pltpu.make_async_copy(source.at[piece - pieces], piece_place(piece), start_sems.at[4 + piece - pieces])
+            for source in sources[4]
+        ]
+        for piece in range(pieces, all_pieces)
+    ]
+    load_own = [pltpu.make_async_copy(source, block_ref.at[0], load_sems.at[2, 0]) for source in sources[5]]
     load_down = pltpu.make_async_copy(down_hbm, down_ref, load_sems.at[3, 0])
-    load_down.start()
 
     def block_at(turn):
         return lax.rem(replica + turn, replicas)
@@ -1093,36 +1050,27 @@
         return pl.ds(pl.multiple_of(block_at(turn) * every, every), every)
 
     def load_gate_up(half, turn, side):
-        cols = pl.ds(side * part + half * half_part, half_part)
+        place = pl.ds(side * part + half * half_part, half_part)
         slot = lax.rem(turn, 2)
         return pltpu.make_async_copy(
-            gate_up_hbm.at[tokens(turn), cols], gate_up_ref.at[slot, side], load_sems.at[side, slot]
+            gate_up_hbm.at[tokens(turn), place], gate_up_ref.at[slot, side], load_sems.at[side, slot]
         )
 
     def block_copies(turn, source):
         slot = lax.rem(turn, 2)
         copies = []
         for at, owner in enumerate(peers + (shard,)):
-            place = pl.ds(pl.multiple_of(owner * rows, rows), rows)
-            if source is early_hbm:
-                own = early_hbm.at[turn, place]
-            else:
-                own = gathered_hbm.at[turn, place] if source is None or at < 3 else source.at[block_at(turn)]
-            copies.append(pltpu.make_async_copy(own, block_ref.at[slot, place], block_sems.at[slot, at]))
+            own = gathered_hbm.at[turn, owned(owner)] if source is None or at < 3 else source.at[block_at(turn)]
+            copies.append(pltpu.make_async_copy(own, block_ref.at[slot, owned(owner)], block_sems.at[slot, at]))
         return copies
 
     def load_block(turn):
-        @pl.when(early & (turn % 2 == 1))
-        def _():
-            for copy in block_copies(turn, early_hbm):
-                copy.start()
-
-        @pl.when(late | (turn % 2 == 0))
-        def _():
-            for copy in block_copies(turn, None)[:3]:
-                copy.start()
-
-        cases = ((turn == 0, None), ((turn > 0) & (turn % 2 == 0), even_hbm), (late & (turn % 2 == 1), odd_hbm))
+        for copy in block_copies(turn, None)[:3]:
+            copy.start()
+        cases = [(turn == 0, None), ((turn > 0) & (turn % 2 == 0), even_hbm)]
+        for section in range(sections):
+            odd_case = here[section] & (turn % 2 == 1)
+            cases.append((odd_case, sources[6][section]))
         for case, source in cases:
 
             @pl.when(case)
@@ -1133,30 +1081,29 @@
         for copy in block_copies(turn, None):
             copy.wait()
 
-    def remote(source, target, at, device):
-        return pltpu.make_async_remote_copy(
-            source, target, send_sems.at[at], recv_sems.at[at], device_id={"shard": device}, device_id_type=MESH
-        )
-
     def landing(turn, owner):
-        return gathered_hbm.at[turn, pl.ds(pl.multiple_of(owner * rows, rows), rows)]
-
-    def over(turn, source):
+        return gathered_hbm.at[turn, owned(owner)]
+
+    def block_over(turn, source):
         return remote(source.at[block_at(turn)], landing(turn, shard), 3 * turn, across)
 
-    def direct(turn, source):
+    def block_direct(turn, source):
         return remote(source.at[block_at(turn)], landing(turn, shard), 3 * turn + 1, beside)
 
-    def relay(turn):
+    def block_relay(turn):
         return remote(landing(turn, across), landing(turn, across), 3 * turn + 2, beside)
 
     def send_block(turn):
-        for parity, source in ((0, even_hbm), (1, odd_hbm)):
-
-            @pl.when((lax.rem(turn, 2) == 1) & late if parity else lax.rem(turn, 2) == 0)
+        cases = [(turn % 2 == 0, even_hbm)]
+        for section in range(sections):
+            odd_case = here[section] & (turn % 2 == 1)
+            cases.append((odd_case, sources[6][section]))
+        for case, source in cases:
+
+            @pl.when(case)
             def _(source=source):
-                over(turn, source).start()
-                direct(turn, source).start()
+                block_over(turn, source).start()
+                block_direct(turn, source).start()
 
     def chain_slot(block, at):
         return replicas - (replicas - block) * ((at - block + replicas - 1) // replicas)
@@ -1175,7 +1122,17 @@
         )
 
     def add_terms(block):
-        chain_ref[block] = (chain_ref[block].astype(F32) + terms_ref[block].astype(F32)).astype(BF)
+        def add(place):
+            total = chain_ref[block, :, place].astype(F32) + terms_ref[block, :, place].astype(F32)
+            chain_ref[block, :, place] = total.astype(BF)
+
+        by_chunk(all_pieces, add)
+
+    def take_terms(block):
+        def take(place):
+            chain_ref[block, :, place] = terms_ref[block, :, place]
+
+        by_chunk(all_pieces, take)
 
     def chain_step(step):
         high = replicas - 1 - step + replica
@@ -1201,57 +1158,11 @@
                 chain_down(low).start()
 
     def gain_copy(peer):
-        return remote(
-            gains_ref, gains_land_ref.at[shard], gain_base + peer, peers[peer]
-        )
-
-    barrier = pltpu.get_barrier_semaphore()
-    for device in peers:
-        pl.semaphore_signal(barrier, inc=1, device_id={"shard": device}, device_id_type=MESH)
-
-    @pl.when(replica > 0)
-    def _():
-        pl.semaphore_signal(barrier, inc=1, device_id={"replica": replica - 1}, device_id_type=MESH)
-
-    @pl.when(replica < replicas - 1)
-    def _():
-        pl.semaphore_signal(barrier, inc=1, device_id={"replica": replica + 1}, device_id_type=MESH)
-
-    below = (replica + replicas - 1) // replicas
-    above = (2 * replicas - 2 - replica) // replicas
-    pl.semaphore_wait(barrier, 3 + below + above)
-
-    for turn in range(1, min(3, replicas)):
-        send_block(turn)
-
-    for block in reversed(range(1, replicas)):
-
-        @pl.when(replica == 0)
-        def _(block=block):
-            chain_ref[block] = terms_ref[block]
-            chain_up(block).start()
-
-    for block in range(replicas - 1):
-
-        @pl.when(replica == replicas - 1)
-        def _(block=block):
-            chain_ref[block] = terms_ref[block]
-            chain_down(block).start()
-
-    for peer in range(3):
-        gain_copy(peer).start()
-    gains_land_ref[shard] = gains_ref[...]
-    load_own = [pltpu.make_async_copy(source, block_ref.at[0], load_sems.at[2, 0]) for source in upstream]
-    start_own(load_own)
-    load_own[0].wait()
-    keep_own = pltpu.make_async_copy(block_ref.at[0], gathered_hbm.at[0], keep_sem)
-    keep_own.start()
-    load_down.wait()
-    keep_own.wait()
+        return remote(gain_part_ref, gains_last_ref.at[shard], last_base + peer, peers[peer])
 
     def send_grad(half, at, peer):
         device = peers[peer]
-        cols = pl.ds(pl.multiple_of(at * CHUNK, CHUNK), CHUNK)
+        place = pl.ds(pl.multiple_of(at * CHUNK, CHUNK), CHUNK)
         target = pl.ds(
             pl.multiple_of(
                 (at // steps) * ff + shard * part + half * half_part + (at % steps) * CHUNK, CHUNK
@@ -1259,107 +1170,202 @@
             CHUNK,
         )
         return remote(
-            stage_ref.at[half, pl.ds(pl.multiple_of(device * out_rows, out_rows), out_rows), cols],
+            stage_ref.at[half, pl.ds(pl.multiple_of(device * out_rows, out_rows), out_rows), place],
             gate_up_grad_ref.at[:, target],
             grad_base + (half * 2 * steps + at) * 3 + peer,
             device,
         )
 
-    def half_pass(half):
+    def clear_sum():
+        def clear(place):
+            sum_ref[:, place] = jnp.zeros((sum_ref.shape[0], CHUNK), F32)
+
+        by_chunk(2 * steps, clear)
+
+    def compute(half, turn):
+        slot = lax.rem(turn, 2)
+        later = lax.rem(turn + 1, replicas)
         for side in range(2):
-            load_gate_up(half, 0, side).start()
-        sum_ref[...] = jnp.zeros_like(sum_ref)
-
-        def work(turn, carry):
-            slot = lax.rem(turn, 2)
-            later = lax.rem(turn + 1, replicas)
+            load_gate_up(half, turn, side).wait()
+
+        @pl.when(turn + 1 < replicas)
+        def _():
             for side in range(2):
-                load_gate_up(half, turn, side).wait()
-
-            @pl.when(turn + 1 < replicas)
+                load_gate_up(half, later, side).start()
+            if half:
+                load_block(later)
+
+        def products(at, inner):
+            place = pl.ds(pl.multiple_of(at * CHUNK, CHUNK), CHUNK)
+            high = pl.ds(pl.multiple_of(half_part + at * CHUNK, CHUNK), CHUNK)
+            down_rows = pl.ds(pl.multiple_of(half * half_part + at * CHUNK, CHUNK), CHUNK)
+            grad_hidden = dot_rows(block_ref[slot], down_ref[down_rows, :])
+            gate = gate_up_ref[slot, 0, :, place].astype(F32)
+            up = gate_up_ref[slot, 1, :, place].astype(F32)
+            sigmoid = jax.nn.sigmoid(gate)
+            mid_ref[:, place] = (grad_hidden * up * sigmoid * (1.0 + gate * (1.0 - sigmoid))).astype(BF)
+            mid_ref[:, high] = (grad_hidden * gate * sigmoid).astype(BF)
+            return inner
+
+        lax.fori_loop(0, steps, products, 0)
+
+        def sums(at, inner):
+            place = pl.ds(pl.multiple_of(at * CHUNK, CHUNK), CHUNK)
+            total = sum_ref[:, place] + dot(left_rows_ref[:, tokens(turn)], mid_ref[:, place])
+
+            @pl.when(turn < replicas - 1)
             def _():
-                for side in range(2):
-                    load_gate_up(half, later, side).start()
-
-            if half:
-
-                @pl.when(turn + 1 < replicas)
-                def _():
-                    load_block(later)
-
-            def products(at, inner):
-                cols = pl.ds(pl.multiple_of(at * CHUNK, CHUNK), CHUNK)
-                high = pl.ds(pl.multiple_of(half_part + at * CHUNK, CHUNK), CHUNK)
-                down_rows = pl.ds(pl.multiple_of(half * half_part + at * CHUNK, CHUNK), CHUNK)
-                grad_hidden = dot_rows(block_ref[slot], down_ref[down_rows, :])
-                gate = gate_up_ref[slot, 0, :, cols].astype(F32)
-                up = gate_up_ref[slot, 1, :, cols].astype(F32)
-                sigmoid = jax.nn.sigmoid(gate)
-                mid_ref[:, cols] = (grad_hidden * up * sigmoid * (1.0 + gate * (1.0 - sigmoid))).astype(BF)
-                mid_ref[:, high] = (grad_hidden * gate * sigmoid).astype(BF)
-                return inner
-
-            lax.fori_loop(0, steps, products, 0)
-
-            def sums(at, inner):
-                cols = pl.ds(pl.multiple_of(at * CHUNK, CHUNK), CHUNK)
-                total = sum_ref[:, cols] + dot(left_ref[:, tokens(turn)], mid_ref[:, cols])
-
-                @pl.when(turn < replicas - 1)
-                def _():
-                    sum_ref[:, cols] = total
-
-                @pl.when(turn == replicas - 1)
-                def _():
-                    stage_ref[half, :, cols] = total.astype(BF)
-                    for peer in range(3):
-                        send_grad(half, at, peer).start()
-
-                return inner
-
-            lax.fori_loop(0, 2 * steps, sums, 0)
-
-            @pl.when(turn + 1 < replicas)
+                sum_ref[:, place] = total
+
+            @pl.when(turn == replicas - 1)
             def _():
-                if half:
-                    wait_block(later)
-                else:
-
-                    @pl.when(late | (later % 2 == 0))
-                    def _():
-                        over(later, even_hbm).wait_recv()
-                        relay(later).start()
-                        direct(later, even_hbm).wait_recv()
-                        relay(later).wait_recv()
-
-                    load_block(later)
-
-                    @pl.when(turn + 3 < replicas)
-                    def _():
-                        send_block(turn + 3)
-
-                    wait_block(later)
-
-            return carry
-
-        return work
-
-    first = half_pass(0)
-    lax.fori_loop(0, replicas - 1, first, 0)
+                stage_ref[half, pl.ds(0, total.shape[0]), place] = total.astype(BF)
+                for peer in range(3):
+                    send_grad(half, at, peer).start()
+
+            return inner
+
+        lax.fori_loop(0, 2 * steps, sums, 0)
+
+    def first_pass(turn, carry):
+        block_over(turn, even_hbm).wait_recv()
+        block_relay(turn).start()
+        block_direct(turn, even_hbm).wait_recv()
+        block_relay(turn).wait_recv()
+        load_block(turn)
+
+        @pl.when(turn + 2 < replicas)
+        def _():
+            send_block(turn + 2)
+
+        wait_block(turn)
+        compute(0, turn)
+        return carry
+
+    def second_pass(turn, carry):
+        compute(1, turn)
+
+        @pl.when(turn + 1 < replicas)
+        def _():
+            wait_block(lax.rem(turn + 1, replicas))
+
+        return carry
+
+    for copies in loads + load_branch + [load_own]:
+        start_own(copies)
+    load_down.start()
+    for side in range(2):
+        load_gate_up(0, 0, side).start()
+
+    barrier = pltpu.get_barrier_semaphore()
+    for device in peers:
+        pl.semaphore_signal(barrier, inc=1, device_id={"shard": device}, device_id_type=MESH)
+    for turn in range(1, replicas):
+        target = lax.rem(replica + turn, replicas)
+        pl.semaphore_signal(barrier, inc=1, device_id={"replica": target}, device_id_type=MESH)
+    pl.semaphore_wait(barrier, 2 + replicas)
+
+    spread_copies = [
+        replica_copy(upstream_ref, even_hbm.at[replica], turn, send_sems, recv_sems, spread_base)
+        for turn in range(2, replicas, 2)
+    ]
+    gain_copies = [
+        replica_copy(gains_ref, gains_land_ref.at[replica], turn, send_sems, recv_sems, gain_base)
+        for turn in range(1, replicas)
+    ]
+    loads[0][0].wait()
+    for place in lefts:
+        hand_left(*place).start()
+    loads[1][0].wait()
+    for piece in range(pieces):
+        piece_place(piece, owned(shard))[...] = projected_ref[:, piece * CHUNK : (piece + 1) * CHUNK]
+        over[piece].start()
+        direct[piece].start()
+    loads[2][0].wait()
+    gains_land_ref[replica] = gains_ref[...]
+    loads[3][0].wait()
+    for copy in gain_copies + spread_copies:
+        copy.start()
+    for kind in range(kinds):
+        for group in range(groups):
+            left_ref[kind, group, :, owned(shard)] = lefts_ref[kind, group, shard]
+    load_own[0].wait()
+    keep_own = pltpu.make_async_copy(block_ref.at[0], gathered_hbm.at[0], keep_sem)
+    keep_own.start()
+    clear_sum()
+    load_down.wait()
+    compute(0, 0)
+    keep_own.wait()
+
+    def product(piece, kind, source):
+        left = jnp.concatenate([left_ref[kind, group] for group in range(groups)], 0)
+        total = dot(left, source).astype(BF)
+        place = pl.ds(pl.multiple_of(piece * CHUNK, CHUNK), CHUNK)
+        for group in range(groups):
+            terms_ref[group, :, place] = total[group * sub_rows : (group + 1) * sub_rows]
+
+    def staged_product(piece, kind):
+        place = pl.ds(pl.multiple_of(piece % staged * CHUNK, CHUNK), CHUNK)
+        product(piece, kind, stage_ref[piece // staged, pl.ds(0, every), place])
+
+    for place in lefts:
+        hand_left(*place).wait_recv()
+    for copies in load_branch:
+        copies[0].wait()
+    repeat(pieces, min(all_pieces, 2 * staged), lambda piece: staged_product(piece, 1))
+    repeat(2 * staged, all_pieces, lambda piece: product(piece, 1, extra_ref[piece - 2 * staged]))
+    for piece in range(pieces):
+        over[piece].wait_recv()
+        relays[piece].start()
+    for copy in over:
+        copy.wait_send()
+    for copy in spread_copies:
+        copy.wait()
+    for turn in range(1, min(3, replicas)):
+        send_block(turn)
+    for copy in direct + relays:
+        copy.wait()
+    repeat(0, pieces, lambda piece: staged_product(piece, 0))
+    for block in reversed(range(1, replicas)):
+
+        @pl.when(replica == 0)
+        def _(block=block):
+            take_terms(block)
+            chain_up(block).start()
+
+    for block in range(replicas - 1):
+
+        @pl.when(replica == replicas - 1)
+        def _(block=block):
+            take_terms(block)
+            chain_down(block).start()
+
+    for copy in gain_copies:
+        copy.wait()
+    gain_part_ref[...] = jnp.sum(gains_land_ref[...], 0)
+    gains_last_ref[shard] = gain_part_ref[...]
+    for peer in range(3):
+        gain_copy(peer).start()
+    lax.fori_loop(1, replicas - 1, first_pass, 0)
     chain_step(1)
-    first(replicas - 1, 0)
+    first_pass(replicas - 1, 0)
+    for side in range(2):
+        load_gate_up(1, 0, side).start()
     load_block(0)
+    clear_sum()
     wait_block(0)
-    second = half_pass(1)
-    lax.fori_loop(0, replicas - 1, second, 0)
+    lax.fori_loop(0, replicas, second_pass, 0)
+    load_block(0)
     if replicas > 2:
         chain_step(2)
-    second(replicas - 1, 0)
-    load_block(0)
     wait_block(0)
-    down_grad_ref[...] = jnp.zeros_like(down_grad_ref)
-
-    def down_work(turn, carry):
+
+    def clear_down(place):
+        down_grad_ref[:, place] = jnp.zeros((down_grad_ref.shape[0], CHUNK), F32)
+
+    by_chunk(wide, clear_down)
+
+    def down_pass(turn, carry):
         slot = lax.rem(turn, 2)
         later = lax.rem(turn + 1, replicas)
 
@@ -1368,8 +1374,8 @@
             load_block(later)
 
         def down_sums(at, inner):
-            cols = pl.ds(pl.multiple_of(at * CHUNK, CHUNK), CHUNK)
-            down_grad_ref[:, cols] += dot(hidden_ref[:, tokens(turn)], block_ref[slot, :, cols])
+            place = pl.ds(pl.multiple_of(at * CHUNK, CHUNK), CHUNK)
+            down_grad_ref[:, place] += dot(hidden_ref[:, tokens(turn)], block_ref[slot, :, place])
             return inner
 
         lax.fori_loop(0, wide, down_sums, 0)
@@ -1380,39 +1386,45 @@
 
         return carry
 
-    lax.fori_loop(0, replicas, down_work, 0)
+    lax.fori_loop(0, replicas, down_pass, 0)
     for peer in range(3):
         gain_copy(peer).wait()
-    gain_sum_ref[...] = jnp.sum(gains_land_ref[...], 0)
+    gain_sum_ref[...] = jnp.sum(gains_last_ref[...], 0)
     own = pl.ds(pl.multiple_of(shard * out_rows, out_rows), out_rows)
     for half in range(2):
 
         def store_own(at, carry, half=half):
-            cols = pl.ds(pl.multiple_of(at * CHUNK, CHUNK), CHUNK)
+            place = pl.ds(pl.multiple_of(at * CHUNK, CHUNK), CHUNK)
             target = pl.ds(
                 pl.multiple_of(
                     (at // steps) * ff + shard * part + half * half_part + (at % steps) * CHUNK, CHUNK
                 ),
                 CHUNK,
             )
-            gate_up_grad_ref[:, target] = stage_ref[half, own, cols]
+            gate_up_grad_ref[:, target] = stage_ref[half, own, place]
             return carry
 
         lax.fori_loop(0, 2 * steps, store_own, 0)
     for step in range(3, replicas):
         chain_step(step)
-    cut = qkv_grad_ref.shape[1]
-    for grad_ref, cols in ((qkv_grad_ref, slice(0, cut)), (out_grad_ref, slice(cut, None))):
-        grad_ref[...] = terms_ref[replica, :, cols].astype(F32)
-
-        @pl.when(replica > 0)
-        def _(grad_ref=grad_ref, cols=cols):
-            grad_ref[...] += chain_ref[replica, :, cols].astype(F32)
-
-        @pl.when(replica < replicas - 1)
-        def _(grad_ref=grad_ref, cols=cols):
-            grad_ref[...] += chain_ref[replicas, :, cols].astype(F32)
-
+
+    def sum_up(grad_ref, first):
+        def add(place):
+            source = pl.ds(pl.multiple_of(first + place.start, CHUNK), CHUNK)
+            grad_ref[:, place] = terms_ref[replica, :, source].astype(F32)
+
+            @pl.when(replica > 0)
+            def _():
+                grad_ref[:, place] += chain_ref[replica, :, source].astype(F32)
+
+            @pl.when(replica < replicas - 1)
+            def _():
+                grad_ref[:, place] += chain_ref[replicas, :, source].astype(F32)
+
+        by_chunk(grad_ref.shape[1] // CHUNK, add)
+
+    sum_up(qkv_grad_ref, 0)
+    sum_up(out_grad_ref, cols)
     for half in range(2):
 
         def finish(at, carry, half=half):
@@ -1421,13 +1433,12 @@
             return carry
 
         lax.fori_loop(0, 2 * steps, finish, 0)
+    for place in lefts:
+        hand_left(*place).wait_send()
     for turn in range(1, replicas):
-
-        @pl.when(late | (turn % 2 == 0))
-        def _(turn=turn):
-            over(turn, even_hbm).wait_send()
-            direct(turn, even_hbm).wait_send()
-            relay(turn).wait_send()
+        block_over(turn, even_hbm).wait_send()
+        block_direct(turn, even_hbm).wait_send()
+        block_relay(turn).wait_send()
 
     for block in range(1, replicas):
 
@@ -1442,36 +1453,51 @@
             chain_down(block).wait_send()
 
 
-def call_feed_grads(left, hidden, terms, gains, upstream, odd, even, early, gate_up, down, qkv_cols, collective):
-    every, width = upstream[0].shape
-    sub_rows, attend_cols = terms.shape[1:]
-    replicas = odd.shape[0]
-    shards = lax.axis_size("shard")
+def call_weight_grads(left_rows, hidden, lefts, projected, gains, upstream, branch, slices, odd, gate_up, down,
+                      collective):
+    replicas, shards, sections = lax.axis_size("replica"), lax.axis_size("shard"), len(projected)
+    rows, cols = projected[0].shape
+    every, width = slices[0].shape
     part = down.shape[0]
-    out_rows = left.shape[0] // shards
+    slice_rows = left_rows.shape[0]
+    sub_rows = slice_rows // shards
+    lefts = [values.reshape(2, replicas, shards, sub_rows, rows) for values in lefts]
+    pieces, all_pieces = cols // CHUNK, (cols + width) // CHUNK
+    copies = 3 * replicas + 3 * pieces + 2 * replicas + 6 * replicas + 2 * replicas + 3 + 3 * 2 * (part // CHUNK)
     vmem, anywhere = pl.BlockSpec(memory_space=pltpu.VMEM), pl.BlockSpec(memory_space=pl.ANY)
-    copies = 5 * replicas + 3 * 2 * (part // CHUNK) + 3
+    gain_shape = gains[0].shape
     return pl.pallas_call(
-        functools.partial(feed_grads_kernel, len(upstream)),
+        functools.partial(weight_grads_kernel, sections),
         out_shape=[
-            jax.ShapeDtypeStruct((out_rows, 2 * part * shards), BF),
+            jax.ShapeDtypeStruct((sub_rows, 2 * part * shards), BF),
             jax.ShapeDtypeStruct((hidden.shape[0], width), F32),
-            jax.ShapeDtypeStruct((sub_rows, qkv_cols), F32),
-            jax.ShapeDtypeStruct((sub_rows, attend_cols - qkv_cols), F32),
-            jax.ShapeDtypeStruct(gains.shape, F32),
+            jax.ShapeDtypeStruct((sub_rows, cols), F32),
+            jax.ShapeDtypeStruct((sub_rows, width), F32),
+            jax.ShapeDtypeStruct(gain_shape, F32),
             jax.ShapeDtypeStruct((replicas, every, width), BF),
+            jax.ShapeDtypeStruct((replicas, rows, width), BF),
         ],
-        in_specs=[vmem] * 4 + [anywhere] * (5 + len(upstream)),
-        out_specs=[vmem] * 5 + [anywhere],
+        in_specs=[vmem] * 2 + [anywhere] * (7 * sections + 2),
+        out_specs=[vmem] * 5 + [anywhere] * 2,
         scratch_shapes=[
+            pltpu.VMEM((rows, cols), BF),
+            pltpu.VMEM((rows, width), BF),
+            pltpu.VMEM(gain_shape, F32),
+            pltpu.VMEM((replicas,) + gain_shape, F32),
+            pltpu.VMEM(gain_shape, F32),
+            pltpu.VMEM((shards,) + gain_shape, F32),
+            pltpu.VMEM(lefts[0].shape, BF),
+            pltpu.VMEM((2, replicas, sub_rows, every), BF),
+            pltpu.VMEM((max(1, all_pieces - 2 * (part // CHUNK)), every, CHUNK), BF),
+            pltpu.VMEM((replicas, sub_rows, cols + width), BF),
+            pltpu.VMEM((replicas + 1, sub_rows, cols + width), BF),
             pltpu.VMEM(down.shape, BF),
             pltpu.VMEM((2, every, width), BF),
             pltpu.VMEM((2, 2, every, part // 2), BF),
             pltpu.VMEM((every, part), BF),
-            pltpu.VMEM((left.shape[0], part), F32),
-            pltpu.VMEM((2, left.shape[0], part), BF),
-            pltpu.VMEM((replicas + 1,) + terms.shape[1:], BF),
-            pltpu.VMEM((shards,) + gains.shape, F32),
+            pltpu.VMEM((slice_rows, part), F32),
+            pltpu.VMEM((2, max(slice_rows, every), part), BF),
+            pltpu.SemaphoreType.DMA((4 + all_pieces - pieces,)),
             pltpu.SemaphoreType.DMA((4, 2)),
             pltpu.SemaphoreType.DMA((2, 4)),
             pltpu.SemaphoreType.DMA,
@@ -1481,8 +1507,8 @@
         compiler_params=pltpu.CompilerParams(
             collective_id=collective, has_side_effects=True, vmem_limit_bytes=VMEM_LIMIT
         ),
-        name="feed_grads",
-    )(left, hidden, terms, gains, *upstream, odd, even, early, gate_up, down)
+        name="weight_grads",
+    )(left_rows, hidden, *lefts, *projected, *gains, *upstream, *branch, *slices, *odd, gate_up, down)
 
 
 def turn_order(replicas):
@@ -1490,10 +1516,10 @@
 
 
 def prepare_kernel(sections, gate_up_hbm, *refs):
-    slices, normed_two = refs[:sections], refs[sections : 2 * sections]
+    slices, normed_two, odd = [refs[at * sections : (at + 1) * sections] for at in range(3)]
     (gathered_hbm, gate_up_all_hbm, hidden_hbm, left_rows_ref,
      normed_two_ref, weight_ref, block_ref, gate_up_ref, hidden_ref, turned_ref,
-     load_sems, store_sems, start_sems, send_sems, recv_sems) = refs[2 * sections :]
+     load_sems, store_sems, block_sems, start_sems, send_sems, recv_sems) = refs[3 * sections :]
     shard, beside, across, diagonal = slice_peers()
     peers = (across, diagonal, beside)
     replica, replicas = lax.axis_index("replica"), lax.axis_size("replica")
@@ -1523,11 +1549,31 @@
     def landing(turn, who):
         return gathered_hbm.at[turn, pl.ds(pl.multiple_of(who * rows, rows), rows)]
 
-    def over(turn):
-        return remote(landing(turn, shard), landing(turn, shard), 3 * turn, across)
-
-    def direct(turn):
-        return remote(landing(turn, shard), landing(turn, shard), 3 * turn + 1, beside)
+    def own_sources(turn):
+        if turn % 2:
+            return [source.at[lax.rem(replica + turn, replicas)] for source in odd]
+        return [landing(turn, shard)]
+
+    def over(turn, source=None):
+        return remote(landing(turn, shard) if source is None else source, landing(turn, shard), 3 * turn, across)
+
+    def direct(turn, source=None):
+        return remote(landing(turn, shard) if source is None else source, landing(turn, shard), 3 * turn + 1, beside)
+
+    def send_block(turn):
+        if turn % 2 == 0:
+            from_replica(turn).wait_recv()
+        copies = [(over(turn, source), direct(turn, source)) for source in own_sources(turn)]
+        for section, pair in enumerate(copies):
+            if len(copies) == 1:
+                for copy in pair:
+                    copy.start()
+            else:
+
+                @pl.when(lax.axis_index("section") == section)
+                def _(pair=pair):
+                    for copy in pair:
+                        copy.start()
 
     def relay(turn):
         return remote(landing(turn, across), landing(turn, across), 3 * turn + 2, beside)
@@ -1539,7 +1585,19 @@
         return pl.ds(pl.multiple_of(lax.rem(replica + turn, replicas) * every, every), every)
 
     def load_block(turn, slot):
-        return pltpu.make_async_copy(gathered_hbm.at[turn], block_ref.at[slot], store_sems.at[0, slot])
+        copies = []
+        for at, owner in enumerate(peers + (shard,)):
+            sources = own_sources(turn) if at == 3 else [landing(turn, owner)]
+            place = block_ref.at[slot, pl.ds(pl.multiple_of(owner * rows, rows), rows)]
+            copies.append([pltpu.make_async_copy(source, place, block_sems.at[slot, at]) for source in sources])
+        return copies
+
+    def start_block(turn, slot):
+        for copies in load_block(turn, slot):
+            if len(copies) == 1:
+                copies[0].start()
+            else:
+                start_own(copies)
 
     def store_block(turn, slot):
         return pltpu.make_async_copy(gate_up_ref.at[slot], gate_up_all_hbm.at[tokens(turn)], store_sems.at[1, slot])
@@ -1564,23 +1622,29 @@
     ]
     for copies in loads:
         start_own(copies)
-    slice_barrier(peers, range(1, replicas))
+    slice_barrier(peers, range(2, replicas, 2))
     order = turn_order(replicas)
     loads[0][0].wait()
-    if replicas > 1:
-        from_replica(order[1]).start()
+    evens = [turn for turn in order if turn and turn % 2 == 0]
+    for turn in evens[:1]:
+        from_replica(turn).start()
+    for turn in order[1:3]:
+        send_block(turn)
 
     for at, turn in enumerate(order):
         later = order[at + 1] if at + 1 < replicas else None
         slot = at % 2
-        if later is not None:
-            from_replica(later).wait_recv()
-            over(later).start()
-            direct(later).start()
-            if at + 2 < replicas:
-                from_replica(later).wait_send()
-                from_replica(order[at + 2]).start()
-        load_block(turn, slot).wait()
+        if at and at + 2 < replicas:
+            send_block(order[at + 2])
+            if order[at + 2] in evens:
+                place = evens.index(order[at + 2]) + 1
+                if place < len(evens):
+                    from_replica(evens[place]).start()
+        if at:
+            for copies in load_block(turn, slot):
+                copies[0].wait()
+        else:
+            loads[1][0].wait()
         if at > 1:
             store_block(order[at - 2], slot).wait()
 
@@ -1625,7 +1689,7 @@
         if later is not None:
             direct(later).wait_recv()
             relay(later).wait_recv()
-            load_block(later, 1 - slot).start()
+            start_block(later, 1 - slot)
 
     for at in range(max(0, replicas - 2), replicas):
         store_block(order[at], at % 2).wait()
@@ -1647,11 +1711,11 @@
             over(turn).wait_send()
             direct(turn).wait_send()
             relay(turn).wait_send()
-        if turn and turn == order[-1]:
+        if turn in evens:
             from_replica(turn).wait_send()
 
 
-def call_prepare(normed_two, gate_up_part, slices, collective):
+def call_prepare(normed_two, gate_up_part, slices, odd, collective):
     rows, width = normed_two[0].shape
     shards, replicas = lax.axis_size("shard"), lax.axis_size("replica")
     part = gate_up_part.shape[1] // 2
@@ -1668,7 +1732,7 @@
             jax.ShapeDtypeStruct((ff_rows, replicas * every), BF),
             jax.ShapeDtypeStruct((slice_rows, replicas * every), BF),
         ],
-        in_specs=[anywhere] * (1 + 2 * len(slices)),
+        in_specs=[anywhere] * (1 + 3 * len(slices)),
         out_specs=[anywhere] * 3 + [vmem],
         scratch_shapes=[
             pltpu.VMEM((rows, width), BF),
@@ -1679,6 +1743,7 @@
             pltpu.VMEM((2, shards, ff_rows, every), BF),
             pltpu.SemaphoreType.DMA((2, part // CHUNK)),
             pltpu.SemaphoreType.DMA((3, 2)),
+            pltpu.SemaphoreType.DMA((2, 4)),
             pltpu.SemaphoreType.DMA((1,)),
             pltpu.SemaphoreType.DMA((copies,)),
             pltpu.SemaphoreType.DMA((copies,)),
@@ -1687,67 +1752,8 @@
             collective_id=collective, has_side_effects=True, vmem_limit_bytes=VMEM_LIMIT
         ),
         name="prepare",
-    )(gate_up_part, *slices, *normed_two)
+    )(gate_up_part, *slices, *normed_two, *odd)
     return outs[1:]
-
-
-def gather_kernel(mine_ref, gathered_hbm, send_sems, recv_sems):
-    shard, beside, across, _ = slice_peers()
-    replicas = lax.axis_size("replica")
-    rows = mine_ref.shape[0]
-
-    def remote(owner, turn, at, device):
-        place = gathered_hbm.at[turn, pl.ds(pl.multiple_of(owner * rows, rows), rows)]
-        return pltpu.make_async_remote_copy(
-            place, place, send_sems.at[at], recv_sems.at[at], device_id={"shard": device}, device_id_type=MESH
-        )
-
-    own_rows = pl.ds(pl.multiple_of(shard * rows, rows), rows)
-    slice_barrier((beside, across), range(1, replicas, 2))
-    order = list(range(1, replicas, 2))
-    spread_copies = [
-        replica_copy(mine_ref, gathered_hbm.at[turn, own_rows], turn, send_sems, recv_sems, 3 * replicas)
-        for turn in order
-    ]
-    over = [remote(shard, turn, 3 * turn, across) for turn in order]
-    direct = [remote(shard, turn, 3 * turn + 1, beside) for turn in order]
-    relays = [remote(across, turn, 3 * turn + 2, beside) for turn in order]
-    spread_copies[0].start()
-    for at in range(len(order)):
-        spread_copies[at].wait_recv()
-        over[at].start()
-        direct[at].start()
-        spread_copies[at].wait_send()
-        if at + 1 < len(order):
-            spread_copies[at + 1].start()
-        if at:
-            over[at - 1].wait_recv()
-            relays[at - 1].start()
-    over[-1].wait_recv()
-    relays[-1].start()
-    for copy in direct + relays:
-        copy.wait_recv()
-    for copy in over + direct + relays:
-        copy.wait_send()
-
-
-def call_gather(section, mine, collective):
-    replicas, shards = lax.axis_size("replica"), lax.axis_size("shard")
-    rows, width = mine.shape
-    return pl.pallas_call(
-        gated(section, gather_kernel),
-        out_shape=jax.ShapeDtypeStruct((replicas, shards * rows, width), BF),
-        in_specs=[pl.BlockSpec(memory_space=pltpu.VMEM)],
-        out_specs=pl.BlockSpec(memory_space=pl.ANY),
-        scratch_shapes=[
-            pltpu.SemaphoreType.DMA((4 * replicas,)),
-            pltpu.SemaphoreType.DMA((4 * replicas,)),
-        ],
-        compiler_params=pltpu.CompilerParams(
-            collective_id=collective, has_side_effects=True, vmem_limit_bytes=VMEM_LIMIT
-        ),
-        name="gather",
-    )(mine)
 
 
 def on_device(
@@ -1763,7 +1769,6 @@
 ):
     sections = lax.axis_size("section")
     rows, width = tokens_in.shape
-    up_steps = [(at, at + 1) for at in range(sections - 1)]
     down_steps = [(at + 1, at) for at in range(sections - 1)]
 
     cosine, sine = rope_tables(positions)
@@ -1781,16 +1786,11 @@
         middle, normed_two, rotated, lefts = (
             call_attend_forward(section, state, *tables, qkv_full, out_full) if section else attend_first
         )
-        block_out, normed_two_slice, gate_up = call_feed(
+        block_out, normed_two_slice, gate_up, normed_two_odd, state_next = call_feed(
             section, False, (normed_two, middle, gate_up_part, down_part), 8 + section
         )
-        forward.append((state, middle, rotated, gate_up, normed_two_slice, normed_two, lefts, block_out))
-        if section + 1 < sections:
-            state = lax.ppermute(block_out, "section", up_steps)
-        if section + 2 == sections:
-            held, _ = lax.optimization_barrier((cotangent, block_out))
-            early = call_gather(sections - 1, held, 7)
-            state, early = lax.optimization_barrier((state, early))
+        forward.append((state, middle, rotated, gate_up, normed_two_slice, normed_two_odd, normed_two, lefts, block_out))
+        state = state_next
 
     def pick(values):
         chosen = values[-1]
@@ -1798,7 +1798,7 @@
             chosen = jnp.where(lax.axis_index("section") == section, values[section], chosen)
         return chosen
 
-    slices, normed_two, lefts, block_out = list(zip(*forward))[4:]
+    slices, normed_two_odd, normed_two, lefts, block_out = list(zip(*forward))[4:]
     block_out = pick(block_out)
     backward = []
     upstream = cotangent
@@ -1817,17 +1817,18 @@
         if section > 0:
             upstream = lax.ppermute(grad_low, "section", down_steps)
         if section == sections - 1:
-            gate_up_all, hidden_rows, left_rows = call_prepare(normed_two, gate_up_part, slices, 6)
+            gate_up_all, hidden_rows, left_rows = call_prepare(
+                normed_two, gate_up_part, slices, normed_two_odd, 6
+            )
             upstream, gate_up_all, left_rows, hidden_rows = lax.optimization_barrier(
                 (upstream, gate_up_all, left_rows, hidden_rows)
             )
 
     upstream, upstream_slice, odd, grad_in, grad_projected, gains, grad_branch = zip(*backward)
     grad_in = pick(grad_in)
-    terms, gains, even = call_attend_grads(lefts, grad_projected, gains, upstream, grad_branch, 4)
-    gate_up_grad, down_grad, qkv_grad, out_grad, gains, _ = call_feed_grads(
-        left_rows, hidden_rows, terms, gains, upstream_slice, pick(odd[:-1]), even, early, gate_up_all, down_part,
-        grad_projected[0].shape[1], 5,
+    gate_up_grad, down_grad, qkv_grad, out_grad, gains, _, _ = call_weight_grads(
+        left_rows, hidden_rows, lefts, grad_projected, gains, upstream, grad_branch, upstream_slice, odd,
+        gate_up_all, down_part, 5,
     )
     gate_up_grad = gate_up_grad.astype(F32)
     return (

time: 605 us -> 584 us (0.965)
  Pallas kernels: 570 us -> 553 us
    pallas_call x1, Pallas kernels: 99.9 us -> 87.6 us  [call_prepare(): pl.pallas_call(functools.partial(prepare_kernel, len(slices)), out_shape=...]
    pallas_call x7 -> x5, Pallas kernels: 263 us -> 259 us  [the longest x1 141 us: call_weight_grads(): pl.pallas_call(functools.partial(weight_grads_kernel, sections), out_shap...]
  transfers between devices with their start and end apart: 2 -> 1, of which waited for: 0 -> 0; matrix products, arithmetic and copies ran while one was open for 0% -> 0% of each run, Pallas kernels for 24% -> 15%
where the time goes in v6:
time: 584 us; the launch traced here: 575 us
  Pallas kernels  553 us (95%)
  other arithmetic  11.7 us (2%)
  local copies, waits for them, and re-layouts  7.25 us (1%)
    pallas_call x1, Pallas kernels, call_weights(): pl.pallas_call(weights_kernel, out_shape=[jax.ShapeDtypeStruct((shards *...  167 us
    pallas_call x1, Pallas kernels, call_weight_grads(): pl.pallas_call(functools.partial(weight_grads_kernel, sections), out_shap...  141 us
    pallas_call x4, Pallas kernels, call_feed(): pl.pallas_call(gated(section, functools.partial(feed_kernel, True, rows,...  118 us
    pallas_call x1, Pallas kernels, call_prepare(): pl.pallas_call(functools.partial(prepare_kernel, len(slices)), out_shape=...  87.6 us
    pallas_call x2, Pallas kernels, call_attend_backward(): pl.pallas_call(gated(section, functools.partial(attend_backward, section...  27.6 us
    pallas_call x1, Pallas kernels, call_attend_forward(): pl.pallas_call(gated(section, attend_forward), out_shape=out_shape, in_sp...  12.2 us
  transfers between devices with their start and end apart: 1, of which 0 were waited for; matrix products, arithmetic and copies ran while one was open for 0% of the time, Pallas kernels for 15%

profile of v6, /device:TPU:11, one launch (start us, length us, event | category | flops | bytes accessed | tf_op | source)
XLA Modules:
  0.0 574.6 jit_solution(4149525412928420135)
XLA Ops:
  0.7 0.7 convert_element_type.4
  1.3 1.4 fusion.2.allowed_ref.refs_5_.refs_9_
  2.7 0.3 fusion.3
  3.0 0.8 pad_maximum_fusion
  3.8 166.6 %weights.1 = (bf16[2048,3072]{1,0:T(8,128)(2,1)}, bf16[2048,2048]{1,0:T(8,128)(2,1)}, bf16[2048,4096]{1,0:T(8,128)(2,1)}, f32[128,2048]{1,0:T(8,128)}, bf16[128,...) custom-call(bf16[512,3072]{1,0:T(8,128)(2,1)} %bitcast.23, bf16[512,2048]{1,0:T(8,128)(2,1)} %bitcast.24, ...), custom_call_target="tpu_custom_call" | custom-call | tf_op jit(solution)/shard_map/weights/pallas_call | solution.py:936
  170.4 44.1 %feed_forward.2 = (bf16[128,2048]{1,0:T(8,128)(2,1)}, bf16[512,2048]{1,0:T(8,128)(2,1)}, bf16[512,4096]{1,0:T(8,128)(2,1)}, bf16[4,128,2048]{2,1,0:T(8,128)(2,1)}, bf16[128,2048]{1,0:T(8,128)(2,1)}) custom-call(bf16[128,2048]{1,0:T(8,128)(2,1)} %get-tuple-element.75.refs_0_.refs_2_, f32[128,2048]{1,0:T(8,128)} %get-tuple-element.59.refs_1_.refs_2_, ...), custom_call_target="tpu_custom_call" | custom-call | tf_op jit(solution)/shard_map/feed_forward/pallas_call | solution.py:738
  214.5 12.2 %attend_forward.1 = (f32[128,2048]{1,0:T(8,128)}, bf16[128,2048]{1,0:T(8,128)(2,1)}, bf16[128,3072]{1,0:T(8,128)(2,1)}, bf16[2,2048,128]{2,1,0:T(8,128)(2,1)}) custom-call(bf16[128,2048]{1,0:T(8,128)(2,1)} %get-tuple-element.62.refs_0_.refs_3_, f32[1,2048]{1,0:T(1,128)} %refs_5_.3, f32[1,2048]{1,0:T(1,128)} %refs_6_.3, ...), custom_call_target="tpu_custom_call" | custom-call | tf_op jit(solution)/shard_map/attend_forward/pallas_call | solution.py:316
  226.7 33.4 %feed_forward.3 = (bf16[128,2048]{1,0:T(8,128)(2,1)}, bf16[512,2048]{1,0:T(8,128)(2,1)}, bf16[512,4096]{1,0:T(8,128)(2,1)}, bf16[4,128,2048]{2,1,0:T(8,128)(2,1)}, bf16[128,2048]{1,0:T(8,128)(2,1)}) custom-call(bf16[128,2048]{1,0:T(8,128)(2,1)} %get-tuple-element.76.refs_0_.refs_3_, f32[128,2048]{1,0:T(8,128)} %get-tuple-element.66.refs_1_.refs_2_, ...), custom_call_target="tpu_custom_call" | custom-call | tf_op jit(solution)/shard_map/feed_forward/pallas_call | solution.py:738
  260.2 38.2 %feed_backward.2 = (f32[128,2048]{1,0:T(8,128)}, bf16[512,2048]{1,0:T(8,128)(2,1)}, bf16[4,128,2048]{2,1,0:T(8,128)(2,1)}) custom-call(bf16[128,2048]{1,0:T(8,128)(2,1)} %refs_7_.1, bf16[512,4096]{1,0:T(8,128)(2,1)} %get-tuple-element.68.refs_1_, bf16[2048,2048]{1,0:T(8,128)(2,1)} %bitcast.18, bf16[2048,4096]{1,0:T(8,128)(2,1)} %get-tuple-element.60.refs_2_.refs_3_.gate_up_hbm), custom_call_target="tpu_custom_call" | custom-call | tf_op jit(solution)/shard_map/feed_backward/pallas_call | solution.py:738
  298.4 23.5 %attend_backward.2 = (f32[128,2048]{1,0:T(8,128)}, bf16[128,2048]{1,0:T(8,128)(2,1)}, bf16[128,3072]{1,0:T(8,128)(2,1)}, f32[2,2048]{1,0:T(2,128)}, bf16[4,512,512]{2,1,0:T(8,128)(2,1)}) custom-call(f32[128,2048]{1,0:T(8,128)} %get-tuple-element.69.refs_0_, bf16[128,2048]{1,0:T(8,128)(2,1)} %refs_7_.1, f32[128,2048]{1,0:T(8,128)} %get-tuple-element.66.refs_1_.refs_2_, ...), custom_call_target="tpu_custom_call" | custom-call | tf_op jit(solution)/shard_map/attend_backward/pallas_call | solution.py:333
  321.9 1.5 collective-permute-start
  323.5 0.0 copy-start.6
  323.5 0.0 copy-start.7
  323.5 87.6 %prepare.1 = (bf16[4,512,2048]{2,1,0:T(8,128)(2,1)}, bf16[2048,4096]{1,0:T(8,128)(2,1)}, bf16[512,2048]{1,0:T(8,128)(2,1)}, bf16[512,2048]{1,0:T(8,128)(2,1)}) custom-call(bf16[2048,4096]{1,0:T(8,128)(2,1)} %get-tuple-element.60.refs_2_.refs_3_.gate_up_hbm, bf16[512,2048]{1,0:T(8,128)(2,1)} %get-tuple-element.73.refs_0_, ...), custom_call_target="tpu_custom_call" | custom-call | tf_op jit(solution)/shard_map/prepare/pallas_call | solution.py:1727
  411.0 0.0 copy-done.6
  411.1 0.0 copy-done.7
  411.1 0.9 select_bitcast_fusion.1
  411.9 0.0 collective-permute-done.refs_0_.refs_1_.refs_6_
  411.9 0.0 copy-start
  411.9 0.8 copy-done
  412.7 2.7 feed_backward.3
  415.5 4.1 attend_backward.3
  419.6 140.5 %weight_grads.1 = (bf16[128,16384]{1,0:T(8,128)(2,1)}, f32[512,2048]{1,0:T(8,128)}, f32[128,3072]{1,0:T(8,128)}, f32[128,2048]{1,0:T(8,128)}, f32[2,2048]{1,0:T(...) custom-call(bf16[512,2048]{1,0:T(8,128)(2,1)} %get-tuple-element.88.left_rows_ref, ...), custom_call_target="tpu_custom_call" | custom-call | tf_op jit(solution)/shard_map/weight_grads/pallas_call | solution.py:1469
  560.1 1.4 fusion.4
  561.5 0.0 copy-start.3
  561.5 0.0 copy-start.4
  561.5 6.6 %bitcast_convert_fusion = f32[1,128,16384]{2,1,0:T(8,128)} fusion(bf16[128,16384]{1,0:T(8,128)(2,1)} %get-tuple-element.106), kind=kLoop, calls=%fused_computation | loop fusion | flops 2097152 | bytes 12582912 | tf_op jit(solution)/shard_map/broadcast_in_dim | solution.py:1841
  568.1 0.0 copy-start.2
  568.1 0.0 copy-done.3
  568.1 0.0 copy-done.4
  568.1 0.0 copy-start.5
  568.1 1.1 select_bitcast_fusion
  569.2 0.0 copy-start.1
  569.2 0.7 copy-done.2
  569.9 1.1 copy.21
  571.0 0.0 copy-done.5
  571.0 1.0 copy.22
  572.0 0.2 copy-done.1
  572.2 2.0 copy.23
  (2 shorter events, 0.0 us)
Async XLA Ops:
  321.9 90.0 %collective-permute-start = (bf16[128,2048]{1,0:T(8,128)(2,1)}, bf16[128,2048]{1,0:T(8,128)(2,1)S(1)}, u32[]{:S(2)}, u32[]{:S(2)}) collective-permute-start(bf16[128,2048]{1,0:T(8,128)(2,1)} %get-tuple-element.72), channel_id=1, source_target_pairs={{16,0},{17,1},{18,2},{19,3},{20,4},{21,5},{22,6},{23,7},{24,8},{25... | collective-permute-start | bytes 1572872 | tf_op jit(solution)/shard_map/ppermute | solution.py:1818
  323.5 87.6 %copy-start.6 = (bf16[128,2048]{1,0:T(8,128)(2,1)S(1)}, bf16[128,2048]{1,0:T(8,128)(2,1)}, u32[]{:S(2)}) copy-start(bf16[128,2048]{1,0:T(8,128)(2,1)} %get-tuple-element.61) | copy-start | bytes 1572868
  323.5 87.6 %copy-start.7 = (bf16[128,2048]{1,0:T(8,128)(2,1)S(1)}, bf16[128,2048]{1,0:T(8,128)(2,1)}, u32[]{:S(2)}) copy-start(bf16[128,2048]{1,0:T(8,128)(2,1)} %get-tuple-element.67) | copy-start | bytes 1572868
  411.9 0.8 copy-start
  561.5 6.6 %copy-start.3 = (f32[128,2048]{1,0:T(8,128)S(1)}, f32[128,2048]{1,0:T(8,128)}, u32[]{:S(2)}) copy-start(f32[128,2048]{1,0:T(8,128)} %get-tuple-element.87) | copy-start | bytes 3145732
  561.5 6.6 %copy-start.4 = (f32[128,2048]{1,0:T(8,128)S(1)}, f32[128,2048]{1,0:T(8,128)}, u32[]{:S(2)}) copy-start(f32[128,2048]{1,0:T(8,128)} %get-tuple-element.86) | copy-start | bytes 3145732
  568.1 1.8 copy-start.2
  568.1 2.9 copy-start.5
  569.2 3.0 copy-start.1

commit v7 on v6

--- a/solution.py
+++ b/solution.py
@@ -396,7 +396,7 @@
 CHUNK = 512
 
 
-def feed_kernel(backward, rows, target, *refs):
+def feed_kernel(backward, rows, target, wide, *refs):
     if backward:
         (mine_ref, gate_up_hbm, first_hbm, second_hbm, result_ref, all_hbm, others_hbm,
          mid_ref, all_ref, gate_up_ref, first_ref, second_ref, part_ref, take_ref, sent_ref, land_ref, own_ref,
@@ -463,7 +463,7 @@
     def owned(owner, part):
         return all_ref.at[place_of(owner, part)]
 
-    turns = range(1, lax.axis_size("replica"), 2)
+    turns = spread_turns(wide)
     base = 6 + (2 * parts + 1) * spans
     slice_barrier((beside, across), turns, 0 if target is None else 1)
 
@@ -636,10 +636,11 @@
         load_extra[0].wait()
     for at in range(spans):
         give_own(at).wait_recv()
-        cols = slice(at * span_cols, (at + 1) * span_cols)
-        for part in range(parts):
+    for part in range(parts):
+        place = slice(part * piece, (part + 1) * piece)
+        for at in range(spans):
             cross(part, at).wait_recv()
-            place = slice(part * piece, (part + 1) * piece)
+            cols = slice(at * span_cols, (at + 1) * span_cols)
             total = (
                 own_ref[at, core, place].astype(F32)
                 + own_take_ref[at, place].astype(F32)
@@ -674,10 +675,57 @@
     )
 
 
-def feed_forward_kernel(section, last, parts, spans, rows, *refs):
+def spread_turns(wide):
+    return range(2, lax.axis_size("replica")) if wide else range(1, lax.axis_size("replica"), 2)
+
+
+def gather_turns(mine_hbm, gathered_hbm, send_sems, recv_sems):
+    shard, beside, across, _ = slice_peers()
+    replicas = lax.axis_size("replica")
+    rows = mine_hbm.shape[0]
+
+    def remote(owner, turn, at, device):
+        place = gathered_hbm.at[turn, pl.ds(pl.multiple_of(owner * rows, rows), rows)]
+        return pltpu.make_async_remote_copy(
+            place, place, send_sems.at[at], recv_sems.at[at], device_id={"shard": device}, device_id_type=MESH
+        )
+
+    own_rows = pl.ds(pl.multiple_of(shard * rows, rows), rows)
+    order = [1]
+    spread_copies = [
+        replica_copy(mine_hbm, gathered_hbm.at[turn, own_rows], turn, send_sems, recv_sems, 3 * replicas)
+        for turn in order
+    ]
+    over = [remote(shard, turn, 3 * turn, across) for turn in order]
+    direct = [remote(shard, turn, 3 * turn + 1, beside) for turn in order]
+    relays = [remote(across, turn, 3 * turn + 2, beside) for turn in order]
+    spread_copies[0].start()
+    for at in range(len(order)):
+        spread_copies[at].wait_recv()
+        over[at].start()
+        direct[at].start()
+        spread_copies[at].wait_send()
+        if at + 1 < len(order):
+            spread_copies[at + 1].start()
+        if at:
+            over[at - 1].wait_recv()
+            relays[at - 1].start()
+    over[-1].wait_recv()
+    relays[-1].start()
+    for copy in direct + relays:
+        copy.wait_recv()
+    for copy in over + direct + relays:
+        copy.wait_send()
+
+
+def feed_forward_kernel(section, last, gathers, parts, spans, rows, *refs):
+    if gathers:
+        cotangent_hbm, early_hbm, gather_send_sems, gather_recv_sems = refs[4], refs[10], refs[-4], refs[-3]
+        refs = refs[:4] + refs[5:10] + refs[11:-4] + refs[-2:]
+
     @pl.when(lax.axis_index("section") == section)
     def _():
-        feed_kernel(False, rows, None if last else section + 1, *refs)
+        feed_kernel(False, rows, None if last else section + 1, False, *refs)
 
     if not last:
 
@@ -685,6 +733,10 @@
         def _():
             barrier = pltpu.get_barrier_semaphore()
             pl.semaphore_signal(barrier, inc=1, device_id={"section": section}, device_id_type=MESH)
+            if gathers:
+                _, beside, across, _ = slice_peers()
+                slice_barrier((beside, across), (1,))
+                gather_turns(cotangent_hbm, early_hbm, gather_send_sems, gather_recv_sems)
             next_hbm, send_sems, recv_sems = refs[8], refs[-2], refs[-1]
             base = 6 + (2 * parts + 1) * spans + lax.axis_size("replica")
             high, wide = rows // parts, next_hbm.shape[1] // spans
@@ -694,7 +746,7 @@
                     section_copy(place, place, base + part * spans + at, send_sems, recv_sems, section).wait_recv()
 
 
-def call_feed(section, backward, operands, collective):
+def call_feed(section, backward, operands, collective, cotangent=None):
     first, second = operands[-2], operands[-1]
     rows, width = operands[0].shape
     shards, replicas = lax.axis_size("shard"), lax.axis_size("replica")
@@ -732,15 +784,20 @@
         pltpu.SemaphoreType.DMA((3, max(ff // CHUNK, spans))),
         pltpu.SemaphoreType.DMA((4 + 2 * shards,)),
         pltpu.SemaphoreType.DMA((2 * shards,)),
+        *([pltpu.SemaphoreType.DMA((4 * replicas,))] * (0 if cotangent is None else 2)),
         pltpu.SemaphoreType.DMA((copies,)),
         pltpu.SemaphoreType.DMA((copies,)),
     ]
+    if cotangent is not None:
+        operands += (cotangent,)
+        out_shape.append(jax.ShapeDtypeStruct((replicas, every, width), BF))
     return pl.pallas_call(
-        gated(section, functools.partial(feed_kernel, True, rows, None))
+        gated(section, functools.partial(feed_kernel, True, rows, None, section == lax.axis_size("section") - 1))
         if backward
-        else functools.partial(feed_forward_kernel, section, section == lax.axis_size("section") - 1, parts, spans, rows),
+        else functools.partial(feed_forward_kernel, section, section == lax.axis_size("section") - 1,
+            cotangent is not None, parts, spans, rows),
         out_shape=out_shape,
-        in_specs=[vmem] + [anywhere] * 3,
+        in_specs=[vmem] + [anywhere] * (len(operands) - 1),
         out_specs=[vmem] + [anywhere] * (len(out_shape) - 1),
         scratch_shapes=scratch,
         compiler_params=pltpu.CompilerParams(
@@ -806,17 +863,17 @@
 
             own = source.at[span(mine * half + offset, count)]
             pieces.append((own, place, across, True))
-    for offset in range(0, half, 128):
+    for offset in range(0, half, 64):
         for side in range(2):
             for device in (across, diagonal):
 
                 def place(owner, part_of, offset=offset, side=side):
                     return gate_up_part.at[
-                        span(owner["shard"] * rows + part_of * half + offset, 128), pl.ds(side * part, part)
+                        span(owner["shard"] * rows + part_of * half + offset, 64), pl.ds(side * part, part)
                     ]
 
                 own = gate_up_ref.at[
-                    span(mine * half + offset, 128), span(side * ff + device["shard"] * part, part)
+                    span(mine * half + offset, 64), span(side * ff + device["shard"] * part, part)
                 ]
                 pieces.append((own, place, device, False))
     count = len(pieces)
@@ -860,7 +917,7 @@
         copy.start()
         started.append(copy)
 
-    ahead = 3
+    ahead = 4
     for copy in over[:ahead]:
         start(copy)
     for copy in direct:
@@ -915,8 +972,8 @@
             work([load_out])
             ready += second
         if at >= qkv_last + 2:
-            work(ready[:3])
-            ready = ready[3:]
+            work(ready[:2])
+            ready = ready[2:]
     work(ready)
     for copy in direct[2:]:
         copy.wait_recv()
@@ -929,7 +986,7 @@
 def call_weights(qkv_weight, out_weight, gate_up_weight, operands, collective):
     shards = lax.axis_size("shard")
     rows = qkv_weight.shape[0]
-    count = 2 * (rows // 128) + rows // 64
+    count = 2 * (rows // 128) + 4 * (rows // 128)
     out_shape, scratch = attend_shapes(*operands[0].shape, qkv_weight.shape[1])
     vmem = pl.BlockSpec(memory_space=pltpu.VMEM)
     anywhere = pl.BlockSpec(memory_space=pl.ANY)
@@ -973,7 +1030,7 @@
 
 def weight_grads_kernel(sections, left_rows_ref, hidden_ref, *refs):
     sources = [refs[at * sections : (at + 1) * sections] for at in range(7)]
-    (gate_up_hbm, down_hbm,
+    (early_hbm, gate_up_hbm, down_hbm,
      gate_up_grad_ref, down_grad_ref, qkv_grad_ref, out_grad_ref, gain_sum_ref, gathered_hbm, even_hbm,
      projected_ref, upstream_ref, gains_ref, gains_land_ref, gain_part_ref, gains_last_ref, lefts_ref, left_ref,
      extra_ref, terms_ref, chain_ref, down_ref, block_ref, gate_up_ref, mid_ref, sum_ref, stage_ref,
@@ -981,6 +1038,8 @@
     shard, beside, across, diagonal = slice_peers()
     peers = (across, diagonal, beside)
     replica, replicas = lax.axis_index("replica"), lax.axis_size("replica")
+    early = lax.axis_index("section") == lax.axis_size("section") - 1
+    late = lax.axis_index("section") < lax.axis_size("section") - 1
     here = [lax.axis_index("section") == section for section in range(sections)]
     rows, cols = projected_ref.shape
     every, width = sources[5][0].shape
@@ -998,7 +1057,7 @@
     gain_base = spread_base + replicas
     left_base = gain_base + replicas
     chain_base = left_base + kinds * groups * 3
-    last_base = chain_base + 2 * replicas
+    last_base = chain_base + 4 * replicas
     grad_base = last_base + 3
 
     def remote(source, target, at, device):
@@ -1060,17 +1119,31 @@
         slot = lax.rem(turn, 2)
         copies = []
         for at, owner in enumerate(peers + (shard,)):
-            own = gathered_hbm.at[turn, owned(owner)] if source is None or at < 3 else source.at[block_at(turn)]
+            if source is early_hbm:
+                own = early_hbm.at[turn, owned(owner)]
+            else:
+                own = gathered_hbm.at[turn, owned(owner)] if source is None or at < 3 else source.at[block_at(turn)]
             copies.append(pltpu.make_async_copy(own, block_ref.at[slot, owned(owner)], block_sems.at[slot, at]))
         return copies
 
+    def own_cases(turn):
+        cases = [(late & (turn > 0) & (turn % 2 == 0), even_hbm), (early & (turn > 1), sources[6][-1])]
+        for section in range(sections - 1):
+            cases.append((here[section] & (turn % 2 == 1), sources[6][section]))
+        return cases
+
     def load_block(turn):
-        for copy in block_copies(turn, None)[:3]:
-            copy.start()
-        cases = [(turn == 0, None), ((turn > 0) & (turn % 2 == 0), even_hbm)]
-        for section in range(sections):
-            odd_case = here[section] & (turn % 2 == 1)
-            cases.append((odd_case, sources[6][section]))
+        @pl.when(early & (turn == 1))
+        def _():
+            for copy in block_copies(turn, early_hbm):
+                copy.start()
+
+        @pl.when(late | (turn != 1))
+        def _():
+            for copy in block_copies(turn, None)[:3]:
+                copy.start()
+
+        cases = [(turn == 0, None)] + own_cases(turn)
         for case, source in cases:
 
             @pl.when(case)
@@ -1094,10 +1167,7 @@
         return remote(landing(turn, across), landing(turn, across), 3 * turn + 2, beside)
 
     def send_block(turn):
-        cases = [(turn % 2 == 0, even_hbm)]
-        for section in range(sections):
-            odd_case = here[section] & (turn % 2 == 1)
-            cases.append((odd_case, sources[6][section]))
+        cases = own_cases(turn)
         for case, source in cases:
 
             @pl.when(case)
@@ -1108,54 +1178,79 @@
     def chain_slot(block, at):
         return replicas - (replicas - block) * ((at - block + replicas - 1) // replicas)
 
-    def chain_up(block):
+    spans = ((cols, width), (0, cols))
+
+    def chain_at(phase, slot):
+        return chain_ref.at[slot, :, pl.ds(*spans[phase])]
+
+    def chain_up(phase, block):
+        at = chain_base + phase * 2 * replicas + block
         return pltpu.make_async_remote_copy(
-            chain_ref.at[block], chain_ref.at[block], send_sems.at[chain_base + block],
-            recv_sems.at[chain_base + block], device_id={"replica": replica + 1}, device_id_type=MESH,
-        )
-
-    def chain_down(block):
+            chain_at(phase, block), chain_at(phase, block), send_sems.at[at], recv_sems.at[at],
+            device_id={"replica": replica + 1}, device_id_type=MESH,
+        )
+
+    def chain_down(phase, block):
+        at = chain_base + phase * 2 * replicas + replicas + block
         return pltpu.make_async_remote_copy(
-            chain_ref.at[block], chain_ref.at[chain_slot(block, replica - 1)],
-            send_sems.at[chain_base + replicas + block],
-            recv_sems.at[chain_base + replicas + block], device_id={"replica": replica - 1}, device_id_type=MESH,
-        )
-
-    def add_terms(block):
+            chain_at(phase, block), chain_at(phase, chain_slot(block, replica - 1)), send_sems.at[at], recv_sems.at[at],
+            device_id={"replica": replica - 1}, device_id_type=MESH,
+        )
+
+    def chain_chunks(phase, body):
+        first, count = spans[phase]
+        repeat(first // CHUNK, (first + count) // CHUNK, lambda at: body(pl.ds(pl.multiple_of(at * CHUNK, CHUNK), CHUNK)))
+
+    def add_terms(phase, block):
         def add(place):
             total = chain_ref[block, :, place].astype(F32) + terms_ref[block, :, place].astype(F32)
             chain_ref[block, :, place] = total.astype(BF)
 
-        by_chunk(all_pieces, add)
-
-    def take_terms(block):
-        def take(place):
-            chain_ref[block, :, place] = terms_ref[block, :, place]
-
-        by_chunk(all_pieces, take)
-
-    def chain_step(step):
+        chain_chunks(phase, add)
+
+    def chain_begin(phase):
+        def take_terms(block):
+            def take(place):
+                chain_ref[block, :, place] = terms_ref[block, :, place]
+
+            chain_chunks(phase, take)
+
+        for block in reversed(range(1, replicas)):
+
+            @pl.when(replica == 0)
+            def _(block=block):
+                take_terms(block)
+                chain_up(phase, block).start()
+
+        for block in range(replicas - 1):
+
+            @pl.when(replica == replicas - 1)
+            def _(block=block):
+                take_terms(block)
+                chain_down(phase, block).start()
+
+    def chain_step(phase, step):
         high = replicas - 1 - step + replica
 
         @pl.when((replica > 0) & (step >= replica))
         def _():
-            chain_up(high).wait_recv()
+            chain_up(phase, high).wait_recv()
 
             @pl.when(step < replicas - 1)
             def _():
-                add_terms(high)
-                chain_up(high).start()
+                add_terms(phase, high)
+                chain_up(phase, high).start()
 
         low = step - (replicas - 1 - replica)
 
         @pl.when((replica < replicas - 1) & (step >= replicas - 1 - replica))
         def _():
-            chain_down(low).wait_recv()
+            chain_down(phase, low).wait_recv()
 
             @pl.when(step < replicas - 1)
             def _():
-                add_terms(low)
-                chain_down(low).start()
+                add_terms(phase, low)
+                chain_down(phase, low).start()
 
     def gain_copy(peer):
         return remote(gain_part_ref, gains_last_ref.at[shard], last_base + peer, peers[peer])
@@ -1228,10 +1323,13 @@
         lax.fori_loop(0, 2 * steps, sums, 0)
 
     def first_pass(turn, carry):
-        block_over(turn, even_hbm).wait_recv()
-        block_relay(turn).start()
-        block_direct(turn, even_hbm).wait_recv()
-        block_relay(turn).wait_recv()
+        @pl.when(late | (turn != 1))
+        def _():
+            block_over(turn, even_hbm).wait_recv()
+            block_relay(turn).start()
+            block_direct(turn, even_hbm).wait_recv()
+            block_relay(turn).wait_recv()
+
         load_block(turn)
 
         @pl.when(turn + 2 < replicas)
@@ -1284,8 +1382,14 @@
     loads[2][0].wait()
     gains_land_ref[replica] = gains_ref[...]
     loads[3][0].wait()
-    for copy in gain_copies + spread_copies:
+    for copy in gain_copies:
         copy.start()
+
+    @pl.when(late)
+    def _():
+        for copy in spread_copies:
+            copy.start()
+
     for kind in range(kinds):
         for group in range(groups):
             left_ref[kind, group, :, owned(shard)] = lefts_ref[kind, group, shard]
@@ -1293,9 +1397,6 @@
     keep_own = pltpu.make_async_copy(block_ref.at[0], gathered_hbm.at[0], keep_sem)
     keep_own.start()
     clear_sum()
-    load_down.wait()
-    compute(0, 0)
-    keep_own.wait()
 
     def product(piece, kind, source):
         left = jnp.concatenate([left_ref[kind, group] for group in range(groups)], 0)
@@ -1308,56 +1409,79 @@
         place = pl.ds(pl.multiple_of(piece % staged * CHUNK, CHUNK), CHUNK)
         product(piece, kind, stage_ref[piece // staged, pl.ds(0, every), place])
 
-    for place in lefts:
+    for place in lefts[: len(lefts) // kinds]:
         hand_left(*place).wait_recv()
     for copies in load_branch:
         copies[0].wait()
     repeat(pieces, min(all_pieces, 2 * staged), lambda piece: staged_product(piece, 1))
     repeat(2 * staged, all_pieces, lambda piece: product(piece, 1, extra_ref[piece - 2 * staged]))
+    chain_begin(0)
+    load_down.wait()
+    compute(0, 0)
+    keep_own.wait()
+    if replicas > 2:
+
+        @pl.when(early)
+        def _():
+            load_block(1)
+            wait_block(1)
+            compute(0, 1)
+
+    for place in lefts[len(lefts) // kinds :]:
+        hand_left(*place).wait_recv()
     for piece in range(pieces):
         over[piece].wait_recv()
         relays[piece].start()
+        if piece == pieces // 2:
+            chain_step(0, 1)
     for copy in over:
         copy.wait_send()
-    for copy in spread_copies:
-        copy.wait()
+
+    @pl.when(late)
+    def _():
+        for copy in spread_copies:
+            copy.wait()
+
     for turn in range(1, min(3, replicas)):
         send_block(turn)
     for copy in direct + relays:
         copy.wait()
     repeat(0, pieces, lambda piece: staged_product(piece, 0))
-    for block in reversed(range(1, replicas)):
-
-        @pl.when(replica == 0)
-        def _(block=block):
-            take_terms(block)
-            chain_up(block).start()
-
-    for block in range(replicas - 1):
-
-        @pl.when(replica == replicas - 1)
-        def _(block=block):
-            take_terms(block)
-            chain_down(block).start()
-
+    chain_begin(1)
+    if replicas > 2:
+        chain_step(0, 2)
     for copy in gain_copies:
         copy.wait()
     gain_part_ref[...] = jnp.sum(gains_land_ref[...], 0)
     gains_last_ref[shard] = gain_part_ref[...]
     for peer in range(3):
         gain_copy(peer).start()
-    lax.fori_loop(1, replicas - 1, first_pass, 0)
-    chain_step(1)
-    first_pass(replicas - 1, 0)
+    if replicas > 2:
+
+        @pl.when(late)
+        def _():
+            first_pass(1, 0)
+
+        if replicas > 3:
+
+            @pl.when(early)
+            def _():
+                send_block(3)
+
+    lax.fori_loop(2, replicas, first_pass, 0)
     for side in range(2):
         load_gate_up(1, 0, side).start()
     load_block(0)
     clear_sum()
+    for step in range(3, replicas):
+        chain_step(0, step)
+    chain_step(1, 1)
     wait_block(0)
-    lax.fori_loop(0, replicas, second_pass, 0)
+    lax.fori_loop(0, 2, second_pass, 0)
+    if replicas > 2:
+        chain_step(1, 2)
+    lax.fori_loop(2, replicas, second_pass, 0)
     load_block(0)
-    if replicas > 2:
-        chain_step(2)
     wait_block(0)
 
     def clear_down(place):
@@ -1406,7 +1530,7 @@
 
         lax.fori_loop(0, 2 * steps, store_own, 0)
     for step in range(3, replicas):
-        chain_step(step)
+        chain_step(1, step)
 
     def sum_up(grad_ref, first):
         def add(place):
@@ -1436,24 +1560,29 @@
     for place in lefts:
         hand_left(*place).wait_send()
     for turn in range(1, replicas):
-        block_over(turn, even_hbm).wait_send()
-        block_direct(turn, even_hbm).wait_send()
-        block_relay(turn).wait_send()
-
-    for block in range(1, replicas):
-
-        @pl.when(replica < block)
-        def _(block=block):
-            chain_up(block).wait_send()
-
-    for block in range(replicas - 1):
-
-        @pl.when(replica > block)
-        def _(block=block):
-            chain_down(block).wait_send()
-
-
-def call_weight_grads(left_rows, hidden, lefts, projected, gains, upstream, branch, slices, odd, gate_up, down,
+
+        @pl.when(late | (turn != 1))
+        def _(turn=turn):
+            block_over(turn, even_hbm).wait_send()
+            block_direct(turn, even_hbm).wait_send()
+            block_relay(turn).wait_send()
+
+
+    for phase in range(2):
+        for block in range(1, replicas):
+
+            @pl.when(replica < block)
+            def _(phase=phase, block=block):
+                chain_up(phase, block).wait_send()
+
+        for block in range(replicas - 1):
+
+            @pl.when(replica > block)
+            def _(phase=phase, block=block):
+                chain_down(phase, block).wait_send()
+
+
+def call_weight_grads(left_rows, hidden, lefts, projected, gains, upstream, branch, slices, odd, early, gate_up, down,
                       collective):
     replicas, shards, sections = lax.axis_size("replica"), lax.axis_size("shard"), len(projected)
     rows, cols = projected[0].shape
@@ -1463,7 +1592,7 @@
     sub_rows = slice_rows // shards
     lefts = [values.reshape(2, replicas, shards, sub_rows, rows) for values in lefts]
     pieces, all_pieces = cols // CHUNK, (cols + width) // CHUNK
-    copies = 3 * replicas + 3 * pieces + 2 * replicas + 6 * replicas + 2 * replicas + 3 + 3 * 2 * (part // CHUNK)
+    copies = 3 * replicas + 3 * pieces + 2 * replicas + 6 * replicas + 4 * replicas + 3 + 3 * 2 * (part // CHUNK)
     vmem, anywhere = pl.BlockSpec(memory_space=pltpu.VMEM), pl.BlockSpec(memory_space=pl.ANY)
     gain_shape = gains[0].shape
     return pl.pallas_call(
@@ -1477,7 +1606,7 @@
             jax.ShapeDtypeStruct((replicas, every, width), BF),
             jax.ShapeDtypeStruct((replicas, rows, width), BF),
         ],
-        in_specs=[vmem] * 2 + [anywhere] * (7 * sections + 2),
+        in_specs=[vmem] * 2 + [anywhere] * (7 * sections + 3),
         out_specs=[vmem] * 5 + [anywhere] * 2,
         scratch_shapes=[
             pltpu.VMEM((rows, cols), BF),
@@ -1508,7 +1637,7 @@
             collective_id=collective, has_side_effects=True, vmem_limit_bytes=VMEM_LIMIT
         ),
         name="weight_grads",
-    )(left_rows, hidden, *lefts, *projected, *gains, *upstream, *branch, *slices, *odd, gate_up, down)
+    )(left_rows, hidden, *lefts, *projected, *gains, *upstream, *branch, *slices, *odd, early, gate_up, down)
 
 
 def turn_order(replicas):
@@ -1782,13 +1911,16 @@
 
     forward = []
     state = tokens_in
+    early = None
     for section in range(sections):
         middle, normed_two, rotated, lefts = (
             call_attend_forward(section, state, *tables, qkv_full, out_full) if section else attend_first
         )
-        block_out, normed_two_slice, gate_up, normed_two_odd, state_next = call_feed(
-            section, False, (normed_two, middle, gate_up_part, down_part), 8 + section
-        )
+        block_out, normed_two_slice, gate_up, normed_two_odd, state_next, *gathered = call_feed(
+            section, False, (normed_two, middle, gate_up_part, down_part), 8 + section,
+            cotangent if section + 2 == sections else None,
+        )
+        early = gathered[0] if gathered else early
         forward.append((state, middle, rotated, gate_up, normed_two_slice, normed_two_odd, normed_two, lefts, block_out))
         state = state_next
 
@@ -1828,7 +1960,7 @@
     grad_in = pick(grad_in)
     gate_up_grad, down_grad, qkv_grad, out_grad, gains, _, _ = call_weight_grads(
         left_rows, hidden_rows, lefts, grad_projected, gains, upstream, grad_branch, upstream_slice, odd,
-        gate_up_all, down_part, 5,
+        early, gate_up_all, down_part, 5,
     )
     gate_up_grad = gate_up_grad.astype(F32)
     return (

time: 584 us -> 571 us (0.978)
  Pallas kernels: 553 us -> 541 us
    pallas_call x1, Pallas kernels: 141 us -> 129 us  [call_weight_grads(): pl.pallas_call(functools.partial(weight_grads_kernel, sections), out_shap...]
  transfers between devices with their start and end apart: 1 -> 1, of which waited for: 0 -> 0; matrix products, arithmetic and copies ran while one was open for 0% -> 0% of each run, Pallas kernels for 15% -> 16%
where the time goes in v7:
time: 571 us; the launch traced here: 562 us
  Pallas kernels  541 us (95%)
  other arithmetic  11.7 us (2%)
  local copies, waits for them, and re-layouts  7.06 us (1%)
    pallas_call x1, Pallas kernels, call_weights(): pl.pallas_call(weights_kernel, out_shape=[jax.ShapeDtypeStruct((shards *...  164 us
    pallas_call x1, Pallas kernels, call_weight_grads(): pl.pallas_call(functools.partial(weight_grads_kernel, sections), out_shap...  129 us
    pallas_call x4, Pallas kernels, call_feed(): pl.pallas_call(gated(section, functools.partial(feed_kernel, True, rows,...  121 us
    pallas_call x1, Pallas kernels, call_prepare(): pl.pallas_call(functools.partial(prepare_kernel, len(slices)), out_shape=...  87.6 us
    pallas_call x2, Pallas kernels, call_attend_backward(): pl.pallas_call(gated(section, functools.partial(attend_backward, section...  27.6 us
    pallas_call x1, Pallas kernels, call_attend_forward(): pl.pallas_call(gated(section, attend_forward), out_shape=out_shape, in_sp...  12 us
  transfers between devices with their start and end apart: 1, of which 0 were waited for; matrix products, arithmetic and copies ran while one was open for 0% of the time, Pallas kernels for 16%

profile of v7, /device:TPU:11, one launch (start us, length us, event | category | flops | bytes accessed | tf_op | source)
XLA Modules:
  0.0 562.2 jit_solution(7498438641759668138)
XLA Ops:
  0.7 0.7 convert_element_type.4
  1.3 1.4 fusion.2.allowed_ref.refs_5_.refs_9_
  2.7 0.3 fusion.3
  3.0 0.8 pad_maximum_fusion
  3.8 163.6 %weights.1 = (bf16[2048,3072]{1,0:T(8,128)(2,1)}, bf16[2048,2048]{1,0:T(8,128)(2,1)}, bf16[2048,4096]{1,0:T(8,128)(2,1)}, f32[128,2048]{1,0:T(8,128)}, bf16[128,...) custom-call(bf16[512,3072]{1,0:T(8,128)(2,1)} %bitcast.23, bf16[512,2048]{1,0:T(8,128)(2,1)} %bitcast.24, ...), custom_call_target="tpu_custom_call" | custom-call | tf_op jit(solution)/shard_map/weights/pallas_call | solution.py:993
  167.4 45.9 %feed_forward.2 = (bf16[128,2048]{1,0:T(8,128)(2,1)}, bf16[512,2048]{1,0:T(8,128)(2,1)}, bf16[512,4096]{1,0:T(8,128)(2,1)}, bf16[4,128,2048]{2,1,0:T(8,128)(2,1)...) custom-call(bf16[128,2048]{1,0:T(8,128)(2,1)} %get-tuple-element.76.refs_0_.refs_2_, ...), custom_call_target="tpu_custom_call" | custom-call | tf_op jit(solution)/shard_map/feed_forward/pallas_call | solution.py:794
  213.4 12.0 %attend_forward.1 = (f32[128,2048]{1,0:T(8,128)}, bf16[128,2048]{1,0:T(8,128)(2,1)}, bf16[128,3072]{1,0:T(8,128)(2,1)}, bf16[2,2048,128]{2,1,0:T(8,128)(2,1)}) custom-call(bf16[128,2048]{1,0:T(8,128)(2,1)} %get-tuple-element.63.refs_0_.refs_3_, f32[1,2048]{1,0:T(1,128)} %refs_5_.3, f32[1,2048]{1,0:T(1,128)} %refs_6_.3, ...), custom_call_target="tpu_custom_call" | custom-call | tf_op jit(solution)/shard_map/attend_forward/pallas_call | solution.py:316
  225.4 32.7 %feed_forward.3 = (bf16[128,2048]{1,0:T(8,128)(2,1)}, bf16[512,2048]{1,0:T(8,128)(2,1)}, bf16[512,4096]{1,0:T(8,128)(2,1)}, bf16[4,128,2048]{2,1,0:T(8,128)(2,1)}, bf16[128,2048]{1,0:T(8,128)(2,1)}) custom-call(bf16[128,2048]{1,0:T(8,128)(2,1)} %get-tuple-element.77.refs_0_.refs_3_, f32[128,2048]{1,0:T(8,128)} %get-tuple-element.67.refs_1_.refs_2_, ...), custom_call_target="tpu_custom_call" | custom-call | tf_op jit(solution)/shard_map/feed_forward/pallas_call | solution.py:794
  258.1 39.2 %feed_backward.2 = (f32[128,2048]{1,0:T(8,128)}, bf16[512,2048]{1,0:T(8,128)(2,1)}, bf16[4,128,2048]{2,1,0:T(8,128)(2,1)}) custom-call(bf16[128,2048]{1,0:T(8,128)(2,1)} %refs_7_.1, bf16[512,4096]{1,0:T(8,128)(2,1)} %get-tuple-element.69.refs_1_, bf16[2048,2048]{1,0:T(8,128)(2,1)} %bitcast.18, bf16[2048,4096]{1,0:T(8,128)(2,1)} %get-tuple-element.61.refs_2_.refs_3_.gate_up_hbm), custom_call_target="tpu_custom_call" | custom-call | tf_op jit(solution)/shard_map/feed_backward/pallas_call | solution.py:794
  297.3 23.5 %attend_backward.2 = (f32[128,2048]{1,0:T(8,128)}, bf16[128,2048]{1,0:T(8,128)(2,1)}, bf16[128,3072]{1,0:T(8,128)(2,1)}, f32[2,2048]{1,0:T(2,128)}, bf16[4,512,512]{2,1,0:T(8,128)(2,1)}) custom-call(f32[128,2048]{1,0:T(8,128)} %get-tuple-element.70.refs_0_, bf16[128,2048]{1,0:T(8,128)(2,1)} %refs_7_.1, f32[128,2048]{1,0:T(8,128)} %get-tuple-element.67.refs_1_.refs_2_, ...), custom_call_target="tpu_custom_call" | custom-call | tf_op jit(solution)/shard_map/attend_backward/pallas_call | solution.py:333
  320.9 1.5 collective-permute-start
  322.4 0.0 copy-start.6
  322.4 0.0 copy-start.7
  322.4 87.6 %prepare.1 = (bf16[4,512,2048]{2,1,0:T(8,128)(2,1)}, bf16[2048,4096]{1,0:T(8,128)(2,1)}, bf16[512,2048]{1,0:T(8,128)(2,1)}, bf16[512,2048]{1,0:T(8,128)(2,1)}) custom-call(bf16[2048,4096]{1,0:T(8,128)(2,1)} %get-tuple-element.61.refs_2_.refs_3_.gate_up_hbm, bf16[512,2048]{1,0:T(8,128)(2,1)} %get-tuple-element.74.refs_0_, ...), custom_call_target="tpu_custom_call" | custom-call | tf_op jit(solution)/shard_map/prepare/pallas_call | solution.py:1856
  410.0 0.0 copy-done.6
  410.0 0.0 copy-done.7
  410.0 0.9 select_bitcast_fusion.1
  410.8 0.0 collective-permute-done.refs_0_.refs_1_.refs_6_
  410.8 0.0 copy-start
  410.8 0.8 copy-done
  411.6 2.8 feed_backward.3
  414.4 4.1 attend_backward.3
  418.5 129.3 %weight_grads.1 = (bf16[128,16384]{1,0:T(8,128)(2,1)}, f32[512,2048]{1,0:T(8,128)}, f32[128,3072]{1,0:T(8,128)}, f32[128,2048]{1,0:T(8,128)}, f32[2,2048]{1,0:T(...) custom-call(bf16[512,2048]{1,0:T(8,128)(2,1)} %get-tuple-element.89.left_rows_ref, ...), custom_call_target="tpu_custom_call" | custom-call | tf_op jit(solution)/shard_map/weight_grads/pallas_call | solution.py:1598
  547.8 1.4 fusion.4
  549.2 0.0 copy-start.3
  549.2 0.0 copy-start.4
  549.2 6.6 %bitcast_convert_fusion = f32[1,128,16384]{2,1,0:T(8,128)} fusion(bf16[128,16384]{1,0:T(8,128)(2,1)} %get-tuple-element.108), kind=kLoop, calls=%fused_computation | loop fusion | flops 2097152 | bytes 12582912 | tf_op jit(solution)/shard_map/broadcast_in_dim | solution.py:1973
  555.8 0.0 copy-start.2
  555.8 0.0 copy-start.5
  555.8 0.0 copy-done.3
  555.8 0.0 copy-done.4
  555.8 0.0 copy-start.1
  555.8 1.1 select_bitcast_fusion
  556.9 0.7 copy-done.2
  557.6 1.1 copy.21
  558.7 0.0 copy-done.5
  558.7 1.0 copy.22
  559.7 0.0 copy-done.1
  559.7 2.0 copy.23
  (2 shorter events, 0.0 us)
Async XLA Ops:
  320.9 90.0 %collective-permute-start = (bf16[128,2048]{1,0:T(8,128)(2,1)}, bf16[128,2048]{1,0:T(8,128)(2,1)S(1)}, u32[]{:S(2)}, u32[]{:S(2)}) collective-permute-start(bf16[128,2048]{1,0:T(8,128)(2,1)} %get-tuple-element.73), channel_id=1, source_target_pairs={{16,0},{17,1},{18,2},{19,3},{20,4},{21,5},{22,6},{23,7},{24,8},{25... | collective-permute-start | bytes 1572872 | tf_op jit(solution)/shard_map/ppermute | solution.py:1950
  322.4 87.6 %copy-start.6 = (bf16[128,2048]{1,0:T(8,128)(2,1)S(1)}, bf16[128,2048]{1,0:T(8,128)(2,1)}, u32[]{:S(2)}) copy-start(bf16[128,2048]{1,0:T(8,128)(2,1)} %get-tuple-element.62) | copy-start | bytes 1572868
  322.4 87.6 %copy-start.7 = (bf16[128,2048]{1,0:T(8,128)(2,1)S(1)}, bf16[128,2048]{1,0:T(8,128)(2,1)}, u32[]{:S(2)}) copy-start(bf16[128,2048]{1,0:T(8,128)(2,1)} %get-tuple-element.68) | copy-start | bytes 1572868
  410.8 0.8 copy-start
  549.2 6.6 %copy-start.3 = (f32[128,2048]{1,0:T(8,128)S(1)}, f32[128,2048]{1,0:T(8,128)}, u32[]{:S(2)}) copy-start(f32[128,2048]{1,0:T(8,128)} %get-tuple-element.88) | copy-start | bytes 3145732
  549.2 6.6 %copy-start.4 = (f32[128,2048]{1,0:T(8,128)S(1)}, f32[128,2048]{1,0:T(8,128)}, u32[]{:S(2)}) copy-start(f32[128,2048]{1,0:T(8,128)} %get-tuple-element.87) | copy-start | bytes 3145732
  555.8 1.8 copy-start.2
  555.8 2.9 copy-start.5
  555.8 3.9 copy-start.1

commit v8 on v7

--- a/solution.py
+++ b/solution.py
@@ -398,7 +398,7 @@
 
 def feed_kernel(backward, rows, target, wide, *refs):
     if backward:
-        (mine_ref, gate_up_hbm, first_hbm, second_hbm, result_ref, all_hbm, others_hbm,
+        (mine_ref, gate_up_hbm, odd_hbm, first_hbm, second_hbm, result_ref, all_hbm, others_hbm, ahead_hbm,
          mid_ref, all_ref, gate_up_ref, first_ref, second_ref, part_ref, take_ref, sent_ref, land_ref, own_ref,
          own_take_ref, load_sems, keep_sems, hold_sems, send_sems, recv_sems) = refs
     else:
@@ -492,6 +492,16 @@
     ]
     for copy in spread_copies:
         copy.start()
+
+    def ahead_rows(owner):
+        return ahead_hbm.at[pl.ds(pl.multiple_of(owner * rows, rows), rows)]
+
+    if wide:
+        next_rows = odd_hbm.at[lax.rem(lax.axis_index("replica") + 1, lax.axis_size("replica"))]
+        ahead_base = base + lax.axis_size("replica")
+        ahead_over = remote(next_rows, ahead_rows(shard), ahead_base, across)
+        ahead_direct = remote(next_rows, ahead_rows(shard), ahead_base + 1, beside)
+        ahead_relay = remote(ahead_rows(across), ahead_rows(across), ahead_base + 2, beside)
 
     def first_product(start, count, waits):
         span = pl.ds(pl.multiple_of(start, count), count)
@@ -577,6 +587,9 @@
         if parts == 1:
             for late in range(2):
                 relay(late).wait_recv()
+            if wide:
+                ahead_over.start()
+                ahead_direct.start()
         else:
             arrive(part)
             relay(part).wait_recv()
@@ -632,6 +645,9 @@
         return carry
 
     lax.fori_loop(0, spans, own_step, 0)
+    if wide:
+        ahead_over.wait_recv()
+        ahead_relay.start()
     if not backward:
         load_extra[0].wait()
     for at in range(spans):
@@ -656,6 +672,10 @@
         beside_copies[part].wait_send()
         across_copy(part).wait_send()
         relay(part).wait_send()
+    if wide:
+        ahead_direct.wait()
+        ahead_relay.wait()
+        ahead_over.wait_send()
     for copy in spread_copies + stores:
         copy.wait()
     if target is not None:
@@ -760,10 +780,12 @@
         jax.ShapeDtypeStruct((every, width), BF),
         jax.ShapeDtypeStruct((replicas, rows, width), BF),
     ]
-    if not backward:
+    if backward:
+        out_shape.append(jax.ShapeDtypeStruct((every, width), BF))
+    else:
         out_shape.insert(2, jax.ShapeDtypeStruct((every, 2 * ff), BF))
         out_shape.append(jax.ShapeDtypeStruct((rows, width), BF))
-    copies = 6 + (3 * parts + 1) * spans + replicas
+    copies = 6 + (3 * parts + 1) * spans + replicas + 3
     piece = pltpu.VMEM((parts, spans, piece_rows, span_cols), BF)
     scratch = [
         pltpu.VMEM((every, 2 * ff if backward else ff), BF),
@@ -1644,7 +1666,7 @@
     return [0] + list(range(1, replicas, 2)) + list(range(2, replicas, 2))
 
 
-def prepare_kernel(sections, gate_up_hbm, *refs):
+def prepare_kernel(sections, gate_up_hbm, ahead_hbm, *refs):
     slices, normed_two, odd = [refs[at * sections : (at + 1) * sections] for at in range(3)]
     (gathered_hbm, gate_up_all_hbm, hidden_hbm, left_rows_ref,
      normed_two_ref, weight_ref, block_ref, gate_up_ref, hidden_ref, turned_ref,
@@ -1678,6 +1700,14 @@
     def landing(turn, who):
         return gathered_hbm.at[turn, pl.ds(pl.multiple_of(who * rows, rows), rows)]
 
+    behind = lax.axis_index("section") < sections - 1
+
+    def fetched(turn, body):
+        if turn == 1:
+            pl.when(behind)(body)
+        else:
+            body()
+
     def own_sources(turn):
         if turn % 2:
             return [source.at[lax.rem(replica + turn, replicas)] for source in odd]
@@ -1694,6 +1724,8 @@
             from_replica(turn).wait_recv()
         copies = [(over(turn, source), direct(turn, source)) for source in own_sources(turn)]
         for section, pair in enumerate(copies):
+            if turn == 1 and section == sections - 1:
+                continue
             if len(copies) == 1:
                 for copy in pair:
                     copy.start()
@@ -1717,6 +1749,9 @@
         copies = []
         for at, owner in enumerate(peers + (shard,)):
             sources = own_sources(turn) if at == 3 else [landing(turn, owner)]
+            if turn == 1 and at < 3:
+                rows_at = ahead_hbm.at[pl.ds(pl.multiple_of(owner * rows, rows), rows)]
+                sources = sources * (sections - 1) + [rows_at]
             place = block_ref.at[slot, pl.ds(pl.multiple_of(owner * rows, rows), rows)]
             copies.append([pltpu.make_async_copy(source, place, block_sems.at[slot, at]) for source in sources])
         return copies
@@ -1793,8 +1828,12 @@
         lax.fori_loop(0, steps, products, 0)
         store_block(turn, slot).start()
         if later is not None:
-            over(later).wait_recv()
-            relay(later).start()
+
+            def pass_on(later=later):
+                over(later).wait_recv()
+                relay(later).start()
+
+            fetched(later, pass_on)
 
         @pl.when(shard == owner)
         def _(at=at, turn=turn, slot=slot):
@@ -1816,8 +1855,12 @@
         slice_cols = pl.ds(pl.multiple_of(replica * slice_rows, slice_rows), slice_rows)
         left_rows_ref[:, tokens(turn)] = block_ref[slot, :, slice_cols].T
         if later is not None:
-            direct(later).wait_recv()
-            relay(later).wait_recv()
+
+            def arrive(later=later):
+                direct(later).wait_recv()
+                relay(later).wait_recv()
+
+            fetched(later, arrive)
             start_block(later, 1 - slot)
 
     for at in range(max(0, replicas - 2), replicas):
@@ -1837,14 +1880,18 @@
                 hand_hidden(turn, 0, peer).wait_recv()
 
         if turn:
-            over(turn).wait_send()
-            direct(turn).wait_send()
-            relay(turn).wait_send()
+
+            def leave(turn=turn):
+                over(turn).wait_send()
+                direct(turn).wait_send()
+                relay(turn).wait_send()
+
+            fetched(turn, leave)
         if turn in evens:
             from_replica(turn).wait_send()
 
 
-def call_prepare(normed_two, gate_up_part, slices, odd, collective):
+def call_prepare(normed_two, gate_up_part, slices, odd, ahead, collective):
     rows, width = normed_two[0].shape
     shards, replicas = lax.axis_size("shard"), lax.axis_size("replica")
     part = gate_up_part.shape[1] // 2
@@ -1861,7 +1908,7 @@
             jax.ShapeDtypeStruct((ff_rows, replicas * every), BF),
             jax.ShapeDtypeStruct((slice_rows, replicas * every), BF),
         ],
-        in_specs=[anywhere] * (1 + 3 * len(slices)),
+        in_specs=[anywhere] * (2 + 3 * len(slices)),
         out_specs=[anywhere] * 3 + [vmem],
         scratch_shapes=[
             pltpu.VMEM((rows, width), BF),
@@ -1881,7 +1928,7 @@
             collective_id=collective, has_side_effects=True, vmem_limit_bytes=VMEM_LIMIT
         ),
         name="prepare",
-    )(gate_up_part, *slices, *normed_two, *odd)
+    )(gate_up_part, ahead, *slices, *normed_two, *odd)
     return outs[1:]
 
 
@@ -1936,8 +1983,8 @@
     upstream = cotangent
     for section in reversed(range(sections)):
         state, middle, rotated, gate_up = forward[section][:4]
-        grad_normed_two, upstream_slice, odd = call_feed(
-            section, True, (upstream, gate_up, down_part, gate_up_part), 8 + sections + section
+        grad_normed_two, upstream_slice, odd, ahead = call_feed(
+            section, True, (upstream, gate_up, normed_two_odd[section], down_part, gate_up_part), 8 + sections + section
         )
         grad_in, grad_low, grad_projected, gains, grad_branch = call_attend_backward(
             section, 8 + 2 * sections + section, grad_normed_two, upstream, middle, state, rotated,
@@ -1950,7 +1997,7 @@
             upstream = lax.ppermute(grad_low, "section", down_steps)
         if section == sections - 1:
             gate_up_all, hidden_rows, left_rows = call_prepare(
-                normed_two, gate_up_part, slices, normed_two_odd, 6
+                normed_two, gate_up_part, slices, normed_two_odd, ahead, 6
             )
             upstream, gate_up_all, left_rows, hidden_rows = lax.optimization_barrier(
                 (upstream, gate_up_all, left_rows, hidden_rows)

time: 571 us -> 565 us (0.989)
  Pallas kernels: 541 us -> 534 us
    pallas_call x1, Pallas kernels: 87.6 us -> 76.3 us  [call_prepare(): pl.pallas_call(functools.partial(prepare_kernel, len(slices)), out_shape=...]
  transfers between devices with their start and end apart: 1 -> 1, of which waited for: 0 -> 0; matrix products, arithmetic and copies ran while one was open for 0% -> 0% of each run, Pallas kernels for 16% -> 14%
where the time goes in v8:
time: 565 us; the launch traced here: 556 us
  Pallas kernels  534 us (95%)
  other arithmetic  11.7 us (2%)
  local copies, waits for them, and re-layouts  7.25 us (1%)
    pallas_call x1, Pallas kernels, call_weights(): pl.pallas_call(weights_kernel, out_shape=[jax.ShapeDtypeStruct((shards *...  164 us
    pallas_call x1, Pallas kernels, call_weight_grads(): pl.pallas_call(functools.partial(weight_grads_kernel, sections), out_shap...  129 us
    pallas_call x4, Pallas kernels, call_feed(): pl.pallas_call(gated(section, functools.partial(feed_kernel, True, rows,...  125 us
    pallas_call x1, Pallas kernels, call_prepare(): pl.pallas_call(functools.partial(prepare_kernel, len(slices)), out_shape=...  76.3 us
    pallas_call x2, Pallas kernels, call_attend_backward(): pl.pallas_call(gated(section, functools.partial(attend_backward, section...  28 us
    pallas_call x1, Pallas kernels, call_attend_forward(): pl.pallas_call(gated(section, attend_forward), out_shape=out_shape, in_sp...  12.1 us
  transfers between devices with their start and end apart: 1, of which 0 were waited for; matrix products, arithmetic and copies ran while one was open for 0% of the time, Pallas kernels for 14%

profile of v8, /device:TPU:11, one launch (start us, length us, event | category | flops | bytes accessed | tf_op | source)
XLA Modules:
  0.0 555.6 jit_solution(18365931211715586357)
XLA Ops:
  0.7 0.7 convert_element_type.4
  1.3 1.4 fusion.2.allowed_ref.refs_5_.refs_9_
  2.7 0.3 fusion.3
  3.0 0.8 pad_maximum_fusion
  3.8 163.6 %weights.1 = (bf16[2048,3072]{1,0:T(8,128)(2,1)}, bf16[2048,2048]{1,0:T(8,128)(2,1)}, bf16[2048,4096]{1,0:T(8,128)(2,1)}, f32[128,2048]{1,0:T(8,128)}, bf16[128,...) custom-call(bf16[512,3072]{1,0:T(8,128)(2,1)} %bitcast.23, bf16[512,2048]{1,0:T(8,128)(2,1)} %bitcast.24, ...), custom_call_target="tpu_custom_call" | custom-call | tf_op jit(solution)/shard_map/weights/pallas_call | solution.py:1015
  167.5 46.0 %feed_forward.2 = (bf16[128,2048]{1,0:T(8,128)(2,1)}, bf16[512,2048]{1,0:T(8,128)(2,1)}, bf16[512,4096]{1,0:T(8,128)(2,1)}, bf16[4,128,2048]{2,1,0:T(8,128)(2,1)...) custom-call(bf16[128,2048]{1,0:T(8,128)(2,1)} %get-tuple-element.79.refs_0_.refs_2_, ...), custom_call_target="tpu_custom_call" | custom-call | tf_op jit(solution)/shard_map/feed_forward/pallas_call | solution.py:816
  213.5 12.1 %attend_forward.1 = (f32[128,2048]{1,0:T(8,128)}, bf16[128,2048]{1,0:T(8,128)(2,1)}, bf16[128,3072]{1,0:T(8,128)(2,1)}, bf16[2,2048,128]{2,1,0:T(8,128)(2,1)}) custom-call(bf16[128,2048]{1,0:T(8,128)(2,1)} %get-tuple-element.64.refs_0_.refs_3_, f32[1,2048]{1,0:T(1,128)} %refs_5_.3, f32[1,2048]{1,0:T(1,128)} %refs_6_.3, ...), custom_call_target="tpu_custom_call" | custom-call | tf_op jit(solution)/shard_map/attend_forward/pallas_call | solution.py:316
  225.5 32.7 %feed_forward.3 = (bf16[128,2048]{1,0:T(8,128)(2,1)}, bf16[512,2048]{1,0:T(8,128)(2,1)}, bf16[512,4096]{1,0:T(8,128)(2,1)}, bf16[4,128,2048]{2,1,0:T(8,128)(2,1)}, bf16[128,2048]{1,0:T(8,128)(2,1)}) custom-call(bf16[128,2048]{1,0:T(8,128)(2,1)} %get-tuple-element.80.refs_0_.refs_3_, f32[128,2048]{1,0:T(8,128)} %get-tuple-element.68.refs_1_.refs_2_, ...), custom_call_target="tpu_custom_call" | custom-call | tf_op jit(solution)/shard_map/feed_forward/pallas_call | solution.py:816
  258.2 43.4 %feed_backward.2 = (f32[128,2048]{1,0:T(8,128)}, bf16[512,2048]{1,0:T(8,128)(2,1)}, bf16[4,128,2048]{2,1,0:T(8,128)(2,1)}, bf16[512,2048]{1,0:T(8,128)(2,1)}) custom-call(bf16[128,2048]{1,0:T(8,128)(2,1)} %refs_7_.1, bf16[512,4096]{1,0:T(8,128)(2,1)} %get-tuple-element.70.refs_1_, bf16[4,128,2048]{2,1,0:T(8,128)(2,1)} %get-tuple-element.71.refs_2_.refs_5_, ...), custom_call_target="tpu_custom_call" | custom-call | tf_op jit(solution)/shard_map/feed_backward/pallas_call | solution.py:816
  301.6 23.9 %attend_backward.2 = (f32[128,2048]{1,0:T(8,128)}, bf16[128,2048]{1,0:T(8,128)(2,1)}, bf16[128,3072]{1,0:T(8,128)(2,1)}, f32[2,2048]{1,0:T(2,128)}, bf16[4,512,512]{2,1,0:T(8,128)(2,1)}) custom-call(f32[128,2048]{1,0:T(8,128)} %get-tuple-element.72.refs_0_, bf16[128,2048]{1,0:T(8,128)(2,1)} %refs_7_.1, f32[128,2048]{1,0:T(8,128)} %get-tuple-element.68.refs_1_.refs_2_, ...), custom_call_target="tpu_custom_call" | custom-call | tf_op jit(solution)/shard_map/attend_backward/pallas_call | solution.py:333
  325.5 1.5 collective-permute-start
  327.0 0.0 copy-start.6
  327.0 0.0 copy-start.7
  327.0 76.3 %prepare.1 = (bf16[4,512,2048]{2,1,0:T(8,128)(2,1)}, bf16[2048,4096]{1,0:T(8,128)(2,1)}, bf16[512,2048]{1,0:T(8,128)(2,1)}, bf16[512,2048]{1,0:T(8,128)(2,1)}) custom-call(bf16[2048,4096]{1,0:T(8,128)(2,1)} %get-tuple-element.62.refs_2_.refs_4_.gate_up_hbm, bf16[512,2048]{1,0:T(8,128)(2,1)} %get-tuple-element.76.ahead_hbm, ...), custom_call_target="tpu_custom_call" | custom-call | tf_op jit(solution)/shard_map/prepare/pallas_call | solution.py:1903
  403.4 0.0 copy-done.6
  403.4 0.0 copy-done.7
  403.4 0.9 select_bitcast_fusion.1
  404.2 0.0 collective-permute-done.refs_0_.refs_1_.refs_6_
  404.3 0.0 copy-start
  404.3 0.8 copy-done
  405.0 2.8 feed_backward.3
  407.9 4.1 attend_backward.3
  412.0 129.1 %weight_grads.1 = (bf16[128,16384]{1,0:T(8,128)(2,1)}, f32[512,2048]{1,0:T(8,128)}, f32[128,3072]{1,0:T(8,128)}, f32[128,2048]{1,0:T(8,128)}, f32[2,2048]{1,0:T(...) custom-call(bf16[512,2048]{1,0:T(8,128)(2,1)} %get-tuple-element.91.left_rows_ref, ...), custom_call_target="tpu_custom_call" | custom-call | tf_op jit(solution)/shard_map/weight_grads/pallas_call | solution.py:1620
  541.0 1.4 fusion.4
  542.4 0.0 copy-start.3
  542.4 0.0 copy-start.4
  542.4 6.6 %bitcast_convert_fusion = f32[1,128,16384]{2,1,0:T(8,128)} fusion(bf16[128,16384]{1,0:T(8,128)(2,1)} %get-tuple-element.110), kind=kLoop, calls=%fused_computation | loop fusion | flops 2097152 | bytes 12582912 | tf_op jit(solution)/shard_map/broadcast_in_dim | solution.py:2020
  549.0 0.0 copy-start.2
  549.0 0.0 copy-done.3
  549.0 0.0 copy-done.4
  549.0 0.0 copy-start.5
  549.0 1.1 select_bitcast_fusion
  550.1 0.0 copy-start.1
  550.1 0.7 copy-done.2
  550.8 1.1 copy.21
  552.0 0.0 copy-done.5
  552.0 1.0 copy.22
  552.9 0.2 copy-done.1
  553.1 2.0 copy.23
  (2 shorter events, 0.0 us)
Async XLA Ops:
  325.5 78.7 %collective-permute-start = (bf16[128,2048]{1,0:T(8,128)(2,1)}, bf16[128,2048]{1,0:T(8,128)(2,1)S(1)}, u32[]{:S(2)}, u32[]{:S(2)}) collective-permute-start(bf16[128,2048]{1,0:T(8,128)(2,1)} %get-tuple-element.75), channel_id=1, source_target_pairs={{16,0},{17,1},{18,2},{19,3},{20,4},{21,5},{22,6},{23,7},{24,8},{25... | collective-permute-start | bytes 1572872 | tf_op jit(solution)/shard_map/ppermute | solution.py:1997
  327.0 76.4 %copy-start.6 = (bf16[128,2048]{1,0:T(8,128)(2,1)S(1)}, bf16[128,2048]{1,0:T(8,128)(2,1)}, u32[]{:S(2)}) copy-start(bf16[128,2048]{1,0:T(8,128)(2,1)} %get-tuple-element.63) | copy-start | bytes 1572868
  327.0 76.4 %copy-start.7 = (bf16[128,2048]{1,0:T(8,128)(2,1)S(1)}, bf16[128,2048]{1,0:T(8,128)(2,1)}, u32[]{:S(2)}) copy-start(bf16[128,2048]{1,0:T(8,128)(2,1)} %get-tuple-element.69) | copy-start | bytes 1572868
  404.3 0.8 copy-start
  542.4 6.6 %copy-start.3 = (f32[128,2048]{1,0:T(8,128)S(1)}, f32[128,2048]{1,0:T(8,128)}, u32[]{:S(2)}) copy-start(f32[128,2048]{1,0:T(8,128)} %get-tuple-element.90) | copy-start | bytes 3145732
  542.4 6.6 %copy-start.4 = (f32[128,2048]{1,0:T(8,128)S(1)}, f32[128,2048]{1,0:T(8,128)}, u32[]{:S(2)}) copy-start(f32[128,2048]{1,0:T(8,128)} %get-tuple-element.89) | copy-start | bytes 3145732
  549.0 1.8 copy-start.2
  549.0 2.9 copy-start.5
  550.1 3.0 copy-start.1

commit v9 on v8

--- a/solution.py
+++ b/solution.py
@@ -885,17 +885,17 @@
 
             own = source.at[span(mine * half + offset, count)]
             pieces.append((own, place, across, True))
-    for offset in range(0, half, 64):
+    for offset in range(0, half, 32):
         for side in range(2):
             for device in (across, diagonal):
 
                 def place(owner, part_of, offset=offset, side=side):
                     return gate_up_part.at[
-                        span(owner["shard"] * rows + part_of * half + offset, 64), pl.ds(side * part, part)
+                        span(owner["shard"] * rows + part_of * half + offset, 32), pl.ds(side * part, part)
                     ]
 
                 own = gate_up_ref.at[
-                    span(mine * half + offset, 64), span(side * ff + device["shard"] * part, part)
+                    span(mine * half + offset, 32), span(side * ff + device["shard"] * part, part)
                 ]
                 pieces.append((own, place, device, False))
     count = len(pieces)
@@ -939,7 +939,7 @@
         copy.start()
         started.append(copy)
 
-    ahead = 4
+    ahead = 6
     for copy in over[:ahead]:
         start(copy)
     for copy in direct:
@@ -1008,7 +1008,7 @@
 def call_weights(qkv_weight, out_weight, gate_up_weight, operands, collective):
     shards = lax.axis_size("shard")
     rows = qkv_weight.shape[0]
-    count = 2 * (rows // 128) + 4 * (rows // 128)
+    count = 2 * (rows // 128) + 8 * (rows // 128)
     out_shape, scratch = attend_shapes(*operands[0].shape, qkv_weight.shape[1])
     vmem = pl.BlockSpec(memory_space=pltpu.VMEM)
     anywhere = pl.BlockSpec(memory_space=pl.ANY)

time: 565 us -> 569 us (level)
  Pallas kernels: 534 us -> 540 us
where the time goes in v9:
time: 569 us; the launch traced here: 561 us
  Pallas kernels  540 us (95%)
  other arithmetic  11.7 us (2%)
  local copies, waits for them, and re-layouts  7.25 us (1%)
    pallas_call x1, Pallas kernels, call_weights(): pl.pallas_call(weights_kernel, out_shape=[jax.ShapeDtypeStruct((shards *...  164 us
    pallas_call x1, Pallas kernels, call_weight_grads(): pl.pallas_call(functools.partial(weight_grads_kernel, sections), out_shap...  130 us
    pallas_call x4, Pallas kernels, call_feed(): pl.pallas_call(gated(section, functools.partial(feed_kernel, True, rows,...  129 us
    pallas_call x1, Pallas kernels, call_prepare(): pl.pallas_call(functools.partial(prepare_kernel, len(slices)), out_shape=...  76.3 us
    pallas_call x2, Pallas kernels, call_attend_backward(): pl.pallas_call(gated(section, functools.partial(attend_backward, section...  28.2 us
    pallas_call x1, Pallas kernels, call_attend_forward(): pl.pallas_call(gated(section, attend_forward), out_shape=out_shape, in_sp...  12 us
  transfers between devices with their start and end apart: 1, of which 0 were waited for; matrix products, arithmetic and copies ran while one was open for 0% of the time, Pallas kernels for 14%

profile of v9, /device:TPU:11, one launch (start us, length us, event | category | flops | bytes accessed | tf_op | source)
XLA Modules:
  0.0 560.9 jit_solution(6440121331062183950)
XLA Ops:
  0.7 0.7 convert_element_type.4
  1.3 1.4 fusion.2.allowed_ref.refs_5_.refs_9_
  2.7 0.3 fusion.3
  3.0 0.8 pad_maximum_fusion
  3.8 164.1 %weights.1 = (bf16[2048,3072]{1,0:T(8,128)(2,1)}, bf16[2048,2048]{1,0:T(8,128)(2,1)}, bf16[2048,4096]{1,0:T(8,128)(2,1)}, f32[128,2048]{1,0:T(8,128)}, bf16[128,...) custom-call(bf16[512,3072]{1,0:T(8,128)(2,1)} %bitcast.23, bf16[512,2048]{1,0:T(8,128)(2,1)} %bitcast.24, ...), custom_call_target="tpu_custom_call" | custom-call | tf_op jit(solution)/shard_map/weights/pallas_call | solution.py:1015
  167.9 49.9 %feed_forward.2 = (bf16[128,2048]{1,0:T(8,128)(2,1)}, bf16[512,2048]{1,0:T(8,128)(2,1)}, bf16[512,4096]{1,0:T(8,128)(2,1)}, bf16[4,128,2048]{2,1,0:T(8,128)(2,1)...) custom-call(bf16[128,2048]{1,0:T(8,128)(2,1)} %get-tuple-element.79.refs_0_.refs_2_, ...), custom_call_target="tpu_custom_call" | custom-call | tf_op jit(solution)/shard_map/feed_forward/pallas_call | solution.py:816
  217.8 12.0 %attend_forward.1 = (f32[128,2048]{1,0:T(8,128)}, bf16[128,2048]{1,0:T(8,128)(2,1)}, bf16[128,3072]{1,0:T(8,128)(2,1)}, bf16[2,2048,128]{2,1,0:T(8,128)(2,1)}) custom-call(bf16[128,2048]{1,0:T(8,128)(2,1)} %get-tuple-element.64.refs_0_.refs_3_, f32[1,2048]{1,0:T(1,128)} %refs_5_.3, f32[1,2048]{1,0:T(1,128)} %refs_6_.3, ...), custom_call_target="tpu_custom_call" | custom-call | tf_op jit(solution)/shard_map/attend_forward/pallas_call | solution.py:316
  229.8 33.0 %feed_forward.3 = (bf16[128,2048]{1,0:T(8,128)(2,1)}, bf16[512,2048]{1,0:T(8,128)(2,1)}, bf16[512,4096]{1,0:T(8,128)(2,1)}, bf16[4,128,2048]{2,1,0:T(8,128)(2,1)}, bf16[128,2048]{1,0:T(8,128)(2,1)}) custom-call(bf16[128,2048]{1,0:T(8,128)(2,1)} %get-tuple-element.80.refs_0_.refs_3_, f32[128,2048]{1,0:T(8,128)} %get-tuple-element.68.refs_1_.refs_2_, ...), custom_call_target="tpu_custom_call" | custom-call | tf_op jit(solution)/shard_map/feed_forward/pallas_call | solution.py:816
  262.8 43.2 %feed_backward.2 = (f32[128,2048]{1,0:T(8,128)}, bf16[512,2048]{1,0:T(8,128)(2,1)}, bf16[4,128,2048]{2,1,0:T(8,128)(2,1)}, bf16[512,2048]{1,0:T(8,128)(2,1)}) custom-call(bf16[128,2048]{1,0:T(8,128)(2,1)} %refs_7_.1, bf16[512,4096]{1,0:T(8,128)(2,1)} %get-tuple-element.70.refs_1_, bf16[4,128,2048]{2,1,0:T(8,128)(2,1)} %get-tuple-element.71.refs_2_.refs_5_, ...), custom_call_target="tpu_custom_call" | custom-call | tf_op jit(solution)/shard_map/feed_backward/pallas_call | solution.py:816
  306.0 24.2 %attend_backward.2 = (f32[128,2048]{1,0:T(8,128)}, bf16[128,2048]{1,0:T(8,128)(2,1)}, bf16[128,3072]{1,0:T(8,128)(2,1)}, f32[2,2048]{1,0:T(2,128)}, bf16[4,512,512]{2,1,0:T(8,128)(2,1)}) custom-call(f32[128,2048]{1,0:T(8,128)} %get-tuple-element.72.refs_0_, bf16[128,2048]{1,0:T(8,128)(2,1)} %refs_7_.1, f32[128,2048]{1,0:T(8,128)} %get-tuple-element.68.refs_1_.refs_2_, ...), custom_call_target="tpu_custom_call" | custom-call | tf_op jit(solution)/shard_map/attend_backward/pallas_call | solution.py:333
  330.3 1.3 collective-permute-start
  331.6 0.0 copy-start.6
  331.6 0.0 copy-start.7
  331.6 76.3 %prepare.1 = (bf16[4,512,2048]{2,1,0:T(8,128)(2,1)}, bf16[2048,4096]{1,0:T(8,128)(2,1)}, bf16[512,2048]{1,0:T(8,128)(2,1)}, bf16[512,2048]{1,0:T(8,128)(2,1)}) custom-call(bf16[2048,4096]{1,0:T(8,128)(2,1)} %get-tuple-element.62.refs_2_.refs_4_.gate_up_hbm, bf16[512,2048]{1,0:T(8,128)(2,1)} %get-tuple-element.76.ahead_hbm, ...), custom_call_target="tpu_custom_call" | custom-call | tf_op jit(solution)/shard_map/prepare/pallas_call | solution.py:1903
  407.9 0.0 copy-done.6
  408.0 0.0 copy-done.7
  408.0 0.9 select_bitcast_fusion.1
  408.8 0.0 collective-permute-done.refs_0_.refs_1_.refs_6_
  408.8 0.0 copy-start
  408.8 0.8 copy-done
  409.6 2.8 feed_backward.3
  412.4 4.0 attend_backward.3
  416.5 130.0 %weight_grads.1 = (bf16[128,16384]{1,0:T(8,128)(2,1)}, f32[512,2048]{1,0:T(8,128)}, f32[128,3072]{1,0:T(8,128)}, f32[128,2048]{1,0:T(8,128)}, f32[2,2048]{1,0:T(...) custom-call(bf16[512,2048]{1,0:T(8,128)(2,1)} %get-tuple-element.91.left_rows_ref, ...), custom_call_target="tpu_custom_call" | custom-call | tf_op jit(solution)/shard_map/weight_grads/pallas_call | solution.py:1620
  546.5 1.4 fusion.4
  547.9 0.0 copy-start.3
  547.9 0.0 copy-start.4
  547.9 6.6 %bitcast_convert_fusion = f32[1,128,16384]{2,1,0:T(8,128)} fusion(bf16[128,16384]{1,0:T(8,128)(2,1)} %get-tuple-element.110), kind=kLoop, calls=%fused_computation | loop fusion | flops 2097152 | bytes 12582912 | tf_op jit(solution)/shard_map/broadcast_in_dim | solution.py:2020
  554.5 0.0 copy-start.2
  554.5 0.0 copy-done.3
  554.5 0.0 copy-done.4
  554.5 0.0 copy-start.5
  554.5 1.1 select_bitcast_fusion
  555.6 0.0 copy-start.1
  555.6 0.7 copy-done.2
  556.3 1.1 copy.21
  557.4 0.0 copy-done.5
  557.4 1.0 copy.22
  558.4 0.2 copy-done.1
  558.6 2.0 copy.23
  (2 shorter events, 0.0 us)
Async XLA Ops:
  330.3 78.6 %collective-permute-start = (bf16[128,2048]{1,0:T(8,128)(2,1)}, bf16[128,2048]{1,0:T(8,128)(2,1)S(1)}, u32[]{:S(2)}, u32[]{:S(2)}) collective-permute-start(bf16[128,2048]{1,0:T(8,128)(2,1)} %get-tuple-element.75), channel_id=1, source_target_pairs={{16,0},{17,1},{18,2},{19,3},{20,4},{21,5},{22,6},{23,7},{24,8},{25... | collective-permute-start | bytes 1572872 | tf_op jit(solution)/shard_map/ppermute | solution.py:1997
  331.6 76.4 %copy-start.6 = (bf16[128,2048]{1,0:T(8,128)(2,1)S(1)}, bf16[128,2048]{1,0:T(8,128)(2,1)}, u32[]{:S(2)}) copy-start(bf16[128,2048]{1,0:T(8,128)(2,1)} %get-tuple-element.63) | copy-start | bytes 1572868
  331.6 76.4 %copy-start.7 = (bf16[128,2048]{1,0:T(8,128)(2,1)S(1)}, bf16[128,2048]{1,0:T(8,128)(2,1)}, u32[]{:S(2)}) copy-start(bf16[128,2048]{1,0:T(8,128)(2,1)} %get-tuple-element.69) | copy-start | bytes 1572868
  408.8 0.8 copy-start
  547.9 6.6 %copy-start.3 = (f32[128,2048]{1,0:T(8,128)S(1)}, f32[128,2048]{1,0:T(8,128)}, u32[]{:S(2)}) copy-start(f32[128,2048]{1,0:T(8,128)} %get-tuple-element.90) | copy-start | bytes 3145732
  547.9 6.6 %copy-start.4 = (f32[128,2048]{1,0:T(8,128)S(1)}, f32[128,2048]{1,0:T(8,128)}, u32[]{:S(2)}) copy-start(f32[128,2048]{1,0:T(8,128)} %get-tuple-element.89) | copy-start | bytes 3145732
  554.5 1.8 copy-start.2
  554.5 2.9 copy-start.5
  555.6 3.0 copy-start.1
